TPU v7x, 32 devices: a whole 2x2x4 slice. The times are simulated.
32 devices in a mesh: pipe: 2 (over core), grp: 4 (over y, x), dp: 4 (over z).
Axes of the slice: x: 2, y: 2, z: 4, core: 2. Of those that a mesh axis runs over, the one named last changes fastest.
Arguments:
- token_ids: int32 [64, 512], P(('grp', 'dp')), may hold values from 0 to 30521
- lengths: int32 [64], P(('grp', 'dp')), may hold values from 1 to 512, as said below
- masked_at: int32 [64, 64], P(('grp', 'dp')), may hold values from 0 to 511, as said below
- labels: int32 [64, 64], P(('grp', 'dp')), may hold values from 0 to 30521
- word_table: float32 [30720, 1024], P(('pipe', 'grp', 'dp')), may hold values from -0.36 to 0.36
- word_first: float32 [30720, 1024], P(('pipe', 'grp', 'dp')), may hold values from -1.9073486e-06 to 1.9073486e-06
- word_second: float32 [30720, 1024], P(('pipe', 'grp', 'dp')), may hold values from 8.798889e-15 to 3.5195557e-14
- pos_table: float32 [512, 1024], P(None, ('pipe', 'grp', 'dp')), may hold values from -0.36 to 0.36
- pos_first: float32 [512, 1024], P(None, ('pipe', 'grp', 'dp')), may hold values from -1.9073486e-06 to 1.9073486e-06
- pos_second: float32 [512, 1024], P(None, ('pipe', 'grp', 'dp')), may hold values from 8.798889e-15 to 3.5195557e-14
- qkv_weight: float32 [1024, 3072], P(('pipe', 'grp', 'dp')), may hold values from -0.1875 to 0.1875
- qkv_first: float32 [1024, 3072], P(('pipe', 'grp', 'dp')), may hold values from -1.9073486e-06 to 1.9073486e-06
- qkv_second: float32 [1024, 3072], P(('pipe', 'grp', 'dp')), may hold values from 8.798889e-15 to 3.5195557e-14
- square_weight: float32 [2, 1024, 1024], P(None, ('pipe', 'grp', 'dp')), may hold values from -0.5 to 0.5
- square_first: float32 [2, 1024, 1024], P(None, ('pipe', 'grp', 'dp')), may hold values from -1.9073486e-06 to 1.9073486e-06
- square_second: float32 [2, 1024, 1024], P(None, ('pipe', 'grp', 'dp')), may hold values from 8.798889e-15 to 3.5195557e-14
- up_weight: float32 [1024, 4096], P(('pipe', 'grp', 'dp')), may hold values from -0.1875 to 0.1875
- up_first: float32 [1024, 4096], P(('pipe', 'grp', 'dp')), may hold values from -1.9073486e-06 to 1.9073486e-06
- up_second: float32 [1024, 4096], P(('pipe', 'grp', 'dp')), may hold values from 8.798889e-15 to 3.5195557e-14
- down_weight: float32 [4096, 1024], P(('pipe', 'grp', 'dp')), may hold values from -0.09375 to 0.09375
- down_first: float32 [4096, 1024], P(('pipe', 'grp', 'dp')), may hold values from -1.9073486e-06 to 1.9073486e-06
- down_second: float32 [4096, 1024], P(('pipe', 'grp', 'dp')), may hold values from 8.798889e-15 to 3.5195557e-14
- vec_table: float32 [19, 1024], P(None, ('pipe', 'grp', 'dp')), may hold values from -1.9 to 1.9
- vec_first: float32 [19, 1024], P(None, ('pipe', 'grp', 'dp')), may hold values from -1.9073486e-06 to 1.9073486e-06
- vec_second: float32 [19, 1024], P(None, ('pipe', 'grp', 'dp')), may hold values from 8.798889e-15 to 3.5195557e-14
- head_bias: float32 [30522], replicated, may hold values from -3 to 3
- bias_first: float32 [30522], replicated, may hold values from -1.9073486e-06 to 1.9073486e-06
- bias_second: float32 [30522], replicated, may hold values from 8.798889e-15 to 3.5195557e-14
Outputs:
- word_new: float32 [30720, 1024], P(('pipe', 'grp', 'dp'))
- word_first_new: float32 [30720, 1024], P(('pipe', 'grp', 'dp'))
- word_second_new: float32 [30720, 1024], P(('pipe', 'grp', 'dp'))
- pos_new: float32 [512, 1024], P(None, ('pipe', 'grp', 'dp'))
- pos_first_new: float32 [512, 1024], P(None, ('pipe', 'grp', 'dp'))
- pos_second_new: float32 [512, 1024], P(None, ('pipe', 'grp', 'dp'))
- qkv_new: float32 [1024, 3072], P(('pipe', 'grp', 'dp'))
- qkv_first_new: float32 [1024, 3072], P(('pipe', 'grp', 'dp'))
- qkv_second_new: float32 [1024, 3072], P(('pipe', 'grp', 'dp'))
- square_new: float32 [2, 1024, 1024], P(None, ('pipe', 'grp', 'dp'))
- square_first_new: float32 [2, 1024, 1024], P(None, ('pipe', 'grp', 'dp'))
- square_second_new: float32 [2, 1024, 1024], P(None, ('pipe', 'grp', 'dp'))
- up_new: float32 [1024, 4096], P(('pipe', 'grp', 'dp'))
- up_first_new: float32 [1024, 4096], P(('pipe', 'grp', 'dp'))
- up_second_new: float32 [1024, 4096], P(('pipe', 'grp', 'dp'))
- down_new: float32 [4096, 1024], P(('pipe', 'grp', 'dp'))
- down_first_new: float32 [4096, 1024], P(('pipe', 'grp', 'dp'))
- down_second_new: float32 [4096, 1024], P(('pipe', 'grp', 'dp'))
- vec_new: float32 [19, 1024], P(None, ('pipe', 'grp', 'dp'))
- vec_first_new: float32 [19, 1024], P(None, ('pipe', 'grp', 'dp'))
- vec_second_new: float32 [19, 1024], P(None, ('pipe', 'grp', 'dp'))
- bias_new: float32 [30522], replicated
- bias_first_new: float32 [30522], replicated
- bias_second_new: float32 [30522], replicated
- loss_sum: float32 [], replicated
- masked_count: float32 [], replicated
- grad_norm: float32 [], replicated
Inputs may be any that keep to these rules, and one draw needn't show every extreme that they name: `lengths`: sequence 0 is 512 long; the others lie between 1 and 512. `masked_at`: every position lies below its sequence's length; the first masked slot of sequence 0 is position 511.
All inputs are finite; a program needn't handle non-finite values.
Results may differ from a plain program's by a relative error of at most 0.012.
The roundings to bfloat16 on the way count: a program that leaves them out, or rounds other values in their place, can miss the bound.
Values may be sent and summed in bfloat16 or wider, within the bound.
A program may use at most 512 MiB of HBM per device.

v0:
```python
import jax
import jax.numpy as jnp
from jax import lax
from jax.sharding import PartitionSpec as P

H = 16
STEP = 10


beta_one = 0.9
beta_two = 0.999
learn_rate = 0.02
vector_rate = 0.2
weight_decay = 0.01
epsilon = 1e-08
clip_norm = 0.02
norm_eps = 1e-05
root_half = 0.7071067811865476
density_scale = 0.3989422804014327


def swapped(shard, axis, distance):
    return lax.ppermute(shard, axis, [(i, i ^ 1 << distance) for i in range(lax.axis_size(axis))])


def matmul(left, right):
    return jnp.dot(left, right, preferred_element_type=jnp.float32)


def left_transposed(left, right):
    return lax.dot_general(
        left, right, (((0,), (0,)), ((), ())), preferred_element_type=jnp.float32
    )


def right_transposed(left, right):
    return lax.dot_general(
        left, right, (((1,), (1,)), ((), ())), preferred_element_type=jnp.float32
    )


def norm_forward(values, gain, shift):
    center = values - jnp.mean(values, -1, keepdims=True)
    scale = lax.rsqrt(jnp.mean(center * center, -1, keepdims=True) + norm_eps)
    normal = center * scale
    return (normal * gain + shift, (normal, scale))


def norm_backward(grad, kept, gain):
    normal, scale = kept
    d_gain = jnp.sum(grad * normal, 0)
    d_shift = jnp.sum(grad, 0)
    d_norm = grad * gain
    d_input = scale * (
        d_norm
        - jnp.mean(d_norm, -1, keepdims=True)
        - normal * jnp.mean(d_norm * normal, -1, keepdims=True)
    )
    return (d_input, d_gain, d_shift)


def gelu_slope(values):
    return (
        0.5 * (1.0 + lax.erf(values * root_half))
        + values * jnp.exp(-0.5 * values * values) * density_scale
    )


def masked_counts(lengths, slots):
    return jnp.minimum(slots, (3 * lengths + 19) // 20)


def split_heads(joined):
    seq_len = joined.shape[0]
    heads = joined.reshape(seq_len, 3, H, joined.shape[1] // (3 * H))
    return (heads[:, 0], heads[:, 1], heads[:, 2])


def section_one_forward(word_rows, pos_low, qkv_low, out_low, vec_rows, length):
    seq_len, width = word_rows.shape
    places = jnp.arange(seq_len, dtype=jnp.int32)
    second = (places >= (length + 1) // 2)[:, None]
    live = (places < length)[None, None, :]
    embedded = (
        word_rows.astype(jnp.float32)
        + pos_low.astype(jnp.float32)
        + jnp.where(second, vec_rows[1], vec_rows[0])
    )
    normed, norm_zero = norm_forward(embedded, vec_rows[2], vec_rows[3])
    normed_low = normed.astype(jnp.bfloat16)
    proj_bias = jnp.concatenate([vec_rows[4], jnp.zeros_like(vec_rows[4]), vec_rows[5]])
    joined = (matmul(normed_low, qkv_low) + proj_bias).astype(jnp.bfloat16)
    queries, key_rows, value_rows = split_heads(joined)
    scale = (width // H) ** (-0.5)
    scores = (
        jnp.einsum("qhd,khd->hqk", queries, key_rows, preferred_element_type=jnp.float32) * scale
    )
    scores = jnp.where(live, scores, -1e30)
    row_peak = jnp.max(scores, -1, keepdims=True)
    exp_scores = jnp.exp(scores - row_peak)
    exp_total = jnp.sum(exp_scores, -1, keepdims=True)
    probs = exp_scores / exp_total
    log_total = row_peak + jnp.log(exp_total)
    context = jnp.einsum(
        "hqk,khd->qhd", probs.astype(jnp.bfloat16), value_rows, preferred_element_type=jnp.float32
    )
    context = context.reshape(seq_len, width).astype(jnp.bfloat16)
    branch = matmul(context, out_low) + vec_rows[6]
    hidden, norm_one = norm_forward(normed + branch, vec_rows[7], vec_rows[8])
    kept = (normed_low, norm_zero, joined, log_total, context, norm_one, second, live)
    return (hidden.astype(jnp.bfloat16), kept)


def section_one_backward(d_hidden, kept, qkv_low, out_low, vec_rows):
    normed_low, norm_zero, joined, log_total, context, norm_one, second, live = kept
    seq_len, width = context.shape
    d_pre, d_gain_one, d_shift_one = norm_backward(
        d_hidden.astype(jnp.float32), norm_one, vec_rows[7]
    )
    d_branch = d_pre.astype(jnp.bfloat16)
    d_out_bias = jnp.sum(d_branch.astype(jnp.float32), 0)
    d_out = left_transposed(context, d_branch)
    d_context = (
        right_transposed(d_branch, out_low).astype(jnp.bfloat16).reshape(seq_len, H, width // H)
    )
    queries, key_rows, value_rows = split_heads(joined)
    scale = (width // H) ** (-0.5)
    scores = (
        jnp.einsum("qhd,khd->hqk", queries, key_rows, preferred_element_type=jnp.float32) * scale
    )
    scores = jnp.where(live, scores, -1e30)
    probs = jnp.exp(scores - log_total)
    d_value = jnp.einsum(
        "hqk,qhd->khd", probs.astype(jnp.bfloat16), d_context, preferred_element_type=jnp.float32
    )
    d_probs = jnp.einsum("qhd,khd->hqk", d_context, value_rows, preferred_element_type=jnp.float32)
    d_scores = (probs * (d_probs - jnp.sum(probs * d_probs, -1, keepdims=True))).astype(
        jnp.bfloat16
    )
    d_query = (
        jnp.einsum("hqk,khd->qhd", d_scores, key_rows, preferred_element_type=jnp.float32) * scale
    )
    d_key = (
        jnp.einsum("hqk,qhd->khd", d_scores, queries, preferred_element_type=jnp.float32) * scale
    )
    d_joined = (
        jnp.stack([d_query, d_key, d_value], 1).reshape(seq_len, 3 * width).astype(jnp.bfloat16)
    )
    joined_wide = d_joined.astype(jnp.float32)
    d_query_bias = jnp.sum(joined_wide[:, :width], 0)
    d_value_bias = jnp.sum(joined_wide[:, 2 * width :], 0)
    d_qkv = left_transposed(normed_low, d_joined)
    d_normed = d_pre + right_transposed(d_joined, qkv_low)
    d_embedded, d_gain_zero, d_shift_zero = norm_backward(d_normed, norm_zero, vec_rows[2])
    d_seg_zero = jnp.sum(jnp.where(second, 0.0, d_embedded), 0)
    d_seg_one = jnp.sum(jnp.where(second, d_embedded, 0.0), 0)
    vec_part = jnp.stack(
        [
            d_seg_zero,
            d_seg_one,
            d_gain_zero,
            d_shift_zero,
            d_query_bias,
            d_value_bias,
            d_out_bias,
            d_gain_one,
            d_shift_one,
        ]
    )
    return (d_embedded, d_qkv, d_out, vec_part)


def section_two_forward(hidden, places, up_low, down_low, turn_low, vec_rows):
    inner = matmul(hidden, up_low) + vec_rows[15:].reshape(-1)
    activ = jax.nn.gelu(inner, approximate=False).astype(jnp.bfloat16)
    branch = matmul(activ, down_low) + vec_rows[9]
    mixed, norm_two = norm_forward(hidden.astype(jnp.float32) + branch, vec_rows[10], vec_rows[11])
    picked = jnp.take(mixed, places, axis=0).astype(jnp.bfloat16)
    turned = matmul(picked, turn_low) + vec_rows[12]
    normed, norm_head = norm_forward(
        jax.nn.gelu(turned, approximate=False), vec_rows[13], vec_rows[14]
    )
    return (normed, (inner, activ, norm_two, picked, turned, norm_head))


def section_two_backward(d_normed, kept, hidden, places, up_low, down_low, turn_low, vec_rows):
    inner, activ, norm_two, picked, turned, norm_head = kept
    width = hidden.shape[1]
    d_gelu, d_gain_head, d_shift_head = norm_backward(d_normed, norm_head, vec_rows[13])
    d_turned = (d_gelu * gelu_slope(turned)).astype(jnp.bfloat16)
    d_turn_bias = jnp.sum(d_turned.astype(jnp.float32), 0)
    d_turn = left_transposed(picked, d_turned)
    d_picked = right_transposed(d_turned, turn_low)
    d_mixed = jnp.zeros(hidden.shape, jnp.float32).at[places].add(d_picked)
    d_pre, d_gain_two, d_shift_two = norm_backward(d_mixed, norm_two, vec_rows[10])
    d_branch = d_pre.astype(jnp.bfloat16)
    d_down_bias = jnp.sum(d_branch.astype(jnp.float32), 0)
    d_down = left_transposed(activ, d_branch)
    d_inner = (right_transposed(d_branch, down_low) * gelu_slope(inner)).astype(jnp.bfloat16)
    d_up_bias = jnp.sum(d_inner.astype(jnp.float32), 0).reshape(-1, width)
    d_up = left_transposed(hidden, d_inner)
    d_hidden = (d_pre + right_transposed(d_inner, up_low)).astype(jnp.bfloat16)
    rows_two = jnp.stack(
        [d_down_bias, d_gain_two, d_shift_two, d_turn_bias, d_gain_head, d_shift_head]
    )
    return (d_hidden, d_up, d_down, d_turn, jnp.concatenate([rows_two, d_up_bias], 0))


def adam_step(weight, first, second, grad, factor, rate):
    clipped = grad * factor
    first = beta_one * first + (1.0 - beta_one) * clipped
    second = beta_two * second + (1.0 - beta_two) * clipped * clipped
    first_hat = first / (1.0 - beta_one**STEP)
    second_hat = second / (1.0 - beta_two**STEP)
    weight = weight - rate * (first_hat / (jnp.sqrt(second_hat) + epsilon) + weight_decay * weight)
    return (weight, first, second)


def per_device(
    token_ids,
    lengths,
    masked_at,
    labels,
    word_table,
    word_first,
    word_second,
    pos_table,
    pos_first,
    pos_second,
    qkv_weight,
    qkv_first,
    qkv_second,
    square_weight,
    square_first,
    square_second,
    up_weight,
    up_first,
    up_second,
    down_weight,
    down_first,
    down_second,
    vec_table,
    vec_first,
    vec_second,
    head_bias,
    bias_first,
    bias_second,
):
    narrow = jnp.bfloat16
    fulls = (
        lax.all_gather(word_table.astype(narrow), ("pipe", "grp", "dp"), axis=0, tiled=True),
        lax.all_gather(pos_table.astype(narrow), ("pipe", "grp", "dp"), axis=1, tiled=True),
        lax.all_gather(qkv_weight.astype(narrow), ("pipe", "grp", "dp"), axis=0, tiled=True),
        lax.all_gather(square_weight.astype(narrow), ("pipe", "grp", "dp"), axis=1, tiled=True),
        lax.all_gather(up_weight.astype(narrow), ("pipe", "grp", "dp"), axis=0, tiled=True),
        lax.all_gather(down_weight.astype(narrow), ("pipe", "grp", "dp"), axis=0, tiled=True),
        lax.all_gather(vec_table.astype(narrow), ("pipe", "grp", "dp"), axis=1, tiled=True),
    )
    word_low, pos_low, qkv_low, square_low, up_low, down_low = fulls[:6]
    vec_rows = fulls[6].astype(jnp.float32)
    vocab = head_bias.shape[0]
    head_low = word_low[:vocab]
    slots = masked_at.shape[1]
    counts = masked_counts(lengths, slots)
    total = lax.psum(jnp.sum(counts).astype(jnp.float32), ("grp", "dp"))
    pipe_index = lax.axis_index("pipe")
    batches = token_ids.shape[0]
    pos_sum = jnp.zeros(pos_low.shape, jnp.float32)
    qkv_sum = jnp.zeros(qkv_low.shape, jnp.float32)
    square_sum = jnp.zeros(square_low.shape, jnp.float32)
    up_sum = jnp.zeros(up_low.shape, jnp.float32)
    down_sum = jnp.zeros(down_low.shape, jnp.float32)
    vec_sum = jnp.zeros(vec_rows.shape, jnp.float32)
    bias_sum = jnp.zeros_like(head_bias)
    loss_part = jnp.zeros((), jnp.float32)
    row_ids, row_grads, head_rows, head_grads = ([], [], [], [])
    slot_index = jnp.arange(slots, dtype=jnp.int32)
    for pair_index in range(batches // 2):
        own_batch = 2 * pair_index + pipe_index
        peer_batch = 2 * pair_index + 1 - pipe_index
        seq_ids = lax.dynamic_index_in_dim(token_ids, own_batch, 0, keepdims=False)
        seq_length = lax.dynamic_index_in_dim(lengths, own_batch, 0, keepdims=False)
        word_rows = jnp.take(word_low, seq_ids, axis=0)
        hidden, kept_one = section_one_forward(
            word_rows, pos_low, qkv_low, square_low[0], vec_rows, seq_length
        )
        arrived = swapped(hidden, "pipe", 0)
        places = lax.dynamic_index_in_dim(masked_at, peer_batch, 0, keepdims=False)
        targets = lax.dynamic_index_in_dim(labels, peer_batch, 0, keepdims=False)
        peer_count = lax.dynamic_index_in_dim(counts, peer_batch, 0, keepdims=False)
        normed, kept_two = section_two_forward(
            arrived, places, up_low, down_low, square_low[1], vec_rows
        )
        normed_low = normed.astype(narrow)
        logits = right_transposed(normed_low, head_low) + head_bias
        row_peak = jnp.max(logits, -1, keepdims=True)
        exp_logits = jnp.exp(logits - row_peak)
        exp_total = jnp.sum(exp_logits, -1, keepdims=True)
        log_total = row_peak[:, 0] + jnp.log(exp_total[:, 0])
        hits = lax.broadcasted_iota(jnp.int32, logits.shape, 1) == targets[:, None]
        picked = jnp.sum(jnp.where(hits, logits, 0.0), -1)
        valid = (slot_index < peer_count).astype(jnp.float32)
        loss_part = loss_part + jnp.sum(valid * (log_total - picked))
        d_logits = valid[:, None] * (exp_logits / exp_total - hits.astype(jnp.float32)) / total
        bias_sum = bias_sum + jnp.sum(d_logits, 0)
        d_logits_low = d_logits.astype(narrow)
        head_rows.append(normed_low)
        head_grads.append(d_logits_low)
        d_normed = matmul(d_logits_low, head_low)
        d_hidden, d_up, d_down, d_turn, vec_two = section_two_backward(
            d_normed, kept_two, arrived, places, up_low, down_low, square_low[1], vec_rows
        )
        returned = swapped(d_hidden, "pipe", 0)
        d_embedded, d_qkv, d_out, vec_one = section_one_backward(
            returned, kept_one, qkv_low, square_low[0], vec_rows
        )
        row_ids.append(seq_ids)
        row_grads.append(d_embedded)
        pos_sum = pos_sum + d_embedded
        qkv_sum = qkv_sum + d_qkv
        square_sum = square_sum + jnp.stack([d_out, d_turn])
        up_sum = up_sum + d_up
        down_sum = down_sum + d_down
        vec_sum = vec_sum + jnp.concatenate([vec_one, vec_two], 0)
    grads_padded = jnp.pad(jnp.concatenate(head_grads, 0), ((0, 0), (0, word_low.shape[0] - vocab)))
    table_grad = left_transposed(grads_padded, jnp.concatenate(head_rows, 0))
    table_grad = table_grad.at[jnp.concatenate(row_ids, 0)].add(jnp.concatenate(row_grads, 0))
    halves = (
        lax.psum_scatter(
            table_grad.astype(jnp.bfloat16), "pipe", scatter_dimension=0, tiled=True
        ).astype(jnp.float32),
        lax.psum_scatter(
            pos_sum.astype(jnp.bfloat16), "pipe", scatter_dimension=1, tiled=True
        ).astype(jnp.float32),
        lax.psum_scatter(
            qkv_sum.astype(jnp.bfloat16), "pipe", scatter_dimension=0, tiled=True
        ).astype(jnp.float32),
        lax.psum_scatter(
            square_sum.astype(jnp.bfloat16), "pipe", scatter_dimension=1, tiled=True
        ).astype(jnp.float32),
        lax.psum_scatter(
            up_sum.astype(jnp.bfloat16), "pipe", scatter_dimension=0, tiled=True
        ).astype(jnp.float32),
        lax.psum_scatter(
            down_sum.astype(jnp.bfloat16), "pipe", scatter_dimension=0, tiled=True
        ).astype(jnp.float32),
        lax.psum_scatter(
            vec_sum.astype(jnp.bfloat16), "pipe", scatter_dimension=1, tiled=True
        ).astype(jnp.float32),
    )
    owned = (
        lax.psum_scatter(halves[0], ("grp", "dp"), scatter_dimension=0, tiled=True),
        lax.psum_scatter(halves[1], ("grp", "dp"), scatter_dimension=1, tiled=True),
        lax.psum_scatter(halves[2], ("grp", "dp"), scatter_dimension=0, tiled=True),
        lax.psum_scatter(halves[3], ("grp", "dp"), scatter_dimension=1, tiled=True),
        lax.psum_scatter(halves[4], ("grp", "dp"), scatter_dimension=0, tiled=True),
        lax.psum_scatter(halves[5], ("grp", "dp"), scatter_dimension=0, tiled=True),
        lax.psum_scatter(halves[6], ("grp", "dp"), scatter_dimension=1, tiled=True),
    )
    loss_total, bias_grad = lax.psum((loss_part, bias_sum), ("pipe", "grp", "dp"))
    local_squares = jnp.zeros((), jnp.float32)
    for grad in owned:
        local_squares = local_squares + jnp.sum(grad * grad)
    squares = lax.psum(local_squares, ("pipe", "grp", "dp")) + jnp.sum(bias_grad * bias_grad)
    grad_norm = jnp.sqrt(squares)
    factor = clip_norm / jnp.maximum(grad_norm, clip_norm)
    masters = (
        word_table,
        pos_table,
        qkv_weight,
        square_weight,
        up_weight,
        down_weight,
        vec_table,
        head_bias,
    )
    states = (
        (word_first, word_second),
        (pos_first, pos_second),
        (qkv_first, qkv_second),
        (square_first, square_second),
        (up_first, up_second),
        (down_first, down_second),
        (vec_first, vec_second),
        (bias_first, bias_second),
    )
    rates = (
        learn_rate,
        learn_rate,
        learn_rate,
        learn_rate,
        learn_rate,
        learn_rate,
        vector_rate,
        vector_rate,
    )
    grads = tuple(owned) + (bias_grad,)
    results = []
    for weight, state, grad, rate in zip(masters, states, grads, rates):
        results.extend(adam_step(weight, state[0], state[1], grad, factor, rate))
    return (
        results[0],
        results[1],
        results[2],
        results[3],
        results[4],
        results[5],
        results[6],
        results[7],
        results[8],
        results[9],
        results[10],
        results[11],
        results[12],
        results[13],
        results[14],
        results[15],
        results[16],
        results[17],
        results[18],
        results[19],
        results[20],
        results[21],
        results[22],
        results[23],
        loss_total,
        total,
        grad_norm,
    )


def solution(mesh):
    placed = (
        P(("grp", "dp"), None),
        P(("grp", "dp")),
        P(("grp", "dp"), None),
        P(("grp", "dp"), None),
        P(("pipe", "grp", "dp"), None),
        P(("pipe", "grp", "dp"), None),
        P(("pipe", "grp", "dp"), None),
        P(None, ("pipe", "grp", "dp")),
        P(None, ("pipe", "grp", "dp")),
        P(None, ("pipe", "grp", "dp")),
        P(("pipe", "grp", "dp"), None),
        P(("pipe", "grp", "dp"), None),
        P(("pipe", "grp", "dp"), None),
        P(None, ("pipe", "grp", "dp"), None),
        P(None, ("pipe", "grp", "dp"), None),
        P(None, ("pipe", "grp", "dp"), None),
        P(("pipe", "grp", "dp"), None),
        P(("pipe", "grp", "dp"), None),
        P(("pipe", "grp", "dp"), None),
        P(("pipe", "grp", "dp"), None),
        P(("pipe", "grp", "dp"), None),
        P(("pipe", "grp", "dp"), None),
        P(None, ("pipe", "grp", "dp")),
        P(None, ("pipe", "grp", "dp")),
        P(None, ("pipe", "grp", "dp")),
        P(),
        P(),
        P(),
    )
    return jax.shard_map(
        per_device,
        mesh=mesh,
        in_specs=placed,
        out_specs=(
            P(("pipe", "grp", "dp"), None),
            P(("pipe", "grp", "dp"), None),
            P(("pipe", "grp", "dp"), None),
            P(None, ("pipe", "grp", "dp")),
            P(None, ("pipe", "grp", "dp")),
            P(None, ("pipe", "grp", "dp")),
            P(("pipe", "grp", "dp"), None),
            P(("pipe", "grp", "dp"), None),
            P(("pipe", "grp", "dp"), None),
            P(None, ("pipe", "grp", "dp"), None),
            P(None, ("pipe", "grp", "dp"), None),
            P(None, ("pipe", "grp", "dp"), None),
            P(("pipe", "grp", "dp"), None),
            P(("pipe", "grp", "dp"), None),
            P(("pipe", "grp", "dp"), None),
            P(("pipe", "grp", "dp"), None),
            P(("pipe", "grp", "dp"), None),
            P(("pipe", "grp", "dp"), None),
            P(None, ("pipe", "grp", "dp")),
            P(None, ("pipe", "grp", "dp")),
            P(None, ("pipe", "grp", "dp")),
            P(),
            P(),
            P(),
            P(),
            P(),
            P(),
        ),
        check_vma=False,
    )
```

profile of v0, /device:TPU:0, one launch (start us, length us, event | category | flops | bytes accessed | tf_op | source)
XLA Modules:
  0.0 3286.6 jit_solution(4821113050280349226)
XLA Ops:
  15.1 72.1 %all-gather = bf16[32,32,19]{1,2,0:T(8,128)(2,1)S(1)} all-gather(bf16[1,32,19]{1,2,0:T(8,128)(2,1)S(1)} %convert_bitcast_fusion), channel_id=1, replica_groups=mesh['pipe'=2,'grp'=4,'dp'=4] {'pipe','grp','dp'}, dimensions={0}, use_global_device_ids=true | all-gather | bytes 40128 | tf_op jit(solution)/shard_map/all_gather | solution.py:257
  93.1 313.8 %all-gather.8.cloned.1.call-done = bf16[30720,1024]{1,0:T(8,128)(2,1)} async-done(((bf16[960,1024]{1,0:T(8,128)(2,1)}), bf16[30720,1024]{1,0:T(8,128)(2,1)}) %all-gather.8.cloned.1.call-update) | async-done | bytes 62914576 | tf_op jit(solution)/shard_map/all_gather | solution.py:251
  418.9 59.1 %all-gather.12.cloned.1.call-done = bf16[1024,3072]{1,0:T(8,128)(2,1)} async-done(((bf16[32,3072]{1,0:T(8,128)(2,1)}), bf16[1024,3072]{1,0:T(8,128)(2,1)}) %all-gather.12.cloned.1.call-update) | async-done | bytes 6291472 | tf_op jit(solution)/shard_map/all_gather | solution.py:253
  528.4 13.5 all-gather.14.cloned.1.call-done
  578.5 41.0 %psum.28 = f32[]{:T(128)} all-reduce(f32[]{:T(128)S(6)} %convert_element_type.292), channel_id=1, replica_groups=mesh['pipe'=2,'grp'=4,'dp'=4] {'grp','dp'}, use_global_device_ids=true, to_apply=%region_13.16 | all-reduce | flops 1 | bytes 8 | tf_op jit(solution)/shard_map/psum | solution.py:265
  635.9 43.3 %fusion.22 = (bf16[512,4096]{1,0:T(8,128)(2,1)}, bf16[512,4096]{1,0:T(8,128)(2,1)}, f32[512,4096]{1,0:T(8,128)}) fusion(f32[4096]{0:T(1024)S(1)} %bitcast.341, f32[512,4096]{1,0:T(8,128)S(1)} %fusion.223, bf16[512,1024]{1,0:T(8,128)(2,1)} %collective-permute-done, bf16[1024,4096]{1,0:T(8,128)(2,1)S(1)} %copy-done.162), kind=kOutput, calls=%fused_computation.45 | convolution fusion | flops 4571791360 | bytes 34619392 | tf_op jit(solution)/shard_map/dot_general | solution.py:27
  679.2 23.4 all-gather.18.cloned.1.call-done
  731.3 29.8 fusion.221
  772.2 24.3 multiply_reduce_fusion.24
  796.6 29.3 fusion.222
  837.0 24.0 convert_reduce_fusion.8
  879.2 11.6 convert_reduce_fusion
  897.3 11.5 convert_reduce_fusion.1
  947.8 11.7 multiply_convert_fusion
  988.8 11.7 multiply_convert_fusion.1
  1068.0 16.0 fusion.185
  1084.0 12.0 add_convert_fusion
  1096.1 15.9 fusion.224
  1123.6 48.6 %fusion.62 = f32[30720,1024]{1,0:T(8,128)} fusion(bf16[64,30522]{1,0:T(8,128)(2,1)} %get-tuple-element.189, bf16[64,30522]{1,0:T(8,128)(2,1)} %get-tuple-element.191, bf16[64,1024]{1,0:T(8,128)(2,1)S(1)} %copy-done.55, bf16[64,1024]{1,0:T(8,128)(2,1)S(1)} %copy-done.53), kind=kOutput, calls=%fused_computation.102 | convolution fusion | flops 8081113088 | bytes 133904896 | tf_op jit(solution)/shard_map/dot_general | solution.py:31
  1176.3 146.9 %scatter_fusion = f32[30720,1024]{1,0:T(8,128)} fusion(f32[30720,1024]{1,0:T(8,128)} %fusion.62, s32[1024]{0:T(1024)S(1)} %bitcast.339, f32[1024,1024]{1,0:T(8,128)} %pad_maximum_fusion), kind=kCustom, calls=%fused_computation.6 | custom fusion | flops 1048576 | bytes 12587008 | tf_op jit(solution)/shard_map/scatter-add | solution.py:327
  1323.1 59.8 %convert_element_type.329 = bf16[30720,1024]{1,0:T(8,128)(2,1)} convert(f32[30720,1024]{1,0:T(8,128)} %scatter_fusion) | non-fusion elementwise | flops 31457280 | bytes 188743680 | tf_op jit(solution)/shard_map/convert_element_type | solution.py:330
  1417.5 44.5 %reduce-scatter.48.cloned.1.call-done = bf16[15360,1024]{1,0:T(8,128)(2,1)} async-done(((bf16[30720,1024]{1,0:T(8,128)(2,1)}), bf16[15360,1024]{1,0:T(8,128)(2,1)}) %reduce-scatter.48.cloned.1.call-update) | async-done | bytes 31457296
  1462.1 30.4 convert_element_type.330
  1497.6 44.7 %reduce-scatter.46.cloned.1.call-done = f32[32,19]{1,0:T(8,128)} async-done(((f32[512,19]{1,0:T(8,128)}), f32[32,19]{1,0:T(8,128)}) %reduce-scatter.46.cloned.1.call-update) | async-done | bytes 2448
  1543.8 76.6 %reduce-scatter.44.cloned.1.call-done = f32[32,512]{1,0:T(8,128)} async-done(((f32[512,512]{1,0:T(8,128)}), f32[32,512]{1,0:T(8,128)}) %reduce-scatter.44.cloned.1.call-update) | async-done | bytes 65552
  1622.1 93.4 %reduce-scatter.32.cloned.1.call-done = f32[2,32,1024]{2,1,0:T(8,128)} async-done(((f32[2,512,1024]{2,1,0:T(8,128)}), f32[2,32,1024]{2,1,0:T(8,128)}) %reduce-scatter.32.cloned.1.call-update) | async-done | bytes 262160 | tf_op jit(solution)/shard_map/reduce_scatter | solution.py:355
  1717.1 148.1 %reduce-scatter.28.cloned.1.call-done = f32[32,3072]{1,0:T(8,128)} async-done(((f32[512,3072]{1,0:T(8,128)}), f32[32,3072]{1,0:T(8,128)}) %reduce-scatter.28.cloned.1.call-update) | async-done | bytes 393232 | tf_op jit(solution)/shard_map/reduce_scatter | solution.py:354
  1866.9 182.0 %reduce-scatter.40.cloned.1.call-done = f32[128,1024]{1,0:T(8,128)} async-done(((f32[2048,1024]{1,0:T(8,128)}), f32[128,1024]{1,0:T(8,128)}) %reduce-scatter.40.cloned.1.call-update) | async-done | bytes 524304 | tf_op jit(solution)/shard_map/reduce_scatter | solution.py:357
  2050.7 180.5 %reduce-scatter.36.cloned.1.call-done = f32[32,4096]{1,0:T(8,128)} async-done(((f32[512,4096]{1,0:T(8,128)}), f32[32,4096]{1,0:T(8,128)}) %reduce-scatter.36.cloned.1.call-update) | async-done | bytes 524304 | tf_op jit(solution)/shard_map/reduce_scatter | solution.py:356
  2232.9 852.0 %reduce-scatter.22.cloned.1.call-done = f32[960,1024]{1,0:T(8,128)} async-done(((f32[15360,1024]{1,0:T(8,128)}), f32[960,1024]{1,0:T(8,128)}) %reduce-scatter.22.cloned.1.call-update) | async-done | bytes 3932176 | tf_op jit(solution)/shard_map/reduce_scatter | solution.py:352
  3093.4 119.1 %all-reduce.5.cloned.1.call-done = f32[30522]{0:T(1024)} async-done(((f32[30522]{0:T(1024)}), f32[30522]{0:T(1024)}) %all-reduce.5.cloned.1.call-update) | async-done | bytes 122104 | tf_op jit(solution)/shard_map/psum | solution.py:360
  3214.0 40.6 %all-reduce.2 = (f32[]{:T(128)}, f32[]{:T(128)}) all-reduce(f32[]{:T(128)S(6)} %add.687, f32[]{:T(128)S(6)} %add.732), channel_id=1, replica_groups=mesh['pipe'=2,'grp'=4,'dp'=4] {'pipe','grp','dp'}, use_global_device_ids=true, to_apply=%region_100.103 | all-reduce | flops 2 | bytes 16 | tf_op jit(solution)/shard_map/psum | solution.py:364
  (594 shorter events, 427.7 us)
Async XLA Ops:
  7.2 84.4 %all-gather.10.cloned.1.call-start = ((), (), s32[]{:S(2)}) async-start(), calls=%async_computation.15 | async-start | bytes 1081344 | tf_op jit(solution)/shard_map/all_gather | solution.py:252
  8.8 398.1 %all-gather.8.cloned.1.call-start = ((), (), s32[]{:S(2)}) async-start(), calls=%async_computation.14 | async-start | bytes 64880640 | tf_op jit(solution)/shard_map/all_gather | solution.py:251
  12.6 465.3 %all-gather.12.cloned.1.call-start = ((), (), s32[]{:S(2)}) async-start(), calls=%async_computation.16 | async-start | bytes 6488064 | tf_op jit(solution)/shard_map/all_gather | solution.py:253
  13.4 528.4 %all-gather.14.cloned.1.call-start = ((), (), s32[]{:S(2)}) async-start(), calls=%async_computation.17 | async-start | bytes 4325376 | tf_op jit(solution)/shard_map/all_gather | solution.py:254
  14.2 611.1 %all-gather.16.cloned.1.call-start = ((), (), s32[]{:S(2)}) async-start(), calls=%async_computation.18 | async-start | bytes 8650752 | tf_op jit(solution)/shard_map/all_gather | solution.py:255
  15.0 687.6 %all-gather.18.cloned.1.call-start = ((), (), s32[]{:S(2)}) async-start(), calls=%async_computation.19 | async-start | bytes 8650752 | tf_op jit(solution)/shard_map/all_gather | solution.py:256
  91.4 483.8 %copy-start.82 = (f32[1,1024]{1,0:T(1,128)}, f32[1,1024]{1,0:T(1,128)S(1)}, u32[]{:S(2)}) copy-start(f32[1,1024]{1,0:T(1,128)S(1)} %get-tuple-element.223) | copy-start | bytes 12292
  576.1 49.1 %collective-permute-start.1 = (bf16[512,1024]{1,0:T(8,128)(2,1)S(1)}, bf16[512,1024]{1,0:T(8,128)(2,1)}, u32[]{:S(2)}, u32[]{:S(2)}) collective-permute-start(bf16[512,1024]{1,0:T(8,128)(2,1)S(1)} %get-tuple-element.238), channel_id=1, source_target_pairs={{0,16},{16,0},{1,17},{17,1},{2,18},{18,2},{3,19},{19,3},{4,20},{20... | collective-permute-start | bytes 3145736 | tf_op jit(solution)/shard_map/ppermute | solution.py:23
  578.5 804.5 %reduce-scatter.42.cloned.1.call-start = ((), (), s32[]{:S(2)}) async-start(), calls=%async_computation.30 | async-start | bytes 73728 | tf_op jit(solution)/shard_map/reduce_scatter | solution.py:347
  625.3 7.4 collective-permute-start
  896.4 18.5 collective-permute-start.3
  914.5 3.5 collective-permute-start.2
  1034.0 350.6 %reduce-scatter.24.cloned.1.call-start = ((), (), s32[]{:S(2)}) async-start(), calls=%async_computation.21 | async-start | bytes 1572864 | tf_op jit(solution)/shard_map/reduce_scatter | solution.py:332
  1037.0 350.0 %reduce-scatter.30.cloned.1.call-start = ((), (), s32[]{:S(2)}) async-start(), calls=%async_computation.24 | async-start | bytes 6291456 | tf_op jit(solution)/shard_map/reduce_scatter | solution.py:338
  1046.6 344.9 %reduce-scatter.26.cloned.1.call-start = ((), (), s32[]{:S(2)}) async-start(), calls=%async_computation.22 | async-start | bytes 9437184 | tf_op jit(solution)/shard_map/reduce_scatter | solution.py:335
  1067.9 330.5 %reduce-scatter.38.cloned.1.call-start = ((), (), s32[]{:S(2)}) async-start(), calls=%async_computation.28 | async-start | bytes 12582912 | tf_op jit(solution)/shard_map/reduce_scatter | solution.py:344
  1096.1 311.9 %reduce-scatter.34.cloned.1.call-start = ((), (), s32[]{:S(2)}) async-start(), calls=%async_computation.26 | async-start | bytes 12582912 | tf_op jit(solution)/shard_map/reduce_scatter | solution.py:341
  1122.6 339.4 %reduce-scatter.48.cloned.1.call-start = ((), (), s32[]{:S(2)}) async-start(), calls=%async_computation.34 | async-start | bytes 94371840
  1382.9 159.4 %reduce-scatter.46.cloned.1.call-start = ((), (), s32[]{:S(2)}) async-start(), calls=%async_computation.33 | async-start | bytes 278528
  1384.6 235.8 %reduce-scatter.44.cloned.1.call-start = ((), (), s32[]{:S(2)}) async-start(), calls=%async_computation.32 | async-start | bytes 1114112
  1386.9 328.5 %reduce-scatter.32.cloned.1.call-start = ((), (), s32[]{:S(2)}) async-start(), calls=%async_computation.25 | async-start | bytes 4456448 | tf_op jit(solution)/shard_map/reduce_scatter | solution.py:355
  1391.5 473.7 %reduce-scatter.28.cloned.1.call-start = ((), (), s32[]{:S(2)}) async-start(), calls=%async_computation.23 | async-start | bytes 6684672 | tf_op jit(solution)/shard_map/reduce_scatter | solution.py:354
  1398.3 650.6 %reduce-scatter.40.cloned.1.call-start = ((), (), s32[]{:S(2)}) async-start(), calls=%async_computation.29 | async-start | bytes 8912896 | tf_op jit(solution)/shard_map/reduce_scatter | solution.py:357
  1407.9 823.3 %reduce-scatter.36.cloned.1.call-start = ((), (), s32[]{:S(2)}) async-start(), calls=%async_computation.27 | async-start | bytes 8912896 | tf_op jit(solution)/shard_map/reduce_scatter | solution.py:356
  1417.5 1667.5 %reduce-scatter.22.cloned.1.call-start = ((), (), s32[]{:S(2)}) async-start(), calls=%async_computation.20 | async-start | bytes 66846720 | tf_op jit(solution)/shard_map/reduce_scatter | solution.py:352
  1492.6 1764.8 %copy-start.70 = (f32[512,32]{0,1:T(8,128)S(1)}, f32[512,32]{0,1:T(8,128)}, u32[]{:S(2)}) copy-start(f32[512,32]{0,1:T(8,128)} %param.39) | copy-start | bytes 196612
  1492.6 1719.9 %all-reduce.5.cloned.1.call-start = ((), (), s32[]{:S(2)}) async-start(), calls=%async_computation.31 | async-start | bytes 245760 | tf_op jit(solution)/shard_map/psum | solution.py:360
  1497.6 1763.3 %copy-start.50 = (f32[2,32,1024]{2,1,0:T(8,128)S(1)}, f32[2,32,1024]{2,1,0:T(8,128)}, u32[]{:S(2)}) copy-start(f32[2,32,1024]{2,1,0:T(8,128)} %param.45) | copy-start | bytes 786436
  1620.3 1637.1 %copy-start.69 = (f32[32,512]{1,0:T(8,128)S(1)}, f32[32,512]{1,0:T(8,128)}, u32[]{:S(2)}) copy-start(f32[32,512]{1,0:T(8,128)} %reduce-scatter.44.cloned.1.call-done) | copy-start | bytes 196612
  1715.4 1545.5 %copy-start.51 = (f32[2,32,1024]{2,1,0:T(8,128)S(1)}, f32[2,32,1024]{2,1,0:T(8,128)}, u32[]{:S(2)}) copy-start(f32[2,32,1024]{2,1,0:T(8,128)} %reduce-scatter.32.cloned.1.call-done) | copy-start | bytes 786436
  2050.7 1212.4 %copy-start.47 = (f32[32,3072]{1,0:T(8,128)S(1)}, f32[32,3072]{1,0:T(8,128)}, u32[]{:S(2)}) copy-start(f32[32,3072]{1,0:T(8,128)} %param.42) | copy-start | bytes 1179652
  2050.7 1212.4 %copy-start.48 = (f32[32,3072]{1,0:T(8,128)S(1)}, f32[32,3072]{1,0:T(8,128)}, u32[]{:S(2)}) copy-start(f32[32,3072]{1,0:T(8,128)} %reduce-scatter.28.cloned.1.call-done) | copy-start | bytes 1179652
  (170 other events, 6933.6 us)
Sparse Core Ops, SparseCore 0:
  11.6 56.6 all-gather.9
  71.7 335.1 all-gather.7
  410.3 67.5 all-gather.11
  481.4 60.3 all-gather.13
  545.3 76.0 all-gather.15
  624.8 77.8 all-gather.17
  1034.2 6.0 reduce-scatter.41
  1042.5 9.6 reduce-scatter.23
  1054.6 13.1 reduce-scatter.29
  1070.0 15.7 reduce-scatter.25
  1096.2 15.7 reduce-scatter.37
  1122.8 16.2 reduce-scatter.33
  1383.0 78.9 reduce-scatter.47
  1464.8 77.4 reduce-scatter.45
  1545.0 75.2 reduce-scatter.43
  1622.6 92.7 reduce-scatter.31
  1721.3 143.8 reduce-scatter.27
  1867.5 181.3 reduce-scatter.39
  2051.3 179.8 reduce-scatter.35
  2238.0 846.8 reduce-scatter.21
  3092.0 120.4 all-reduce.4
where the time goes:
time: 3300 us; the launch traced here: 3290 us
  waiting for transfers between devices  2150 us (65%)
  matrix products  473 us (14%)
  other arithmetic  434 us (13%)
  blocking collectives  154 us (5%)
  local copies, waits for them, and re-layouts  45.8 us (1%)
    reduce_scatter x1, waiting for transfers between devices, per_device(): lax.psum_scatter(halves[0], ('grp', 'dp'), scatter_dimension=0, tiled=True)  852 us
    all_gather x1, waiting for transfers between devices, per_device(): lax.all_gather(word_table.astype(narrow), ('pipe', 'grp', 'dp'), axis=0,...  314 us
    reduce_scatter x1, waiting for transfers between devices, per_device(): lax.psum_scatter(halves[5], ('grp', 'dp'), scatter_dimension=0, tiled=True)  182 us
    reduce_scatter x1, waiting for transfers between devices, per_device(): lax.psum_scatter(halves[4], ('grp', 'dp'), scatter_dimension=0, tiled=True)  180 us
    unnamed x24, waiting for transfers between devices  166 us
    reduce_scatter x1, waiting for transfers between devices, per_device(): lax.psum_scatter(halves[2], ('grp', 'dp'), scatter_dimension=0, tiled=True)  148 us
    scatter-add x1, other arithmetic, per_device(): table_grad.at[jnp.concatenate(row_ids, 0)]  147 us
    dot_general x12, matrix products, matmul(): return jnp.dot(left, right, preferred_element_type=jnp.float32)  144 us
  transfers between devices with their start and end apart: 25, of which 13 were waited for; matrix products, arithmetic and copies ran while one was open for 19% of the time, Pallas kernels for 0%

commit v1 on v0

v1 whole, which is shorter than its diff:
```python
import functools
import math

import jax
import jax.numpy as jnp
from jax import lax
from jax.experimental import pallas as pl
from jax.experimental.pallas import tpu as pltpu
from jax.sharding import PartitionSpec as P

H = 16
STEP = 10


beta_one = 0.9
beta_two = 0.999
learn_rate = 0.02
vector_rate = 0.2
weight_decay = 0.01
epsilon = 1e-08
clip_norm = 0.02
norm_eps = 1e-05
root_half = 0.7071067811865476
density_scale = 0.3989422804014327
AXES = ("pipe", "grp", "dp")
CHIPS = ("grp", "dp")
highest = lax.Precision.HIGHEST


def matmul(left, right):
    return jnp.dot(left, right, preferred_element_type=jnp.float32)


def left_transposed(left, right):
    return lax.dot_general(
        left, right, (((0,), (0,)), ((), ())), preferred_element_type=jnp.float32
    )


def right_transposed(left, right):
    return lax.dot_general(
        left, right, (((1,), (1,)), ((), ())), preferred_element_type=jnp.float32
    )


def norm_forward(values, gain, shift):
    center = values - jnp.mean(values, -1, keepdims=True)
    scale = lax.rsqrt(jnp.mean(center * center, -1, keepdims=True) + norm_eps)
    normal = center * scale
    return (normal * gain + shift, (normal, scale))


def norm_backward(grad, kept, gain):
    normal, scale = kept
    d_gain = jnp.sum(grad * normal, 0)
    d_shift = jnp.sum(grad, 0)
    d_norm = grad * gain
    d_input = scale * (
        d_norm
        - jnp.mean(d_norm, -1, keepdims=True)
        - normal * jnp.mean(d_norm * normal, -1, keepdims=True)
    )
    return (d_input, d_gain, d_shift)


def gelu_slope(values):
    return (
        0.5 * (1.0 + lax.erf(values * root_half))
        + values * jnp.exp(-0.5 * values * values) * density_scale
    )


def masked_counts(lengths, slots):
    return jnp.minimum(slots, (3 * lengths + 19) // 20)


def one_hot(indices, size, dtype):
    places = lax.broadcasted_iota(jnp.int32, indices.shape + (size,), indices.ndim)
    return (indices[..., None] == places).astype(dtype)


def rows_by_seq(pick, rows):
    return jnp.einsum("sjp,spw->sjw", pick, rows, precision=highest)


def rows_to_seq(pick, rows):
    return jnp.einsum("sjp,sjw->spw", pick, rows, precision=highest)


class Routes:
    def __init__(self, all_ids, all_live, rows_per):
        self.parts, tokens = all_ids.shape
        self.rows_per = rows_per
        self.me = lax.axis_index(AXES)
        mean = tokens / self.parts
        self.room = max(16, int(math.ceil((mean + 2.8 * math.sqrt(mean)) / 16)) * 16)
        owners = jnp.where(all_live, all_ids // rows_per, -1)
        counts = jnp.sum(one_hot(owners, self.parts, jnp.int32), 1)
        self.rounds = (jnp.max(counts) + self.room - 1) // self.room
        mine = owners == self.me
        self.out_rank = jnp.where(mine, jnp.cumsum(mine.astype(jnp.int32), 1) - 1, -1)
        self.out_row = all_ids - self.me * rows_per
        own_owners = lax.dynamic_index_in_dim(owners, self.me, 0, keepdims=False)
        hits = one_hot(own_owners, self.parts, jnp.int32)
        ranks = jnp.sum(hits * jnp.cumsum(hits, 0), 1) - 1
        self.in_rank = ranks
        self.in_owner = own_owners

    def owner_pick(self, turn):
        slots = turn * self.room + jnp.arange(self.room, dtype=jnp.int32)
        at = self.out_rank[:, None, :] == slots[None, :, None]
        row = jnp.sum(jnp.where(at, self.out_row[:, None, :] + 1, 0), 2) - 1
        return one_hot(row.reshape(-1), self.rows_per, jnp.bfloat16)

    def token_pick(self, turn):
        rank = self.in_rank - turn * self.room
        inside = (self.in_owner >= 0) & (rank >= 0) & (rank < self.room)
        slot = jnp.where(inside, self.in_owner * self.room + rank, -1)
        return one_hot(slot, self.parts * self.room, jnp.bfloat16)

    def exchange(self, rows):
        shaped = rows.reshape(self.parts, self.room, rows.shape[1])
        return lax.all_to_all(shaped, AXES, 0, 0).reshape(rows.shape)

    def table_rows(self, table, turn):
        return matmul(self.owner_pick(turn), table).astype(jnp.bfloat16)

    def token_rows(self, rows, turn):
        return left_transposed(self.token_pick(turn), rows).astype(jnp.bfloat16)

    def fetch(self, table, arrived):
        def more(turn, kept):
            rows = self.exchange(self.table_rows(table, turn))
            return kept + matmul(self.token_pick(turn), rows)

        return lax.fori_loop(1, self.rounds, more, matmul(self.token_pick(0), arrived))

    def give(self, rows, arrived):
        def more(turn, kept):
            back = self.exchange(self.token_rows(rows, turn))
            return kept + left_transposed(self.owner_pick(turn), back)

        return lax.fori_loop(
            1, self.rounds, more, left_transposed(self.owner_pick(0), arrived)
        )


def swapped(shard):
    return lax.ppermute(shard, "pipe", [(0, 1), (1, 0)])


def both_cores(rows):
    return jnp.concatenate([rows, swapped(rows)], 0)


def half_columns(rows, index):
    half = rows.shape[1] // 2
    return lax.dynamic_slice_in_dim(rows, index * half, half, 1)


def chip_sum(left, right):
    pipe = lax.axis_index("pipe")
    left = jnp.concatenate([half_columns(left, pipe), swapped(half_columns(left, 1 - pipe))], 0)
    return left_transposed(left, both_cores(right)).astype(jnp.bfloat16)


def chip_half(partial):
    half = partial.shape[0] // 2
    pipe = lax.axis_index("pipe")
    partial = partial.astype(jnp.bfloat16)
    keep = lax.dynamic_slice_in_dim(partial, pipe * half, half, 0)
    give = lax.dynamic_slice_in_dim(partial, (1 - pipe) * half, half, 0)
    return (keep.astype(jnp.float32) + swapped(give).astype(jnp.float32)).astype(jnp.bfloat16)


def device(pipe, grp, dp):
    return {"pipe": pipe, "grp": grp, "dp": dp}


def remote(source, target, send, arrive, to):
    return pltpu.make_async_remote_copy(
        src_ref=source,
        dst_ref=target,
        send_sem=send,
        recv_sem=arrive,
        device_id=device(*to),
        device_id_type=pl.DeviceIdType.MESH,
    )


def greet(others):
    barrier = pltpu.get_barrier_semaphore()
    for to in others:
        pl.semaphore_signal(
            barrier, inc=1, device_id=device(*to), device_id_type=pl.DeviceIdType.MESH
        )
    pl.semaphore_wait(barrier, len(others))


class Place:
    def __init__(self, sizes):
        self.pipes, self.grps, self.dps = sizes
        self.pipe, self.grp, self.dp = [lax.axis_index(axis) for axis in AXES]
        column, row = self.grp % 2, self.grp // 2
        self.beside = 2 * row + 1 - column
        self.below = 2 * (1 - row) + column
        self.across = 3 - self.grp

    def line(self, step):
        return (self.dp + step) % self.dps

    def behind(self, step):
        return (self.dp + self.dps - step) % self.dps

    def others(self):
        found = []
        for a in range(self.pipes):
            for b in range(self.grps):
                for c in range(self.dps):
                    if (a, b, c) != (0, 0, 0):
                        ahead = (
                            (self.pipe + a) % self.pipes,
                            (self.grp + b) % self.grps,
                            (self.dp + c) % self.dps,
                        )
                        back = (
                            (self.pipe + self.pipes - a) % self.pipes,
                            (self.grp + self.grps - b) % self.grps,
                            (self.dp + self.dps - c) % self.dps,
                        )
                        found.append((ahead, back))
        return found

    def index(self, pipe, grp, dp):
        return (pipe * self.grps + grp) * self.dps + dp


def swap_all(place, rows, arrived, send, arrive, own):
    me = place.index(place.pipe, place.grp, place.dp)
    copies = []
    for i, (ahead, back) in enumerate(place.others()):
        to = place.index(*ahead)
        copies.append(remote(rows.at[to], arrived.at[me], send.at[i], arrive.at[i], ahead))
        copies[-1].start()
    kept = pltpu.make_async_copy(rows.at[me], arrived.at[me], own)
    kept.start()

    def finish():
        for i, (ahead, back) in enumerate(place.others()):
            origin = place.index(*back)
            copies[i].wait_send()
            remote(rows.at[me], arrived.at[origin], send.at[i], arrive.at[i], ahead).wait_recv()
        kept.wait()

    return finish


def spread_kernel(sizes, row_ref, all_ref, send, arrive, own):
    place = Place(sizes)
    others = place.others()
    greet([ahead for ahead, _ in others])
    me = place.index(place.pipe, place.grp, place.dp)
    copies = []
    for i, (ahead, _) in enumerate(others):
        copies.append(remote(row_ref, all_ref.at[me], send.at[i], arrive.at[i], ahead))
        copies[-1].start()
    kept = pltpu.make_async_copy(row_ref, all_ref.at[me], own)
    kept.start()
    for i, (ahead, back) in enumerate(others):
        copies[i].wait_send()
        remote(
            row_ref, all_ref.at[place.index(*back)], send.at[i], arrive.at[i], ahead
        ).wait_recv()
    kept.wait()


def spread(row, sizes, collective):
    parts = math.prod(sizes)
    sems = pltpu.SemaphoreType.DMA((parts - 1,))
    return pl.pallas_call(
        functools.partial(spread_kernel, sizes),
        out_shape=jax.ShapeDtypeStruct((parts,) + row.shape, row.dtype),
        in_specs=[pl.BlockSpec(memory_space=pltpu.VMEM)],
        out_specs=pl.BlockSpec(memory_space=pltpu.VMEM),
        scratch_shapes=[sems, sems, pltpu.SemaphoreType.DMA],
        compiler_params=pltpu.CompilerParams(
            collective_id=collective, has_side_effects=True, vmem_limit_bytes=8 << 20
        ),
    )(row)


def stats_kernel(sizes, own_ref, all_ref, held, result, send, arrive, own, send_two, arrive_two):
    place = Place(sizes)
    others = place.others()
    greet([ahead for ahead, _ in others])
    swap_all(place, own_ref, held, send, arrive, own)()
    peaks = held[:, 0]
    peak = jnp.max(peaks, 0, keepdims=True)
    total = jnp.sum(held[:, 1] * jnp.exp(peaks - peak), 0, keepdims=True)
    label = jnp.sum(held[:, 2], 0, keepdims=True)
    result[0:1] = peak
    result[1:2] = total
    result[2:3] = label
    result[3:8] = jnp.zeros((5, result.shape[1]), jnp.float32)
    me = place.index(place.pipe, place.grp, place.dp)
    copies = []
    for i, (ahead, _) in enumerate(others):
        copies.append(remote(result, all_ref.at[me], send_two.at[i], arrive_two.at[i], ahead))
        copies[-1].start()
    all_ref[me] = result[...]
    for i, (ahead, back) in enumerate(others):
        copies[i].wait_send()
        remote(
            result, all_ref.at[place.index(*back)], send_two.at[i], arrive_two.at[i], ahead
        ).wait_recv()


def combine_stats(own, sizes, collective):
    parts, _, rows = own.shape
    sems = pltpu.SemaphoreType.DMA((parts - 1,))
    return pl.pallas_call(
        functools.partial(stats_kernel, sizes),
        out_shape=jax.ShapeDtypeStruct(own.shape, jnp.float32),
        in_specs=[pl.BlockSpec(memory_space=pltpu.VMEM)],
        out_specs=pl.BlockSpec(memory_space=pltpu.VMEM),
        scratch_shapes=[
            pltpu.VMEM(own.shape, jnp.float32),
            pltpu.VMEM((8, rows), jnp.float32),
            sems,
            sems,
            pltpu.SemaphoreType.DMA,
            sems,
            sems,
        ],
        compiler_params=pltpu.CompilerParams(
            collective_id=collective, has_side_effects=True, vmem_limit_bytes=8 << 20
        ),
    )(own)


def gather_kernel(sizes, pieces, routed, *refs):
    count = max(piece[0] for piece in pieces) + 1
    shards, refs = refs[:count], refs[count:]
    if routed:
        rows_ref, refs = refs[0], refs[1:]
    fulls, refs = refs[:count], refs[count:]
    if routed:
        arrived_ref, refs = refs[0], refs[1:]
    send, arrive, own, swap_send, swap_arrive, swap_own = refs
    place = Place(sizes)
    pipe, grp, dp = place.pipe, place.grp, place.dp
    near = place.beside * (1 - pipe) + place.below * pipe
    far = place.below * (1 - pipe) + place.beside * pipe
    core = (1 - pipe, grp, dp)
    lines = place.dps - 1
    if routed:
        greet([ahead for ahead, _ in place.others()])
    else:
        greet(
            [(pipe, grp, place.line(k + 1)) for k in range(lines)]
            + [(pipe, near, dp), (pipe, far, dp), core]
        )
    waits = []

    def view(piece, *at):
        array, first, rows = piece
        return fulls[array].at[at + ((slice(None),) * (3 - len(at))) + (pl.ds(first, rows),)]

    def launch(n, index, source, piece, to, *at):
        copy = remote(source, view(piece, *at), send.at[n, index], arrive.at[n, index], to)
        copy.start()
        waits.append(copy)

    def landed(n, index, piece, *at):
        target = view(piece, *at)
        remote(target, target, send.at[n, index], arrive.at[n, index], core).wait_recv()

    keeps = []
    for n, piece in enumerate(pieces):
        array, first, rows = piece
        source = shards[array].at[pl.ds(first, rows)]
        for k in range(lines):
            launch(n, k, source, piece, (pipe, grp, place.line(k + 1)), pipe, grp, dp)
        keeps.append(pltpu.make_async_copy(source, view(piece, pipe, grp, dp), own.at[n]))
        keeps[-1].start()
        if n == 0 and routed:
            finish = swap_all(place, rows_ref, arrived_ref, swap_send, swap_arrive, swap_own)

    def over_plane(n, piece):
        for k in range(lines):
            landed(n, k, piece, pipe, grp, place.behind(k + 1))
        keeps[n].wait()
        group = view(piece, pipe, grp)
        launch(n, lines, group, piece, (pipe, near, dp), pipe, grp)
        launch(n, lines + 1, group, piece, (pipe, far, dp), pipe, grp)
        launch(n, lines + 3, group, piece, core, pipe, grp)

    def pass_on(n, piece):
        landed(n, lines, piece, pipe, near)
        group = view(piece, pipe, near)
        launch(n, lines + 2, group, piece, (pipe, far, dp), pipe, near)
        launch(n, lines + 4, group, piece, core, pipe, near)
        landed(n, lines + 1, piece, pipe, far)
        launch(n, lines + 5, view(piece, pipe, far), piece, core, pipe, far)

    def last(n, piece):
        landed(n, lines + 2, piece, pipe, place.across)
        launch(n, lines + 6, view(piece, pipe, place.across), piece, core, pipe, place.across)

    total = len(pieces)
    for n in range(total + 2):
        if n < total:
            over_plane(n, pieces[n])
        if 1 <= n < total + 1:
            pass_on(n - 1, pieces[n - 1])
        if n >= 2:
            last(n - 2, pieces[n - 2])
    for n, piece in enumerate(pieces):
        landed(n, lines + 3, piece, 1 - pipe, grp)
        core_near = place.below * (1 - pipe) + place.beside * pipe
        core_far = place.beside * (1 - pipe) + place.below * pipe
        landed(n, lines + 4, piece, 1 - pipe, core_near)
        landed(n, lines + 5, piece, 1 - pipe, core_far)
        landed(n, lines + 6, piece, 1 - pipe, place.across)
    for copy in waits:
        copy.wait_send()
    if routed:
        finish()


def gather_all(shards, pieces, sizes, collective, rows=None):
    parts = math.prod(sizes)
    routed = rows is not None
    kinds = sizes[2] - 1 + 7
    out_shape = [jax.ShapeDtypeStruct(sizes + shard.shape, shard.dtype) for shard in shards]
    if routed:
        out_shape.append(jax.ShapeDtypeStruct(rows.shape, rows.dtype))
    operands = list(shards) + ([rows] if routed else [])
    sems = pltpu.SemaphoreType.DMA((len(pieces), kinds))
    swaps = pltpu.SemaphoreType.DMA((parts - 1 if routed else 1,))
    return pl.pallas_call(
        functools.partial(gather_kernel, sizes, tuple(pieces), routed),
        out_shape=out_shape,
        in_specs=[pl.BlockSpec(memory_space=pl.ANY)] * len(operands),
        out_specs=[pl.BlockSpec(memory_space=pl.ANY)] * len(out_shape),
        scratch_shapes=[
            sems,
            sems,
            pltpu.SemaphoreType.DMA((len(pieces),)),
            swaps,
            swaps,
            pltpu.SemaphoreType.DMA,
        ],
        compiler_params=pltpu.CompilerParams(collective_id=collective, has_side_effects=True),
    )(*operands)


def reduce_kernel(sizes, count, routed, *refs):
    partials, refs = refs[:count], refs[count:]
    if routed:
        rows_ref, refs = refs[0], refs[1:]
    sums, refs = refs[:count], refs[count:]
    if routed:
        arrived_ref, refs = refs[0], refs[1:]
    planes, refs = refs[:count], refs[count:]
    groups, refs = refs[:count], refs[count:]
    line_parts, refs = refs[:count], refs[count:]
    send, arrive, own, swap_send, swap_arrive, swap_own = refs
    place = Place(sizes)
    pipe, grp, dp = place.pipe, place.grp, place.dp
    partners = (place.beside, place.below, place.across)
    lines = place.dps - 1
    if routed:
        greet([ahead for ahead, _ in place.others()])
    else:
        greet(
            [(pipe, grp, place.line(k + 1)) for k in range(lines)]
            + [(pipe, other, dp) for other in partners]
        )
    copies, keeps = [], []
    for n in range(count):
        for j, other in enumerate(partners):
            copies.append(
                remote(
                    partials[n].at[other],
                    planes[n].at[j],
                    send.at[n, j],
                    arrive.at[n, j],
                    (pipe, other, dp),
                )
            )
            copies[-1].start()
        keeps.append(pltpu.make_async_copy(partials[n].at[grp], groups[n], own.at[n]))
        keeps[-1].start()
        if n == 0 and routed:
            finish = swap_all(place, rows_ref, arrived_ref, swap_send, swap_arrive, swap_own)
    for n in range(count):
        keeps[n].wait()
        for j in range(3):
            copies[3 * n + j].wait_recv()
        block = 16
        depth = groups[n].shape[0] // place.dps

        def add_plane(i, _, n=n):
            at = pl.ds(pl.multiple_of(i * block, block), block)
            total = groups[n][at].astype(jnp.float32)
            for j in range(3):
                total = total + planes[n][j, at].astype(jnp.float32)
            groups[n][at] = total.astype(jnp.bfloat16)
            return 0

        lax.fori_loop(0, groups[n].shape[0] // block, add_plane, 0)
        for k in range(lines):
            first = pl.multiple_of(place.line(k + 1) * depth, 16)
            copies.append(
                remote(
                    groups[n].at[pl.ds(first, depth)],
                    line_parts[n].at[k],
                    send.at[n, 3 + k],
                    arrive.at[n, 3 + k],
                    (pipe, grp, place.line(k + 1)),
                )
            )
            copies[-1].start()
    for n in range(count):
        depth = groups[n].shape[0] // place.dps
        for k in range(lines):
            copies[3 * count + lines * n + k].wait_recv()

        def add_line(i, _, n=n, depth=depth):
            at = pl.ds(pl.multiple_of(i * block, block), block)
            first = pl.multiple_of(dp * depth + i * block, block)
            total = groups[n][pl.ds(first, block)].astype(jnp.float32)
            for k in range(lines):
                total = total + line_parts[n][k, at].astype(jnp.float32)
            sums[n][at] = total
            return 0

        lax.fori_loop(0, depth // block, add_line, 0)
    for copy in copies:
        copy.wait_send()
    if routed:
        finish()


def reduce_all(partials, sizes, collective, rows=None):
    parts = math.prod(sizes)
    count = len(partials)
    routed = rows is not None
    low = jnp.bfloat16
    tall = [(partial.shape[1], partial.shape[2]) for partial in partials]
    flat = [(height // sizes[2], columns) for height, columns in tall]
    out_shape = [jax.ShapeDtypeStruct(shape, jnp.float32) for shape in flat]
    out_specs = [pl.BlockSpec(memory_space=pltpu.VMEM)] * count
    if routed:
        out_shape.append(jax.ShapeDtypeStruct(rows.shape, rows.dtype))
        out_specs.append(pl.BlockSpec(memory_space=pl.ANY))
    operands = list(partials) + ([rows] if routed else [])
    sems = pltpu.SemaphoreType.DMA((count, 3 + sizes[2] - 1))
    swaps = pltpu.SemaphoreType.DMA((parts - 1 if routed else 1,))
    return pl.pallas_call(
        functools.partial(reduce_kernel, sizes, count, routed),
        out_shape=out_shape,
        in_specs=[pl.BlockSpec(memory_space=pl.ANY)] * len(operands),
        out_specs=out_specs,
        scratch_shapes=[pltpu.VMEM((3,) + shape, low) for shape in tall]
        + [pltpu.VMEM(shape, low) for shape in tall]
        + [pltpu.VMEM((sizes[2] - 1,) + shape, low) for shape in flat]
        + [
            sems,
            sems,
            pltpu.SemaphoreType.DMA((count,)),
            swaps,
            swaps,
            pltpu.SemaphoreType.DMA,
        ],
        compiler_params=pltpu.CompilerParams(
            collective_id=collective, has_side_effects=True, vmem_limit_bytes=48 << 20
        ),
    )(*operands)


def gather_weights(shards, sizes, collective, pieces, rows=None):
    if collective is not None:
        *fulls, arrived = gather_all(shards, pieces, sizes, collective, rows)
    else:
        fulls = [lax.all_gather(shard, AXES, axis=0) for shard in shards]
        arrived = lax.all_to_all(rows, AXES, 0, 0)
    return [full.reshape(-1, full.shape[-1]) for full in fulls], arrived


def gather_rows(shard, sizes, collective):
    if collective is None:
        return lax.all_gather(shard, AXES, axis=0, tiled=True)
    cuts = 4
    size = shard.shape[0] // cuts
    pieces = [(0, i * size, size) for i in range(cuts)]
    (full,) = gather_all([shard], pieces, sizes, collective)
    return full.reshape(-1, full.shape[-1])


def reduce_chips(partials, sizes, collective, rows=None):
    if collective is not None:
        shaped = [p.reshape(sizes[1], -1, p.shape[1]) for p in partials]
        sums = reduce_all(shaped, sizes, collective, rows)
        return (sums[:-1], sums[-1]) if rows is not None else (sums, None)
    sums = [
        lax.psum_scatter(p, CHIPS, scatter_dimension=0, tiled=True).astype(jnp.float32)
        for p in partials
    ]
    return sums, lax.all_to_all(rows, AXES, 0, 0) if rows is not None else None


def spread_row(row, sizes, collective):
    if collective is None:
        return lax.all_gather(row, AXES, axis=0)
    return spread(row, sizes, collective)


def share_stats(peak, total, label, sizes, collective):
    if collective is None:
        top = lax.pmax(peak, AXES)
        total, label = lax.psum((total * jnp.exp(peak - top), label), AXES)
        return top, total, label
    parts = math.prod(sizes)
    stats = jnp.stack([peak, total, label])
    stats = jnp.pad(stats.reshape(3, parts, -1).swapaxes(0, 1), ((0, 0), (0, 5), (0, 0)))
    stats = combine_stats(stats, sizes, collective)
    return [stats[:, i].reshape(-1) for i in range(3)]


def adam_step(weight, first, second, grad, factor, rate):
    clipped = grad * factor
    first = beta_one * first + (1.0 - beta_one) * clipped
    second = beta_two * second + (1.0 - beta_two) * clipped * clipped
    first_hat = first / (1.0 - beta_one**STEP)
    second_hat = second / (1.0 - beta_two**STEP)
    weight = weight - rate * (first_hat / (jnp.sqrt(second_hat) + epsilon) + weight_decay * weight)
    return (weight, first, second)


def per_device(
    token_ids,
    lengths,
    masked_at,
    labels,
    word_table,
    word_first,
    word_second,
    pos_table,
    pos_first,
    pos_second,
    qkv_weight,
    qkv_first,
    qkv_second,
    square_weight,
    square_first,
    square_second,
    up_weight,
    up_first,
    up_second,
    down_weight,
    down_first,
    down_second,
    vec_table,
    vec_first,
    vec_second,
    head_bias,
    bias_first,
    bias_second,
):
    narrow = jnp.bfloat16
    seq_len, slots = token_ids.shape[1], masked_at.shape[1]
    width = word_table.shape[1]
    vocab = head_bias.shape[0]
    rows_per = word_table.shape[0]
    parts = lax.axis_size(AXES)
    halves = lax.axis_size("pipe")
    me = lax.axis_index(AXES)
    own = token_ids.shape[0] // halves
    first_own = lax.axis_index("pipe") * own
    head_dim = width // H
    sizes = tuple(lax.axis_size(axis) for axis in AXES)
    shards = (word_table, qkv_weight, square_weight[0], up_weight, down_weight)
    direct = sizes[:2] == (2, 4) and all(shard.shape[0] % 32 == 0 for shard in shards)
    ids = tuple(range(7)) if direct else (None,) * 7

    spare = -(seq_len + slots + 1) % 128
    packed = jnp.concatenate(
        [token_ids, labels, lengths[:, None], jnp.zeros((token_ids.shape[0], spare), jnp.int32)], 1
    )
    packed = lax.dynamic_slice_in_dim(packed, first_own, own, 0)
    packed = spread_row(packed, sizes, ids[0])
    all_ids = packed[:, :, :seq_len]
    all_labels = packed[:, :, seq_len : seq_len + slots].reshape(-1)
    all_lengths = packed[:, :, seq_len + slots]
    places = jnp.arange(seq_len, dtype=jnp.int32)
    all_live = places[None, None, :] < all_lengths[:, :, None]
    all_counts = masked_counts(all_lengths, slots)
    total = jnp.sum(all_counts).astype(jnp.float32)
    slot_index = jnp.arange(slots, dtype=jnp.int32)
    all_valid = (slot_index < all_counts[:, :, None]).astype(jnp.float32).reshape(-1)
    own_lengths = lax.dynamic_slice_in_dim(lengths, first_own, own, 0)
    masked = lax.dynamic_slice_in_dim(masked_at, first_own, own, 0)

    word_low = word_table.astype(narrow)
    routes = Routes(all_ids.reshape(parts, -1), all_live.reshape(parts, -1), rows_per)
    small = pos_table.shape[0] + vec_table.shape[0]
    spare = -small % 128
    small_low = jnp.concatenate(
        [pos_table.T, vec_table.T, jnp.zeros((pos_table.shape[1], spare), jnp.float32)], 1
    ).astype(narrow)
    low = [
        small_low,
        qkv_weight.astype(narrow),
        square_weight[0].astype(narrow),
        up_weight.astype(narrow),
        down_weight.astype(narrow),
        square_weight[1].astype(narrow),
    ]
    pieces = [(i, 0, shard.shape[0]) for i, shard in enumerate(low)]
    send = routes.table_rows(word_low, 0).reshape(parts, -1, width)
    (small_full, qkv_low, out_low, up_low, down_low, turn_low), arrived = gather_weights(
        low, sizes, ids[1], pieces, send
    )
    word_rows = routes.fetch(word_low, arrived.reshape(-1, width))
    small_full = small_full.T
    pos_low = small_full[:seq_len]
    vec_rows = small_full[seq_len:small].astype(jnp.float32)
    query_low, both_low = qkv_low[:, :width], qkv_low[:, width:]

    second = (places[None, :] >= ((own_lengths + 1) // 2)[:, None]).reshape(-1, 1)
    live = (places[None, :] < own_lengths[:, None])[:, None, None, :]
    embedded = (
        word_rows
        + jnp.tile(pos_low.astype(jnp.float32), (own, 1))
        + jnp.where(second, vec_rows[1], vec_rows[0])
    )
    start, norm_zero = norm_forward(embedded, vec_rows[2], vec_rows[3])
    start_low = start.astype(narrow)
    both_bias = jnp.concatenate([jnp.zeros_like(vec_rows[5]), vec_rows[5]])
    both = (matmul(start_low, both_low) + both_bias).astype(narrow)
    both = both.reshape(own, seq_len, 2, H, head_dim)
    key_rows, value_rows = both[:, :, 0], both[:, :, 1]
    pick = one_hot(masked, seq_len, jnp.float32)
    chosen = rows_by_seq(pick, start.reshape(own, seq_len, width)).reshape(-1, width)
    chosen_low = chosen.astype(narrow)
    queries = (matmul(chosen_low, query_low) + vec_rows[4]).astype(narrow)
    queries = queries.reshape(own, slots, H, head_dim)
    scale = head_dim ** (-0.5)
    scores = (
        jnp.einsum("sqhd,skhd->shqk", queries, key_rows, preferred_element_type=jnp.float32)
        * scale
    )
    scores = jnp.where(live, scores, -1e30)
    exp_scores = jnp.exp(scores - jnp.max(scores, -1, keepdims=True))
    probs = exp_scores / jnp.sum(exp_scores, -1, keepdims=True)
    probs_low = probs.astype(narrow)
    context = jnp.einsum(
        "shqk,skhd->sqhd", probs_low, value_rows, preferred_element_type=jnp.float32
    )
    context = context.reshape(-1, width).astype(narrow)
    branch = matmul(context, out_low) + vec_rows[6]
    hidden, norm_one = norm_forward(chosen + branch, vec_rows[7], vec_rows[8])
    hidden = hidden.astype(narrow)

    inner = matmul(hidden, up_low) + vec_rows[15:].reshape(-1)
    activ = jax.nn.gelu(inner, approximate=False).astype(narrow)
    branch = matmul(activ, down_low) + vec_rows[9]
    mixed, norm_two = norm_forward(hidden.astype(jnp.float32) + branch, vec_rows[10], vec_rows[11])
    picked = mixed.astype(narrow)
    turned = matmul(picked, turn_low) + vec_rows[12]
    normed, norm_head = norm_forward(
        jax.nn.gelu(turned, approximate=False), vec_rows[13], vec_rows[14]
    )

    all_normed = gather_rows(normed.astype(narrow), sizes, ids[2])
    column = me * rows_per + jnp.arange(rows_per, dtype=jnp.int32)
    bias_row = jnp.pad(head_bias, (0, parts * rows_per - vocab))
    bias_row = lax.dynamic_slice_in_dim(bias_row, me * rows_per, rows_per, 0)
    logits = right_transposed(all_normed, word_low) + bias_row
    logits = jnp.where(column < vocab, logits, -1e30)
    own_peak = jnp.max(logits, -1)
    own_total = jnp.sum(jnp.exp(logits - own_peak[:, None]), -1)
    hits = all_labels[:, None] == column
    own_label = jnp.sum(jnp.where(hits, logits, 0.0), -1)
    peak, exp_total, label_logit = share_stats(own_peak, own_total, own_label, sizes, ids[3])
    loss_total = jnp.sum(all_valid * (peak + jnp.log(exp_total) - label_logit))
    d_logits = (all_valid / total)[:, None] * (
        jnp.exp(logits - peak[:, None]) / exp_total[:, None] - hits.astype(jnp.float32)
    )
    d_bias = jnp.sum(d_logits, 0)
    d_logits_low = d_logits.astype(narrow)
    d_word = left_transposed(d_logits_low, all_normed)
    d_normed = chip_half(matmul(d_logits_low, word_low))
    columns = width // 2
    d_normed, _ = reduce_chips([d_normed[:, :columns], d_normed[:, columns:]], sizes, ids[4])
    d_normed = jnp.concatenate(d_normed, 1)

    d_gelu, d_gain_head, d_shift_head = norm_backward(d_normed, norm_head, vec_rows[13])
    d_turned = (d_gelu * gelu_slope(turned)).astype(narrow)
    d_turn_bias = jnp.sum(d_turned.astype(jnp.float32), 0)
    d_turn = chip_sum(picked, d_turned)
    d_picked = right_transposed(d_turned, turn_low)
    same = masked[:, :, None] == masked[:, None, :]
    earlier = slot_index[None, :] < slot_index[:, None]
    first_slot = jnp.logical_not(jnp.any(same & earlier, 2))
    merge = (same & first_slot[:, :, None]).astype(jnp.float32)
    d_mixed = rows_by_seq(merge, d_picked.reshape(own, slots, width)).reshape(-1, width)
    d_pre, d_gain_two, d_shift_two = norm_backward(d_mixed, norm_two, vec_rows[10])
    d_branch = d_pre.astype(narrow)
    d_down_bias = jnp.sum(d_branch.astype(jnp.float32), 0)
    d_down = chip_sum(activ, d_branch)
    d_inner = (right_transposed(d_branch, down_low) * gelu_slope(inner)).astype(narrow)
    d_up_bias = jnp.sum(d_inner.astype(jnp.float32), 0).reshape(-1, width)
    d_up = chip_sum(hidden, d_inner)
    d_hidden = (d_pre + right_transposed(d_inner, up_low)).astype(narrow)

    d_pre, d_gain_one, d_shift_one = norm_backward(
        d_hidden.astype(jnp.float32), norm_one, vec_rows[7]
    )
    d_branch = d_pre.astype(narrow)
    d_out_bias = jnp.sum(d_branch.astype(jnp.float32), 0)
    d_out = chip_sum(context, d_branch)
    d_context = right_transposed(d_branch, out_low).astype(narrow)
    d_context = d_context.reshape(own, slots, H, head_dim)
    d_value = jnp.einsum(
        "shqk,sqhd->skhd", probs_low, d_context, preferred_element_type=jnp.float32
    )
    d_probs = jnp.einsum(
        "sqhd,skhd->shqk", d_context, value_rows, preferred_element_type=jnp.float32
    )
    d_scores = (probs * (d_probs - jnp.sum(probs * d_probs, -1, keepdims=True))).astype(narrow)
    d_query = (
        jnp.einsum("shqk,skhd->sqhd", d_scores, key_rows, preferred_element_type=jnp.float32)
        * scale
    )
    d_query = d_query.reshape(-1, width).astype(narrow)
    d_key = (
        jnp.einsum("shqk,sqhd->skhd", d_scores, queries, preferred_element_type=jnp.float32)
        * scale
    )
    d_both = jnp.stack([d_key, d_value], 2).reshape(own * seq_len, 2 * width).astype(narrow)
    d_query_bias = jnp.sum(d_query.astype(jnp.float32), 0)
    d_value_bias = jnp.sum(d_both[:, width:].astype(jnp.float32), 0)
    d_qkv = jnp.concatenate(
        [chip_sum(chosen_low, d_query), chip_sum(start_low, d_both)], 1
    )
    d_chosen = d_pre + right_transposed(d_query, query_low)
    d_start = right_transposed(d_both, both_low) + rows_to_seq(
        pick, d_chosen.reshape(own, slots, width)
    ).reshape(-1, width)
    d_embedded, d_gain_zero, d_shift_zero = norm_backward(d_start, norm_zero, vec_rows[2])
    d_seg_zero = jnp.sum(jnp.where(second, 0.0, d_embedded), 0)
    d_seg_one = jnp.sum(jnp.where(second, d_embedded, 0.0), 0)
    d_embedded_low = d_embedded.astype(narrow)
    send = routes.token_rows(d_embedded_low, 0).reshape(parts, -1, width)
    d_small = jnp.concatenate(
        [
            jnp.sum(d_embedded.reshape(own, seq_len, width), 0),
            jnp.stack(
                [
                    d_seg_zero,
                    d_seg_one,
                    d_gain_zero,
                    d_shift_zero,
                    d_query_bias,
                    d_value_bias,
                    d_out_bias,
                    d_gain_one,
                    d_shift_one,
                    d_down_bias,
                    d_gain_two,
                    d_shift_two,
                    d_turn_bias,
                    d_gain_head,
                    d_shift_head,
                ]
            ),
            d_up_bias,
            jnp.zeros((spare, width), jnp.float32),
        ],
        0,
    )
    (own_up, own_down, own_qkv, own_turn, own_out, own_small), arrived = reduce_chips(
        [d_up, d_down, d_qkv, d_turn, d_out, chip_half(d_small.T)], sizes, ids[5], send
    )
    d_word = d_word + routes.give(d_embedded_low, arrived.reshape(-1, width))
    owned = (
        d_word,
        own_small[:, :seq_len].T,
        own_qkv,
        jnp.stack([own_out, own_turn]),
        own_up,
        own_down,
        own_small[:, seq_len:small].T,
    )
    local_squares = jnp.sum(d_bias * d_bias)
    for grad in owned:
        local_squares = local_squares + jnp.sum(grad * grad)
    spare = -(rows_per + 1) % 128
    last = jnp.concatenate([d_bias, local_squares[None], jnp.zeros((spare,), jnp.float32)])
    last = spread_row(last.reshape(8, -1), sizes, ids[6]).reshape(parts, -1)
    bias_grad = last[:, :rows_per].reshape(-1)[:vocab]
    grad_norm = jnp.sqrt(jnp.sum(last[:, rows_per]))
    factor = clip_norm / jnp.maximum(grad_norm, clip_norm)
    masters = (
        word_table,
        pos_table,
        qkv_weight,
        square_weight,
        up_weight,
        down_weight,
        vec_table,
        head_bias,
    )
    states = (
        (word_first, word_second),
        (pos_first, pos_second),
        (qkv_first, qkv_second),
        (square_first, square_second),
        (up_first, up_second),
        (down_first, down_second),
        (vec_first, vec_second),
        (bias_first, bias_second),
    )
    rates = (
        learn_rate,
        learn_rate,
        learn_rate,
        learn_rate,
        learn_rate,
        learn_rate,
        vector_rate,
        vector_rate,
    )
    grads = tuple(owned) + (bias_grad,)
    results = []
    for weight, state, grad, rate in zip(masters, states, grads, rates):
        results.extend(adam_step(weight, state[0], state[1], grad, factor, rate))
    return (
        results[0],
        results[1],
        results[2],
        results[3],
        results[4],
        results[5],
        results[6],
        results[7],
        results[8],
        results[9],
        results[10],
        results[11],
        results[12],
        results[13],
        results[14],
        results[15],
        results[16],
        results[17],
        results[18],
        results[19],
        results[20],
        results[21],
        results[22],
        results[23],
        loss_total,
        total,
        grad_norm,
    )


def solution(mesh):
    placed = (
        P(("grp", "dp"), None),
        P(("grp", "dp")),
        P(("grp", "dp"), None),
        P(("grp", "dp"), None),
        P(("pipe", "grp", "dp"), None),
        P(("pipe", "grp", "dp"), None),
        P(("pipe", "grp", "dp"), None),
        P(None, ("pipe", "grp", "dp")),
        P(None, ("pipe", "grp", "dp")),
        P(None, ("pipe", "grp", "dp")),
        P(("pipe", "grp", "dp"), None),
        P(("pipe", "grp", "dp"), None),
        P(("pipe", "grp", "dp"), None),
        P(None, ("pipe", "grp", "dp"), None),
        P(None, ("pipe", "grp", "dp"), None),
        P(None, ("pipe", "grp", "dp"), None),
        P(("pipe", "grp", "dp"), None),
        P(("pipe", "grp", "dp"), None),
        P(("pipe", "grp", "dp"), None),
        P(("pipe", "grp", "dp"), None),
        P(("pipe", "grp", "dp"), None),
        P(("pipe", "grp", "dp"), None),
        P(None, ("pipe", "grp", "dp")),
        P(None, ("pipe", "grp", "dp")),
        P(None, ("pipe", "grp", "dp")),
        P(),
        P(),
        P(),
    )
    return jax.shard_map(
        per_device,
        mesh=mesh,
        in_specs=placed,
        out_specs=(
            P(("pipe", "grp", "dp"), None),
            P(("pipe", "grp", "dp"), None),
            P(("pipe", "grp", "dp"), None),
            P(None, ("pipe", "grp", "dp")),
            P(None, ("pipe", "grp", "dp")),
            P(None, ("pipe", "grp", "dp")),
            P(("pipe", "grp", "dp"), None),
            P(("pipe", "grp", "dp"), None),
            P(("pipe", "grp", "dp"), None),
            P(None, ("pipe", "grp", "dp"), None),
            P(None, ("pipe", "grp", "dp"), None),
            P(None, ("pipe", "grp", "dp"), None),
            P(("pipe", "grp", "dp"), None),
            P(("pipe", "grp", "dp"), None),
            P(("pipe", "grp", "dp"), None),
            P(("pipe", "grp", "dp"), None),
            P(("pipe", "grp", "dp"), None),
            P(("pipe", "grp", "dp"), None),
            P(None, ("pipe", "grp", "dp")),
            P(None, ("pipe", "grp", "dp")),
            P(None, ("pipe", "grp", "dp")),
            P(),
            P(),
            P(),
            P(),
            P(),
            P(),
        ),
        check_vma=False,
    )
```

time: 3300 us -> 998 us (0.30)
  waiting for transfers between devices: 2150 us -> 0.04 us
  Pallas kernels: 0 us -> 594 us
  other arithmetic: 434 us -> 108 us
  matrix products: 473 us -> 169 us
  blocking collectives: 154 us -> 0 us
  local copies, waits for them, and re-layouts: 45.8 us -> 100 us
    reduce_scatter x11 -> x0, waiting for transfers between devices: 1460 us -> none  [the longest x1 852 us: per_device(): lax.psum_scatter(halves[0], ('grp', 'dp'), scatter_dimension=0, tiled=True)]
    pallas_call x0 -> x7, Pallas kernels: none -> 594 us  [the longest x2 288 us: gather_all(): pl.pallas_call(functools.partial(gather_kernel, sizes, tuple(pieces), rou...]
    all_gather x6 -> x0, waiting for transfers between devices: 410 us -> none  [the longest x1 314 us: per_device(): lax.all_gather(word_table.astype(narrow), ('pipe', 'grp', 'dp'), axis=0,...]
    unnamed x24 -> x0, waiting for transfers between devices: 166 us -> none
    scatter-add x3 -> x0, other arithmetic: 152 us -> none  [the longest x1 147 us: per_device(): table_grad.at[jnp.concatenate(row_ids, 0)]]
    convert_element_type x21 -> x14, other arithmetic: 161 us -> 17.3 us  [the longest x2 5.77 us: chip_half(): (keep.astype(jnp.float32) + swapped(give).astype(jnp.float32)).astype(jnp...]
    psum x1 -> x0, waiting for transfers between devices: 119 us -> none  [per_device(): lax.psum((loss_part, bias_sum), ('pipe', 'grp', 'dp'))]
    dot_general x12 -> x9, matrix products: 144 us -> 55.4 us  [matmul(): return jnp.dot(left, right, preferred_element_type=jnp.float32)]
  transfers between devices with their start and end apart: 25 -> 14, of which waited for: 13 -> 0; matrix products, arithmetic and copies ran while one was open for 19% -> 12% of each run, Pallas kernels for 0% -> 6%
where the time goes in v1:
time: 998 us; the launch traced here: 988 us
  Pallas kernels  594 us (60%)
  matrix products  169 us (17%)
  other arithmetic  108 us (11%)
  local copies, waits for them, and re-layouts  100 us (10%)
  between operations  12.7 us (1%)
    pallas_call x2, Pallas kernels, gather_all(): pl.pallas_call(functools.partial(gather_kernel, sizes, tuple(pieces), rou...  288 us
    pallas_call x2, Pallas kernels, reduce_all(): pl.pallas_call(functools.partial(reduce_kernel, sizes, count, routed), ou...  267 us
    dot_general x9, matrix products, matmul(): return jnp.dot(left, right, preferred_element_type=jnp.float32)  55.4 us
    dot_general x9, matrix products, left_transposed(): lax.dot_general(left, right, (((0,), (0,)), ((), ())), preferred_element_...  54 us
    dot_general x7, matrix products, right_transposed(): lax.dot_general(left, right, (((1,), (1,)), ((), ())), preferred_element_...  42.3 us
    unnamed x271, local copies, waits for them, and re-layouts  33.6 us
    pallas_call x2, Pallas kernels, spread(): pl.pallas_call(functools.partial(spread_kernel, sizes), out_shape=jax.Sha...  21.8 us
    sub x8, other arithmetic, adam_step(): weight - rate * (first_hat / (jnp.sqrt(second_hat) + epsilon) + weight_de...  21 us
  transfers between devices with their start and end apart: 14, of which 0 were waited for; matrix products, arithmetic and copies ran while one was open for 12% of the time, Pallas kernels for 6%

profile of v1, /device:TPU:0, one launch (start us, length us, event | category | flops | bytes accessed | tf_op | source)
XLA Modules:
  0.0 988.4 jit_solution(17961795158111906128)
XLA Ops:
  2.3 12.5 %shard_map.475 = s32[32,2,640]{2,1,0:T(2,128)S(1)} custom-call(s32[2,640]{1,0:T(2,128)S(1)} %fusion.191.row_ref), custom_call_target="tpu_custom_call" | custom-call | tf_op jit(solution)/shard_map/pallas_call | solution.py:280
  16.7 9.0 reduce-window.16
  36.1 6.6 fusion.32
  43.4 234.1 %shard_map.476 = (bf16[2,4,4,32,640]{4,3,2,1,0:T(8,128)(2,1)}, bf16[2,4,4,32,3072]{4,3,2,1,0:T(8,128)(2,1)}, bf16[2,4,4,32,1024]{4,3,2,1,0:T(8,128)(2,1)}, bf16[...) custom-call(bf16[32,640]{1,0:T(8,128)(2,1)} %maximum_maximum_fusion., ...), custom_call_target="tpu_custom_call" | custom-call | tf_op jit(solution)/shard_map/pallas_call | solution.py:441
  283.9 9.0 reduce-window.14
  293.5 7.0 fusion.24
  314.2 8.4 add_convert_fusion.1
  322.6 12.9 %reshape.689 = bf16[2,512,2,16,64]{4,3,2,1,0:T(8,128)(2,1)} reshape(bf16[1024,2048]{1,0:T(8,128)(2,1)} %add_convert_fusion.1) | data formatting | bytes 8388608 | tf_op jit(solution)/shard_map/reshape | solution.py:743
  335.5 6.2 fusion.226
  341.7 5.4 copy.217
  347.3 5.4 copy.216
  366.0 9.1 fusion.46
  384.7 53.8 %shard_map.477 = bf16[2,4,4,128,1024]{4,3,2,1,0:T(8,128)(2,1)} custom-call(bf16[128,1024]{1,0:T(8,128)(2,1)} %add_convert_fusion.2.refs_0_), custom_call_target="tpu_custom_call" | custom-call | tf_op jit(solution)/shard_map/pallas_call | solution.py:441
  439.5 11.5 %fusion.16 = (f32[4096]{0:T(1024)S(1)}, f32[4096,960]{0,1:T(8,128)S(1)}) fusion(f32[960]{0:T(1024)S(1)} %pad_dynamic-slice_fusion, pred[960]{0:T(1024)(128)(4,1)S(1)} %copy-done.120, bf16[4096,1024]{1,0:T(8,128)(2,1)} %bitcast.277, bf16[960,1024]{1,0:T(8,128)(2,1)} %convert_element_type.237), kind=kOutput, calls=%fused_computation.34 | convolution fusion | flops 8064856064 | bytes 26104512 | tf_op jit(solution)/shard_map/dot_general | solution.py:41
  451.0 6.2 exponential_reduce_fusion
  457.2 17.2 %shard_map.478 = f32[32,8,128]{2,1,0:T(8,128)S(1)} custom-call(f32[32,8,128]{2,1,0:T(8,128)S(1)} %pad.10.own_ref), custom_call_target="tpu_custom_call" | custom-call | tf_op jit(solution)/shard_map/pallas_call | solution.py:321
  486.9 10.8 %fusion.212 = (f32[960]{0:T(1024)S(1)}, bf16[4096,960]{0,1:T(8,128)(2,1)S(1)}) fusion(s32[960]{0:T(1024)} %iota_add_fusion.2, s32[4096]{0:T(1024)S(1)} %eq.245, f32[4096]{0:T(1024)S(1)} %bitcast.319, f32[4096]{0:T(1024)S(1)} %bitcast.320, f32[4096,960]{0,1:T(8,128)} %copy-done.6, f32[960]{0:T(1024)} %copy-done.88, pred[960]{0:T(1024)(128)(4,1)} %broadcast_compare_fusion, ...), kind=kLoop, calls=%fused_computation.400 | loop fusion | flops 39320640 | bytes 23670976 | tf_op jit(solution)/shard_map/reduce_sum | solution.py:792
  500.9 12.8 %convolution_convert_fusion = bf16[4096,1024]{1,0:T(8,128)(2,1)} fusion(bf16[960,1024]{1,0:T(8,128)(2,1)} %convert_element_type.237, bf16[4096,960]{0,1:T(8,128)(2,1)S(1)} %get-tuple-element.480), kind=kOutput, calls=%fused_computation.41 | convolution fusion | flops 8057257984 | bytes 18219008 | tf_op jit(solution)/shard_map/dot_general | solution.py:31
  532.6 5.6 add_convert_fusion
  538.5 61.7 %shard_map.479 = (f32[128,512]{1,0:T(8,128)S(1)}, f32[128,512]{1,0:T(8,128)S(1)}) custom-call(bf16[4,512,512]{2,1,0:T(8,128)(2,1)S(1)} %bitcast.254, bf16[4,512,512]{2,1,0:T(8,128)(2,1)S(1)} %bitcast.253), custom_call_target="tpu_custom_call" | custom-call | tf_op jit(solution)/shard_map/pallas_call | solution.py:561
  604.1 8.7 fusion.233
  612.9 7.5 fusion.121
  643.8 6.4 copy.204
  650.2 5.5 copy.227
  655.8 10.2 %multiply_reduce_fusion = (bf16[1024]{0:T(1024)(128)(2,1)S(1)}, f32[1024]{0:T(1024)S(1)}, f32[1024]{0:T(1024)S(1)}, bf16[1024]{0:T(1024)(128)(2,1)S(1)}, f32[1024,1024]{1,0:T(8,128)S(1)}) fusion(f32[1024,1024]{1,0:T(8,128)S(1)} %copy-done.5, f32[1024]{0:T(1024)S(1)} %copy-done.87, f32[1024]{0:T(1024)S(1)} %copy-done.71, f32[1024]{0:T(1024)S(1)} %bitcast.325, ...), kind=kOutput, calls=%fused_computation.59 | convolution fusion | flops 4305448960 | bytes 20996096 | tf_op jit(solution)/shard_map/dot_general | solution.py:41
  678.9 6.8 fusion.31
  702.8 8.4 fusion.41
  713.2 205.3 %shard_map.480 = (f32[32,4096]{1,0:T(8,128)S(1)}, f32[128,1024]{1,0:T(8,128)S(1)}, f32[32,3072]{1,0:T(8,128)S(1)}, f32[32,1024]{1,0:T(8,128)S(1)}, f32[32,1024]{...) custom-call(bf16[4,128,4096]{2,1,0:T(8,128)(2,1)} %bitcast.273, bf16[4,512,1024]{2,1,0:T(8,128)(2,1)} %bitcast.284, ...), custom_call_target="tpu_custom_call" | custom-call | tf_op jit(solution)/shard_map/pallas_call | solution.py:561
  919.8 7.2 fusion.21
  927.1 15.9 %multiply_reduce_fusion.4 = (f32[]{:T(128)}, f32[960,1024]{1,0:T(8,128)}) fusion(f32[960,1024]{1,0:T(8,128)} %get-tuple-element.262, bf16[4096,1024]{1,0:T(8,128)(2,1)} %bitcast.278, bf16[4096,960]{0,1:T(8,128)(2,1)} %copy-done.17), kind=kOutput, calls=%fused_computation.77 | convolution fusion | flops 8056012800 | bytes 24117252 | tf_op jit(solution)/shard_map/dot_general | solution.py:35
  951.1 9.3 shard_map.481
  978.4 7.3 multiply_subtract_fusion
  (496 shorter events, 171.8 us)
Async XLA Ops:
  0.7 304.8 %copy-start = (s32[4,64]{1,0:T(4,128)S(1)}, s32[4,64]{1,0:T(4,128)}, u32[]{:S(2)}) copy-start(s32[4,64]{1,0:T(4,128)} %param.34) | copy-start | bytes 3076
  14.8 267.9 %copy-start.2 = (s32[32,2,640]{2,1,0:T(2,128)}, s32[32,2,640]{2,1,0:T(2,128)S(1)}, u32[]{:S(2)}) copy-start(s32[32,2,640]{2,1,0:T(2,128)S(1)} %shard_map.475) | copy-start | bytes 491524
  281.4 83.7 %copy-start.72 = (f32[1,1024]{1,0:T(1,128)}, f32[1,1024]{1,0:T(1,128)S(1)}, u32[]{:S(2)}) copy-start(f32[1,1024]{1,0:T(1,128)S(1)} %get-tuple-element.533) | copy-start | bytes 12292
  281.4 99.2 %copy-start.68 = (f32[1,1024]{1,0:T(1,128)}, f32[1,1024]{1,0:T(1,128)S(1)}, u32[]{:S(2)}) copy-start(f32[1,1024]{1,0:T(1,128)S(1)} %get-tuple-element.530) | copy-start | bytes 12292
  281.4 101.9 %copy-start.74 = (f32[1,1024]{1,0:T(1,128)}, f32[1,1024]{1,0:T(1,128)S(1)}, u32[]{:S(2)}) copy-start(f32[1,1024]{1,0:T(1,128)S(1)} %get-tuple-element.526) | copy-start | bytes 12292
  314.2 38.5 %copy-start.19 = (bf16[2,64,16,64]{1,3,2,0:T(8,128)(2,1)}, bf16[2,64,16,64]{1,3,2,0:T(8,128)(2,1)S(1)}, u32[]{:S(2)}) copy-start(bf16[2,64,16,64]{1,3,2,0:T(8,128)(2,1)S(1)} %copy.202) | copy-start | bytes 786436
  383.1 55.5 %copy-start.112 = (f32[128]{0:T(128)}, f32[128]{0:T(128)S(1)}, u32[]{:S(2)}) copy-start(f32[128]{0:T(128)S(1)} %broadcast_multiply_fusion.9) | copy-start | bytes 1540
  383.3 55.3 %copy-start.118 = (f32[128]{0:T(128)}, f32[128]{0:T(128)S(1)}, u32[]{:S(2)}) copy-start(f32[128]{0:T(128)S(1)} %add_rsqrt_fusion.1) | copy-start | bytes 1540
  384.7 53.8 %slice-start = ((s32[32,2,640]{2,1,0:T(2,128)}), s32[32,2,64]{2,1,0:T(2,128)S(1)}, s32[]{:S(2)}) async-start(s32[32,2,640]{2,1,0:T(2,128)} %copy-done.2), calls=%async_computation.2 | async-start | bytes 65536 | tf_op jit(solution)/shard_map/slice | solution.py:695
  384.7 54.7 %copy-start.120 = (pred[960]{0:T(1024)(128)(4,1)S(1)}, pred[960]{0:T(1024)(128)(4,1)}, u32[]{:S(2)}) copy-start(pred[960]{0:T(1024)(128)(4,1)} %broadcast_compare_fusion) | copy-start | bytes 2884
  518.4 14.1 %collective-permute-start.1 = (bf16[2048,1024]{1,0:T(8,128)(2,1)}, bf16[2048,1024]{1,0:T(8,128)(2,1)}, u32[]{:S(2)}, u32[]{:S(2)}) collective-permute-start(bf16[2048,1024]{1,0:T(8,128)(2,1)} %constant_dynamic-slice_fusion.10), channel_id=1, source_target_pairs={{0,16},{16,0},{1,17},{17,1},{2,18},{18,2},{3,19},{19,3},{4,20},{20... | collective-permute-start | bytes 12582920 | tf_op jit(solution)/shard_map/ppermute | solution.py:149
  520.7 150.4 %collective-permute-start.11 = (bf16[128,512]{1,0:T(8,128)(2,1)}, bf16[128,512]{1,0:T(8,128)(2,1)}, u32[]{:S(2)}, u32[]{:S(2)}) collective-permute-start(bf16[128,512]{1,0:T(8,128)(2,1)} %get-tuple-element.510), channel_id=1, source_target_pairs={{0,16},{16,0},{1,17},{17,1},{2,18},{18,2},{3,19},{19,3},{4,20},{20... | collective-permute-start | bytes 393224 | tf_op jit(solution)/shard_map/ppermute | solution.py:149
  522.4 155.4 %collective-permute-start.9 = (bf16[128,512]{1,0:T(8,128)(2,1)}, bf16[128,512]{1,0:T(8,128)(2,1)}, u32[]{:S(2)}, u32[]{:S(2)}) collective-permute-start(bf16[128,512]{1,0:T(8,128)(2,1)} %get-tuple-element.512), channel_id=1, source_target_pairs={{0,16},{16,0},{1,17},{17,1},{2,18},{18,2},{3,19},{19,3},{4,20},{20... | collective-permute-start | bytes 393224 | tf_op jit(solution)/shard_map/ppermute | solution.py:149
  524.6 153.3 %collective-permute-start.5 = (bf16[128,512]{1,0:T(8,128)(2,1)}, bf16[128,512]{1,0:T(8,128)(2,1)}, u32[]{:S(2)}, u32[]{:S(2)}) collective-permute-start(bf16[128,512]{1,0:T(8,128)(2,1)} %get-tuple-element.514), channel_id=1, source_target_pairs={{0,16},{16,0},{1,17},{17,1},{2,18},{18,2},{3,19},{19,3},{4,20},{20... | collective-permute-start | bytes 393224 | tf_op jit(solution)/shard_map/ppermute | solution.py:149
  526.9 151.5 %collective-permute-start.3 = (bf16[128,2048]{1,0:T(8,128)(2,1)}, bf16[128,2048]{1,0:T(8,128)(2,1)}, u32[]{:S(2)}, u32[]{:S(2)}) collective-permute-start(bf16[128,2048]{1,0:T(8,128)(2,1)} %get-tuple-element.507), channel_id=1, source_target_pairs={{0,16},{16,0},{1,17},{17,1},{2,18},{18,2},{3,19},{19,3},{4,20},{20... | collective-permute-start | bytes 1572872 | tf_op jit(solution)/shard_map/ppermute | solution.py:149
  538.4 61.9 %copy-start.16 = (f32[128,1024]{1,0:T(8,128)S(1)}, f32[128,1024]{1,0:T(8,128)}, u32[]{:S(2)}) copy-start(f32[128,1024]{1,0:T(8,128)} %copy-done.15) | copy-start | bytes 1572868
  538.4 61.9 %copy-start.75 = (f32[1,1024]{1,0:T(1,128)S(1)}, f32[1,1024]{1,0:T(1,128)}, u32[]{:S(2)}) copy-start(f32[1,1024]{1,0:T(1,128)} %copy-done.74) | copy-start | bytes 12292
  538.4 61.9 %copy-start.113 = (f32[128]{0:T(128)S(1)}, f32[128]{0:T(128)}, u32[]{:S(2)}) copy-start(f32[128]{0:T(128)} %copy-done.112) | copy-start | bytes 1540
  538.5 61.9 %copy-start.119 = (f32[128]{0:T(128)S(1)}, f32[128]{0:T(128)}, u32[]{:S(2)}) copy-start(f32[128]{0:T(128)} %copy-done.118) | copy-start | bytes 1540
  538.5 62.2 %copy-start.52 = (f32[128,1024]{1,0:T(8,128)S(1)}, f32[128,1024]{1,0:T(8,128)}, u32[]{:S(2)}) copy-start(f32[128,1024]{1,0:T(8,128)} %get-tuple-element.551) | copy-start | bytes 1572868
  538.5 62.6 %copy-start.30 = (bf16[2,4,4,32,1024]{4,3,2,1,0:T(8,128)(2,1)S(1)}, bf16[2,4,4,32,1024]{4,3,2,1,0:T(8,128)(2,1)}, u32[]{:S(2)}) copy-start(bf16[2,4,4,32,1024]{4,3,2,1,0:T(8,128)(2,1)} %get-tuple-element.258) | copy-start | bytes 6291460
  655.7 47.1 %collective-permute-start.8 = (bf16[1024,2048]{0,1:T(8,128)(2,1)}, bf16[1024,2048]{0,1:T(8,128)(2,1)}, u32[]{:S(2)}, u32[]{:S(2)}) collective-permute-start(bf16[1024,2048]{0,1:T(8,128)(2,1)} %bitcast.110), channel_id=1, source_target_pairs={{0,16},{16,0},{1,17},{17,1},{2,18},{18,2},{3,19},{19,3},{4,20},{20... | collective-permute-start | bytes 12582920 | tf_op jit(solution)/shard_map/ppermute | solution.py:149
  671.2 7.3 collective-permute-start.12
  677.8 8.0 collective-permute-start.10
  677.9 9.6 collective-permute-start.6
  678.4 19.4 %collective-permute-start.2 = (bf16[128,4096]{1,0:T(8,128)(2,1)}, bf16[128,4096]{1,0:T(8,128)(2,1)}, u32[]{:S(2)}, u32[]{:S(2)}) collective-permute-start(bf16[128,4096]{1,0:T(8,128)(2,1)} %get-tuple-element.562), channel_id=1, source_target_pairs={{0,16},{16,0},{1,17},{17,1},{2,18},{18,2},{3,19},{19,3},{4,20},{20... | collective-permute-start | bytes 3145736 | tf_op jit(solution)/shard_map/ppermute | solution.py:149
  678.5 18.8 %collective-permute-start.13 = (bf16[512,640]{0,1:T(8,128)(2,1)S(1)}, bf16[512,640]{0,1:T(8,128)(2,1)S(1)}, u32[]{:S(2)}, u32[]{:S(2)}) collective-permute-start(bf16[512,640]{0,1:T(8,128)(2,1)S(1)} %dynamic-slice_bitcast_fusion), channel_id=1, source_target_pairs={{0,16},{16,0},{1,17},{17,1},{2,18},{18,2},{3,19},{19,3},{4,20},{20... | collective-permute-start | bytes 1966088 | tf_op jit(solution)/shard_map/ppermute | solution.py:149
  685.8 17.0 %collective-permute-start.7 = (bf16[1024,512]{1,0:T(8,128)(2,1)}, bf16[1024,512]{1,0:T(8,128)(2,1)}, u32[]{:S(2)}, u32[]{:S(2)}) collective-permute-start(bf16[1024,512]{1,0:T(8,128)(2,1)} %get-tuple-element.505), channel_id=1, source_target_pairs={{0,16},{16,0},{1,17},{17,1},{2,18},{18,2},{3,19},{19,3},{4,20},{20... | collective-permute-start | bytes 3145736 | tf_op jit(solution)/shard_map/ppermute | solution.py:149
  687.5 5.2 collective-permute-start.4
  692.7 5.1 collective-permute-start
  713.2 206.6 %copy-start.106 = (s32[1536]{0:T(1024)S(1)}, s32[1536]{0:T(1024)}, u32[]{:S(2)}) copy-start(s32[1536]{0:T(1024)} %copy-done.105) | copy-start | bytes 18436
  927.1 48.0 %copy-start.79 = (f32[512,32]{0,1:T(8,128)S(1)}, f32[512,32]{0,1:T(8,128)}, u32[]{:S(2)}) copy-start(f32[512,32]{0,1:T(8,128)} %param.40) | copy-start | bytes 196612
  (108 other events, 864.5 us)

commit v2 on v1

--- a/solution.py
+++ b/solution.py
@@ -24,6 +24,7 @@
 density_scale = 0.3989422804014327
 AXES = ("pipe", "grp", "dp")
 CHIPS = ("grp", "dp")
+PLANE = ("pipe", "grp")
 highest = lax.Precision.HIGHEST
 
 
@@ -98,11 +99,15 @@
         counts = jnp.sum(one_hot(owners, self.parts, jnp.int32), 1)
         self.rounds = (jnp.max(counts) + self.room - 1) // self.room
         mine = owners == self.me
-        self.out_rank = jnp.where(mine, jnp.cumsum(mine.astype(jnp.int32), 1) - 1, -1)
+        order = jnp.arange(tokens, dtype=jnp.int32)
+        upto = (order[:, None] <= order[None, :]).astype(jnp.bfloat16)
+        ranks = matmul(mine.astype(jnp.bfloat16), upto).astype(jnp.int32)
+        self.out_rank = jnp.where(mine, ranks - 1, -1)
         self.out_row = all_ids - self.me * rows_per
         own_owners = lax.dynamic_index_in_dim(owners, self.me, 0, keepdims=False)
-        hits = one_hot(own_owners, self.parts, jnp.int32)
-        ranks = jnp.sum(hits * jnp.cumsum(hits, 0), 1) - 1
+        hits = one_hot(own_owners, self.parts, jnp.bfloat16)
+        ranks = jnp.sum(hits.astype(jnp.float32) * left_transposed(upto, hits), 1)
+        ranks = ranks.astype(jnp.int32) - 1
         self.in_rank = ranks
         self.in_owner = own_owners
 
@@ -188,23 +193,45 @@
     )
 
 
+def tell(barrier, to):
+    pl.semaphore_signal(
+        barrier, inc=1, device_id=device(*to), device_id_type=pl.DeviceIdType.MESH
+    )
+
+
 def greet(others):
     barrier = pltpu.get_barrier_semaphore()
     for to in others:
-        pl.semaphore_signal(
-            barrier, inc=1, device_id=device(*to), device_id_type=pl.DeviceIdType.MESH
-        )
+        tell(barrier, to)
     pl.semaphore_wait(barrier, len(others))
 
 
 class Place:
     def __init__(self, sizes):
         self.pipes, self.grps, self.dps = sizes
+        self.plane_only = self.dps == 1
         self.pipe, self.grp, self.dp = [lax.axis_index(axis) for axis in AXES]
         column, row = self.grp % 2, self.grp // 2
         self.beside = 2 * row + 1 - column
         self.below = 2 * (1 - row) + column
         self.across = 3 - self.grp
+
+    @property
+    def spot(self):
+        return 0 if self.plane_only else self.dp
+
+    def plane(self):
+        found = []
+        for a in range(self.pipes):
+            for b in range(self.grps):
+                if (a, b) != (0, 0):
+                    ahead = ((self.pipe + a) % self.pipes, (self.grp + b) % self.grps)
+                    back = (
+                        (self.pipe + self.pipes - a) % self.pipes,
+                        (self.grp + self.grps - b) % self.grps,
+                    )
+                    found.append((ahead, back))
+        return found
 
     def line(self, step):
         return (self.dp + step) % self.dps
@@ -253,6 +280,78 @@
         kept.wait()
 
     return finish
+
+
+def swap_plane(place, rows, arrived, send, arrive, own):
+    me = place.pipe * place.grps + place.grp
+    copies = []
+    for i, (ahead, back) in enumerate(place.plane()):
+        to = ahead[0] * place.grps + ahead[1]
+        copies.append(
+            remote(rows.at[to], arrived.at[me], send.at[i], arrive.at[i], ahead + (place.dp,))
+        )
+        copies[-1].start()
+    kept = pltpu.make_async_copy(rows.at[me], arrived.at[me], own)
+    kept.start()
+
+    def finish():
+        for i, (ahead, back) in enumerate(place.plane()):
+            origin = back[0] * place.grps + back[1]
+            copies[i].wait_send()
+            remote(
+                rows.at[me], arrived.at[origin], send.at[i], arrive.at[i], ahead + (place.dp,)
+            ).wait_recv()
+        kept.wait()
+
+    return finish
+
+
+def begin_kernel(sizes, row_ref, up_ref, all_ref, arrived_ref, *sems):
+    send, arrive, own, plane_send, plane_arrive, plane_own = sems
+    place = Place(sizes)
+    others = place.others()
+    greet([ahead for ahead, _ in others])
+    finish = swap_plane(place, up_ref, arrived_ref, plane_send, plane_arrive, plane_own)
+    me = place.index(place.pipe, place.grp, place.dp)
+    copies = []
+    for i, (ahead, _) in enumerate(others):
+        copies.append(remote(row_ref, all_ref.at[me], send.at[i], arrive.at[i], ahead))
+        copies[-1].start()
+    kept = pltpu.make_async_copy(row_ref, all_ref.at[me], own)
+    kept.start()
+    for i, (ahead, back) in enumerate(others):
+        copies[i].wait_send()
+        remote(
+            row_ref, all_ref.at[place.index(*back)], send.at[i], arrive.at[i], ahead
+        ).wait_recv()
+    kept.wait()
+    finish()
+
+
+def begin(row, blocks, sizes, collective):
+    parts = math.prod(sizes)
+    sems = pltpu.SemaphoreType.DMA((parts - 1,))
+    plane_sems = pltpu.SemaphoreType.DMA((sizes[0] * sizes[1] - 1,))
+    return pl.pallas_call(
+        functools.partial(begin_kernel, sizes),
+        out_shape=(
+            jax.ShapeDtypeStruct((parts,) + row.shape, row.dtype),
+            jax.ShapeDtypeStruct(blocks.shape, blocks.dtype),
+        ),
+        in_specs=[pl.BlockSpec(memory_space=pltpu.VMEM)] * 2,
+        out_specs=[pl.BlockSpec(memory_space=pltpu.VMEM)] * 2,
+        scratch_shapes=[
+            sems,
+            sems,
+            pltpu.SemaphoreType.DMA,
+            plane_sems,
+            plane_sems,
+            pltpu.SemaphoreType.DMA,
+        ],
+        compiler_params=pltpu.CompilerParams(
+            collective_id=collective, has_side_effects=True, vmem_limit_bytes=8 << 20
+        ),
+    )(row, blocks)
 
 
 def spread_kernel(sizes, row_ref, all_ref, send, arrive, own):
@@ -352,12 +451,16 @@
     near = place.beside * (1 - pipe) + place.below * pipe
     far = place.below * (1 - pipe) + place.beside * pipe
     core = (1 - pipe, grp, dp)
-    lines = place.dps - 1
+    hops = place.dps - 1
+    spot = place.spot
+    ends = (dp < hops, dp > 0)
+    sides = ((pipe, grp, dp + 1), (pipe, grp, dp - 1))
+    both = range(2 if hops else 0)
     if routed:
         greet([ahead for ahead, _ in place.others()])
     else:
         greet(
-            [(pipe, grp, place.line(k + 1)) for k in range(lines)]
+            [(pipe, grp, place.line(k + 1)) for k in range(hops)]
             + [(pipe, near, dp), (pipe, far, dp), core]
         )
     waits = []
@@ -375,53 +478,87 @@
         target = view(piece, *at)
         remote(target, target, send.at[n, index], arrive.at[n, index], core).wait_recv()
 
-    keeps = []
-    for n, piece in enumerate(pieces):
-        array, first, rows = piece
-        source = shards[array].at[pl.ds(first, rows)]
-        for k in range(lines):
-            launch(n, k, source, piece, (pipe, grp, place.line(k + 1)), pipe, grp, dp)
-        keeps.append(pltpu.make_async_copy(source, view(piece, pipe, grp, dp), own.at[n]))
-        keeps[-1].start()
-        if n == 0 and routed:
-            finish = swap_all(place, rows_ref, arrived_ref, swap_send, swap_arrive, swap_own)
-
-    def over_plane(n, piece):
-        for k in range(lines):
-            landed(n, k, piece, pipe, grp, place.behind(k + 1))
+    def along(n, side, hop, finish=False):
+        origin = dp - hop if side == 0 else dp + hop
+        here = origin >= 0 if side == 0 else origin <= hops
+        piece, index = pieces[n], side * hops + hop
+
+        def copy():
+            array, first, rows = piece
+            target = view(piece, pipe, grp, origin)
+            source = shards[array].at[pl.ds(first, rows)] if hop == 0 else target
+            return remote(source, target, send.at[n, index], arrive.at[n, index], sides[side])
+
+        if finish:
+
+            @pl.when(here & ends[side])
+            def _():
+                copy().wait_send()
+
+            return
+        if hop > 0:
+
+            @pl.when(here)
+            def _():
+                landed(n, index - 1, piece, pipe, grp, origin)
+
+        if hop < hops:
+
+            @pl.when(here & ends[side])
+            def _():
+                copy().start()
+
+    keeps = {}
+
+    def over_line(n, hop):
+        if hop == 0:
+            array, first, rows = pieces[n]
+            source = shards[array].at[pl.ds(first, rows)]
+            keeps[n] = pltpu.make_async_copy(source, view(pieces[n], pipe, grp, spot), own.at[n])
+            keeps[n].start()
+        for side in both:
+            along(n, side, hop)
+
+    def over_plane(n):
+        piece = pieces[n]
+        over_line(n, hops)
         keeps[n].wait()
         group = view(piece, pipe, grp)
-        launch(n, lines, group, piece, (pipe, near, dp), pipe, grp)
-        launch(n, lines + 1, group, piece, (pipe, far, dp), pipe, grp)
-        launch(n, lines + 3, group, piece, core, pipe, grp)
-
-    def pass_on(n, piece):
-        landed(n, lines, piece, pipe, near)
+        launch(n, 2 * hops, group, piece, (pipe, near, dp), pipe, grp)
+        launch(n, 2 * hops + 1, group, piece, (pipe, far, dp), pipe, grp)
+        launch(n, 2 * hops + 3, group, piece, core, pipe, grp)
+
+    def pass_on(n):
+        piece = pieces[n]
+        landed(n, 2 * hops, piece, pipe, near)
         group = view(piece, pipe, near)
-        launch(n, lines + 2, group, piece, (pipe, far, dp), pipe, near)
-        launch(n, lines + 4, group, piece, core, pipe, near)
-        landed(n, lines + 1, piece, pipe, far)
-        launch(n, lines + 5, view(piece, pipe, far), piece, core, pipe, far)
-
-    def last(n, piece):
-        landed(n, lines + 2, piece, pipe, place.across)
-        launch(n, lines + 6, view(piece, pipe, place.across), piece, core, pipe, place.across)
-
+        launch(n, 2 * hops + 2, group, piece, (pipe, far, dp), pipe, near)
+        launch(n, 2 * hops + 4, group, piece, core, pipe, near)
+        landed(n, 2 * hops + 1, piece, pipe, far)
+        launch(n, 2 * hops + 5, view(piece, pipe, far), piece, core, pipe, far)
+
+    def last(n):
+        piece = pieces[n]
+        landed(n, 2 * hops + 2, piece, pipe, place.across)
+        launch(n, 2 * hops + 6, view(piece, pipe, place.across), piece, core, pipe, place.across)
+
+    stages = [functools.partial(over_line, hop=hop) for hop in range(hops)]
+    stages += [over_plane, pass_on, last]
     total = len(pieces)
-    for n in range(total + 2):
-        if n < total:
-            over_plane(n, pieces[n])
-        if 1 <= n < total + 1:
-            pass_on(n - 1, pieces[n - 1])
-        if n >= 2:
-            last(n - 2, pieces[n - 2])
+    for turn in range(total + len(stages) - 1):
+        for at, stage in enumerate(stages):
+            if 0 <= turn - at < total:
+                stage(turn - at)
+        if turn == 5 and routed:
+            finish = swap_all(place, rows_ref, arrived_ref, swap_send, swap_arrive, swap_own)
     for n, piece in enumerate(pieces):
-        landed(n, lines + 3, piece, 1 - pipe, grp)
-        core_near = place.below * (1 - pipe) + place.beside * pipe
-        core_far = place.beside * (1 - pipe) + place.below * pipe
-        landed(n, lines + 4, piece, 1 - pipe, core_near)
-        landed(n, lines + 5, piece, 1 - pipe, core_far)
-        landed(n, lines + 6, piece, 1 - pipe, place.across)
+        landed(n, 2 * hops + 3, piece, 1 - pipe, grp)
+        landed(n, 2 * hops + 4, piece, 1 - pipe, far)
+        landed(n, 2 * hops + 5, piece, 1 - pipe, near)
+        landed(n, 2 * hops + 6, piece, 1 - pipe, place.across)
+        for side in both:
+            for hop in range(hops):
+                along(n, side, hop, finish=True)
     for copy in waits:
         copy.wait_send()
     if routed:
@@ -431,7 +568,7 @@
 def gather_all(shards, pieces, sizes, collective, rows=None):
     parts = math.prod(sizes)
     routed = rows is not None
-    kinds = sizes[2] - 1 + 7
+    kinds = 2 * (sizes[2] - 1) + 7
     out_shape = [jax.ShapeDtypeStruct(sizes + shard.shape, shard.dtype) for shard in shards]
     if routed:
         out_shape.append(jax.ShapeDtypeStruct(rows.shape, rows.dtype))
@@ -455,123 +592,195 @@
     )(*operands)
 
 
-def reduce_kernel(sizes, count, routed, *refs):
-    partials, refs = refs[:count], refs[count:]
+def reduce_kernel(sizes, pieces, cores, routed, *refs):
+    arrays, total = max(piece[0] for piece in pieces) + 1, len(pieces)
+    partials, refs = refs[:arrays], refs[arrays:]
     if routed:
-        rows_ref, refs = refs[0], refs[1:]
-    sums, refs = refs[:count], refs[count:]
+        rows_ref, blocks_ref, refs = refs[0], refs[1], refs[2:]
+    sums, refs = refs[:arrays], refs[arrays:]
     if routed:
-        arrived_ref, refs = refs[0], refs[1:]
-    planes, refs = refs[:count], refs[count:]
-    groups, refs = refs[:count], refs[count:]
-    line_parts, refs = refs[:count], refs[count:]
-    send, arrive, own, swap_send, swap_arrive, swap_own = refs
+        arrived_ref, blocks_arrived_ref, refs = refs[0], refs[1], refs[2:]
+    chips, refs = refs[: total if cores else 0], refs[total if cores else 0 :]
+    others, refs = refs[: total if cores else 0], refs[total if cores else 0 :]
+    mine, refs = refs[:total], refs[total:]
+    planes, refs = refs[:total], refs[total:]
+    lines, refs = refs[:total], refs[total:]
+    send, arrive, own, swap_send, swap_arrive, swap_own, plane_send, plane_arrive, plane_own = refs
     place = Place(sizes)
     pipe, grp, dp = place.pipe, place.grp, place.dp
-    partners = (place.beside, place.below, place.across)
-    lines = place.dps - 1
+    near = place.beside * (1 - pipe) + place.below * pipe
+    far = place.below * (1 - pipe) + place.beside * pipe
+    core = (1 - pipe, grp, dp)
+    hops = place.dps - 1
+    block = 16
     if routed:
         greet([ahead for ahead, _ in place.others()])
     else:
         greet(
-            [(pipe, grp, place.line(k + 1)) for k in range(lines)]
-            + [(pipe, other, dp) for other in partners]
+            [(pipe, grp, place.line(k + 1)) for k in range(hops)]
+            + [(pipe, near, dp), (pipe, far, dp)]
+            + ([core] if cores else [])
         )
-    copies, keeps = [], []
-    for n in range(count):
-        for j, other in enumerate(partners):
-            copies.append(
-                remote(
-                    partials[n].at[other],
-                    planes[n].at[j],
-                    send.at[n, j],
-                    arrive.at[n, j],
-                    (pipe, other, dp),
-                )
+    copies = {}
+
+    def launch(n, index, source, target, to):
+        copies[n, index] = remote(source, target, send.at[n, index], arrive.at[n, index], to)
+        copies[n, index].start()
+
+    def blocks(n, body):
+        deep = pieces[n][2] // block
+
+        def one(i, _):
+            at = pl.ds(pl.multiple_of(i % deep * block, block), block)
+            body(i // deep, at)
+            return 0
+
+        lax.fori_loop(0, place.dps * deep, one, 0)
+
+    def to_core(n):
+        array, first, rows = pieces[n]
+        if cores:
+            part = partials[array].at[1 - pipe, :, :, pl.ds(first, rows)]
+            launch(n, 0, part, others[n], core)
+            part = partials[array].at[pipe, :, :, pl.ds(first, rows)]
+            copies[n, "own"] = pltpu.make_async_copy(part, chips[n], own.at[n, 0])
+            copies[n, "own"].start()
+
+    def to_near(n):
+        array, first, rows = pieces[n]
+        if cores:
+            copies[n, "own"].wait()
+            copies[n, 0].wait_recv()
+            for g in range(place.grps):
+
+                def add(d, at, g=g):
+                    left = chips[n][g, d, at].astype(jnp.float32)
+                    chips[n][g, d, at] = (left + others[n][g, d, at].astype(jnp.float32)).astype(
+                        jnp.bfloat16
+                    )
+
+                blocks(n, add)
+            part = lambda g: chips[n].at[g]
+        else:
+            part = lambda g: partials[array].at[g, :, pl.ds(first, rows)]
+            for j, g in enumerate((far, grp)):
+                copies[n, "own", j] = pltpu.make_async_copy(part(g), mine[n].at[j], own.at[n, j])
+                copies[n, "own", j].start()
+        launch(n, 1, part(near), planes[n].at[1], (pipe, near, dp))
+        launch(n, 2, part(place.across), planes[n].at[0], (pipe, near, dp))
+
+    def to_far(n):
+        if not cores:
+            copies[n, "own", 0].wait()
+            copies[n, "own", 1].wait()
+        copies[n, 1].wait_recv()
+        copies[n, 2].wait_recv()
+        for j, g in enumerate((far, grp)):
+
+            def add(d, at, j=j, g=g):
+                left = chips[n][g, d, at] if cores else mine[n][j, d, at]
+                right = planes[n][j, d, at].astype(jnp.float32)
+                mine[n][j, d, at] = (left.astype(jnp.float32) + right).astype(jnp.bfloat16)
+
+            blocks(n, add)
+            if j == 0:
+                launch(n, 3, mine[n].at[0], planes[n].at[2], (pipe, far, dp))
+
+    def to_lines(n):
+        copies[n, 3].wait_recv()
+
+        def add(d, at):
+            left = mine[n][1, d, at].astype(jnp.float32)
+            mine[n][1, d, at] = (left + planes[n][2, d, at].astype(jnp.float32)).astype(
+                jnp.bfloat16
             )
-            copies[-1].start()
-        keeps.append(pltpu.make_async_copy(partials[n].at[grp], groups[n], own.at[n]))
-        keeps[-1].start()
-        if n == 0 and routed:
-            finish = swap_all(place, rows_ref, arrived_ref, swap_send, swap_arrive, swap_own)
-    for n in range(count):
-        keeps[n].wait()
-        for j in range(3):
-            copies[3 * n + j].wait_recv()
-        block = 16
-        depth = groups[n].shape[0] // place.dps
-
-        def add_plane(i, _, n=n):
+
+        def add_last(d, at):
+            array, first, rows = pieces[n]
+            left = mine[n][1, d, at].astype(jnp.float32)
+            to = pl.ds(pl.multiple_of(first + at.start, block), block)
+            sums[array][to] = left + planes[n][2, d, at].astype(jnp.float32)
+
+        if hops == 0:
+            blocks(n, add_last)
+            return
+        blocks(n, add)
+        for k in range(hops):
+            to = place.line(k + 1)
+            launch(n, 4 + k, mine[n].at[1, to], lines[n].at[k], (pipe, grp, to))
+
+    def to_sum(n):
+        array, first, rows = pieces[n]
+        for k in range(hops):
+            copies[n, 4 + k].wait_recv()
+
+        def add(i, _):
             at = pl.ds(pl.multiple_of(i * block, block), block)
-            total = groups[n][at].astype(jnp.float32)
-            for j in range(3):
-                total = total + planes[n][j, at].astype(jnp.float32)
-            groups[n][at] = total.astype(jnp.bfloat16)
+            total = mine[n][1, place.spot, at].astype(jnp.float32)
+            for k in range(hops):
+                total = total + lines[n][k, at].astype(jnp.float32)
+            sums[array][pl.ds(pl.multiple_of(first + i * block, block), block)] = total
             return 0
 
-        lax.fori_loop(0, groups[n].shape[0] // block, add_plane, 0)
-        for k in range(lines):
-            first = pl.multiple_of(place.line(k + 1) * depth, 16)
-            copies.append(
-                remote(
-                    groups[n].at[pl.ds(first, depth)],
-                    line_parts[n].at[k],
-                    send.at[n, 3 + k],
-                    arrive.at[n, 3 + k],
-                    (pipe, grp, place.line(k + 1)),
-                )
+        lax.fori_loop(0, rows // block, add, 0)
+
+    stages = ([to_core] if cores else []) + [to_near, to_far, to_lines]
+    stages += [to_sum] if hops else []
+    for turn in range(total + len(stages) - 1):
+        for at, stage in enumerate(stages):
+            if 0 <= turn - at < total:
+                stage(turn - at)
+        if turn == 0 and routed:
+            finish = (
+                swap_all(place, rows_ref, arrived_ref, swap_send, swap_arrive, swap_own),
+                swap_plane(
+                    place, blocks_ref, blocks_arrived_ref, plane_send, plane_arrive, plane_own
+                ),
             )
-            copies[-1].start()
-    for n in range(count):
-        depth = groups[n].shape[0] // place.dps
-        for k in range(lines):
-            copies[3 * count + lines * n + k].wait_recv()
-
-        def add_line(i, _, n=n, depth=depth):
-            at = pl.ds(pl.multiple_of(i * block, block), block)
-            first = pl.multiple_of(dp * depth + i * block, block)
-            total = groups[n][pl.ds(first, block)].astype(jnp.float32)
-            for k in range(lines):
-                total = total + line_parts[n][k, at].astype(jnp.float32)
-            sums[n][at] = total
-            return 0
-
-        lax.fori_loop(0, depth // block, add_line, 0)
-    for copy in copies:
-        copy.wait_send()
+    for key, copy in copies.items():
+        if key[1] != "own":
+            copy.wait_send()
     if routed:
-        finish()
-
-
-def reduce_all(partials, sizes, collective, rows=None):
+        finish[0]()
+        finish[1]()
+
+
+def reduce_all(partials, pieces, sizes, collective, rows=None, plane_rows=None, cores=False):
     parts = math.prod(sizes)
-    count = len(partials)
+    total = len(pieces)
     routed = rows is not None
     low = jnp.bfloat16
-    tall = [(partial.shape[1], partial.shape[2]) for partial in partials]
-    flat = [(height // sizes[2], columns) for height, columns in tall]
-    out_shape = [jax.ShapeDtypeStruct(shape, jnp.float32) for shape in flat]
-    out_specs = [pl.BlockSpec(memory_space=pltpu.VMEM)] * count
+    _, grps, dps = sizes
+    shapes = [(dps, size, partials[array].shape[-1]) for array, _, size in pieces]
+    out_shape = [jax.ShapeDtypeStruct(partial.shape[-2:], jnp.float32) for partial in partials]
+    out_specs = [pl.BlockSpec(memory_space=pltpu.VMEM)] * len(partials)
     if routed:
-        out_shape.append(jax.ShapeDtypeStruct(rows.shape, rows.dtype))
-        out_specs.append(pl.BlockSpec(memory_space=pl.ANY))
-    operands = list(partials) + ([rows] if routed else [])
-    sems = pltpu.SemaphoreType.DMA((count, 3 + sizes[2] - 1))
+        for extra in (rows, plane_rows):
+            out_shape.append(jax.ShapeDtypeStruct(extra.shape, extra.dtype))
+            out_specs.append(pl.BlockSpec(memory_space=pl.ANY))
+    operands = list(partials) + ([rows, plane_rows] if routed else [])
+    sems = pltpu.SemaphoreType.DMA((total, 4 + dps - 1))
     swaps = pltpu.SemaphoreType.DMA((parts - 1 if routed else 1,))
+    plane_swaps = pltpu.SemaphoreType.DMA((sizes[0] * grps - 1,))
+    scratch = [pltpu.VMEM((grps,) + shape, low) for shape in shapes] * (2 if cores else 0)
+    scratch += [pltpu.VMEM((2,) + shape, low) for shape in shapes]
+    scratch += [pltpu.VMEM((3,) + shape, low) for shape in shapes]
+    scratch += [pltpu.VMEM((max(dps - 1, 1),) + shape[1:], low) for shape in shapes]
     return pl.pallas_call(
-        functools.partial(reduce_kernel, sizes, count, routed),
+        functools.partial(reduce_kernel, sizes, tuple(pieces), cores, routed),
         out_shape=out_shape,
         in_specs=[pl.BlockSpec(memory_space=pl.ANY)] * len(operands),
         out_specs=out_specs,
-        scratch_shapes=[pltpu.VMEM((3,) + shape, low) for shape in tall]
-        + [pltpu.VMEM(shape, low) for shape in tall]
-        + [pltpu.VMEM((sizes[2] - 1,) + shape, low) for shape in flat]
+        scratch_shapes=scratch
         + [
             sems,
             sems,
-            pltpu.SemaphoreType.DMA((count,)),
+            pltpu.SemaphoreType.DMA((total, 2)),
             swaps,
             swaps,
+            pltpu.SemaphoreType.DMA,
+            plane_swaps,
+            plane_swaps,
             pltpu.SemaphoreType.DMA,
         ],
         compiler_params=pltpu.CompilerParams(
@@ -580,35 +789,167 @@
     )(*operands)
 
 
-def gather_weights(shards, sizes, collective, pieces, rows=None):
-    if collective is not None:
-        *fulls, arrived = gather_all(shards, pieces, sizes, collective, rows)
-    else:
+def pair_rows(pair, first):
+    pair = pair.astype(jnp.float32)
+    low = jnp.bfloat16
+    return jnp.concatenate(
+        [jnp.where(first, pair, 0.0).astype(low), jnp.where(first, 0.0, pair).astype(low)], 0
+    )
+
+
+def pair_probs(rows, keys, live, scale):
+    scores = jnp.where(live, right_transposed(rows, keys) * scale, -1e30)
+    exp_scores = jnp.exp(scores - jnp.max(scores, -1, keepdims=True))
+    return exp_scores / jnp.sum(exp_scores, -1, keepdims=True)
+
+
+def attention_masks(lengths_ref, slots, seq_len, lanes):
+    live = lax.broadcasted_iota(jnp.int32, (1, seq_len), 1) < lengths_ref[pl.program_id(0)]
+    first = lax.broadcasted_iota(jnp.int32, (slots, lanes), 1) < lanes // 2
+    return live, first
+
+
+def attention_kernel(scale, lanes, lengths_ref, q_ref, k_ref, v_ref, out_ref):
+    slots = q_ref.shape[0]
+    live, first = attention_masks(lengths_ref, slots, k_ref.shape[0], lanes)
+    for pair in range(q_ref.shape[1] // lanes):
+        at = slice(pair * lanes, (pair + 1) * lanes)
+        probs = pair_probs(pair_rows(q_ref[:, at], first), k_ref[:, at], live, scale)
+        context = matmul(probs.astype(jnp.bfloat16), v_ref[:, at])
+        out_ref[:, at] = jnp.where(first, context[:slots], context[slots:]).astype(jnp.bfloat16)
+
+
+def attention_back_kernel(
+    scale, lanes, lengths_ref, q_ref, k_ref, v_ref, grad_ref, dq_ref, dk_ref, dv_ref
+):
+    slots = q_ref.shape[0]
+    low = jnp.bfloat16
+    live, first = attention_masks(lengths_ref, slots, k_ref.shape[0], lanes)
+    for pair in range(q_ref.shape[1] // lanes):
+        at = slice(pair * lanes, (pair + 1) * lanes)
+        rows, grads = pair_rows(q_ref[:, at], first), pair_rows(grad_ref[:, at], first)
+        probs = pair_probs(rows, k_ref[:, at], live, scale)
+        dv_ref[:, at] = left_transposed(probs.astype(low), grads).astype(low)
+        d_probs = right_transposed(grads, v_ref[:, at])
+        d_scores = probs * (d_probs - jnp.sum(probs * d_probs, -1, keepdims=True))
+        d_scores = d_scores.astype(low)
+        d_query = matmul(d_scores, k_ref[:, at]) * scale
+        dq_ref[:, at] = jnp.where(first, d_query[:slots], d_query[slots:]).astype(low)
+        dk_ref[:, at] = (left_transposed(d_scores, rows) * scale).astype(low)
+
+
+def attention(lengths, queries, both, grads=None):
+    own = lengths.shape[0]
+    width = queries.shape[1]
+    slots, seq_len = queries.shape[0] // own, both.shape[0] // own
+    lanes = 2 * width // H
+    scale = (width // H) ** (-0.5)
+    cuts = 2
+    part = width // cuts
+    row = pl.BlockSpec((slots, part), lambda s, h: (s, h))
+    keys = pl.BlockSpec((seq_len, part), lambda s, h: (s, h))
+    values = pl.BlockSpec((seq_len, part), lambda s, h: (s, cuts + h))
+    in_specs = [pl.BlockSpec(memory_space=pltpu.SMEM), row, keys, values]
+    flat = jax.ShapeDtypeStruct(queries.shape, jnp.bfloat16)
+    tall = jax.ShapeDtypeStruct((both.shape[0], width), jnp.bfloat16)
+    if grads is None:
+        return pl.pallas_call(
+            functools.partial(attention_kernel, scale, lanes),
+            grid=(own, cuts),
+            out_shape=flat,
+            in_specs=in_specs,
+            out_specs=row,
+        )(lengths, queries, both, both)
+    return pl.pallas_call(
+        functools.partial(attention_back_kernel, scale, lanes),
+        grid=(own, cuts),
+        out_shape=(flat, tall, tall),
+        in_specs=in_specs + [row],
+        out_specs=(row, keys, keys),
+    )(lengths, queries, both, both, grads)
+
+
+def even_pieces(array, rows, cuts):
+    size = rows // cuts
+    return [(array, i * size, size) for i in range(cuts)]
+
+
+def start_all(row, blocks, sizes, collective):
+    if collective is None:
+        return lax.all_gather(row, AXES, axis=0), lax.all_to_all(blocks, PLANE, 0, 0)
+    return begin(row, blocks, sizes, collective)
+
+
+def gather_weights(shards, pieces, sizes, collective, rows):
+    if collective is None:
         fulls = [lax.all_gather(shard, AXES, axis=0) for shard in shards]
         arrived = lax.all_to_all(rows, AXES, 0, 0)
+    else:
+        *fulls, arrived = gather_all(shards, pieces, sizes, collective, rows)
     return [full.reshape(-1, full.shape[-1]) for full in fulls], arrived
 
 
-def gather_rows(shard, sizes, collective):
+def gather_rows(shard, sizes, collective, cuts):
     if collective is None:
-        return lax.all_gather(shard, AXES, axis=0, tiled=True)
-    cuts = 4
-    size = shard.shape[0] // cuts
-    pieces = [(0, i * size, size) for i in range(cuts)]
-    (full,) = gather_all([shard], pieces, sizes, collective)
+        axes = AXES if sizes[2] > 1 else PLANE
+        return lax.all_gather(shard, axes, axis=0, tiled=True)
+    (full,) = gather_all([shard], even_pieces(0, shard.shape[0], cuts), sizes, collective)
     return full.reshape(-1, full.shape[-1])
 
 
-def reduce_chips(partials, sizes, collective, rows=None):
+def sum_rows(partial, sizes, collective, cuts):
+    if collective is None:
+        axes = AXES if sizes[2] > 1 else PLANE
+        total = lax.psum_scatter(partial, axes, scatter_dimension=0, tiled=True)
+        return total.astype(jnp.float32)
+    shaped = partial.reshape(sizes + (-1, partial.shape[1]))
+    pieces = even_pieces(0, shaped.shape[3], cuts)
+    (total,) = reduce_all([shaped], pieces, sizes, collective, cores=True)
+    return total
+
+
+def sum_chips(partials, pieces, sizes, collective, rows, blocks):
     if collective is not None:
-        shaped = [p.reshape(sizes[1], -1, p.shape[1]) for p in partials]
-        sums = reduce_all(shaped, sizes, collective, rows)
-        return (sums[:-1], sums[-1]) if rows is not None else (sums, None)
+        shaped = [p.reshape(sizes[1:] + (-1, p.shape[1])) for p in partials]
+        *sums, rows, blocks = reduce_all(shaped, pieces, sizes, collective, rows, blocks)
+        return sums, rows, blocks
     sums = [
         lax.psum_scatter(p, CHIPS, scatter_dimension=0, tiled=True).astype(jnp.float32)
         for p in partials
     ]
-    return sums, lax.all_to_all(rows, AXES, 0, 0) if rows is not None else None
+    return sums, lax.all_to_all(rows, AXES, 0, 0), lax.all_to_all(blocks, PLANE, 0, 0)
+
+
+def line_shift(shard, step):
+    size = lax.axis_size("dp")
+    return lax.ppermute(shard, "dp", [(i, (i + step) % size) for i in range(size)])
+
+
+def line_gather(shard, collective):
+    if collective is None:
+        return lax.all_gather(shard, "dp", axis=0)
+    size = lax.axis_size("dp")
+    me = lax.axis_index("dp")
+    kept = jnp.stack([shard] + [line_shift(shard, step) for step in range(1, size)])
+    order = [(me + size - i) % size for i in range(size)]
+    return jnp.concatenate([lax.dynamic_slice_in_dim(kept, at, 1, 0) for at in order], 0)
+
+
+def line_sum(partial, collective):
+    partial = partial.astype(jnp.bfloat16)
+    if collective is None:
+        total = lax.psum_scatter(partial, "dp", scatter_dimension=0, tiled=False)
+        return total.astype(jnp.float32)
+    size = lax.axis_size("dp")
+    me = lax.axis_index("dp")
+
+    def entry(step):
+        return lax.dynamic_index_in_dim(partial, (me + step) % size, 0, keepdims=False)
+
+    total = entry(0).astype(jnp.float32)
+    for step in range(1, size):
+        total = total + line_shift(entry(step), step).astype(jnp.float32)
+    return total
 
 
 def spread_row(row, sizes, collective):
@@ -683,14 +1024,21 @@
     sizes = tuple(lax.axis_size(axis) for axis in AXES)
     shards = (word_table, qkv_weight, square_weight[0], up_weight, down_weight)
     direct = sizes[:2] == (2, 4) and all(shard.shape[0] % 32 == 0 for shard in shards)
-    ids = tuple(range(7)) if direct else (None,) * 7
+    ids = tuple(range(11)) if direct else (None,) * 11
+    plane_sizes = sizes[:2] + (1,)
 
     spare = -(seq_len + slots + 1) % 128
     packed = jnp.concatenate(
         [token_ids, labels, lengths[:, None], jnp.zeros((token_ids.shape[0], spare), jnp.int32)], 1
     )
     packed = lax.dynamic_slice_in_dim(packed, first_own, own, 0)
-    packed = spread_row(packed, sizes, ids[0])
+    planes = sizes[0] * sizes[1]
+    units = up_weight.shape[1] // planes
+    cut = me // sizes[2]
+    blocks = up_weight.astype(narrow).reshape(up_weight.shape[0], planes, units).swapaxes(0, 1)
+    packed, blocks = start_all(packed, blocks, sizes, ids[0])
+    down_low = line_gather(down_weight.astype(narrow), ids[0]).reshape(units, width)
+    up_low = line_gather(blocks, ids[0]).swapaxes(0, 1).reshape(width, units)
     all_ids = packed[:, :, :seq_len]
     all_labels = packed[:, :, seq_len : seq_len + slots].reshape(-1)
     all_lengths = packed[:, :, seq_len + slots]
@@ -714,14 +1062,13 @@
         small_low,
         qkv_weight.astype(narrow),
         square_weight[0].astype(narrow),
-        up_weight.astype(narrow),
-        down_weight.astype(narrow),
         square_weight[1].astype(narrow),
     ]
-    pieces = [(i, 0, shard.shape[0]) for i, shard in enumerate(low)]
+    deep = small_low.shape[0]
+    pieces = [(0, 0, deep), (1, 0, deep // 2), (1, deep // 2, deep // 2), (2, 0, deep), (3, 0, deep)]
     send = routes.table_rows(word_low, 0).reshape(parts, -1, width)
-    (small_full, qkv_low, out_low, up_low, down_low, turn_low), arrived = gather_weights(
-        low, sizes, ids[1], pieces, send
+    (small_full, qkv_low, out_low, turn_low), arrived = gather_weights(
+        low, pieces, sizes, ids[1], send
     )
     word_rows = routes.fetch(word_low, arrived.reshape(-1, width))
     small_full = small_full.T
@@ -730,7 +1077,6 @@
     query_low, both_low = qkv_low[:, :width], qkv_low[:, width:]
 
     second = (places[None, :] >= ((own_lengths + 1) // 2)[:, None]).reshape(-1, 1)
-    live = (places[None, :] < own_lengths[:, None])[:, None, None, :]
     embedded = (
         word_rows
         + jnp.tile(pos_low.astype(jnp.float32), (own, 1))
@@ -740,33 +1086,20 @@
     start_low = start.astype(narrow)
     both_bias = jnp.concatenate([jnp.zeros_like(vec_rows[5]), vec_rows[5]])
     both = (matmul(start_low, both_low) + both_bias).astype(narrow)
-    both = both.reshape(own, seq_len, 2, H, head_dim)
-    key_rows, value_rows = both[:, :, 0], both[:, :, 1]
     pick = one_hot(masked, seq_len, jnp.float32)
     chosen = rows_by_seq(pick, start.reshape(own, seq_len, width)).reshape(-1, width)
     chosen_low = chosen.astype(narrow)
     queries = (matmul(chosen_low, query_low) + vec_rows[4]).astype(narrow)
-    queries = queries.reshape(own, slots, H, head_dim)
-    scale = head_dim ** (-0.5)
-    scores = (
-        jnp.einsum("sqhd,skhd->shqk", queries, key_rows, preferred_element_type=jnp.float32)
-        * scale
-    )
-    scores = jnp.where(live, scores, -1e30)
-    exp_scores = jnp.exp(scores - jnp.max(scores, -1, keepdims=True))
-    probs = exp_scores / jnp.sum(exp_scores, -1, keepdims=True)
-    probs_low = probs.astype(narrow)
-    context = jnp.einsum(
-        "shqk,skhd->sqhd", probs_low, value_rows, preferred_element_type=jnp.float32
-    )
-    context = context.reshape(-1, width).astype(narrow)
+    context = attention(own_lengths, queries, both)
     branch = matmul(context, out_low) + vec_rows[6]
     hidden, norm_one = norm_forward(chosen + branch, vec_rows[7], vec_rows[8])
     hidden = hidden.astype(narrow)
 
-    inner = matmul(hidden, up_low) + vec_rows[15:].reshape(-1)
+    plane_hidden = gather_rows(hidden, plane_sizes, ids[2], 2)
+    up_bias = lax.dynamic_slice_in_dim(vec_rows[15:].reshape(-1), cut * units, units, 0)
+    inner = matmul(plane_hidden, up_low) + up_bias
     activ = jax.nn.gelu(inner, approximate=False).astype(narrow)
-    branch = matmul(activ, down_low) + vec_rows[9]
+    branch = sum_rows(matmul(activ, down_low).astype(narrow), plane_sizes, ids[3], 2) + vec_rows[9]
     mixed, norm_two = norm_forward(hidden.astype(jnp.float32) + branch, vec_rows[10], vec_rows[11])
     picked = mixed.astype(narrow)
     turned = matmul(picked, turn_low) + vec_rows[12]
@@ -774,7 +1107,7 @@
         jax.nn.gelu(turned, approximate=False), vec_rows[13], vec_rows[14]
     )
 
-    all_normed = gather_rows(normed.astype(narrow), sizes, ids[2])
+    all_normed = gather_rows(normed.astype(narrow), sizes, ids[4], 4)
     column = me * rows_per + jnp.arange(rows_per, dtype=jnp.int32)
     bias_row = jnp.pad(head_bias, (0, parts * rows_per - vocab))
     bias_row = lax.dynamic_slice_in_dim(bias_row, me * rows_per, rows_per, 0)
@@ -784,7 +1117,7 @@
     own_total = jnp.sum(jnp.exp(logits - own_peak[:, None]), -1)
     hits = all_labels[:, None] == column
     own_label = jnp.sum(jnp.where(hits, logits, 0.0), -1)
-    peak, exp_total, label_logit = share_stats(own_peak, own_total, own_label, sizes, ids[3])
+    peak, exp_total, label_logit = share_stats(own_peak, own_total, own_label, sizes, ids[5])
     loss_total = jnp.sum(all_valid * (peak + jnp.log(exp_total) - label_logit))
     d_logits = (all_valid / total)[:, None] * (
         jnp.exp(logits - peak[:, None]) / exp_total[:, None] - hits.astype(jnp.float32)
@@ -792,10 +1125,7 @@
     d_bias = jnp.sum(d_logits, 0)
     d_logits_low = d_logits.astype(narrow)
     d_word = left_transposed(d_logits_low, all_normed)
-    d_normed = chip_half(matmul(d_logits_low, word_low))
-    columns = width // 2
-    d_normed, _ = reduce_chips([d_normed[:, :columns], d_normed[:, columns:]], sizes, ids[4])
-    d_normed = jnp.concatenate(d_normed, 1)
+    d_normed = sum_rows(matmul(d_logits_low, word_low).astype(narrow), sizes, ids[6], 8)
 
     d_gelu, d_gain_head, d_shift_head = norm_backward(d_normed, norm_head, vec_rows[13])
     d_turned = (d_gelu * gelu_slope(turned)).astype(narrow)
@@ -810,11 +1140,19 @@
     d_pre, d_gain_two, d_shift_two = norm_backward(d_mixed, norm_two, vec_rows[10])
     d_branch = d_pre.astype(narrow)
     d_down_bias = jnp.sum(d_branch.astype(jnp.float32), 0)
-    d_down = chip_sum(activ, d_branch)
-    d_inner = (right_transposed(d_branch, down_low) * gelu_slope(inner)).astype(narrow)
-    d_up_bias = jnp.sum(d_inner.astype(jnp.float32), 0).reshape(-1, width)
-    d_up = chip_sum(hidden, d_inner)
-    d_hidden = (d_pre + right_transposed(d_inner, up_low)).astype(narrow)
+    plane_branch = gather_rows(d_branch, plane_sizes, ids[7], 2)
+    own_down = line_sum(
+        left_transposed(activ, plane_branch).reshape(sizes[2], -1, width), ids[7]
+    )
+    d_inner = (right_transposed(plane_branch, down_low) * gelu_slope(inner)).astype(narrow)
+    d_up_bias = jnp.sum(d_inner.astype(jnp.float32), 0)
+    d_up_bias = lax.dynamic_update_slice_in_dim(
+        jnp.zeros((planes * units,), jnp.float32), d_up_bias, cut * units, 0
+    ).reshape(-1, width)
+    d_up = left_transposed(plane_hidden, d_inner).reshape(planes, sizes[2], -1, units)
+    up_blocks = line_sum(d_up.swapaxes(0, 1), ids[7]).astype(narrow)
+    d_hidden = sum_rows(right_transposed(d_inner, up_low).astype(narrow), plane_sizes, ids[8], 2)
+    d_hidden = (d_pre + d_hidden).astype(narrow)
 
     d_pre, d_gain_one, d_shift_one = norm_backward(
         d_hidden.astype(jnp.float32), norm_one, vec_rows[7]
@@ -823,30 +1161,16 @@
     d_out_bias = jnp.sum(d_branch.astype(jnp.float32), 0)
     d_out = chip_sum(context, d_branch)
     d_context = right_transposed(d_branch, out_low).astype(narrow)
-    d_context = d_context.reshape(own, slots, H, head_dim)
-    d_value = jnp.einsum(
-        "shqk,sqhd->skhd", probs_low, d_context, preferred_element_type=jnp.float32
-    )
-    d_probs = jnp.einsum(
-        "sqhd,skhd->shqk", d_context, value_rows, preferred_element_type=jnp.float32
-    )
-    d_scores = (probs * (d_probs - jnp.sum(probs * d_probs, -1, keepdims=True))).astype(narrow)
-    d_query = (
-        jnp.einsum("shqk,skhd->sqhd", d_scores, key_rows, preferred_element_type=jnp.float32)
-        * scale
-    )
-    d_query = d_query.reshape(-1, width).astype(narrow)
-    d_key = (
-        jnp.einsum("shqk,sqhd->skhd", d_scores, queries, preferred_element_type=jnp.float32)
-        * scale
-    )
-    d_both = jnp.stack([d_key, d_value], 2).reshape(own * seq_len, 2 * width).astype(narrow)
+    d_query, d_key, d_value = attention(own_lengths, queries, both, d_context)
     d_query_bias = jnp.sum(d_query.astype(jnp.float32), 0)
-    d_value_bias = jnp.sum(d_both[:, width:].astype(jnp.float32), 0)
-    d_qkv = jnp.concatenate(
-        [chip_sum(chosen_low, d_query), chip_sum(start_low, d_both)], 1
-    )
+    d_value_bias = jnp.sum(d_value.astype(jnp.float32), 0)
+    d_qkv = [
+        chip_sum(chosen_low, d_query),
+        chip_sum(start_low, d_key),
+        chip_sum(start_low, d_value),
+    ]
     d_chosen = d_pre + right_transposed(d_query, query_low)
+    d_both = jnp.concatenate([d_key, d_value], 1)
     d_start = right_transposed(d_both, both_low) + rows_to_seq(
         pick, d_chosen.reshape(own, slots, width)
     ).reshape(-1, width)
@@ -882,9 +1206,13 @@
         ],
         0,
     )
-    (own_up, own_down, own_qkv, own_turn, own_out, own_small), arrived = reduce_chips(
-        [d_up, d_down, d_qkv, d_turn, d_out, chip_half(d_small.T)], sizes, ids[5], send
-    )
+    partials = [d_out, d_turn] + d_qkv + [chip_half(d_small.T)]
+    pieces = [(i, 0, deep) for i in range(6)]
+    (own_out, own_turn, own_q, own_k, own_v, own_small), arrived, up_blocks = sum_chips(
+        partials, pieces, sizes, ids[9], send, up_blocks
+    )
+    own_qkv = jnp.concatenate([own_q, own_k, own_v], 1)
+    own_up = up_blocks.swapaxes(0, 1).reshape(up_weight.shape).astype(jnp.float32)
     d_word = d_word + routes.give(d_embedded_low, arrived.reshape(-1, width))
     owned = (
         d_word,
@@ -900,7 +1228,7 @@
         local_squares = local_squares + jnp.sum(grad * grad)
     spare = -(rows_per + 1) % 128
     last = jnp.concatenate([d_bias, local_squares[None], jnp.zeros((spare,), jnp.float32)])
-    last = spread_row(last.reshape(8, -1), sizes, ids[6]).reshape(parts, -1)
+    last = spread_row(last.reshape(8, -1), sizes, ids[10]).reshape(parts, -1)
     bias_grad = last[:, :rows_per].reshape(-1)[:vocab]
     grad_norm = jnp.sqrt(jnp.sum(last[:, rows_per]))
     factor = clip_norm / jnp.maximum(grad_norm, clip_norm)

time: 998 us -> 771 us (0.77)
  Pallas kernels: 594 us -> 464 us
  local copies, waits for them, and re-layouts: 100 us -> 35.1 us
  matrix products: 169 us -> 137 us
  other arithmetic: 108 us -> 80.9 us
  starting transfers between devices: 3.98 us -> 21 us
  waiting for transfers between devices: 0.04 us -> 11.4 us
    pallas_call x2 -> x4, Pallas kernels: 288 us -> 214 us  [gather_all(): pl.pallas_call(functools.partial(gather_kernel, sizes, tuple(pieces), rou...]
    pallas_call x2 -> x7, Pallas kernels: 267 us -> 225 us  [the longest x4 192 us: reduce_all(): pl.pallas_call(functools.partial(reduce_kernel, sizes, tuple(pieces), cor...]
    unnamed x271 -> x207, local copies, waits for them, and re-layouts: 33.6 us -> 11.2 us
    ppermute x0 -> x12, starting transfers between devices: none -> 19 us  [line_shift(): lax.ppermute(shard, 'dp', [(i, (i + step) % size) for i in range(size)])]
    reshape x6 -> x2, local copies, waits for them, and re-layouts: 17.1 us -> 0.03 us  [the longest x1 0.02 us: per_device(): up_weight.astype(narrow).reshape(up_weight.shape[0], planes, units)]
    another operation x8 -> x5, other arithmetic: 18.6 us -> 2.6 us  [the longest x3 2.58 us: line_gather(): jnp.stack([shard] + [line_shift(shard, step) for step in range(1, size)])]
    dot_general x7, matrix products: 42.3 us -> 29 us  [right_transposed(): lax.dot_general(left, right, (((1,), (1,)), ((), ())), preferred_element_...]
    pallas_call x2 -> x1, Pallas kernels: 21.8 us -> 9.87 us  [spread(): pl.pallas_call(functools.partial(spread_kernel, sizes), out_shape=jax.Sha...]
  transfers between devices with their start and end apart: 14 -> 22, of which waited for: 0 -> 4; matrix products, arithmetic and copies ran while one was open for 12% -> 25% of each run, Pallas kernels for 6% -> 43%
where the time goes in v2:
time: 771 us; the launch traced here: 762 us
  Pallas kernels  464 us (60%)
  matrix products  137 us (18%)
  other arithmetic  80.9 us (10%)
  local copies, waits for them, and re-layouts  35.1 us (5%)
  starting transfers between devices  21 us (3%)
  between operations  12.4 us (2%)
  waiting for transfers between devices  11.4 us (1%)
    pallas_call x4, Pallas kernels, gather_all(): pl.pallas_call(functools.partial(gather_kernel, sizes, tuple(pieces), rou...  214 us
    pallas_call x4, Pallas kernels, reduce_all(): pl.pallas_call(functools.partial(reduce_kernel, sizes, tuple(pieces), cor...  192 us
    dot_general x10, matrix products, matmul(): return jnp.dot(left, right, preferred_element_type=jnp.float32)  54 us
    dot_general x11, matrix products, left_transposed(): lax.dot_general(left, right, (((0,), (0,)), ((), ())), preferred_element_...  49.7 us
    dot_general x7, matrix products, right_transposed(): lax.dot_general(left, right, (((1,), (1,)), ((), ())), preferred_element_...  29 us
    sub x8, other arithmetic, adam_step(): weight - rate * (first_hat / (jnp.sqrt(second_hat) + epsilon) + weight_de...  19.5 us
    ppermute x12, starting transfers between devices, line_shift(): lax.ppermute(shard, 'dp', [(i, (i + step) % size) for i in range(size)])  19 us
  transfers between devices with their start and end apart: 22, of which 4 were waited for; matrix products, arithmetic and copies ran while one was open for 25% of the time, Pallas kernels for 43%

profile of v2, /device:TPU:0, one launch (start us, length us, event | category | flops | bytes accessed | tf_op | source)
XLA Modules:
  0.0 762.0 jit_solution(1872729386939498806)
XLA Ops:
  3.4 13.9 %shard_map.475 = (s32[32,2,640]{2,1,0:T(2,128)S(1)}, bf16[8,32,512]{2,1,0:T(8,128)(2,1)S(1)}) custom-call(s32[2,640]{1,0:T(2,128)S(1)} %fusion.225.row_ref, bf16[8,32,512]{2,1,0:T(8,128)(2,1)S(1)} %bitcast.306), custom_call_target="tpu_custom_call" | custom-call | tf_op jit(solution)/shard_map/pallas_call | solution.py:335
  33.5 5.0 fusion.40
  39.3 117.8 %shard_map.476 = (bf16[2,4,4,32,640]{4,3,2,1,0:T(8,128)(2,1)}, bf16[2,4,4,32,3072]{4,3,2,1,0:T(8,128)(2,1)}, bf16[2,4,4,32,1024]{4,3,2,1,0:T(8,128)(2,1)}, bf16[...) custom-call(bf16[32,640]{1,0:T(8,128)(2,1)} %maximum_maximum_fusion.refs_0_, ...), custom_call_target="tpu_custom_call" | custom-call | tf_op jit(solution)/shard_map/pallas_call | solution.py:578
  164.3 7.0 fusion.19
  181.8 8.2 %add_convert_fusion.k_ref.v_ref = bf16[1024,2048]{1,0:T(8,128)(2,1)} fusion(f32[2048]{0:T(1024)S(1)} %concatenate.60, bf16[1024,1024]{1,0:T(8,128)(2,1)S(1)} %get-tuple-element.502, bf16[1024,3072]{1,0:T(8,128)(2,1)} %bitcast.399), kind=kOutput, calls=%fused_computation.34 | convolution fusion | flops 4299161600 | bytes 10493952 | tf_op jit(solution)/shard_map/dot_general | solution.py:32
  192.8 8.2 %shard_map.477 = bf16[128,1024]{1,0:T(8,128)(2,1)} custom-call(s32[2]{0:T(128)} %get-tuple-element.507.lengths_ref, bf16[128,1024]{1,0:T(8,128)(2,1)} %fusion.109.q_ref, bf16[1024,2048]{1,0:T(8,128)(2,1)} %add_convert_fusion.k_ref.v_ref, bf16[1024,2048]{1,0:T(8,128)(2,1)} %add_convert_fusion.k_ref.v_ref), custom_call_target="tpu_custom_call" | custom-call | tf_op jit(solution)/shard_map/pallas_call | solution.py:856
  207.5 23.3 %shard_map.478 = bf16[2,4,1,128,1024]{4,3,2,1,0:T(8,128)(2,1)} custom-call(bf16[128,1024]{1,0:T(8,128)(2,1)} %add_convert_fusion.4.refs_0_), custom_call_target="tpu_custom_call" | custom-call | tf_op jit(solution)/shard_map/pallas_call | solution.py:578
  232.4 4.0 copy.167
  240.6 6.6 collective-permute-done.5
  249.0 6.7 fusion.58
  255.8 6.0 convolution_convert_fusion.2
  261.8 15.8 %shard_map.479 = f32[128,1024]{1,0:T(8,128)S(1)} custom-call(bf16[2,4,1,128,1024]{4,3,2,1,0:T(8,128)(2,1)S(1)} %bitcast.301), custom_call_target="tpu_custom_call" | custom-call | tf_op jit(solution)/shard_map/pallas_call | solution.py:769
  282.9 49.8 %shard_map.480 = bf16[2,4,4,128,1024]{4,3,2,1,0:T(8,128)(2,1)} custom-call(bf16[128,1024]{1,0:T(8,128)(2,1)} %add_convert_fusion.2.refs_0_), custom_call_target="tpu_custom_call" | custom-call | tf_op jit(solution)/shard_map/pallas_call | solution.py:578
  332.7 11.6 %fusion.15 = (f32[4096]{0:T(1024)S(1)}, f32[4096,960]{0,1:T(8,128)S(1)}) fusion(f32[960]{0:T(1024)S(1)} %pad_dynamic-slice_fusion, pred[960]{0:T(1024)(128)(4,1)S(1)} %broadcast_compare_fusion, bf16[4096,1024]{1,0:T(8,128)(2,1)} %bitcast.321, bf16[960,1024]{1,0:T(8,128)(2,1)} %get-tuple-element.742), kind=kOutput, calls=%fused_computation.33 | convolution fusion | flops 8064856064 | bytes 26104512 | tf_op jit(solution)/shard_map/dot_general | solution.py:42
  344.4 6.3 exponential_reduce_fusion
  350.8 14.9 %shard_map.481 = f32[32,8,128]{2,1,0:T(8,128)S(1)} custom-call(f32[32,8,128]{2,1,0:T(8,128)S(1)} %pad.10.own_ref), custom_call_target="tpu_custom_call" | custom-call | tf_op jit(solution)/shard_map/pallas_call | solution.py:420
  366.3 8.5 %fusion.275 = (f32[960]{0:T(1024)S(1)}, bf16[4096,960]{0,1:T(8,128)(2,1)S(1)}) fusion(s32[960]{0:T(1024)S(1)} %copy-done.74, s32[4096]{0:T(1024)S(1)} %eq.240, f32[4096]{0:T(1024)S(1)} %bitcast.371, f32[4096]{0:T(1024)S(1)} %bitcast.372, f32[4096,960]{0,1:T(8,128)S(1)} %get-tuple-element.560, f32[960]{0:T(1024)S(1)} %pad_dynamic-slice_fusion, ...), kind=kLoop, calls=%fused_computation.470 | loop fusion | flops 39320640 | bytes 23670976 | tf_op jit(solution)/shard_map/reduce_sum | solution.py:1125
  374.9 14.3 %convolution_convert_fusion = bf16[4096,1024]{1,0:T(8,128)(2,1)} fusion(bf16[960,1024]{1,0:T(8,128)(2,1)} %get-tuple-element.742, bf16[4096,960]{0,1:T(8,128)(2,1)S(1)} %get-tuple-element.486), kind=kOutput, calls=%fused_computation.35 | convolution fusion | flops 8057257984 | bytes 18219008 | tf_op jit(solution)/shard_map/dot_general | solution.py:32
  389.2 48.7 %shard_map.482 = f32[128,1024]{1,0:T(8,128)S(1)} custom-call(bf16[2,4,4,128,1024]{4,3,2,1,0:T(8,128)(2,1)} %bitcast.323), custom_call_target="tpu_custom_call" | custom-call | tf_op jit(solution)/shard_map/pallas_call | solution.py:769
  444.2 23.0 %shard_map.483 = bf16[2,4,1,128,1024]{4,3,2,1,0:T(8,128)(2,1)} custom-call(bf16[128,1024]{1,0:T(8,128)(2,1)} %get-tuple-element.492.refs_0_), custom_call_target="tpu_custom_call" | custom-call | tf_op jit(solution)/shard_map/pallas_call | solution.py:578
  481.4 14.5 %shard_map.484 = f32[128,1024]{1,0:T(8,128)S(1)} custom-call(bf16[2,4,1,128,1024]{4,3,2,1,0:T(8,128)(2,1)S(1)} %bitcast.300), custom_call_target="tpu_custom_call" | custom-call | tf_op jit(solution)/shard_map/pallas_call | solution.py:769
  498.1 11.5 %shard_map.485 = (bf16[128,1024]{1,0:T(8,128)(2,1)}, bf16[1024,1024]{1,0:T(8,128)(2,1)}, bf16[1024,1024]{1,0:T(8,128)(2,1)}) custom-call(s32[2]{0:T(128)} %get-tuple-element.507.lengths_ref, bf16[128,1024]{1,0:T(8,128)(2,1)} %fusion.109.q_ref, bf16[1024,2048]{1,0:T(8,128)(2,1)} %add_convert_fusion.k_ref.v_ref, ...), custom_call_target="tpu_custom_call" | custom-call | tf_op jit(solution)/shard_map/pallas_call | solution.py:863
  514.4 8.8 %multiply_reduce_fusion = (bf16[1024]{0:T(1024)(128)(2,1)S(1)}, f32[1024]{0:T(1024)S(1)}, f32[1024]{0:T(1024)S(1)}, bf16[1024]{0:T(1024)(128)(2,1)S(1)}, f32[1024,1024]{1,0:T(8,128)S(1)}) fusion(f32[1024,1024]{1,0:T(8,128)S(1)} %copy-done.6, f32[1024]{0:T(1024)S(1)} %add_rsqrt_fusion, f32[1024]{0:T(1024)S(1)} %broadcast_multiply_fusion.2, ...), kind=kOutput, calls=%fused_computation.60 | convolution fusion | flops 4313837568 | bytes 20996096 | tf_op jit(solution)/shard_map/dot_general | solution.py:42
  527.9 5.0 fusion.39
  552.4 6.8 collective-permute-start.21
  570.3 6.3 fusion.95
  576.6 5.0 fusion.98
  581.6 112.5 %shard_map.486 = (f32[32,1024]{1,0:T(8,128)S(1)}, f32[32,1024]{1,0:T(8,128)S(1)}, f32[32,1024]{1,0:T(8,128)S(1)}, f32[32,1024]{1,0:T(8,128)S(1)}, f32[32,1024]{1...) custom-call(bf16[4,4,32,1024]{3,2,1,0:T(8,128)(2,1)S(1)} %bitcast.304, ...), custom_call_target="tpu_custom_call" | custom-call | tf_op jit(solution)/shard_map/pallas_call | solution.py:769
  696.2 7.3 fusion.16
  703.8 15.7 %multiply_reduce_fusion.3 = (f32[]{:T(128)}, f32[960,1024]{1,0:T(8,128)}) fusion(f32[960,1024]{1,0:T(8,128)} %get-tuple-element.265, bf16[4096,1024]{1,0:T(8,128)(2,1)} %bitcast.322, bf16[4096,960]{0,1:T(8,128)(2,1)} %copy-done.17), kind=kOutput, calls=%fused_computation.76 | convolution fusion | flops 8056012800 | bytes 24117252 | tf_op jit(solution)/shard_map/dot_general | solution.py:36
  726.2 9.9 %shard_map.487 = f32[32,8,128]{2,1,0:T(8,128)S(1)} custom-call(f32[8,128]{1,0:T(8,128)S(1)} %maximum_bitcast_fusion.2.row_ref), custom_call_target="tpu_custom_call" | custom-call | tf_op jit(solution)/shard_map/pallas_call | solution.py:379
  752.1 7.3 multiply_subtract_fusion
  (428 shorter events, 139.3 us)
Async XLA Ops:
  0.7 174.8 %copy-start = (s32[4,64]{1,0:T(4,128)S(1)}, s32[4,64]{1,0:T(4,128)}, u32[]{:S(2)}) copy-start(s32[4,64]{1,0:T(4,128)} %param.34) | copy-start | bytes 3076
  17.3 220.6 %collective-permute-start = (bf16[8,32,512]{2,1,0:T(8,128)(2,1)S(1)}, bf16[8,32,512]{2,1,0:T(8,128)(2,1)}, u32[]{:S(2)}, u32[]{:S(2)}) collective-permute-start(bf16[8,32,512]{2,1,0:T(8,128)(2,1)S(1)} %get-tuple-element.259), channel_id=1, source_target_pairs={{0,1},{1,2},{2,3},{3,0},{4,5},{5,6},{6,7},{7,4},{8,9},{9,10},{10,1... | collective-permute-start | bytes 786440 | tf_op jit(solution)/shard_map/ppermute | solution.py:925
  17.9 220.5 %collective-permute-start.1 = (bf16[8,32,512]{2,1,0:T(8,128)(2,1)S(1)}, bf16[8,32,512]{2,1,0:T(8,128)(2,1)}, u32[]{:S(2)}, u32[]{:S(2)}) collective-permute-start(bf16[8,32,512]{2,1,0:T(8,128)(2,1)S(1)} %get-tuple-element.259), channel_id=1, source_target_pairs={{0,2},{1,3},{2,0},{3,1},{4,6},{5,7},{6,4},{7,5},{8,10},{9,11},{10,... | collective-permute-start | bytes 786440 | tf_op jit(solution)/shard_map/ppermute | solution.py:925
  18.9 219.9 %collective-permute-start.2 = (bf16[8,32,512]{2,1,0:T(8,128)(2,1)S(1)}, bf16[8,32,512]{2,1,0:T(8,128)(2,1)}, u32[]{:S(2)}, u32[]{:S(2)}) collective-permute-start(bf16[8,32,512]{2,1,0:T(8,128)(2,1)S(1)} %get-tuple-element.259), channel_id=1, source_target_pairs={{0,3},{1,0},{2,1},{3,2},{4,7},{5,4},{6,5},{7,6},{8,11},{9,8},{10,9... | collective-permute-start | bytes 786440 | tf_op jit(solution)/shard_map/ppermute | solution.py:925
  22.9 217.7 %collective-permute-start.3 = (bf16[128,1024]{1,0:T(8,128)(2,1)}, bf16[128,1024]{1,0:T(8,128)(2,1)}, u32[]{:S(2)}, u32[]{:S(2)}) collective-permute-start(bf16[128,1024]{1,0:T(8,128)(2,1)} %convert_element_type.270), channel_id=1, source_target_pairs={{0,1},{1,2},{2,3},{3,0},{4,5},{5,6},{6,7},{7,4},{8,9},{9,10},{10,1... | collective-permute-start | bytes 786440 | tf_op jit(solution)/shard_map/ppermute | solution.py:925
  23.5 217.1 %collective-permute-start.4 = (bf16[128,1024]{1,0:T(8,128)(2,1)}, bf16[128,1024]{1,0:T(8,128)(2,1)}, u32[]{:S(2)}, u32[]{:S(2)}) collective-permute-start(bf16[128,1024]{1,0:T(8,128)(2,1)} %convert_element_type.270), channel_id=1, source_target_pairs={{0,2},{1,3},{2,0},{3,1},{4,6},{5,7},{6,4},{7,5},{8,10},{9,11},{10,... | collective-permute-start | bytes 786440 | tf_op jit(solution)/shard_map/ppermute | solution.py:925
  237.9 9.3 %collective-permute-start.5 = (bf16[128,1024]{1,0:T(8,128)(2,1)}, bf16[128,1024]{1,0:T(8,128)(2,1)S(1)}, u32[]{:S(2)}, u32[]{:S(2)}) collective-permute-start(bf16[128,1024]{1,0:T(8,128)(2,1)} %convert_element_type.270), channel_id=1, source_target_pairs={{0,3},{1,0},{2,1},{3,2},{4,7},{5,4},{6,5},{7,6},{8,11},{9,8},{10,9... | collective-permute-start | bytes 786440 | tf_op jit(solution)/shard_map/ppermute | solution.py:925
  238.4 287.2 %collective-permute-start.10 = (bf16[128,512]{1,0:T(8,128)(2,1)}, bf16[128,512]{1,0:T(8,128)(2,1)}, u32[]{:S(2)}, u32[]{:S(2)}) collective-permute-start(bf16[128,512]{1,0:T(8,128)(2,1)} %get-tuple-element.525), channel_id=1, source_target_pairs={{0,16},{16,0},{1,17},{17,1},{2,18},{18,2},{3,19},{19,3},{4,20},{20... | collective-permute-start | bytes 393224 | tf_op jit(solution)/shard_map/ppermute | solution.py:154
  238.9 288.9 %collective-permute-start.6 = (bf16[128,512]{1,0:T(8,128)(2,1)}, bf16[128,512]{1,0:T(8,128)(2,1)}, u32[]{:S(2)}, u32[]{:S(2)}) collective-permute-start(bf16[128,512]{1,0:T(8,128)(2,1)} %get-tuple-element.529), channel_id=1, source_target_pairs={{0,16},{16,0},{1,17},{17,1},{2,18},{18,2},{3,19},{19,3},{4,20},{20... | collective-permute-start | bytes 393224 | tf_op jit(solution)/shard_map/ppermute | solution.py:154
  344.4 21.3 %copy-start.89 = (s32[128]{0:T(128)S(1)}, s32[128]{0:T(128)}, u32[]{:S(2)}) copy-start(s32[128]{0:T(128)} %lt.263) | copy-start | bytes 1540
  389.2 48.7 %copy-start.15 = (f32[128,1024]{1,0:T(8,128)S(1)}, f32[128,1024]{1,0:T(8,128)}, u32[]{:S(2)}) copy-start(f32[128,1024]{1,0:T(8,128)} %copy-done.14) | copy-start | bytes 1572868
  389.2 49.0 %copy-start.56 = (f32[128,1024]{1,0:T(8,128)S(1)}, f32[128,1024]{1,0:T(8,128)}, u32[]{:S(2)}) copy-start(f32[128,1024]{1,0:T(8,128)} %get-tuple-element.558) | copy-start | bytes 1572868
  472.4 61.1 %collective-permute-start.19 = (bf16[128,1024]{1,0:T(8,128)(2,1)}, bf16[128,1024]{1,0:T(8,128)(2,1)}, u32[]{:S(2)}, u32[]{:S(2)}) collective-permute-start(bf16[128,1024]{1,0:T(8,128)(2,1)} %get-tuple-element.510), channel_id=1, source_target_pairs={{0,1},{1,2},{2,3},{3,0},{4,5},{5,6},{6,7},{7,4},{8,9},{9,10},{10,1... | collective-permute-start | bytes 786440 | tf_op jit(solution)/shard_map/ppermute | solution.py:925
  473.3 60.2 %collective-permute-start.20 = (bf16[128,1024]{1,0:T(8,128)(2,1)}, bf16[128,1024]{1,0:T(8,128)(2,1)}, u32[]{:S(2)}, u32[]{:S(2)}) collective-permute-start(bf16[128,1024]{1,0:T(8,128)(2,1)} %get-tuple-element.512), channel_id=1, source_target_pairs={{0,2},{1,3},{2,0},{3,1},{4,6},{5,7},{6,4},{7,5},{8,10},{9,11},{10,... | collective-permute-start | bytes 786440 | tf_op jit(solution)/shard_map/ppermute | solution.py:925
  514.1 56.2 %collective-permute-start.14 = (bf16[1024,1024]{1,0:T(8,128)(2,1)}, bf16[1024,1024]{1,0:T(8,128)(2,1)}, u32[]{:S(2)}, u32[]{:S(2)}) collective-permute-start(bf16[1024,1024]{1,0:T(8,128)(2,1)} %get-tuple-element.263), channel_id=1, source_target_pairs={{0,16},{16,0},{1,17},{17,1},{2,18},{18,2},{3,19},{19,3},{4,20},{20... | collective-permute-start | bytes 6291464 | tf_op jit(solution)/shard_map/ppermute | solution.py:154
  525.6 10.3 %collective-permute-start.16 = (bf16[8,32,512]{2,1,0:T(8,128)(2,1)S(1)}, bf16[8,32,512]{2,1,0:T(8,128)(2,1)S(1)}, u32[]{:S(2)}, u32[]{:S(2)}) collective-permute-start(bf16[8,32,512]{2,1,0:T(8,128)(2,1)S(1)} %get-tuple-element.513), channel_id=1, source_target_pairs={{0,1},{1,2},{2,3},{3,0},{4,5},{5,6},{6,7},{7,4},{8,9},{9,10},{10,1... | collective-permute-start | bytes 786440 | tf_op jit(solution)/shard_map/ppermute | solution.py:925
  527.8 5.1 collective-permute-start.8
  532.9 43.7 %collective-permute-start.13 = (bf16[1024,1024]{1,0:T(8,128)(2,1)}, bf16[1024,1024]{1,0:T(8,128)(2,1)}, u32[]{:S(2)}, u32[]{:S(2)}) collective-permute-start(bf16[1024,1024]{1,0:T(8,128)(2,1)} %get-tuple-element.262), channel_id=1, source_target_pairs={{0,16},{16,0},{1,17},{17,1},{2,18},{18,2},{3,19},{19,3},{4,20},{20... | collective-permute-start | bytes 6291464 | tf_op jit(solution)/shard_map/ppermute | solution.py:154
  533.5 16.3 %collective-permute-start.11 = (bf16[128,1024]{1,0:T(8,128)(2,1)}, bf16[128,1024]{1,0:T(8,128)(2,1)}, u32[]{:S(2)}, u32[]{:S(2)}) collective-permute-start(bf16[128,1024]{1,0:T(8,128)(2,1)} %get-tuple-element.261), channel_id=1, source_target_pairs={{0,16},{16,0},{1,17},{17,1},{2,18},{18,2},{3,19},{19,3},{4,20},{20... | collective-permute-start | bytes 786440 | tf_op jit(solution)/shard_map/ppermute | solution.py:154
  533.6 15.5 %collective-permute-start.17 = (bf16[8,32,512]{2,1,0:T(8,128)(2,1)}, bf16[8,32,512]{2,1,0:T(8,128)(2,1)}, u32[]{:S(2)}, u32[]{:S(2)}) collective-permute-start(bf16[8,32,512]{2,1,0:T(8,128)(2,1)} %get-tuple-element.515), channel_id=1, source_target_pairs={{0,2},{1,3},{2,0},{3,1},{4,6},{5,7},{6,4},{7,5},{8,10},{9,11},{10,... | collective-permute-start | bytes 786440 | tf_op jit(solution)/shard_map/ppermute | solution.py:925
  536.0 13.7 %collective-permute-start.18 = (bf16[8,32,512]{2,1,0:T(8,128)(2,1)}, bf16[8,32,512]{2,1,0:T(8,128)(2,1)}, u32[]{:S(2)}, u32[]{:S(2)}) collective-permute-start(bf16[8,32,512]{2,1,0:T(8,128)(2,1)} %get-tuple-element.514), channel_id=1, source_target_pairs={{0,3},{1,0},{2,1},{3,2},{4,7},{5,4},{6,5},{7,6},{8,11},{9,8},{10,9... | collective-permute-start | bytes 786440 | tf_op jit(solution)/shard_map/ppermute | solution.py:925
  549.1 2.7 collective-permute-start.9
  549.7 20.6 %collective-permute-start.12 = (bf16[1024,512]{1,0:T(8,128)(2,1)}, bf16[1024,512]{1,0:T(8,128)(2,1)}, u32[]{:S(2)}, u32[]{:S(2)}) collective-permute-start(bf16[1024,512]{1,0:T(8,128)(2,1)} %get-tuple-element.509), channel_id=1, source_target_pairs={{0,16},{16,0},{1,17},{17,1},{2,18},{18,2},{3,19},{19,3},{4,20},{20... | collective-permute-start | bytes 3145736 | tf_op jit(solution)/shard_map/ppermute | solution.py:154
  549.8 2.7 collective-permute-start.7
  551.8 16.0 %collective-permute-start.15 = (bf16[512,640]{0,1:T(8,128)(2,1)S(1)}, bf16[512,640]{0,1:T(8,128)(2,1)S(1)}, u32[]{:S(2)}, u32[]{:S(2)}) collective-permute-start(bf16[512,640]{0,1:T(8,128)(2,1)S(1)} %dynamic-slice_bitcast_fusion), channel_id=1, source_target_pairs={{0,16},{16,0},{1,17},{17,1},{2,18},{18,2},{3,19},{19,3},{4,20},{20... | collective-permute-start | bytes 1966088 | tf_op jit(solution)/shard_map/ppermute | solution.py:154
  552.4 12.7 %collective-permute-start.21 = (bf16[128,1024]{1,0:T(8,128)(2,1)S(1)}, bf16[128,1024]{1,0:T(8,128)(2,1)S(1)}, u32[]{:S(2)}, u32[]{:S(2)}) collective-permute-start(bf16[128,1024]{1,0:T(8,128)(2,1)S(1)} %copy-done.62), channel_id=1, source_target_pairs={{0,3},{1,0},{2,1},{3,2},{4,7},{5,4},{6,5},{7,6},{8,11},{9,8},{10,9... | collective-permute-start | bytes 786440 | tf_op jit(solution)/shard_map/ppermute | solution.py:925
  581.6 114.5 %copy-start.81 = (s32[1536]{0:T(1024)S(1)}, s32[1536]{0:T(1024)}, u32[]{:S(2)}) copy-start(s32[1536]{0:T(1024)} %copy-done.80) | copy-start | bytes 18436
  703.8 33.9 %copy-start.4 = (f32[32,640]{1,0:T(8,128)S(1)}, f32[32,640]{1,0:T(8,128)}, u32[]{:S(2)}) copy-start(f32[32,640]{1,0:T(8,128)} %copy-done.3) | copy-start | bytes 245764
  703.8 33.9 %copy-start.70 = (f32[19,32]{0,1:T(8,128)S(1)}, f32[19,32]{0,1:T(8,128)}, u32[]{:S(2)}) copy-start(f32[19,32]{0,1:T(8,128)} %copy.175) | copy-start | bytes 7300
  703.8 33.9 %copy-start.71 = (f32[19,32]{0,1:T(8,128)S(1)}, f32[19,32]{0,1:T(8,128)}, u32[]{:S(2)}) copy-start(f32[19,32]{0,1:T(8,128)} %copy.171) | copy-start | bytes 7300
  703.8 33.9 %copy-start.72 = (f32[19,32]{0,1:T(8,128)S(1)}, f32[19,32]{0,1:T(8,128)}, u32[]{:S(2)}) copy-start(f32[19,32]{0,1:T(8,128)} %copy.173) | copy-start | bytes 7300
  719.5 20.4 %copy-start.49 = (f32[2,32,1024]{2,1,0:T(8,128)S(1)}, f32[2,32,1024]{2,1,0:T(8,128)}, u32[]{:S(2)}) copy-start(f32[2,32,1024]{2,1,0:T(8,128)} %param.45) | copy-start | bytes 786436
  (84 other events, 481.5 us)

commit v3 on v2

--- a/solution.py
+++ b/solution.py
@@ -97,7 +97,8 @@
         self.room = max(16, int(math.ceil((mean + 2.8 * math.sqrt(mean)) / 16)) * 16)
         owners = jnp.where(all_live, all_ids // rows_per, -1)
         counts = jnp.sum(one_hot(owners, self.parts, jnp.int32), 1)
-        self.rounds = (jnp.max(counts) + self.room - 1) // self.room
+        self.more = 16
+        self.rounds = (jnp.maximum(jnp.max(counts) - self.room, 0) + self.more - 1) // self.more
         mine = owners == self.me
         order = jnp.arange(tokens, dtype=jnp.int32)
         upto = (order[:, None] <= order[None, :]).astype(jnp.bfloat16)
@@ -111,43 +112,48 @@
         self.in_rank = ranks
         self.in_owner = own_owners
 
-    def owner_pick(self, turn):
-        slots = turn * self.room + jnp.arange(self.room, dtype=jnp.int32)
+    def owner_pick(self, first, room):
+        slots = first + jnp.arange(room, dtype=jnp.int32)
         at = self.out_rank[:, None, :] == slots[None, :, None]
         row = jnp.sum(jnp.where(at, self.out_row[:, None, :] + 1, 0), 2) - 1
         return one_hot(row.reshape(-1), self.rows_per, jnp.bfloat16)
 
-    def token_pick(self, turn):
-        rank = self.in_rank - turn * self.room
-        inside = (self.in_owner >= 0) & (rank >= 0) & (rank < self.room)
-        slot = jnp.where(inside, self.in_owner * self.room + rank, -1)
-        return one_hot(slot, self.parts * self.room, jnp.bfloat16)
+    def token_pick(self, first, room):
+        rank = self.in_rank - first
+        inside = (self.in_owner >= 0) & (rank >= 0) & (rank < room)
+        slot = jnp.where(inside, self.in_owner * room + rank, -1)
+        return one_hot(slot, self.parts * room, jnp.bfloat16)
 
     def exchange(self, rows):
-        shaped = rows.reshape(self.parts, self.room, rows.shape[1])
+        shaped = rows.reshape(self.parts, -1, rows.shape[-1])
         return lax.all_to_all(shaped, AXES, 0, 0).reshape(rows.shape)
 
-    def table_rows(self, table, turn):
-        return matmul(self.owner_pick(turn), table).astype(jnp.bfloat16)
-
-    def token_rows(self, rows, turn):
-        return left_transposed(self.token_pick(turn), rows).astype(jnp.bfloat16)
+    def table_rows(self, table, first, room):
+        return matmul(self.owner_pick(first, room), table).astype(jnp.bfloat16)
+
+    def token_rows(self, rows, first, room):
+        return left_transposed(self.token_pick(first, room), rows).astype(jnp.bfloat16)
+
+    def later(self, more, start):
+        def one(turn, kept):
+            return kept + more(self.room + turn * self.more)
+
+        return lax.fori_loop(0, self.rounds, one, start)
 
     def fetch(self, table, arrived):
-        def more(turn, kept):
-            rows = self.exchange(self.table_rows(table, turn))
-            return kept + matmul(self.token_pick(turn), rows)
-
-        return lax.fori_loop(1, self.rounds, more, matmul(self.token_pick(0), arrived))
-
-    def give(self, rows, arrived):
-        def more(turn, kept):
-            back = self.exchange(self.token_rows(rows, turn))
-            return kept + left_transposed(self.owner_pick(turn), back)
-
-        return lax.fori_loop(
-            1, self.rounds, more, left_transposed(self.owner_pick(0), arrived)
-        )
+        def more(first):
+            rows = self.exchange(self.table_rows(table, first, self.more))
+            return matmul(self.token_pick(first, self.more), rows)
+
+        return self.later(more, matmul(self.token_pick(0, self.room), arrived))
+
+    def give(self, rows, arrived, start):
+        def more(first):
+            back = self.exchange(self.token_rows(rows, first, self.more))
+            return left_transposed(self.owner_pick(first, self.more), back)
+
+        start = start + left_transposed(self.owner_pick(0, self.room), arrived)
+        return self.later(more, start)
 
 
 def swapped(shard):
@@ -520,13 +526,16 @@
             along(n, side, hop)
 
     def over_plane(n):
-        piece = pieces[n]
+        array, first, rows = piece = pieces[n]
         over_line(n, hops)
-        keeps[n].wait()
-        group = view(piece, pipe, grp)
-        launch(n, 2 * hops, group, piece, (pipe, near, dp), pipe, grp)
-        launch(n, 2 * hops + 1, group, piece, (pipe, far, dp), pipe, grp)
-        launch(n, 2 * hops + 3, group, piece, core, pipe, grp)
+        if hops:
+            keeps[n].wait()
+            group, at = view(piece, pipe, grp), (pipe, grp)
+        else:
+            group, at = shards[array].at[pl.ds(first, rows)], (pipe, grp, 0)
+        launch(n, 2 * hops, group, piece, (pipe, near, dp), *at)
+        launch(n, 2 * hops + 1, group, piece, (pipe, far, dp), *at)
+        launch(n, 2 * hops + 3, group, piece, core, *at)
 
     def pass_on(n):
         piece = pieces[n]
@@ -561,6 +570,9 @@
                 along(n, side, hop, finish=True)
     for copy in waits:
         copy.wait_send()
+    if not hops:
+        for keep in keeps.values():
+            keep.wait()
     if routed:
         finish()
 
@@ -569,6 +581,7 @@
     parts = math.prod(sizes)
     routed = rows is not None
     kinds = 2 * (sizes[2] - 1) + 7
+    space = pltpu.VMEM if sizes[2] == 1 else pl.ANY
     out_shape = [jax.ShapeDtypeStruct(sizes + shard.shape, shard.dtype) for shard in shards]
     if routed:
         out_shape.append(jax.ShapeDtypeStruct(rows.shape, rows.dtype))
@@ -578,8 +591,8 @@
     return pl.pallas_call(
         functools.partial(gather_kernel, sizes, tuple(pieces), routed),
         out_shape=out_shape,
-        in_specs=[pl.BlockSpec(memory_space=pl.ANY)] * len(operands),
-        out_specs=[pl.BlockSpec(memory_space=pl.ANY)] * len(out_shape),
+        in_specs=[pl.BlockSpec(memory_space=space)] * len(operands),
+        out_specs=[pl.BlockSpec(memory_space=space)] * len(out_shape),
         scratch_shapes=[
             sems,
             sems,
@@ -588,24 +601,26 @@
             swaps,
             pltpu.SemaphoreType.DMA,
         ],
-        compiler_params=pltpu.CompilerParams(collective_id=collective, has_side_effects=True),
+        compiler_params=pltpu.CompilerParams(
+            collective_id=collective, has_side_effects=True, vmem_limit_bytes=16 << 20
+        ),
     )(*operands)
 
 
-def reduce_kernel(sizes, pieces, cores, routed, *refs):
+def reduce_kernel(sizes, pieces, cores, swaps, *refs):
     arrays, total = max(piece[0] for piece in pieces) + 1, len(pieces)
     partials, refs = refs[:arrays], refs[arrays:]
-    if routed:
-        rows_ref, blocks_ref, refs = refs[0], refs[1], refs[2:]
+    if swaps:
+        blocks_ref, refs = refs[0], refs[1:]
     sums, refs = refs[:arrays], refs[arrays:]
-    if routed:
-        arrived_ref, blocks_arrived_ref, refs = refs[0], refs[1], refs[2:]
+    if swaps:
+        blocks_arrived_ref, refs = refs[0], refs[1:]
     chips, refs = refs[: total if cores else 0], refs[total if cores else 0 :]
     others, refs = refs[: total if cores else 0], refs[total if cores else 0 :]
     mine, refs = refs[:total], refs[total:]
     planes, refs = refs[:total], refs[total:]
     lines, refs = refs[:total], refs[total:]
-    send, arrive, own, swap_send, swap_arrive, swap_own, plane_send, plane_arrive, plane_own = refs
+    send, arrive, own, plane_send, plane_arrive, plane_own = refs
     place = Place(sizes)
     pipe, grp, dp = place.pipe, place.grp, place.dp
     near = place.beside * (1 - pipe) + place.below * pipe
@@ -613,14 +628,12 @@
     core = (1 - pipe, grp, dp)
     hops = place.dps - 1
     block = 16
-    if routed:
-        greet([ahead for ahead, _ in place.others()])
+    to_greet = [(pipe, grp, place.line(k + 1)) for k in range(hops)]
+    if swaps:
+        to_greet += [ahead + (dp,) for ahead, _ in place.plane()]
     else:
-        greet(
-            [(pipe, grp, place.line(k + 1)) for k in range(hops)]
-            + [(pipe, near, dp), (pipe, far, dp)]
-            + ([core] if cores else [])
-        )
+        to_greet += [(pipe, near, dp), (pipe, far, dp)] + ([core] if cores else [])
+    greet(to_greet)
     copies = {}
 
     def launch(n, index, source, target, to):
@@ -730,44 +743,37 @@
         for at, stage in enumerate(stages):
             if 0 <= turn - at < total:
                 stage(turn - at)
-        if turn == 0 and routed:
-            finish = (
-                swap_all(place, rows_ref, arrived_ref, swap_send, swap_arrive, swap_own),
-                swap_plane(
-                    place, blocks_ref, blocks_arrived_ref, plane_send, plane_arrive, plane_own
-                ),
+        if turn == 0 and swaps:
+            finish = swap_plane(
+                place, blocks_ref, blocks_arrived_ref, plane_send, plane_arrive, plane_own
             )
     for key, copy in copies.items():
         if key[1] != "own":
             copy.wait_send()
-    if routed:
-        finish[0]()
-        finish[1]()
-
-
-def reduce_all(partials, pieces, sizes, collective, rows=None, plane_rows=None, cores=False):
-    parts = math.prod(sizes)
+    if swaps:
+        finish()
+
+
+def reduce_all(partials, pieces, sizes, collective, blocks=None, cores=False):
     total = len(pieces)
-    routed = rows is not None
+    swaps = blocks is not None
     low = jnp.bfloat16
     _, grps, dps = sizes
     shapes = [(dps, size, partials[array].shape[-1]) for array, _, size in pieces]
     out_shape = [jax.ShapeDtypeStruct(partial.shape[-2:], jnp.float32) for partial in partials]
     out_specs = [pl.BlockSpec(memory_space=pltpu.VMEM)] * len(partials)
-    if routed:
-        for extra in (rows, plane_rows):
-            out_shape.append(jax.ShapeDtypeStruct(extra.shape, extra.dtype))
-            out_specs.append(pl.BlockSpec(memory_space=pl.ANY))
-    operands = list(partials) + ([rows, plane_rows] if routed else [])
+    if swaps:
+        out_shape.append(jax.ShapeDtypeStruct(blocks.shape, blocks.dtype))
+        out_specs.append(pl.BlockSpec(memory_space=pl.ANY))
+    operands = list(partials) + ([blocks] if swaps else [])
     sems = pltpu.SemaphoreType.DMA((total, 4 + dps - 1))
-    swaps = pltpu.SemaphoreType.DMA((parts - 1 if routed else 1,))
     plane_swaps = pltpu.SemaphoreType.DMA((sizes[0] * grps - 1,))
     scratch = [pltpu.VMEM((grps,) + shape, low) for shape in shapes] * (2 if cores else 0)
     scratch += [pltpu.VMEM((2,) + shape, low) for shape in shapes]
     scratch += [pltpu.VMEM((3,) + shape, low) for shape in shapes]
     scratch += [pltpu.VMEM((max(dps - 1, 1),) + shape[1:], low) for shape in shapes]
     return pl.pallas_call(
-        functools.partial(reduce_kernel, sizes, tuple(pieces), cores, routed),
+        functools.partial(reduce_kernel, sizes, tuple(pieces), cores, swaps),
         out_shape=out_shape,
         in_specs=[pl.BlockSpec(memory_space=pl.ANY)] * len(operands),
         out_specs=out_specs,
@@ -776,9 +782,6 @@
             sems,
             sems,
             pltpu.SemaphoreType.DMA((total, 2)),
-            swaps,
-            swaps,
-            pltpu.SemaphoreType.DMA,
             plane_swaps,
             plane_swaps,
             pltpu.SemaphoreType.DMA,
@@ -908,16 +911,16 @@
     return total
 
 
-def sum_chips(partials, pieces, sizes, collective, rows, blocks):
+def sum_chips(partials, pieces, sizes, collective, blocks):
     if collective is not None:
         shaped = [p.reshape(sizes[1:] + (-1, p.shape[1])) for p in partials]
-        *sums, rows, blocks = reduce_all(shaped, pieces, sizes, collective, rows, blocks)
-        return sums, rows, blocks
+        *sums, blocks = reduce_all(shaped, pieces, sizes, collective, blocks)
+        return sums, blocks
     sums = [
         lax.psum_scatter(p, CHIPS, scatter_dimension=0, tiled=True).astype(jnp.float32)
         for p in partials
     ]
-    return sums, lax.all_to_all(rows, AXES, 0, 0), lax.all_to_all(blocks, PLANE, 0, 0)
+    return sums, lax.all_to_all(blocks, PLANE, 0, 0)
 
 
 def line_shift(shard, step):
@@ -1037,8 +1040,12 @@
     cut = me // sizes[2]
     blocks = up_weight.astype(narrow).reshape(up_weight.shape[0], planes, units).swapaxes(0, 1)
     packed, blocks = start_all(packed, blocks, sizes, ids[0])
-    down_low = line_gather(down_weight.astype(narrow), ids[0]).reshape(units, width)
-    up_low = line_gather(blocks, ids[0]).swapaxes(0, 1).reshape(width, units)
+    halves_low = down_weight.astype(narrow).reshape(-1, units)
+    both_low = jnp.concatenate([blocks.reshape(-1, units), halves_low], 0)
+    both_low = line_gather(both_low, ids[0])
+    down_low = both_low[:, -halves_low.shape[0] :].reshape(units, width)
+    up_low = both_low[:, : -halves_low.shape[0]].reshape(sizes[2], planes, -1, units)
+    up_low = up_low.swapaxes(0, 1).reshape(width, units)
     all_ids = packed[:, :, :seq_len]
     all_labels = packed[:, :, seq_len : seq_len + slots].reshape(-1)
     all_lengths = packed[:, :, seq_len + slots]
@@ -1066,7 +1073,7 @@
     ]
     deep = small_low.shape[0]
     pieces = [(0, 0, deep), (1, 0, deep // 2), (1, deep // 2, deep // 2), (2, 0, deep), (3, 0, deep)]
-    send = routes.table_rows(word_low, 0).reshape(parts, -1, width)
+    send = routes.table_rows(word_low, 0, routes.room).reshape(parts, -1, width)
     (small_full, qkv_low, out_low, turn_low), arrived = gather_weights(
         low, pieces, sizes, ids[1], send
     )
@@ -1178,7 +1185,7 @@
     d_seg_zero = jnp.sum(jnp.where(second, 0.0, d_embedded), 0)
     d_seg_one = jnp.sum(jnp.where(second, d_embedded, 0.0), 0)
     d_embedded_low = d_embedded.astype(narrow)
-    send = routes.token_rows(d_embedded_low, 0).reshape(parts, -1, width)
+    arrived = routes.exchange(routes.token_rows(d_embedded_low, 0, routes.room))
     d_small = jnp.concatenate(
         [
             jnp.sum(d_embedded.reshape(own, seq_len, width), 0),
@@ -1208,12 +1215,12 @@
     )
     partials = [d_out, d_turn] + d_qkv + [chip_half(d_small.T)]
     pieces = [(i, 0, deep) for i in range(6)]
-    (own_out, own_turn, own_q, own_k, own_v, own_small), arrived, up_blocks = sum_chips(
-        partials, pieces, sizes, ids[9], send, up_blocks
+    (own_out, own_turn, own_q, own_k, own_v, own_small), up_blocks = sum_chips(
+        partials, pieces, sizes, ids[9], up_blocks
     )
     own_qkv = jnp.concatenate([own_q, own_k, own_v], 1)
     own_up = up_blocks.swapaxes(0, 1).reshape(up_weight.shape).astype(jnp.float32)
-    d_word = d_word + routes.give(d_embedded_low, arrived.reshape(-1, width))
+    d_word = routes.give(d_embedded_low, arrived, lax.optimization_barrier(d_word))
     owned = (
         d_word,
         own_small[:, :seq_len].T,

time: 771 us -> 801 us (1.039)
  Pallas kernels: 464 us -> 407 us
  waiting for transfers between devices: 11.4 us -> 59.7 us
  starting transfers between devices: 21 us -> 42 us
  local copies, waits for them, and re-layouts: 35.1 us -> 46.7 us
  other arithmetic: 80.9 us -> 89.6 us
    ppermute x12 -> x9, waiting for transfers between devices: 11.4 us -> 59.7 us  [line_shift(): lax.ppermute(shard, 'dp', [(i, (i + step) % size) for i in range(size)])]
    pallas_call x4, Pallas kernels: 192 us -> 147 us  [reduce_all(): pl.pallas_call(functools.partial(reduce_kernel, sizes, tuple(pieces), cor...]
    ppermute x12 -> x9, starting transfers between devices: 19 us -> 36.2 us  [line_shift(): lax.ppermute(shard, 'dp', [(i, (i + step) % size) for i in range(size)])]
    pallas_call x4, Pallas kernels: 214 us -> 201 us  [gather_all(): pl.pallas_call(functools.partial(gather_kernel, sizes, tuple(pieces), rou...]
    unnamed x207 -> x243, local copies, waits for them, and re-layouts: 11.2 us -> 17.3 us
  transfers between devices with their start and end apart: 22 -> 20, of which waited for: 4 -> 3; matrix products, arithmetic and copies ran while one was open for 25% -> 28% of each run, Pallas kernels for 43% -> 48%
where the time goes in v3:
time: 801 us; the launch traced here: 792 us
  Pallas kernels  407 us (51%)
  matrix products  134 us (17%)
  other arithmetic  89.6 us (11%)
  waiting for transfers between devices  59.7 us (7%)
  local copies, waits for them, and re-layouts  46.7 us (6%)
  starting transfers between devices  42 us (5%)
  between operations  12.4 us (2%)
    pallas_call x4, Pallas kernels, gather_all(): pl.pallas_call(functools.partial(gather_kernel, sizes, tuple(pieces), rou...  201 us
    pallas_call x4, Pallas kernels, reduce_all(): pl.pallas_call(functools.partial(reduce_kernel, sizes, tuple(pieces), cor...  147 us
    ppermute x9, waiting for transfers between devices, line_shift(): lax.ppermute(shard, 'dp', [(i, (i + step) % size) for i in range(size)])  59.7 us
    dot_general x10, matrix products, matmul(): return jnp.dot(left, right, preferred_element_type=jnp.float32)  53 us
    dot_general x11, matrix products, left_transposed(): lax.dot_general(left, right, (((0,), (0,)), ((), ())), preferred_element_...  48.4 us
    ppermute x9, starting transfers between devices, line_shift(): lax.ppermute(shard, 'dp', [(i, (i + step) % size) for i in range(size)])  36.2 us
    dot_general x7, matrix products, right_transposed(): lax.dot_general(left, right, (((1,), (1,)), ((), ())), preferred_element_...  28.8 us
    sub x8, other arithmetic, adam_step(): weight - rate * (first_hat / (jnp.sqrt(second_hat) + epsilon) + weight_de...  17.3 us
  transfers between devices with their start and end apart: 20, of which 3 were waited for; matrix products, arithmetic and copies ran while one was open for 28% of the time, Pallas kernels for 48%

profile of v3, /device:TPU:0, one launch (start us, length us, event | category | flops | bytes accessed | tf_op | source)
XLA Modules:
  0.0 792.4 jit_solution(11919115165012065490)
XLA Ops:
  3.9 13.9 %shard_map.475 = (s32[32,2,640]{2,1,0:T(2,128)S(1)}, bf16[8,32,512]{2,1,0:T(8,128)(2,1)S(1)}) custom-call(s32[2,640]{1,0:T(2,128)S(1)} %fusion.221.row_ref, bf16[8,32,512]{2,1,0:T(8,128)(2,1)S(1)} %bitcast.311), custom_call_target="tpu_custom_call" | custom-call | tf_op jit(solution)/shard_map/pallas_call | solution.py:341
  32.9 5.5 fusion.38
  38.5 124.9 %shard_map.476 = (bf16[2,4,4,32,640]{4,3,2,1,0:T(8,128)(2,1)S(1)}, bf16[2,4,4,32,3072]{4,3,2,1,0:T(8,128)(2,1)S(1)}, bf16[2,4,4,32,1024]{4,3,2,1,0:T(8,128)(2,1)...) custom-call(bf16[32,640]{1,0:T(8,128)(2,1)S(1)} %maximum_maximum_fusion.refs_0_, ...), custom_call_target="tpu_custom_call" | custom-call | tf_op jit(solution)/shard_map/pallas_call | solution.py:591
  177.4 7.0 fusion.17
  198.2 8.5 %add_convert_fusion.k_ref.v_ref = bf16[1024,2048]{1,0:T(8,128)(2,1)} fusion(f32[2048]{0:T(1024)S(1)} %concatenate.60, bf16[1024,1024]{1,0:T(8,128)(2,1)S(1)} %copy-done.24, bf16[1024,3072]{1,0:T(8,128)(2,1)} %bitcast.323), kind=kOutput, calls=%fused_computation.33 | convolution fusion | flops 4299161600 | bytes 10493952 | tf_op jit(solution)/shard_map/dot_general | solution.py:32
  206.7 8.1 %shard_map.477 = bf16[128,1024]{1,0:T(8,128)(2,1)} custom-call(s32[2]{0:T(128)} %get-tuple-element.531.lengths_ref, bf16[128,1024]{1,0:T(8,128)(2,1)} %fusion.105.q_ref, bf16[1024,2048]{1,0:T(8,128)(2,1)} %add_convert_fusion.k_ref.v_ref, bf16[1024,2048]{1,0:T(8,128)(2,1)} %add_convert_fusion.k_ref.v_ref), custom_call_target="tpu_custom_call" | custom-call | tf_op jit(solution)/shard_map/pallas_call | solution.py:859
  220.7 15.2 %shard_map.478 = bf16[2,4,1,128,1024]{4,3,2,1,0:T(8,128)(2,1)S(1)} custom-call(bf16[128,1024]{1,0:T(8,128)(2,1)S(1)} %add_convert_fusion.4.refs_0_), custom_call_target="tpu_custom_call" | custom-call | tf_op jit(solution)/shard_map/pallas_call | solution.py:591
  251.0 8.3 %fusion.56 = (bf16[512,1024]{1,0:T(8,128)(2,1)}, f32[1024,512]{0,1:T(8,128)S(1)}) fusion(f32[512]{0:T(512)S(1)} %dynamic_slice.89, bf16[1024,1024]{1,0:T(8,128)(2,1)} %bitcast.301, bf16[1024,512]{1,0:T(8,128)(2,1)} %bitcast.344), kind=kOutput, calls=%fused_computation.102 | convolution fusion | flops 1108344832 | bytes 6293504 | tf_op jit(solution)/shard_map/dot_general | solution.py:32
  259.3 6.0 convolution_convert_fusion.2
  265.3 18.3 %shard_map.479 = f32[128,1024]{1,0:T(8,128)S(1)} custom-call(bf16[2,4,1,128,1024]{4,3,2,1,0:T(8,128)(2,1)S(1)} %bitcast.305), custom_call_target="tpu_custom_call" | custom-call | tf_op jit(solution)/shard_map/pallas_call | solution.py:775
  287.2 46.3 %shard_map.480 = bf16[2,4,4,128,1024]{4,3,2,1,0:T(8,128)(2,1)S(1)} custom-call(bf16[128,1024]{1,0:T(8,128)(2,1)S(1)} %add_convert_fusion.2.refs_0_), custom_call_target="tpu_custom_call" | custom-call | tf_op jit(solution)/shard_map/pallas_call | solution.py:591
  333.5 11.5 %fusion.13 = (f32[4096]{0:T(1024)S(1)}, f32[4096,960]{0,1:T(8,128)}) fusion(f32[960]{0:T(1024)S(1)} %pad_dynamic-slice_fusion, pred[960]{0:T(1024)(128)(4,1)S(1)} %broadcast_compare_fusion, bf16[4096,1024]{1,0:T(8,128)(2,1)S(1)} %bitcast.298, bf16[960,1024]{1,0:T(8,128)(2,1)S(1)} %copy-done.35), kind=kOutput, calls=%fused_computation.32 | convolution fusion | flops 8064856064 | bytes 26104512 | tf_op jit(solution)/shard_map/dot_general | solution.py:42
  345.0 10.0 %exponential_reduce_fusion = (f32[4096]{0:T(1024)S(1)}, f32[4096]{0:T(1024)S(1)}) fusion(f32[4096,960]{0,1:T(8,128)} %get-tuple-element.584, f32[4096]{0:T(1024)S(1)} %get-tuple-element.583, f32[960]{0:T(1024)S(1)} %pad_dynamic-slice_fusion, pred[960]{0:T(1024)(128)(4,1)S(1)} %broadcast_compare_fusion, s32[960]{0:T(1024)S(1)} %iota_add_fusion.2, ...), kind=kLoop, calls=%fused_computation.30 | loop fusion | flops 27516928 | bytes 15802816 | tf_op jit(solution)/shard_map/reduce_sum | solution.py:1124
  355.1 16.2 %shard_map.481 = f32[32,8,128]{2,1,0:T(8,128)S(1)} custom-call(f32[32,8,128]{2,1,0:T(8,128)S(1)} %pad.10.own_ref), custom_call_target="tpu_custom_call" | custom-call | tf_op jit(solution)/shard_map/pallas_call | solution.py:426
  371.9 8.6 %fusion.278 = (f32[960]{0:T(1024)S(1)}, bf16[4096,960]{0,1:T(8,128)(2,1)S(1)}) fusion(s32[960]{0:T(1024)S(1)} %iota_add_fusion.2, s32[4096]{0:T(1024)S(1)} %eq.236, f32[4096]{0:T(1024)S(1)} %bitcast.373, f32[4096]{0:T(1024)S(1)} %bitcast.374, f32[4096,960]{0,1:T(8,128)S(1)} %copy-done.16, f32[960]{0:T(1024)S(1)} %pad_dynamic-slice_fusion, ...), kind=kLoop, calls=%fused_computation.469 | loop fusion | flops 39320640 | bytes 23670976 | tf_op jit(solution)/shard_map/reduce_sum | solution.py:1132
  380.6 11.5 %convolution_convert_fusion = bf16[4096,1024]{1,0:T(8,128)(2,1)} fusion(bf16[960,1024]{1,0:T(8,128)(2,1)S(1)} %copy-done.35, bf16[4096,960]{0,1:T(8,128)(2,1)S(1)} %get-tuple-element.521), kind=kOutput, calls=%fused_computation.34 | convolution fusion | flops 8057257984 | bytes 18219008 | tf_op jit(solution)/shard_map/dot_general | solution.py:32
  392.1 48.4 %shard_map.482 = f32[128,1024]{1,0:T(8,128)S(1)} custom-call(bf16[2,4,4,128,1024]{4,3,2,1,0:T(8,128)(2,1)} %bitcast.335), custom_call_target="tpu_custom_call" | custom-call | tf_op jit(solution)/shard_map/pallas_call | solution.py:775
  445.2 14.5 %shard_map.483 = bf16[2,4,1,128,1024]{4,3,2,1,0:T(8,128)(2,1)S(1)} custom-call(bf16[128,1024]{1,0:T(8,128)(2,1)S(1)} %get-tuple-element.513.refs_0_), custom_call_target="tpu_custom_call" | custom-call | tf_op jit(solution)/shard_map/pallas_call | solution.py:591
  469.6 15.0 %shard_map.484 = f32[128,1024]{1,0:T(8,128)S(1)} custom-call(bf16[2,4,1,128,1024]{4,3,2,1,0:T(8,128)(2,1)S(1)} %bitcast.304), custom_call_target="tpu_custom_call" | custom-call | tf_op jit(solution)/shard_map/pallas_call | solution.py:775
  486.7 11.5 %shard_map.485 = (bf16[128,1024]{1,0:T(8,128)(2,1)}, bf16[1024,1024]{1,0:T(8,128)(2,1)}, bf16[1024,1024]{1,0:T(8,128)(2,1)}) custom-call(s32[2]{0:T(128)} %get-tuple-element.531.lengths_ref, bf16[128,1024]{1,0:T(8,128)(2,1)} %fusion.105.q_ref, bf16[1024,2048]{1,0:T(8,128)(2,1)} %add_convert_fusion.k_ref.v_ref, ...), custom_call_target="tpu_custom_call" | custom-call | tf_op jit(solution)/shard_map/pallas_call | solution.py:866
  503.0 8.8 %multiply_reduce_fusion = (bf16[1024]{0:T(1024)(128)(2,1)S(1)}, f32[1024]{0:T(1024)S(1)}, f32[1024]{0:T(1024)S(1)}, bf16[1024]{0:T(1024)(128)(2,1)S(1)}, f32[1024,1024]{1,0:T(8,128)S(1)}) fusion(f32[1024,1024]{1,0:T(8,128)S(1)} %copy-done.15, f32[1024]{0:T(1024)S(1)} %copy-done.82, f32[1024]{0:T(1024)S(1)} %broadcast_multiply_fusion.2, ...), kind=kOutput, calls=%fused_computation.59 | convolution fusion | flops 4313837568 | bytes 20996096 | tf_op jit(solution)/shard_map/dot_general | solution.py:42
  516.7 6.6 fusion.37
  537.9 50.9 %collective-permute-done.13 = bf16[8,32,512]{2,1,0:T(8,128)(2,1)} collective-permute-done((bf16[8,32,512]{2,1,0:T(8,128)(2,1)S(1)}, bf16[8,32,512]{2,1,0:T(8,128)(2,1)}, u32[]{:S(2)}, u32[]{:S(2)}) %collective-permute-start.13) | collective-permute-done | bytes 262176 | tf_op jit(solution)/shard_map/ppermute | solution.py:928
  588.8 14.2 %fusion.35 = f32[960,1024]{1,0:T(8,128)} fusion(bf16[4096,1024]{1,0:T(8,128)(2,1)} %bitcast.299, bf16[4096,960]{0,1:T(8,128)(2,1)} %copy-done.26), kind=kOutput, calls=%fused_computation.77 | convolution fusion | flops 8053063680 | bytes 20185088 | tf_op jit(solution)/shard_map/dot_general | solution.py:36
  615.8 5.7 collective-permute-done.15
  625.1 25.1 %collective-permute-start.18 = (bf16[128,1024]{1,0:T(8,128)(2,1)S(1)}, bf16[128,1024]{1,0:T(8,128)(2,1)S(1)}, u32[]{:S(2)}, u32[]{:S(2)}) collective-permute-start(bf16[128,1024]{1,0:T(8,128)(2,1)S(1)} %copy-done.64), channel_id=1, source_target_pairs={{0,3},{1,0},{2,1},{3,2},{4,7},{5,4},{6,5},{7,6},{8,11},{9,8},{10,9... | collective-permute-start | bytes 786440 | tf_op jit(solution)/shard_map/ppermute | solution.py:928
  661.2 6.3 fusion.91
  667.5 5.0 fusion.94
  672.5 65.4 %shard_map.486 = (f32[32,1024]{1,0:T(8,128)S(1)}, f32[32,1024]{1,0:T(8,128)S(1)}, f32[32,1024]{1,0:T(8,128)S(1)}, f32[32,1024]{1,0:T(8,128)S(1)}, f32[32,1024]{1...) custom-call(bf16[4,4,32,1024]{3,2,1,0:T(8,128)(2,1)S(1)} %bitcast.314, ...), custom_call_target="tpu_custom_call" | custom-call | tf_op jit(solution)/shard_map/pallas_call | solution.py:775
  741.4 7.7 fusion.83
  758.5 9.4 %shard_map.487 = f32[32,8,128]{2,1,0:T(8,128)S(1)} custom-call(f32[8,128]{1,0:T(8,128)S(1)} %maximum_bitcast_fusion.1.row_ref), custom_call_target="tpu_custom_call" | custom-call | tf_op jit(solution)/shard_map/pallas_call | solution.py:385
  777.6 8.5 %multiply_subtract_fusion = (f32[960,1024]{1,0:T(8,128)}, f32[960,1024]{1,0:T(8,128)}, f32[960,1024]{1,0:T(8,128)}) fusion(f32[960,1024]{1,0:T(8,128)} %param.36, f32[960,1024]{1,0:T(8,128)S(1)} %copy-done.13, f32[]{:T(128)S(6)} %div.275, f32[960,1024]{1,0:T(8,128)} %param.37, f32[960,1024]{1,0:T(8,128)} %param.38), kind=kLoop, calls=%fused_computation.73 | loop fusion | flops 15728640 | bytes 27525124 | tf_op jit(solution)/shard_map/sub | solution.py:982
  (461 shorter events, 157.1 us)
Async XLA Ops:
  0.7 188.3 %copy-start = (s32[4,64]{1,0:T(4,128)S(1)}, s32[4,64]{1,0:T(4,128)}, u32[]{:S(2)}) copy-start(s32[4,64]{1,0:T(4,128)} %param.34) | copy-start | bytes 3076
  18.9 225.6 %collective-permute-start = (bf16[512,512]{1,0:T(8,128)(2,1)}, bf16[512,512]{1,0:T(8,128)(2,1)}, u32[]{:S(2)}, u32[]{:S(2)}) collective-permute-start(bf16[512,512]{1,0:T(8,128)(2,1)} %get-tuple-element.547), channel_id=1, source_target_pairs={{0,1},{1,2},{2,3},{3,0},{4,5},{5,6},{6,7},{7,4},{8,9},{9,10},{10,1... | collective-permute-start | bytes 1572872 | tf_op jit(solution)/shard_map/ppermute | solution.py:928
  19.4 225.0 %collective-permute-start.1 = (bf16[512,512]{1,0:T(8,128)(2,1)}, bf16[512,512]{1,0:T(8,128)(2,1)}, u32[]{:S(2)}, u32[]{:S(2)}) collective-permute-start(bf16[512,512]{1,0:T(8,128)(2,1)} %get-tuple-element.547), channel_id=1, source_target_pairs={{0,2},{1,3},{2,0},{3,1},{4,6},{5,7},{6,4},{7,5},{8,10},{9,11},{10,... | collective-permute-start | bytes 1572872 | tf_op jit(solution)/shard_map/ppermute | solution.py:928
  20.5 224.0 %collective-permute-start.2 = (bf16[512,512]{1,0:T(8,128)(2,1)}, bf16[512,512]{1,0:T(8,128)(2,1)}, u32[]{:S(2)}, u32[]{:S(2)}) collective-permute-start(bf16[512,512]{1,0:T(8,128)(2,1)} %get-tuple-element.547), channel_id=1, source_target_pairs={{0,3},{1,0},{2,1},{3,2},{4,7},{5,4},{6,5},{7,6},{8,11},{9,8},{10,9... | collective-permute-start | bytes 1572872 | tf_op jit(solution)/shard_map/ppermute | solution.py:928
  195.1 337.8 %collective-permute-start.7 = (bf16[128,512]{1,0:T(8,128)(2,1)}, bf16[128,512]{1,0:T(8,128)(2,1)}, u32[]{:S(2)}, u32[]{:S(2)}) collective-permute-start(bf16[128,512]{1,0:T(8,128)(2,1)} %get-tuple-element.549), channel_id=1, source_target_pairs={{0,16},{16,0},{1,17},{17,1},{2,18},{18,2},{3,19},{19,3},{4,20},{20... | collective-permute-start | bytes 393224 | tf_op jit(solution)/shard_map/ppermute | solution.py:160
  216.5 317.9 %collective-permute-start.3 = (bf16[128,512]{1,0:T(8,128)(2,1)}, bf16[128,512]{1,0:T(8,128)(2,1)}, u32[]{:S(2)}, u32[]{:S(2)}) collective-permute-start(bf16[128,512]{1,0:T(8,128)(2,1)} %get-tuple-element.553), channel_id=1, source_target_pairs={{0,16},{16,0},{1,17},{17,1},{2,18},{18,2},{3,19},{19,3},{4,20},{20... | collective-permute-start | bytes 393224 | tf_op jit(solution)/shard_map/ppermute | solution.py:160
  287.2 46.3 %copy-start.35 = (bf16[960,1024]{1,0:T(8,128)(2,1)S(1)}, bf16[960,1024]{1,0:T(8,128)(2,1)}, u32[]{:S(2)}) copy-start(bf16[960,1024]{1,0:T(8,128)(2,1)} %get-tuple-element.769) | copy-start | bytes 5898244
  345.0 26.9 %copy-start.16 = (f32[4096,960]{0,1:T(8,128)S(1)}, f32[4096,960]{0,1:T(8,128)}, u32[]{:S(2)}) copy-start(f32[4096,960]{0,1:T(8,128)} %get-tuple-element.584) | copy-start | bytes 47185924
  462.9 72.1 %collective-permute-start.16 = (bf16[128,1024]{1,0:T(8,128)(2,1)}, bf16[128,1024]{1,0:T(8,128)(2,1)}, u32[]{:S(2)}, u32[]{:S(2)}) collective-permute-start(bf16[128,1024]{1,0:T(8,128)(2,1)} %get-tuple-element.540), channel_id=1, source_target_pairs={{0,1},{1,2},{2,3},{3,0},{4,5},{5,6},{6,7},{7,4},{8,9},{9,10},{10,1... | collective-permute-start | bytes 786440 | tf_op jit(solution)/shard_map/ppermute | solution.py:928
  463.8 71.6 %collective-permute-start.17 = (bf16[128,1024]{1,0:T(8,128)(2,1)S(1)}, bf16[128,1024]{1,0:T(8,128)(2,1)}, u32[]{:S(2)}, u32[]{:S(2)}) collective-permute-start(bf16[128,1024]{1,0:T(8,128)(2,1)S(1)} %get-tuple-element.542), channel_id=1, source_target_pairs={{0,2},{1,3},{2,0},{3,1},{4,6},{5,7},{6,4},{7,5},{8,10},{9,11},{10,... | collective-permute-start | bytes 786440 | tf_op jit(solution)/shard_map/ppermute | solution.py:928
  523.2 218.1 %all-to-all-start.2 = ((bf16[32,48,1024]{2,1,0:T(8,128)(2,1)}), bf16[32,48,1024]{2,1,0:T(8,128)(2,1)}, u32[]{:S(2)}, u32[]{:S(2)}) async-start(bf16[32,48,1024]{2,1,0:T(8,128)(2,1)} %bitcast.340), calls=%async_computation.2 | async-start | bytes 6291456 | tf_op jit(solution)/shard_map/all_to_all | solution.py:129
  530.4 58.4 %collective-permute-start.13 = (bf16[8,32,512]{2,1,0:T(8,128)(2,1)S(1)}, bf16[8,32,512]{2,1,0:T(8,128)(2,1)}, u32[]{:S(2)}, u32[]{:S(2)}) collective-permute-start(bf16[8,32,512]{2,1,0:T(8,128)(2,1)S(1)} %get-tuple-element.543), channel_id=1, source_target_pairs={{0,1},{1,2},{2,3},{3,0},{4,5},{5,6},{6,7},{7,4},{8,9},{9,10},{10,1... | collective-permute-start | bytes 786440 | tf_op jit(solution)/shard_map/ppermute | solution.py:928
  532.8 2.1 collective-permute-start.5
  534.4 126.8 %collective-permute-start.11 = (bf16[1024,1024]{1,0:T(8,128)(2,1)}, bf16[1024,1024]{1,0:T(8,128)(2,1)}, u32[]{:S(2)}, u32[]{:S(2)}) collective-permute-start(bf16[1024,1024]{1,0:T(8,128)(2,1)} %get-tuple-element.261), channel_id=1, source_target_pairs={{0,16},{16,0},{1,17},{17,1},{2,18},{18,2},{3,19},{19,3},{4,20},{20... | collective-permute-start | bytes 6291464 | tf_op jit(solution)/shard_map/ppermute | solution.py:160
  534.9 53.9 %copy-start.106 = (bf16[128,512]{1,0:T(8,128)(2,1)}, bf16[128,512]{1,0:T(8,128)(2,1)S(1)}, u32[]{:S(2)}) copy-start(bf16[128,512]{1,0:T(8,128)(2,1)S(1)} %collective-permute-done.5) | copy-start | bytes 393220
  534.9 132.6 %collective-permute-start.10 = (bf16[1024,1024]{1,0:T(8,128)(2,1)}, bf16[1024,1024]{1,0:T(8,128)(2,1)}, u32[]{:S(2)}, u32[]{:S(2)}) collective-permute-start(bf16[1024,1024]{1,0:T(8,128)(2,1)} %get-tuple-element.260), channel_id=1, source_target_pairs={{0,16},{16,0},{1,17},{17,1},{2,18},{18,2},{3,19},{19,3},{4,20},{20... | collective-permute-start | bytes 6291464 | tf_op jit(solution)/shard_map/ppermute | solution.py:160
  535.0 86.5 %collective-permute-start.8 = (bf16[128,1024]{1,0:T(8,128)(2,1)}, bf16[128,1024]{1,0:T(8,128)(2,1)}, u32[]{:S(2)}, u32[]{:S(2)}) collective-permute-start(bf16[128,1024]{1,0:T(8,128)(2,1)} %get-tuple-element.262), channel_id=1, source_target_pairs={{0,16},{16,0},{1,17},{17,1},{2,18},{18,2},{3,19},{19,3},{4,20},{20... | collective-permute-start | bytes 786440 | tf_op jit(solution)/shard_map/ppermute | solution.py:160
  535.4 80.2 %collective-permute-start.14 = (bf16[8,32,512]{2,1,0:T(8,128)(2,1)}, bf16[8,32,512]{2,1,0:T(8,128)(2,1)S(1)}, u32[]{:S(2)}, u32[]{:S(2)}) collective-permute-start(bf16[8,32,512]{2,1,0:T(8,128)(2,1)} %get-tuple-element.545), channel_id=1, source_target_pairs={{0,2},{1,3},{2,0},{3,1},{4,6},{5,7},{6,4},{7,5},{8,10},{9,11},{10,... | collective-permute-start | bytes 786440 | tf_op jit(solution)/shard_map/ppermute | solution.py:928
  588.8 32.7 %collective-permute-start.15 = (bf16[8,32,512]{2,1,0:T(8,128)(2,1)}, bf16[8,32,512]{2,1,0:T(8,128)(2,1)}, u32[]{:S(2)}, u32[]{:S(2)}) collective-permute-start(bf16[8,32,512]{2,1,0:T(8,128)(2,1)} %get-tuple-element.544), channel_id=1, source_target_pairs={{0,3},{1,0},{2,1},{3,2},{4,7},{5,4},{6,5},{7,6},{8,11},{9,8},{10,9... | collective-permute-start | bytes 786440 | tf_op jit(solution)/shard_map/ppermute | solution.py:928
  615.7 8.9 %collective-permute-start.6 = (bf16[128,1024]{1,0:T(8,128)(2,1)S(1)}, bf16[128,1024]{1,0:T(8,128)(2,1)S(1)}, u32[]{:S(2)}, u32[]{:S(2)}) collective-permute-start(bf16[128,1024]{1,0:T(8,128)(2,1)S(1)} %copy-done.49), channel_id=1, source_target_pairs={{0,16},{16,0},{1,17},{17,1},{2,18},{18,2},{3,19},{19,3},{4,20},{20... | collective-permute-start | bytes 786440 | tf_op jit(solution)/shard_map/ppermute | solution.py:160
  615.8 34.5 %copy-start.70 = (bf16[128,512]{1,0:T(8,128)(2,1)S(1)}, bf16[128,512]{1,0:T(8,128)(2,1)}, u32[]{:S(2)}) copy-start(bf16[128,512]{1,0:T(8,128)(2,1)} %get-tuple-element.552) | copy-start | bytes 393220
  621.5 39.6 %collective-permute-start.9 = (bf16[1024,512]{1,0:T(8,128)(2,1)}, bf16[1024,512]{1,0:T(8,128)(2,1)}, u32[]{:S(2)}, u32[]{:S(2)}) collective-permute-start(bf16[1024,512]{1,0:T(8,128)(2,1)} %get-tuple-element.533), channel_id=1, source_target_pairs={{0,16},{16,0},{1,17},{17,1},{2,18},{18,2},{3,19},{19,3},{4,20},{20... | collective-permute-start | bytes 3145736 | tf_op jit(solution)/shard_map/ppermute | solution.py:160
  621.5 3.6 collective-permute-start.4
  624.6 34.1 %collective-permute-start.12 = (bf16[512,640]{0,1:T(8,128)(2,1)S(1)}, bf16[512,640]{0,1:T(8,128)(2,1)S(1)}, u32[]{:S(2)}, u32[]{:S(2)}) collective-permute-start(bf16[512,640]{0,1:T(8,128)(2,1)S(1)} %dynamic-slice_bitcast_fusion), channel_id=1, source_target_pairs={{0,16},{16,0},{1,17},{17,1},{2,18},{18,2},{3,19},{19,3},{4,20},{20... | collective-permute-start | bytes 1966088 | tf_op jit(solution)/shard_map/ppermute | solution.py:160
  624.7 27.1 %copy-start.66 = (bf16[8,32,512]{2,1,0:T(8,128)(2,1)S(1)}, bf16[8,32,512]{2,1,0:T(8,128)(2,1)}, u32[]{:S(2)}) copy-start(bf16[8,32,512]{2,1,0:T(8,128)(2,1)} %copy-done.65) | copy-start | bytes 786436
  625.1 30.9 %collective-permute-start.18 = (bf16[128,1024]{1,0:T(8,128)(2,1)S(1)}, bf16[128,1024]{1,0:T(8,128)(2,1)S(1)}, u32[]{:S(2)}, u32[]{:S(2)}) collective-permute-start(bf16[128,1024]{1,0:T(8,128)(2,1)S(1)} %copy-done.64), channel_id=1, source_target_pairs={{0,3},{1,0},{2,1},{3,2},{4,7},{5,4},{6,5},{7,6},{8,11},{9,8},{10,9... | collective-permute-start | bytes 786440 | tf_op jit(solution)/shard_map/ppermute | solution.py:928
  672.5 68.9 %copy-start.96 = (s32[1536]{0:T(1024)S(1)}, s32[1536]{0:T(1024)}, u32[]{:S(2)}) copy-start(s32[1536]{0:T(1024)} %copy-done.95) | copy-start | bytes 18436
  749.3 20.9 %copy-start.10 = (f32[32,640]{1,0:T(8,128)S(1)}, f32[32,640]{1,0:T(8,128)}, u32[]{:S(2)}) copy-start(f32[32,640]{1,0:T(8,128)} %copy-done.9) | copy-start | bytes 245764
  749.3 20.9 %copy-start.75 = (f32[19,32]{0,1:T(8,128)S(1)}, f32[19,32]{0,1:T(8,128)}, u32[]{:S(2)}) copy-start(f32[19,32]{0,1:T(8,128)} %copy.211) | copy-start | bytes 7300
  749.3 20.9 %copy-start.76 = (f32[19,32]{0,1:T(8,128)S(1)}, f32[19,32]{0,1:T(8,128)}, u32[]{:S(2)}) copy-start(f32[19,32]{0,1:T(8,128)} %copy.207) | copy-start | bytes 7300
  749.4 20.9 %copy-start.77 = (f32[19,32]{0,1:T(8,128)S(1)}, f32[19,32]{0,1:T(8,128)}, u32[]{:S(2)}) copy-start(f32[19,32]{0,1:T(8,128)} %copy.209) | copy-start | bytes 7300
  753.1 19.2 %copy-start.47 = (f32[2,32,1024]{2,1,0:T(8,128)S(1)}, f32[2,32,1024]{2,1,0:T(8,128)}, u32[]{:S(2)}) copy-start(f32[2,32,1024]{2,1,0:T(8,128)} %param.45) | copy-start | bytes 786436
  (100 other events, 578.0 us)

commit v4 on v3

--- a/solution.py
+++ b/solution.py
@@ -169,10 +169,13 @@
     return lax.dynamic_slice_in_dim(rows, index * half, half, 1)
 
 
+def both_halves(rows):
+    pipe = lax.axis_index("pipe")
+    return jnp.concatenate([half_columns(rows, pipe), swapped(half_columns(rows, 1 - pipe))], 0)
+
+
 def chip_sum(left, right):
-    pipe = lax.axis_index("pipe")
-    left = jnp.concatenate([half_columns(left, pipe), swapped(half_columns(left, 1 - pipe))], 0)
-    return left_transposed(left, both_cores(right)).astype(jnp.bfloat16)
+    return left_transposed(both_halves(left), both_cores(right)).astype(jnp.bfloat16)
 
 
 def chip_half(partial):
@@ -607,187 +610,348 @@
     )(*operands)
 
 
-def reduce_kernel(sizes, pieces, cores, swaps, *refs):
-    arrays, total = max(piece[0] for piece in pieces) + 1, len(pieces)
-    partials, refs = refs[:arrays], refs[arrays:]
-    if swaps:
-        blocks_ref, refs = refs[0], refs[1:]
-    sums, refs = refs[:arrays], refs[arrays:]
-    if swaps:
-        blocks_arrived_ref, refs = refs[0], refs[1:]
-    chips, refs = refs[: total if cores else 0], refs[total if cores else 0 :]
-    others, refs = refs[: total if cores else 0], refs[total if cores else 0 :]
-    mine, refs = refs[:total], refs[total:]
-    planes, refs = refs[:total], refs[total:]
-    lines, refs = refs[:total], refs[total:]
-    send, arrive, own, plane_send, plane_arrive, plane_own = refs
-    place = Place(sizes)
-    pipe, grp, dp = place.pipe, place.grp, place.dp
-    near = place.beside * (1 - pipe) + place.below * pipe
-    far = place.below * (1 - pipe) + place.beside * pipe
-    core = (1 - pipe, grp, dp)
-    hops = place.dps - 1
+class Sums:
     block = 16
-    to_greet = [(pipe, grp, place.line(k + 1)) for k in range(hops)]
-    if swaps:
-        to_greet += [ahead + (dp,) for ahead, _ in place.plane()]
-    else:
-        to_greet += [(pipe, near, dp), (pipe, far, dp)] + ([core] if cores else [])
-    greet(to_greet)
-    copies = {}
-
-    def launch(n, index, source, target, to):
-        copies[n, index] = remote(source, target, send.at[n, index], arrive.at[n, index], to)
-        copies[n, index].start()
-
-    def blocks(n, body):
-        deep = pieces[n][2] // block
+
+    def __init__(self, place, sources, chips, others, mine, planes, lines, send, arrive, own, store):
+        self.place, self.sources, self.chips, self.others = place, sources, chips, others
+        self.mine, self.planes, self.lines = mine, planes, lines
+        self.send, self.arrive, self.own, self.store = send, arrive, own, store
+        pipe, grp, dp = place.pipe, place.grp, place.dp
+        self.near = place.beside * (1 - pipe) + place.below * pipe
+        self.far = place.below * (1 - pipe) + place.beside * pipe
+        self.copies, self.kept = {}, {}
+
+    def launch(self, n, index, source, target, to):
+        copy = remote(source, target, self.send.at[n, index], self.arrive.at[n, index], to)
+        self.copies[n, index] = copy
+        copy.start()
+
+    def keep(self, n, index, source, target):
+        self.kept[n, index] = pltpu.make_async_copy(source, target, self.own.at[n, index])
+        self.kept[n, index].start()
+
+    def blocks(self, n, body):
+        deep = self.mine[n].shape[2] // self.block
 
         def one(i, _):
-            at = pl.ds(pl.multiple_of(i % deep * block, block), block)
-            body(i // deep, at)
+            body(i // deep, pl.ds(pl.multiple_of(i % deep * self.block, self.block), self.block))
             return 0
 
-        lax.fori_loop(0, place.dps * deep, one, 0)
-
-    def to_core(n):
-        array, first, rows = pieces[n]
-        if cores:
-            part = partials[array].at[1 - pipe, :, :, pl.ds(first, rows)]
-            launch(n, 0, part, others[n], core)
-            part = partials[array].at[pipe, :, :, pl.ds(first, rows)]
-            copies[n, "own"] = pltpu.make_async_copy(part, chips[n], own.at[n, 0])
-            copies[n, "own"].start()
-
-    def to_near(n):
-        array, first, rows = pieces[n]
-        if cores:
-            copies[n, "own"].wait()
-            copies[n, 0].wait_recv()
+        lax.fori_loop(0, self.place.dps * deep, one, 0)
+
+    def to_core(self, n):
+        place = self.place
+        if self.chips[n] is not None:
+            core = (1 - place.pipe, place.grp, place.dp)
+            self.launch(n, 0, self.sources[n].at[1 - place.pipe], self.others[n], core)
+            self.keep(n, 0, self.sources[n].at[place.pipe], self.chips[n])
+
+    def to_near(self, n):
+        place, chip, other = self.place, self.chips[n], self.others[n]
+        part = self.sources[n]
+        if chip is not None:
+            self.kept[n, 0].wait()
+            self.copies[n, 0].wait_recv()
             for g in range(place.grps):
 
                 def add(d, at, g=g):
-                    left = chips[n][g, d, at].astype(jnp.float32)
-                    chips[n][g, d, at] = (left + others[n][g, d, at].astype(jnp.float32)).astype(
+                    left = chip[g, d, at].astype(jnp.float32)
+                    chip[g, d, at] = (left + other[g, d, at].astype(jnp.float32)).astype(
                         jnp.bfloat16
                     )
 
-                blocks(n, add)
-            part = lambda g: chips[n].at[g]
+                self.blocks(n, add)
+            part = chip
         else:
-            part = lambda g: partials[array].at[g, :, pl.ds(first, rows)]
-            for j, g in enumerate((far, grp)):
-                copies[n, "own", j] = pltpu.make_async_copy(part(g), mine[n].at[j], own.at[n, j])
-                copies[n, "own", j].start()
-        launch(n, 1, part(near), planes[n].at[1], (pipe, near, dp))
-        launch(n, 2, part(place.across), planes[n].at[0], (pipe, near, dp))
-
-    def to_far(n):
-        if not cores:
-            copies[n, "own", 0].wait()
-            copies[n, "own", 1].wait()
-        copies[n, 1].wait_recv()
-        copies[n, 2].wait_recv()
-        for j, g in enumerate((far, grp)):
+            for j, g in enumerate((self.far, place.grp)):
+                self.keep(n, j, part.at[g], self.mine[n].at[j])
+        to = (place.pipe, self.near, place.dp)
+        self.launch(n, 1, part.at[self.near], self.planes[n].at[1], to)
+        self.launch(n, 2, part.at[place.across], self.planes[n].at[0], to)
+
+    def to_far(self, n):
+        place, mine, plane, chip = self.place, self.mine[n], self.planes[n], self.chips[n]
+        if chip is None:
+            self.kept[n, 0].wait()
+            self.kept[n, 1].wait()
+        self.copies[n, 1].wait_recv()
+        self.copies[n, 2].wait_recv()
+        for j, g in enumerate((self.far, place.grp)):
 
             def add(d, at, j=j, g=g):
-                left = chips[n][g, d, at] if cores else mine[n][j, d, at]
-                right = planes[n][j, d, at].astype(jnp.float32)
-                mine[n][j, d, at] = (left.astype(jnp.float32) + right).astype(jnp.bfloat16)
-
-            blocks(n, add)
+                left = mine[j, d, at] if chip is None else chip[g, d, at]
+                total = left.astype(jnp.float32) + plane[j, d, at].astype(jnp.float32)
+                mine[j, d, at] = total.astype(jnp.bfloat16)
+
+            self.blocks(n, add)
             if j == 0:
-                launch(n, 3, mine[n].at[0], planes[n].at[2], (pipe, far, dp))
-
-    def to_lines(n):
-        copies[n, 3].wait_recv()
+                self.launch(n, 3, mine.at[0], plane.at[2], (place.pipe, self.far, place.dp))
+
+    def to_lines(self, n):
+        place, mine, plane = self.place, self.mine[n], self.planes[n]
+        self.copies[n, 3].wait_recv()
+        hops = place.dps - 1
 
         def add(d, at):
-            left = mine[n][1, d, at].astype(jnp.float32)
-            mine[n][1, d, at] = (left + planes[n][2, d, at].astype(jnp.float32)).astype(
-                jnp.bfloat16
-            )
-
-        def add_last(d, at):
-            array, first, rows = pieces[n]
-            left = mine[n][1, d, at].astype(jnp.float32)
-            to = pl.ds(pl.multiple_of(first + at.start, block), block)
-            sums[array][to] = left + planes[n][2, d, at].astype(jnp.float32)
-
-        if hops == 0:
-            blocks(n, add_last)
-            return
-        blocks(n, add)
+            total = mine[1, d, at].astype(jnp.float32) + plane[2, d, at].astype(jnp.float32)
+            if hops:
+                mine[1, d, at] = total.astype(jnp.bfloat16)
+            else:
+                self.store(n, at, total)
+
+        self.blocks(n, add)
         for k in range(hops):
             to = place.line(k + 1)
-            launch(n, 4 + k, mine[n].at[1, to], lines[n].at[k], (pipe, grp, to))
-
-    def to_sum(n):
-        array, first, rows = pieces[n]
-        for k in range(hops):
-            copies[n, 4 + k].wait_recv()
+            self.launch(
+                n, 4 + k, mine.at[1, to], self.lines[n].at[k], (place.pipe, place.grp, to)
+            )
+
+    def to_sum(self, n):
+        place, mine, lines = self.place, self.mine[n], self.lines[n]
+        for k in range(place.dps - 1):
+            self.copies[n, 4 + k].wait_recv()
 
         def add(i, _):
-            at = pl.ds(pl.multiple_of(i * block, block), block)
-            total = mine[n][1, place.spot, at].astype(jnp.float32)
-            for k in range(hops):
-                total = total + lines[n][k, at].astype(jnp.float32)
-            sums[array][pl.ds(pl.multiple_of(first + i * block, block), block)] = total
+            at = pl.ds(pl.multiple_of(i * self.block, self.block), self.block)
+            total = mine[1, place.spot, at].astype(jnp.float32)
+            for k in range(place.dps - 1):
+                total = total + lines[k, at].astype(jnp.float32)
+            self.store(n, at, total)
             return 0
 
-        lax.fori_loop(0, rows // block, add, 0)
-
-    stages = ([to_core] if cores else []) + [to_near, to_far, to_lines]
-    stages += [to_sum] if hops else []
+        lax.fori_loop(0, mine.shape[2] // self.block, add, 0)
+
+    def settle(self):
+        for copy in self.copies.values():
+            copy.wait_send()
+
+
+def sum_scratch(shapes, cores, sizes):
+    low = jnp.bfloat16
+    _, grps, dps = sizes
+    wide = [(dps,) + shape for shape in shapes]
+    chips = [pltpu.VMEM((grps,) + shape, low) for shape, core in zip(wide, cores) if core]
+    scratch = chips + chips
+    scratch += [pltpu.VMEM((2,) + shape, low) for shape in wide]
+    scratch += [pltpu.VMEM((3,) + shape, low) for shape in wide]
+    scratch += [pltpu.VMEM((max(dps - 1, 1),) + shape, low) for shape in shapes]
+    sems = pltpu.SemaphoreType.DMA((len(shapes), 4 + dps - 1))
+    return scratch + [sems, sems, pltpu.SemaphoreType.DMA((len(shapes), 2))]
+
+
+def sum_refs(refs, cores):
+    total = len(cores)
+
+    def spread_out(found):
+        found = iter(found)
+        return [next(found) if core else None for core in cores]
+
+    chosen = sum(cores)
+    groups = []
+    for count in (chosen, chosen, total, total, total):
+        groups.append(refs[:count])
+        refs = refs[count:]
+    chips, others, mine, planes, lines = groups
+    return (spread_out(chips), spread_out(others), mine, planes, lines) + tuple(refs[:3]), refs[3:]
+
+
+def reduce_kernel(sizes, pieces, *refs):
+    partial, out, refs = refs[0], refs[1], refs[2:]
+    place = Place(sizes)
+    scratch, _ = sum_refs(refs, (True,) * len(pieces))
+
+    def store(n, at, total):
+        to = pl.multiple_of(pieces[n][0] + at.start, Sums.block)
+        out[pl.ds(to, Sums.block)] = total
+
+    sources = [partial.at[:, :, :, pl.ds(first, rows)] for first, rows in pieces]
+    sums = Sums(place, sources, *scratch, store)
+    line = [(place.pipe, place.grp, place.line(k + 1)) for k in range(place.dps - 1)]
+    near, far = [(place.pipe, grp, place.dp) for grp in (sums.near, sums.far)]
+    greet(line + [near, far, (1 - place.pipe, place.grp, place.dp)])
+    stages = [sums.to_core, sums.to_near, sums.to_far, sums.to_lines]
+    stages += [sums.to_sum] if place.dps > 1 else []
+    total = len(pieces)
     for turn in range(total + len(stages) - 1):
         for at, stage in enumerate(stages):
             if 0 <= turn - at < total:
                 stage(turn - at)
-        if turn == 0 and swaps:
-            finish = swap_plane(
-                place, blocks_ref, blocks_arrived_ref, plane_send, plane_arrive, plane_own
-            )
-    for key, copy in copies.items():
-        if key[1] != "own":
-            copy.wait_send()
-    if swaps:
-        finish()
-
-
-def reduce_all(partials, pieces, sizes, collective, blocks=None, cores=False):
-    total = len(pieces)
-    swaps = blocks is not None
+    sums.settle()
+
+
+def reduce_all(partial, pieces, sizes, collective):
+    shapes = [(rows, partial.shape[-1]) for _, rows in pieces]
+    return pl.pallas_call(
+        functools.partial(reduce_kernel, sizes, tuple(pieces)),
+        out_shape=jax.ShapeDtypeStruct(partial.shape[-2:], jnp.float32),
+        in_specs=[pl.BlockSpec(memory_space=pl.ANY)],
+        out_specs=pl.BlockSpec(memory_space=pltpu.VMEM),
+        scratch_shapes=sum_scratch(shapes, (True,) * len(pieces), sizes),
+        compiler_params=pltpu.CompilerParams(
+            collective_id=collective, has_side_effects=True, vmem_limit_bytes=48 << 20
+        ),
+    )(partial)
+
+
+def finish_kernel(sizes, cut, *refs):
+    partials, refs = refs[:3], refs[3:]
+    start_ref, chosen_ref, grads, refs = refs[0], refs[1], refs[2:5], refs[5:]
+    logits_ref, normed_ref, rows_ref, blocks_ref, refs = refs[0], refs[1], refs[2], refs[3], refs[4:]
+    outs, refs = refs[:6], refs[6:]
+    word_ref, arrived_ref, blocks_arrived_ref, refs = refs[0], refs[1], refs[2], refs[3:]
+    cores = (False, False, True, False, False, False)
+    scratch, refs = sum_refs(refs, cores)
+    start, chosen, held, made, refs = refs[0], refs[1], refs[2:5], refs[5:8], refs[8:]
+    logits, normed, refs = refs[0], refs[1], refs[2:]
+    swap_send, swap_arrive, swap_own, plane_send, plane_arrive, plane_own = refs[:6]
+    load, word_load, core_send, core_arrive = refs[6:]
+    place = Place(sizes)
+    pipe, grp, dp = place.pipe, place.grp, place.dp
+    greet([ahead for ahead, _ in place.others()])
+
+    exchanged = []
+    for i in range(3):
+        pltpu.make_async_copy(grads[i], held[i].at[0], load.at[2 + i]).start()
+        exchanged.append(
+            remote(grads[i], held[i].at[1], core_send.at[i], core_arrive.at[i], (1 - pipe, grp, dp))
+        )
+        exchanged[-1].start()
+    pltpu.make_async_copy(start_ref, start, load.at[0]).start()
+    pltpu.make_async_copy(chosen_ref, chosen, load.at[1]).start()
+
+    def store(n, at, total):
+        outs[n][at] = total
+
+    sums = Sums(place, tuple(partials) + tuple(made), *scratch, store)
+    sums.to_core(2)
+    sums.to_near(0)
+    sums.to_near(1)
+    swap = swap_all(place, rows_ref, arrived_ref, swap_send, swap_arrive, swap_own)
+    plane_swap = swap_plane(
+        place, blocks_ref, blocks_arrived_ref, plane_send, plane_arrive, plane_own
+    )
+    sums.to_near(2)
+
+    steps = logits_ref.shape[0] // cut
+
+    def word_copies(step):
+        slot = step % 2
+        at = pl.ds(pl.multiple_of(step * cut, cut), cut)
+        return (
+            pltpu.make_async_copy(logits_ref.at[at], logits.at[slot], word_load.at[0, slot]),
+            pltpu.make_async_copy(normed_ref.at[at], normed.at[slot], word_load.at[1, slot]),
+        )
+
+    for copy in word_copies(0):
+        copy.start()
+
+    def word_steps(first, last):
+        def one(step, _):
+            @pl.when(step + 1 < steps)
+            def _():
+                for copy in word_copies(step + 1):
+                    copy.start()
+
+            for copy in word_copies(step):
+                copy.wait()
+            slot = step % 2
+            word_ref[...] += left_transposed(logits[slot], normed[slot])
+            return 0
+
+        lax.fori_loop(first, last, one, 0)
+
+    word_ref[...] = jnp.zeros_like(word_ref)
+
+    def form(i):
+        pltpu.make_async_copy(grads[i], held[i].at[0], load.at[2 + i]).wait()
+        exchanged[i].wait_recv()
+        if i == 0:
+            pltpu.make_async_copy(chosen_ref, chosen, load.at[1]).wait()
+        if i == 1:
+            pltpu.make_async_copy(start_ref, start, load.at[0]).wait()
+        left = chosen if i == 0 else start
+        right = held[i]
+        wide = left.shape[1] // place.grps
+        tokens = right.shape[1]
+
+        for g in range(place.grps):
+            at = pl.ds(g * wide, wide)
+            total = left_transposed(left[0:tokens, at], right[0])
+            total = total + left_transposed(left[tokens:, at], right[1])
+            made[i][g] = total.astype(jnp.bfloat16).reshape(made[i].shape[1:])
+
+    form(0)
+    sums.to_near(3)
+    sums.to_far(0)
+    form(1)
+    sums.to_near(4)
+    sums.to_far(1)
+    form(2)
+    sums.to_near(5)
+    sums.to_far(2)
+    sums.to_lines(0)
+    sums.to_lines(1)
+    word_steps(0, steps // 2)
+    sums.to_far(3)
+    sums.to_lines(2)
+    sums.to_far(4)
+    sums.to_lines(3)
+    sums.to_far(5)
+    sums.to_lines(4)
+    word_steps(steps // 2, steps)
+    sums.to_lines(5)
+    for n in range(6):
+        sums.to_sum(n)
+    sums.settle()
+    for copy in exchanged:
+        copy.wait_send()
+    plane_swap()
+    swap()
+
+
+def finish_all(partials, start, chosen, grads, logits, normed, rows, blocks, sizes, collective):
     low = jnp.bfloat16
+    parts = math.prod(sizes)
     _, grps, dps = sizes
-    shapes = [(dps, size, partials[array].shape[-1]) for array, _, size in pieces]
-    out_shape = [jax.ShapeDtypeStruct(partial.shape[-2:], jnp.float32) for partial in partials]
-    out_specs = [pl.BlockSpec(memory_space=pltpu.VMEM)] * len(partials)
-    if swaps:
-        out_shape.append(jax.ShapeDtypeStruct(blocks.shape, blocks.dtype))
-        out_specs.append(pl.BlockSpec(memory_space=pl.ANY))
-    operands = list(partials) + ([blocks] if swaps else [])
-    sems = pltpu.SemaphoreType.DMA((total, 4 + dps - 1))
+    shapes = [(partial.shape[-2], partial.shape[-1]) for partial in partials]
+    made = (grps, dps) + shapes[0]
+    shapes += [shapes[0]] * 3
+    cut = 512
+    anywhere = pl.BlockSpec(memory_space=pl.ANY)
+    near = pl.BlockSpec(memory_space=pltpu.VMEM)
+    swaps = pltpu.SemaphoreType.DMA((parts - 1,))
     plane_swaps = pltpu.SemaphoreType.DMA((sizes[0] * grps - 1,))
-    scratch = [pltpu.VMEM((grps,) + shape, low) for shape in shapes] * (2 if cores else 0)
-    scratch += [pltpu.VMEM((2,) + shape, low) for shape in shapes]
-    scratch += [pltpu.VMEM((3,) + shape, low) for shape in shapes]
-    scratch += [pltpu.VMEM((max(dps - 1, 1),) + shape[1:], low) for shape in shapes]
+    one = pltpu.SemaphoreType.DMA
+    operands = (*partials, start, chosen, *grads, logits, normed, rows, blocks)
+    out_shape = [jax.ShapeDtypeStruct(shape, jnp.float32) for shape in shapes]
+    out_shape += [jax.ShapeDtypeStruct((logits.shape[1], normed.shape[1]), jnp.float32)]
+    out_shape += [jax.ShapeDtypeStruct(extra.shape, extra.dtype) for extra in (rows, blocks)]
     return pl.pallas_call(
-        functools.partial(reduce_kernel, sizes, tuple(pieces), cores, swaps),
+        functools.partial(finish_kernel, sizes, cut),
         out_shape=out_shape,
-        in_specs=[pl.BlockSpec(memory_space=pl.ANY)] * len(operands),
-        out_specs=out_specs,
-        scratch_shapes=scratch
+        in_specs=[anywhere] * len(operands),
+        out_specs=[near] * 7 + [anywhere] * 2,
+        scratch_shapes=sum_scratch(shapes, (False, False, True, False, False, False), sizes)
+        + [pltpu.VMEM(start.shape, low), pltpu.VMEM(chosen.shape, low)]
+        + [pltpu.VMEM((2,) + grad.shape, low) for grad in grads]
+        + [pltpu.VMEM(made, low)] * 3
         + [
-            sems,
-            sems,
-            pltpu.SemaphoreType.DMA((total, 2)),
+            pltpu.VMEM((2, cut, logits.shape[1]), low),
+            pltpu.VMEM((2, cut, normed.shape[1]), low),
+            swaps,
+            swaps,
+            one,
             plane_swaps,
             plane_swaps,
-            pltpu.SemaphoreType.DMA,
+            one,
+            pltpu.SemaphoreType.DMA((5,)),
+            pltpu.SemaphoreType.DMA((2, 2)),
+            pltpu.SemaphoreType.DMA((3,)),
+            pltpu.SemaphoreType.DMA((3,)),
         ],
         compiler_params=pltpu.CompilerParams(
-            collective_id=collective, has_side_effects=True, vmem_limit_bytes=48 << 20
+            collective_id=collective, has_side_effects=True, vmem_limit_bytes=56 << 20
         ),
     )(*operands)
 
@@ -906,21 +1070,33 @@
         total = lax.psum_scatter(partial, axes, scatter_dimension=0, tiled=True)
         return total.astype(jnp.float32)
     shaped = partial.reshape(sizes + (-1, partial.shape[1]))
-    pieces = even_pieces(0, shaped.shape[3], cuts)
-    (total,) = reduce_all([shaped], pieces, sizes, collective, cores=True)
-    return total
-
-
-def sum_chips(partials, pieces, sizes, collective, blocks):
+    size = shaped.shape[3] // cuts
+    return reduce_all(shaped, [(i * size, size) for i in range(cuts)], sizes, collective)
+
+
+def sum_chips(partials, start, chosen, grads, logits, normed, rows, blocks, sizes, collective):
     if collective is not None:
-        shaped = [p.reshape(sizes[1:] + (-1, p.shape[1])) for p in partials]
-        *sums, blocks = reduce_all(shaped, pieces, sizes, collective, blocks)
-        return sums, blocks
+        cores = len(partials) - 1
+        shaped = [
+            p.reshape(sizes[1 if i < cores else 0 :] + (-1, p.shape[1]))
+            for i, p in enumerate(partials)
+        ]
+        *sums, word, rows, blocks = finish_all(
+            shaped, start, chosen, grads, logits, normed, rows, blocks, sizes, collective
+        )
+        return sums, word, rows, blocks
+    made = [
+        left_transposed(left, both_cores(right)).astype(jnp.bfloat16)
+        for left, right in zip((chosen, start, start), grads)
+    ]
+    partials = list(partials[:-1]) + [chip_half(partials[-1])] + made
     sums = [
         lax.psum_scatter(p, CHIPS, scatter_dimension=0, tiled=True).astype(jnp.float32)
         for p in partials
     ]
-    return sums, lax.all_to_all(blocks, PLANE, 0, 0)
+    rows = lax.all_to_all(rows, AXES, 0, 0)
+    blocks = lax.all_to_all(blocks, PLANE, 0, 0)
+    return sums, left_transposed(logits, normed), rows, blocks
 
 
 def line_shift(shard, step):
@@ -1096,6 +1272,7 @@
     pick = one_hot(masked, seq_len, jnp.float32)
     chosen = rows_by_seq(pick, start.reshape(own, seq_len, width)).reshape(-1, width)
     chosen_low = chosen.astype(narrow)
+    start_half, chosen_half = both_halves(start_low), both_halves(chosen_low)
     queries = (matmul(chosen_low, query_low) + vec_rows[4]).astype(narrow)
     context = attention(own_lengths, queries, both)
     branch = matmul(context, out_low) + vec_rows[6]
@@ -1131,7 +1308,6 @@
     )
     d_bias = jnp.sum(d_logits, 0)
     d_logits_low = d_logits.astype(narrow)
-    d_word = left_transposed(d_logits_low, all_normed)
     d_normed = sum_rows(matmul(d_logits_low, word_low).astype(narrow), sizes, ids[6], 8)
 
     d_gelu, d_gain_head, d_shift_head = norm_backward(d_normed, norm_head, vec_rows[13])
@@ -1171,11 +1347,6 @@
     d_query, d_key, d_value = attention(own_lengths, queries, both, d_context)
     d_query_bias = jnp.sum(d_query.astype(jnp.float32), 0)
     d_value_bias = jnp.sum(d_value.astype(jnp.float32), 0)
-    d_qkv = [
-        chip_sum(chosen_low, d_query),
-        chip_sum(start_low, d_key),
-        chip_sum(start_low, d_value),
-    ]
     d_chosen = d_pre + right_transposed(d_query, query_low)
     d_both = jnp.concatenate([d_key, d_value], 1)
     d_start = right_transposed(d_both, both_low) + rows_to_seq(
@@ -1185,7 +1356,7 @@
     d_seg_zero = jnp.sum(jnp.where(second, 0.0, d_embedded), 0)
     d_seg_one = jnp.sum(jnp.where(second, d_embedded, 0.0), 0)
     d_embedded_low = d_embedded.astype(narrow)
-    arrived = routes.exchange(routes.token_rows(d_embedded_low, 0, routes.room))
+    send = routes.token_rows(d_embedded_low, 0, routes.room).reshape(parts, -1, width)
     d_small = jnp.concatenate(
         [
             jnp.sum(d_embedded.reshape(own, seq_len, width), 0),
@@ -1213,14 +1384,21 @@
         ],
         0,
     )
-    partials = [d_out, d_turn] + d_qkv + [chip_half(d_small.T)]
-    pieces = [(i, 0, deep) for i in range(6)]
-    (own_out, own_turn, own_q, own_k, own_v, own_small), up_blocks = sum_chips(
-        partials, pieces, sizes, ids[9], up_blocks
+    (own_out, own_turn, own_small, own_q, own_k, own_v), d_word, arrived, up_blocks = sum_chips(
+        [d_out, d_turn, d_small.T.astype(narrow)],
+        start_half,
+        chosen_half,
+        [d_query, d_key, d_value],
+        d_logits_low,
+        all_normed,
+        send,
+        up_blocks,
+        sizes,
+        ids[9],
     )
     own_qkv = jnp.concatenate([own_q, own_k, own_v], 1)
     own_up = up_blocks.swapaxes(0, 1).reshape(up_weight.shape).astype(jnp.float32)
-    d_word = routes.give(d_embedded_low, arrived, lax.optimization_barrier(d_word))
+    d_word = routes.give(d_embedded_low, arrived.reshape(-1, width), d_word)
     owned = (
         d_word,
         own_small[:, :seq_len].T,

time: 801 us -> 772 us (0.964)
  Pallas kernels: 407 us -> 450 us
  waiting for transfers between devices: 59.7 us -> 24.8 us
  matrix products: 134 us -> 111 us
  starting transfers between devices: 42 us -> 21.1 us
  other arithmetic: 89.6 us -> 97.7 us
    pallas_call x4, Pallas kernels: 147 us -> 188 us  [the longest x1 108 us: finish_all(): pl.pallas_call(functools.partial(finish_kernel, sizes, cut), out_shape=ou...]
    ppermute x9, waiting for transfers between devices: 59.7 us -> 24.8 us  [line_shift(): lax.ppermute(shard, 'dp', [(i, (i + step) % size) for i in range(size)])]
    dot_general x11 -> x7, matrix products: 48.4 us -> 20.5 us  [left_transposed(): lax.dot_general(left, right, (((0,), (0,)), ((), ())), preferred_element_...]
    ppermute x9, starting transfers between devices: 36.2 us -> 19.7 us  [line_shift(): lax.ppermute(shard, 'dp', [(i, (i + step) % size) for i in range(size)])]
    unnamed x243 -> x307, local copies, waits for them, and re-layouts: 17.3 us -> 19.5 us
  transfers between devices with their start and end apart: 20 -> 15, of which waited for: 3 -> 3; matrix products, arithmetic and copies ran while one was open for 28% -> 26% of each run, Pallas kernels for 48% -> 42%
where the time goes in v4:
time: 772 us; the launch traced here: 763 us
  Pallas kernels  450 us (58%)
  matrix products  111 us (14%)
  other arithmetic  97.7 us (13%)
  local copies, waits for them, and re-layouts  44.8 us (6%)
  waiting for transfers between devices  24.8 us (3%)
  starting transfers between devices  21.1 us (3%)
  between operations  12.8 us (2%)
    pallas_call x4, Pallas kernels, gather_all(): pl.pallas_call(functools.partial(gather_kernel, sizes, tuple(pieces), rou...  203 us
    pallas_call x1, Pallas kernels, finish_all(): pl.pallas_call(functools.partial(finish_kernel, sizes, cut), out_shape=ou...  108 us
    pallas_call x3, Pallas kernels, reduce_all(): pl.pallas_call(functools.partial(reduce_kernel, sizes, tuple(pieces)), ou...  79.8 us
    dot_general x10, matrix products, matmul(): return jnp.dot(left, right, preferred_element_type=jnp.float32)  47.9 us
    dot_general x7, matrix products, right_transposed(): lax.dot_general(left, right, (((1,), (1,)), ((), ())), preferred_element_...  34.3 us
    ppermute x9, waiting for transfers between devices, line_shift(): lax.ppermute(shard, 'dp', [(i, (i + step) % size) for i in range(size)])  24.8 us
    dot_general x7, matrix products, left_transposed(): lax.dot_general(left, right, (((0,), (0,)), ((), ())), preferred_element_...  20.5 us
    ppermute x9, starting transfers between devices, line_shift(): lax.ppermute(shard, 'dp', [(i, (i + step) % size) for i in range(size)])  19.7 us
  transfers between devices with their start and end apart: 15, of which 3 were waited for; matrix products, arithmetic and copies ran while one was open for 26% of the time, Pallas kernels for 42%

profile of v4, /device:TPU:0, one launch (start us, length us, event | category | flops | bytes accessed | tf_op | source)
XLA Modules:
  0.0 762.5 jit_solution(11599230716289159592)
XLA Ops:
  3.9 13.9 %shard_map.475 = (s32[32,2,640]{2,1,0:T(2,128)S(1)}, bf16[8,32,512]{2,1,0:T(8,128)(2,1)S(1)}) custom-call(s32[2,640]{1,0:T(2,128)S(1)} %fusion.196.row_ref, bf16[8,32,512]{2,1,0:T(8,128)(2,1)S(1)} %bitcast.300), custom_call_target="tpu_custom_call" | custom-call | tf_op jit(solution)/shard_map/pallas_call | solution.py:344
  32.3 5.5 fusion.27
  37.8 124.2 %shard_map.476 = (bf16[2,4,4,32,640]{4,3,2,1,0:T(8,128)(2,1)S(1)}, bf16[2,4,4,32,3072]{4,3,2,1,0:T(8,128)(2,1)S(1)}, bf16[2,4,4,32,1024]{4,3,2,1,0:T(8,128)(2,1)...) custom-call(bf16[32,640]{1,0:T(8,128)(2,1)S(1)} %maximum_maximum_fusion.refs_0_, ...), custom_call_target="tpu_custom_call" | custom-call | tf_op jit(solution)/shard_map/pallas_call | solution.py:594
  174.8 7.1 fusion.17
  192.5 6.5 add_convert_fusion.k_ref.v_ref
  199.0 8.1 %shard_map.477 = bf16[128,1024]{1,0:T(8,128)(2,1)} custom-call(s32[2]{0:T(128)} %get-tuple-element.536.lengths_ref, bf16[128,1024]{1,0:T(8,128)(2,1)} %fusion.86.q_ref, bf16[1024,2048]{1,0:T(8,128)(2,1)} %add_convert_fusion.k_ref.v_ref, bf16[1024,2048]{1,0:T(8,128)(2,1)} %add_convert_fusion.k_ref.v_ref), custom_call_target="tpu_custom_call" | custom-call | tf_op jit(solution)/shard_map/pallas_call | solution.py:1023
  222.1 15.0 %shard_map.478 = bf16[2,4,1,128,1024]{4,3,2,1,0:T(8,128)(2,1)S(1)} custom-call(bf16[128,1024]{1,0:T(8,128)(2,1)S(1)} %add_convert_fusion.4.refs_0_), custom_call_target="tpu_custom_call" | custom-call | tf_op jit(solution)/shard_map/pallas_call | solution.py:594
  239.6 4.0 copy.209
  255.6 6.6 fusion.45
  262.2 6.2 convolution_convert_fusion.2
  268.5 15.1 %shard_map.479 = f32[128,1024]{1,0:T(8,128)S(1)} custom-call(bf16[2,4,1,128,1024]{4,3,2,1,0:T(8,128)(2,1)S(1)} %bitcast.294), custom_call_target="tpu_custom_call" | custom-call | tf_op jit(solution)/shard_map/pallas_call | solution.py:785
  287.5 49.4 %shard_map.480 = bf16[2,4,4,128,1024]{4,3,2,1,0:T(8,128)(2,1)S(1)} custom-call(bf16[128,1024]{1,0:T(8,128)(2,1)S(1)} %add_convert_fusion.2.refs_0_), custom_call_target="tpu_custom_call" | custom-call | tf_op jit(solution)/shard_map/pallas_call | solution.py:594
  336.9 12.6 %fusion.13 = (f32[4096]{0:T(1024)S(1)}, f32[4096,960]{1,0:T(8,128)}) fusion(f32[960]{0:T(1024)S(1)} %pad_dynamic-slice_fusion, pred[960]{0:T(1024)(128)(4,1)S(1)} %copy-done.120, bf16[4096,1024]{1,0:T(8,128)(2,1)S(1)} %bitcast.286, bf16[960,1024]{1,0:T(8,128)(2,1)S(1)} %copy-done.33), kind=kOutput, calls=%fused_computation.32 | convolution fusion | flops 8064856064 | bytes 26104512 | tf_op jit(solution)/shard_map/dot_general | solution.py:42
  349.5 10.2 %exponential_reduce_fusion = (f32[4096]{0:T(1024)S(1)}, f32[4096]{0:T(1024)S(1)}) fusion(f32[4096,960]{1,0:T(8,128)} %get-tuple-element.589, f32[4096]{0:T(1024)S(1)} %get-tuple-element.588, f32[960]{0:T(1024)S(1)} %pad_dynamic-slice_fusion, pred[960]{0:T(1024)(128)(4,1)S(1)} %copy-done.120, s32[960]{0:T(1024)S(1)} %copy-done.92, s32[4096]{0:T(1024)S(1)} %eq.239), kind=kLoop, calls=%fused_computation.30 | loop fusion | flops 27516928 | bytes 15802816 | tf_op jit(solution)/shard_map/reduce_sum | solution.py:1301
  359.8 15.8 %shard_map.481 = f32[32,8,128]{2,1,0:T(8,128)S(1)} custom-call(f32[32,8,128]{2,1,0:T(8,128)S(1)} %pad.10.own_ref), custom_call_target="tpu_custom_call" | custom-call | tf_op jit(solution)/shard_map/pallas_call | solution.py:429
  376.3 9.1 %fusion.244 = (f32[960]{0:T(1024)}, bf16[4096,960]{1,0:T(8,128)(2,1)S(1)}) fusion(s32[960]{0:T(1024)S(1)} %copy-done.92, s32[4096]{0:T(1024)S(1)} %eq.239, f32[4096]{0:T(1024)S(1)} %bitcast.362, f32[4096]{0:T(1024)S(1)} %bitcast.363, f32[4096,960]{1,0:T(8,128)S(1)} %copy-done.15, f32[960]{0:T(1024)S(1)} %pad_dynamic-slice_fusion, ...), kind=kLoop, calls=%fused_computation.439 | loop fusion | flops 39320640 | bytes 23670976 | tf_op jit(solution)/shard_map/reduce_sum | solution.py:1309
  385.5 10.9 %convolution_convert_fusion = bf16[4096,1024]{1,0:T(8,128)(2,1)} fusion(bf16[4096,960]{1,0:T(8,128)(2,1)S(1)} %get-tuple-element.515.refs_8_, bf16[960,1024]{1,0:T(8,128)(2,1)S(1)} %copy-done.33), kind=kOutput, calls=%fused_computation.34 | convolution fusion | flops 8057257984 | bytes 18219008 | tf_op jit(solution)/shard_map/dot_general | solution.py:32
  396.4 48.4 %shard_map.482 = f32[128,1024]{1,0:T(8,128)S(1)} custom-call(bf16[2,4,4,128,1024]{4,3,2,1,0:T(8,128)(2,1)} %bitcast.318), custom_call_target="tpu_custom_call" | custom-call | tf_op jit(solution)/shard_map/pallas_call | solution.py:785
  453.7 14.4 %shard_map.483 = bf16[2,4,1,128,1024]{4,3,2,1,0:T(8,128)(2,1)S(1)} custom-call(bf16[128,1024]{1,0:T(8,128)(2,1)S(1)} %get-tuple-element.521.refs_0_), custom_call_target="tpu_custom_call" | custom-call | tf_op jit(solution)/shard_map/pallas_call | solution.py:594
  472.3 16.3 %shard_map.484 = f32[128,1024]{1,0:T(8,128)S(1)} custom-call(bf16[2,4,1,128,1024]{4,3,2,1,0:T(8,128)(2,1)S(1)} %bitcast.293), custom_call_target="tpu_custom_call" | custom-call | tf_op jit(solution)/shard_map/pallas_call | solution.py:785
  492.4 11.5 %shard_map.485 = (bf16[128,1024]{1,0:T(8,128)(2,1)}, bf16[1024,1024]{1,0:T(8,128)(2,1)}, bf16[1024,1024]{1,0:T(8,128)(2,1)}) custom-call(s32[2]{0:T(128)} %get-tuple-element.536.lengths_ref, bf16[128,1024]{1,0:T(8,128)(2,1)} %fusion.86.q_ref, bf16[1024,2048]{1,0:T(8,128)(2,1)} %add_convert_fusion.k_ref.v_ref, ...), custom_call_target="tpu_custom_call" | custom-call | tf_op jit(solution)/shard_map/pallas_call | solution.py:1030
  508.4 5.2 fusion.173
  514.5 11.0 %multiply_reduce_fusion = (bf16[1024]{0:T(1024)(128)(2,1)}, f32[1024]{0:T(1024)S(1)}, f32[1024]{0:T(1024)S(1)}, bf16[1024]{0:T(1024)(128)(2,1)}, f32[1024,1024]{1,0:T(8,128)S(1)}) fusion(f32[1024,1024]{1,0:T(8,128)} %copy-done.13, f32[1024]{0:T(1024)S(1)} %copy-done.89, f32[1024]{0:T(1024)S(1)} %broadcast_multiply_fusion.2, f32[1024]{0:T(1024)S(1)} %bitcast.368, ...), kind=kOutput, calls=%fused_computation.51 | convolution fusion | flops 4313837568 | bytes 20996096 | tf_op jit(solution)/shard_map/dot_general | solution.py:42
  535.9 6.9 fusion.26
  555.0 10.8 %collective-permute-start.13 = (bf16[128,1024]{1,0:T(8,128)(2,1)S(1)}, bf16[128,1024]{1,0:T(8,128)(2,1)S(1)}, u32[]{:S(2)}, u32[]{:S(2)}) collective-permute-start(bf16[128,1024]{1,0:T(8,128)(2,1)S(1)} %get-tuple-element.547), channel_id=1, source_target_pairs={{0,2},{1,3},{2,0},{3,1},{4,6},{5,7},{6,4},{7,5},{8,10},{9,11},{10,... | collective-permute-start | bytes 786440 | tf_op jit(solution)/shard_map/ppermute | solution.py:1104
  565.9 15.1 %collective-permute-done.10 = bf16[8,32,512]{2,1,0:T(8,128)(2,1)S(1)} collective-permute-done((bf16[8,32,512]{2,1,0:T(8,128)(2,1)S(1)}, bf16[8,32,512]{2,1,0:T(8,128)(2,1)S(1)}, u32[]{:S(2)}, u32[]{:S(2)}) %collective-permute-start.10) | collective-permute-done | bytes 262176 | tf_op jit(solution)/shard_map/ppermute | solution.py:1104
  584.4 9.6 %collective-permute-done.13 = bf16[128,1024]{1,0:T(8,128)(2,1)S(1)} collective-permute-done((bf16[128,1024]{1,0:T(8,128)(2,1)S(1)}, bf16[128,1024]{1,0:T(8,128)(2,1)S(1)}, u32[]{:S(2)}, u32[]{:S(2)}) %collective-permute-start.13) | collective-permute-done | bytes 262176 | tf_op jit(solution)/shard_map/ppermute | solution.py:1104
  597.6 108.0 %shard_map.486 = (f32[32,1024]{1,0:T(8,128)}, f32[32,1024]{1,0:T(8,128)}, f32[32,640]{1,0:T(8,128)}, f32[32,1024]{1,0:T(8,128)}, f32[32,1024]{1,0:T(8,128)}, /*i...) custom-call(bf16[4,4,32,1024]{3,2,1,0:T(8,128)(2,1)} %bitcast.331, ...), custom_call_target="tpu_custom_call" | custom-call | tf_op jit(solution)/shard_map/pallas_call | solution.py:930
  708.4 5.5 fusion.14
  716.9 3.8 multiply_reduce_fusion.3
  728.2 10.3 %shard_map.487 = f32[32,8,128]{2,1,0:T(8,128)S(1)} custom-call(f32[8,128]{1,0:T(8,128)S(1)} %maximum_bitcast_fusion.1.row_ref), custom_call_target="tpu_custom_call" | custom-call | tf_op jit(solution)/shard_map/pallas_call | solution.py:388
  742.4 10.2 %multiply_subtract_fusion = (f32[960,1024]{1,0:T(8,128)}, f32[960,1024]{1,0:T(8,128)}, f32[960,1024]{1,0:T(8,128)}) fusion(f32[960,1024]{1,0:T(8,128)} %param.36, f32[960,1024]{1,0:T(8,128)} %get-tuple-element.267, f32[]{:T(128)S(6)} %div.275, f32[960,1024]{1,0:T(8,128)} %param.37, f32[960,1024]{1,0:T(8,128)} %param.38), kind=kLoop, calls=%fused_computation.65 | loop fusion | flops 15728640 | bytes 27525124 | tf_op jit(solution)/shard_map/sub | solution.py:1158
  (513 shorter events, 142.4 us)
Async XLA Ops:
  0.7 185.9 %copy-start = (s32[4,64]{1,0:T(4,128)S(1)}, s32[4,64]{1,0:T(4,128)}, u32[]{:S(2)}) copy-start(s32[4,64]{1,0:T(4,128)} %param.34) | copy-start | bytes 3076
  2.6 20.0 %copy-start.130 = (s32[4]{0:T(128)S(1)}, s32[4]{0:T(128)}, u32[]{:S(2)}) copy-start(s32[4]{0:T(128)} %param.33) | copy-start | bytes 52
  18.9 228.9 %collective-permute-start.3 = (bf16[512,512]{1,0:T(8,128)(2,1)}, bf16[512,512]{1,0:T(8,128)(2,1)}, u32[]{:S(2)}, u32[]{:S(2)}) collective-permute-start(bf16[512,512]{1,0:T(8,128)(2,1)} %get-tuple-element.552), channel_id=1, source_target_pairs={{0,3},{1,0},{2,1},{3,2},{4,7},{5,4},{6,5},{7,6},{8,11},{9,8},{10,9... | collective-permute-start | bytes 1572872 | tf_op jit(solution)/shard_map/ppermute | solution.py:1104
  19.9 227.9 %collective-permute-start.2 = (bf16[512,512]{1,0:T(8,128)(2,1)}, bf16[512,512]{1,0:T(8,128)(2,1)}, u32[]{:S(2)}, u32[]{:S(2)}) collective-permute-start(bf16[512,512]{1,0:T(8,128)(2,1)} %get-tuple-element.552), channel_id=1, source_target_pairs={{0,2},{1,3},{2,0},{3,1},{4,6},{5,7},{6,4},{7,5},{8,10},{9,11},{10,... | collective-permute-start | bytes 1572872 | tf_op jit(solution)/shard_map/ppermute | solution.py:1104
  20.9 226.9 %collective-permute-start.1 = (bf16[512,512]{1,0:T(8,128)(2,1)}, bf16[512,512]{1,0:T(8,128)(2,1)}, u32[]{:S(2)}, u32[]{:S(2)}) collective-permute-start(bf16[512,512]{1,0:T(8,128)(2,1)} %get-tuple-element.552), channel_id=1, source_target_pairs={{0,1},{1,2},{2,3},{3,0},{4,5},{5,6},{6,7},{7,4},{8,9},{9,10},{10,1... | collective-permute-start | bytes 1572872 | tf_op jit(solution)/shard_map/ppermute | solution.py:1104
  208.8 337.3 %collective-permute-start = (bf16[128,512]{1,0:T(8,128)(2,1)}, bf16[128,512]{1,0:T(8,128)(2,1)}, u32[]{:S(2)}, u32[]{:S(2)}) collective-permute-start(bf16[128,512]{1,0:T(8,128)(2,1)} %get-tuple-element.558), channel_id=1, source_target_pairs={{0,16},{16,0},{1,17},{17,1},{2,18},{18,2},{3,19},{19,3},{4,20},{20... | collective-permute-start | bytes 393224 | tf_op jit(solution)/shard_map/ppermute | solution.py:160
  209.9 35.9 %collective-permute-start.8 = (bf16[128,512]{1,0:T(8,128)(2,1)}, bf16[128,512]{1,0:T(8,128)(2,1)}, u32[]{:S(2)}, u32[]{:S(2)}) collective-permute-start(bf16[128,512]{1,0:T(8,128)(2,1)} %get-tuple-element.554), channel_id=1, source_target_pairs={{0,16},{16,0},{1,17},{17,1},{2,18},{18,2},{3,19},{19,3},{4,20},{20... | collective-permute-start | bytes 393224 | tf_op jit(solution)/shard_map/ppermute | solution.py:160
  245.7 16.5 %copy-start.128 = (f32[512]{0:T(512)}, f32[512]{0:T(512)S(1)}, u32[]{:S(2)}) copy-start(f32[512]{0:T(512)S(1)} %dynamic_slice.83) | copy-start | bytes 6148
  245.8 349.1 %collective-permute-start.7 = (bf16[1024,512]{1,0:T(8,128)(2,1)}, bf16[1024,512]{1,0:T(8,128)(2,1)}, u32[]{:S(2)}, u32[]{:S(2)}) collective-permute-start(bf16[1024,512]{1,0:T(8,128)(2,1)} %get-tuple-element.538), channel_id=1, source_target_pairs={{0,16},{16,0},{1,17},{17,1},{2,18},{18,2},{3,19},{19,3},{4,20},{20... | collective-permute-start | bytes 3145736 | tf_op jit(solution)/shard_map/ppermute | solution.py:160
  287.5 49.4 %copy-start.33 = (bf16[960,1024]{1,0:T(8,128)(2,1)S(1)}, bf16[960,1024]{1,0:T(8,128)(2,1)}, u32[]{:S(2)}) copy-start(bf16[960,1024]{1,0:T(8,128)(2,1)} %get-tuple-element.772) | copy-start | bytes 5898244
  287.5 49.4 %copy-start.120 = (pred[960]{0:T(1024)(128)(4,1)S(1)}, pred[960]{0:T(1024)(128)(4,1)}, u32[]{:S(2)}) copy-start(pred[960]{0:T(1024)(128)(4,1)} %broadcast_compare_fusion) | copy-start | bytes 2884
  349.5 26.8 %copy-start.15 = (f32[4096,960]{1,0:T(8,128)S(1)}, f32[4096,960]{1,0:T(8,128)}, u32[]{:S(2)}) copy-start(f32[4096,960]{1,0:T(8,128)} %get-tuple-element.589) | copy-start | bytes 47185924
  396.4 49.2 %copy-start.49 = (f32[128,1024]{1,0:T(8,128)S(1)}, f32[128,1024]{1,0:T(8,128)}, u32[]{:S(2)}) copy-start(f32[128,1024]{1,0:T(8,128)} %get-tuple-element.587) | copy-start | bytes 1572868
  447.2 104.5 %collective-permute-start.6 = (bf16[128,1024]{1,0:T(8,128)(2,1)}, bf16[128,1024]{1,0:T(8,128)(2,1)}, u32[]{:S(2)}, u32[]{:S(2)}) collective-permute-start(bf16[128,1024]{1,0:T(8,128)(2,1)} %get-tuple-element.519), channel_id=1, source_target_pairs={{0,16},{16,0},{1,17},{17,1},{2,18},{18,2},{3,19},{19,3},{4,20},{20... | collective-permute-start | bytes 786440 | tf_op jit(solution)/shard_map/ppermute | solution.py:160
  451.7 16.4 %copy-start.37 = (bf16[512,1024]{1,0:T(8,128)(2,1)S(1)}, bf16[512,1024]{1,0:T(8,128)(2,1)}, u32[]{:S(2)}) copy-start(bf16[512,1024]{1,0:T(8,128)(2,1)} %reshape.570) | copy-start | bytes 3145732
  451.7 16.4 %copy-start.129 = (f32[512]{0:T(512)S(1)}, f32[512]{0:T(512)}, u32[]{:S(2)}) copy-start(f32[512]{0:T(512)} %copy-done.128) | copy-start | bytes 6148
  451.7 16.4 %copy-start.141 = (f32[1024,512]{0,1:T(8,128)S(1)}, f32[1024,512]{0,1:T(8,128)}, u32[]{:S(2)}) copy-start(f32[1024,512]{0,1:T(8,128)} %copy-done.140) | copy-start | bytes 6291460
  472.3 17.0 %copy-start.98 = (f32[128]{0:T(128)S(1)}, f32[128]{0:T(128)}, u32[]{:S(2)}) copy-start(f32[128]{0:T(128)} %copy-done.96) | copy-start | bytes 1540
  472.3 17.0 %copy-start.105 = (f32[128]{0:T(128)S(1)}, f32[128]{0:T(128)}, u32[]{:S(2)}) copy-start(f32[128]{0:T(128)} %copy-done.103) | copy-start | bytes 1540
  490.9 57.7 %collective-permute-start.4 = (bf16[128,1024]{1,0:T(8,128)(2,1)S(1)}, bf16[128,1024]{1,0:T(8,128)(2,1)}, u32[]{:S(2)}, u32[]{:S(2)}) collective-permute-start(bf16[128,1024]{1,0:T(8,128)(2,1)S(1)} %get-tuple-element.526), channel_id=1, source_target_pairs={{0,16},{16,0},{1,17},{17,1},{2,18},{18,2},{3,19},{19,3},{4,20},{20... | collective-permute-start | bytes 786440 | tf_op jit(solution)/shard_map/ppermute | solution.py:160
  507.9 40.0 %collective-permute-start.5 = (bf16[128,512]{1,0:T(8,128)(2,1)}, bf16[128,512]{1,0:T(8,128)(2,1)}, u32[]{:S(2)}, u32[]{:S(2)}) collective-permute-start(bf16[128,512]{1,0:T(8,128)(2,1)} %get-tuple-element.556), channel_id=1, source_target_pairs={{0,16},{16,0},{1,17},{17,1},{2,18},{18,2},{3,19},{19,3},{4,20},{20... | collective-permute-start | bytes 393224 | tf_op jit(solution)/shard_map/ppermute | solution.py:160
  546.1 9.0 %collective-permute-start.11 = (bf16[8,32,512]{2,1,0:T(8,128)(2,1)S(1)}, bf16[8,32,512]{2,1,0:T(8,128)(2,1)S(1)}, u32[]{:S(2)}, u32[]{:S(2)}) collective-permute-start(bf16[8,32,512]{2,1,0:T(8,128)(2,1)S(1)} %get-tuple-element.549), channel_id=1, source_target_pairs={{0,3},{1,0},{2,1},{3,2},{4,7},{5,4},{6,5},{7,6},{8,11},{9,8},{10,9... | collective-permute-start | bytes 786440 | tf_op jit(solution)/shard_map/ppermute | solution.py:1104
  547.9 33.0 %collective-permute-start.10 = (bf16[8,32,512]{2,1,0:T(8,128)(2,1)S(1)}, bf16[8,32,512]{2,1,0:T(8,128)(2,1)S(1)}, u32[]{:S(2)}, u32[]{:S(2)}) collective-permute-start(bf16[8,32,512]{2,1,0:T(8,128)(2,1)S(1)} %get-tuple-element.550), channel_id=1, source_target_pairs={{0,2},{1,3},{2,0},{3,1},{4,6},{5,7},{6,4},{7,5},{8,10},{9,11},{10,... | collective-permute-start | bytes 786440 | tf_op jit(solution)/shard_map/ppermute | solution.py:1104
  548.6 35.0 %collective-permute-start.9 = (bf16[8,32,512]{2,1,0:T(8,128)(2,1)S(1)}, bf16[8,32,512]{2,1,0:T(8,128)(2,1)S(1)}, u32[]{:S(2)}, u32[]{:S(2)}) collective-permute-start(bf16[8,32,512]{2,1,0:T(8,128)(2,1)S(1)} %get-tuple-element.548), channel_id=1, source_target_pairs={{0,1},{1,2},{2,3},{3,0},{4,5},{5,6},{6,7},{7,4},{8,9},{9,10},{10,1... | collective-permute-start | bytes 786440 | tf_op jit(solution)/shard_map/ppermute | solution.py:1104
  551.7 32.7 %collective-permute-start.14 = (bf16[128,1024]{1,0:T(8,128)(2,1)S(1)}, bf16[128,1024]{1,0:T(8,128)(2,1)S(1)}, u32[]{:S(2)}, u32[]{:S(2)}) collective-permute-start(bf16[128,1024]{1,0:T(8,128)(2,1)S(1)} %get-tuple-element.546), channel_id=1, source_target_pairs={{0,3},{1,0},{2,1},{3,2},{4,7},{5,4},{6,5},{7,6},{8,11},{9,8},{10,9... | collective-permute-start | bytes 786440 | tf_op jit(solution)/shard_map/ppermute | solution.py:1104
  555.0 39.0 %collective-permute-start.13 = (bf16[128,1024]{1,0:T(8,128)(2,1)S(1)}, bf16[128,1024]{1,0:T(8,128)(2,1)S(1)}, u32[]{:S(2)}, u32[]{:S(2)}) collective-permute-start(bf16[128,1024]{1,0:T(8,128)(2,1)S(1)} %get-tuple-element.547), channel_id=1, source_target_pairs={{0,2},{1,3},{2,0},{3,1},{4,6},{5,7},{6,4},{7,5},{8,10},{9,11},{10,... | collective-permute-start | bytes 786440 | tf_op jit(solution)/shard_map/ppermute | solution.py:1104
  581.0 13.1 %collective-permute-start.12 = (bf16[128,1024]{1,0:T(8,128)(2,1)S(1)}, bf16[128,1024]{1,0:T(8,128)(2,1)S(1)}, u32[]{:S(2)}, u32[]{:S(2)}) collective-permute-start(bf16[128,1024]{1,0:T(8,128)(2,1)S(1)} %get-tuple-element.545), channel_id=1, source_target_pairs={{0,1},{1,2},{2,3},{3,0},{4,5},{5,6},{6,7},{7,4},{8,9},{9,10},{10,1... | collective-permute-start | bytes 786440 | tf_op jit(solution)/shard_map/ppermute | solution.py:1104
  597.6 110.8 %copy-start.117 = (s32[1536]{0:T(1024)S(1)}, s32[1536]{0:T(1024)}, u32[]{:S(2)}) copy-start(s32[1536]{0:T(1024)} %copy-done.116) | copy-start | bytes 18436
  720.7 19.4 %copy-start.60 = (f32[32,640]{1,0:T(8,128)S(1)}, f32[32,640]{1,0:T(8,128)}, u32[]{:S(2)}) copy-start(f32[32,640]{1,0:T(8,128)} %get-tuple-element.268) | copy-start | bytes 245764
  720.7 19.4 %copy-start.74 = (f32[19,32]{0,1:T(8,128)S(1)}, f32[19,32]{0,1:T(8,128)}, u32[]{:S(2)}) copy-start(f32[19,32]{0,1:T(8,128)} %copy.217) | copy-start | bytes 7300
  720.7 19.4 %copy-start.75 = (f32[19,32]{0,1:T(8,128)S(1)}, f32[19,32]{0,1:T(8,128)}, u32[]{:S(2)}) copy-start(f32[19,32]{0,1:T(8,128)} %copy.213) | copy-start | bytes 7300
  720.7 19.4 %copy-start.76 = (f32[19,32]{0,1:T(8,128)S(1)}, f32[19,32]{0,1:T(8,128)}, u32[]{:S(2)}) copy-start(f32[19,32]{0,1:T(8,128)} %copy.215) | copy-start | bytes 7300
  (127 other events, 658.9 us)

commit v5 on v4

--- a/solution.py
+++ b/solution.py
@@ -397,53 +397,149 @@
     )(row)
 
 
-def stats_kernel(sizes, own_ref, all_ref, held, result, send, arrive, own, send_two, arrive_two):
-    place = Place(sizes)
-    others = place.others()
-    greet([ahead for ahead, _ in others])
-    swap_all(place, own_ref, held, send, arrive, own)()
-    peaks = held[:, 0]
-    peak = jnp.max(peaks, 0, keepdims=True)
-    total = jnp.sum(held[:, 1] * jnp.exp(peaks - peak), 0, keepdims=True)
-    label = jnp.sum(held[:, 2], 0, keepdims=True)
-    result[0:1] = peak
-    result[1:2] = total
-    result[2:3] = label
-    result[3:8] = jnp.zeros((5, result.shape[1]), jnp.float32)
-    me = place.index(place.pipe, place.grp, place.dp)
-    copies = []
-    for i, (ahead, _) in enumerate(others):
-        copies.append(remote(result, all_ref.at[me], send_two.at[i], arrive_two.at[i], ahead))
-        copies[-1].start()
-    all_ref[me] = result[...]
-    for i, (ahead, back) in enumerate(others):
-        copies[i].wait_send()
+class Gather:
+    def __init__(self, place, pieces, shards, fulls, send, arrive, own):
+        self.place, self.pieces, self.shards, self.fulls = place, pieces, shards, fulls
+        self.send, self.arrive, self.own = send, arrive, own
+        pipe, grp, dp = place.pipe, place.grp, place.dp
+        self.near = place.beside * (1 - pipe) + place.below * pipe
+        self.far = place.below * (1 - pipe) + place.beside * pipe
+        self.core = (1 - pipe, grp, dp)
+        self.hops = place.dps - 1
+        self.ends = (dp < self.hops, dp > 0)
+        self.sides = ((pipe, grp, dp + 1), (pipe, grp, dp - 1))
+        self.both = range(2 if self.hops else 0)
+        self.waits, self.keeps = [], {}
+        self.stages = [functools.partial(self.over_line, hop=hop) for hop in range(self.hops)]
+        self.stages += [self.over_plane, self.pass_on, self.last]
+
+    def partners(self):
+        place = self.place
+        pipe, grp, dp = place.pipe, place.grp, place.dp
+        line = [(pipe, grp, place.line(k + 1)) for k in range(self.hops)]
+        return line + [(pipe, self.near, dp), (pipe, self.far, dp), self.core]
+
+    def view(self, n, *at):
+        array, first, rows = self.pieces[n]
+        return self.fulls[array].at[at + ((slice(None),) * (3 - len(at))) + (pl.ds(first, rows),)]
+
+    def shard(self, n):
+        array, first, rows = self.pieces[n]
+        return self.shards[array].at[pl.ds(first, rows)]
+
+    def launch(self, n, index, source, to, *at):
+        copy = remote(
+            source, self.view(n, *at), self.send.at[n, index], self.arrive.at[n, index], to
+        )
+        copy.start()
+        self.waits.append(copy)
+
+    def landed(self, n, index, *at):
+        target = self.view(n, *at)
         remote(
-            result, all_ref.at[place.index(*back)], send_two.at[i], arrive_two.at[i], ahead
+            target, target, self.send.at[n, index], self.arrive.at[n, index], self.core
         ).wait_recv()
 
-
-def combine_stats(own, sizes, collective):
-    parts, _, rows = own.shape
-    sems = pltpu.SemaphoreType.DMA((parts - 1,))
-    return pl.pallas_call(
-        functools.partial(stats_kernel, sizes),
-        out_shape=jax.ShapeDtypeStruct(own.shape, jnp.float32),
-        in_specs=[pl.BlockSpec(memory_space=pltpu.VMEM)],
-        out_specs=pl.BlockSpec(memory_space=pltpu.VMEM),
-        scratch_shapes=[
-            pltpu.VMEM(own.shape, jnp.float32),
-            pltpu.VMEM((8, rows), jnp.float32),
-            sems,
-            sems,
-            pltpu.SemaphoreType.DMA,
-            sems,
-            sems,
-        ],
-        compiler_params=pltpu.CompilerParams(
-            collective_id=collective, has_side_effects=True, vmem_limit_bytes=8 << 20
-        ),
-    )(own)
+    def along(self, n, side, hop, finish=False):
+        place, hops = self.place, self.hops
+        origin = place.dp - hop if side == 0 else place.dp + hop
+        here = origin >= 0 if side == 0 else origin <= hops
+        index = side * hops + hop
+
+        def copy():
+            target = self.view(n, place.pipe, place.grp, origin)
+            source = self.shard(n) if hop == 0 else target
+            return remote(
+                source, target, self.send.at[n, index], self.arrive.at[n, index], self.sides[side]
+            )
+
+        if finish:
+
+            @pl.when(here & self.ends[side])
+            def _():
+                copy().wait_send()
+
+            return
+        if hop > 0:
+
+            @pl.when(here)
+            def _():
+                self.landed(n, index - 1, place.pipe, place.grp, origin)
+
+        if hop < hops:
+
+            @pl.when(here & self.ends[side])
+            def _():
+                copy().start()
+
+    def over_line(self, n, hop):
+        place = self.place
+        if hop == 0:
+            target = self.view(n, place.pipe, place.grp, place.spot)
+            self.keeps[n] = pltpu.make_async_copy(self.shard(n), target, self.own.at[n])
+            self.keeps[n].start()
+        for side in self.both:
+            self.along(n, side, hop)
+
+    def over_plane(self, n):
+        place, first = self.place, 2 * self.hops
+        pipe, grp, dp = place.pipe, place.grp, place.dp
+        self.over_line(n, self.hops)
+        if self.hops:
+            self.keeps[n].wait()
+            group, at = self.view(n, pipe, grp), (pipe, grp)
+        else:
+            group, at = self.shard(n), (pipe, grp, 0)
+        self.launch(n, first, group, (pipe, self.near, dp), *at)
+        self.launch(n, first + 1, group, (pipe, self.far, dp), *at)
+        self.launch(n, first + 3, group, self.core, *at)
+
+    def pass_on(self, n):
+        pipe, first = self.place.pipe, 2 * self.hops
+        self.landed(n, first, pipe, self.near)
+        group = self.view(n, pipe, self.near)
+        self.launch(n, first + 2, group, (pipe, self.far, self.place.dp), pipe, self.near)
+        self.launch(n, first + 4, group, self.core, pipe, self.near)
+        self.landed(n, first + 1, pipe, self.far)
+        self.launch(n, first + 5, self.view(n, pipe, self.far), self.core, pipe, self.far)
+
+    def last(self, n):
+        pipe, first, across = self.place.pipe, 2 * self.hops, self.place.across
+        self.landed(n, first + 2, pipe, across)
+        self.launch(n, first + 6, self.view(n, pipe, across), self.core, pipe, across)
+
+    def core_order(self):
+        return (
+            (),
+            ((3, self.place.grp),),
+            ((4, self.far), (5, self.near)),
+            ((6, self.place.across),),
+        )
+
+    def from_core(self, n):
+        for step in self.core_order():
+            for index, grp in step:
+                self.landed(n, 2 * self.hops + index, 1 - self.place.pipe, grp)
+
+    def settle(self):
+        for n in range(len(self.pieces)):
+            for side in self.both:
+                for hop in range(self.hops):
+                    self.along(n, side, hop, finish=True)
+        for copy in self.waits:
+            copy.wait_send()
+        if not self.hops:
+            for keep in self.keeps.values():
+                keep.wait()
+
+
+def run_stages(stages, total, after=None):
+    for turn in range(total + len(stages) - 1):
+        for at, stage in enumerate(stages):
+            if 0 <= turn - at < total:
+                stage(turn - at)
+        if after is not None:
+            after(turn)
 
 
 def gather_kernel(sizes, pieces, routed, *refs):
@@ -456,127 +552,21 @@
         arrived_ref, refs = refs[0], refs[1:]
     send, arrive, own, swap_send, swap_arrive, swap_own = refs
     place = Place(sizes)
-    pipe, grp, dp = place.pipe, place.grp, place.dp
-    near = place.beside * (1 - pipe) + place.below * pipe
-    far = place.below * (1 - pipe) + place.beside * pipe
-    core = (1 - pipe, grp, dp)
-    hops = place.dps - 1
-    spot = place.spot
-    ends = (dp < hops, dp > 0)
-    sides = ((pipe, grp, dp + 1), (pipe, grp, dp - 1))
-    both = range(2 if hops else 0)
-    if routed:
-        greet([ahead for ahead, _ in place.others()])
-    else:
-        greet(
-            [(pipe, grp, place.line(k + 1)) for k in range(hops)]
-            + [(pipe, near, dp), (pipe, far, dp), core]
-        )
-    waits = []
-
-    def view(piece, *at):
-        array, first, rows = piece
-        return fulls[array].at[at + ((slice(None),) * (3 - len(at))) + (pl.ds(first, rows),)]
-
-    def launch(n, index, source, piece, to, *at):
-        copy = remote(source, view(piece, *at), send.at[n, index], arrive.at[n, index], to)
-        copy.start()
-        waits.append(copy)
-
-    def landed(n, index, piece, *at):
-        target = view(piece, *at)
-        remote(target, target, send.at[n, index], arrive.at[n, index], core).wait_recv()
-
-    def along(n, side, hop, finish=False):
-        origin = dp - hop if side == 0 else dp + hop
-        here = origin >= 0 if side == 0 else origin <= hops
-        piece, index = pieces[n], side * hops + hop
-
-        def copy():
-            array, first, rows = piece
-            target = view(piece, pipe, grp, origin)
-            source = shards[array].at[pl.ds(first, rows)] if hop == 0 else target
-            return remote(source, target, send.at[n, index], arrive.at[n, index], sides[side])
-
-        if finish:
-
-            @pl.when(here & ends[side])
-            def _():
-                copy().wait_send()
-
-            return
-        if hop > 0:
-
-            @pl.when(here)
-            def _():
-                landed(n, index - 1, piece, pipe, grp, origin)
-
-        if hop < hops:
-
-            @pl.when(here & ends[side])
-            def _():
-                copy().start()
-
-    keeps = {}
-
-    def over_line(n, hop):
-        if hop == 0:
-            array, first, rows = pieces[n]
-            source = shards[array].at[pl.ds(first, rows)]
-            keeps[n] = pltpu.make_async_copy(source, view(pieces[n], pipe, grp, spot), own.at[n])
-            keeps[n].start()
-        for side in both:
-            along(n, side, hop)
-
-    def over_plane(n):
-        array, first, rows = piece = pieces[n]
-        over_line(n, hops)
-        if hops:
-            keeps[n].wait()
-            group, at = view(piece, pipe, grp), (pipe, grp)
-        else:
-            group, at = shards[array].at[pl.ds(first, rows)], (pipe, grp, 0)
-        launch(n, 2 * hops, group, piece, (pipe, near, dp), *at)
-        launch(n, 2 * hops + 1, group, piece, (pipe, far, dp), *at)
-        launch(n, 2 * hops + 3, group, piece, core, *at)
-
-    def pass_on(n):
-        piece = pieces[n]
-        landed(n, 2 * hops, piece, pipe, near)
-        group = view(piece, pipe, near)
-        launch(n, 2 * hops + 2, group, piece, (pipe, far, dp), pipe, near)
-        launch(n, 2 * hops + 4, group, piece, core, pipe, near)
-        landed(n, 2 * hops + 1, piece, pipe, far)
-        launch(n, 2 * hops + 5, view(piece, pipe, far), piece, core, pipe, far)
-
-    def last(n):
-        piece = pieces[n]
-        landed(n, 2 * hops + 2, piece, pipe, place.across)
-        launch(n, 2 * hops + 6, view(piece, pipe, place.across), piece, core, pipe, place.across)
-
-    stages = [functools.partial(over_line, hop=hop) for hop in range(hops)]
-    stages += [over_plane, pass_on, last]
-    total = len(pieces)
-    for turn in range(total + len(stages) - 1):
-        for at, stage in enumerate(stages):
-            if 0 <= turn - at < total:
-                stage(turn - at)
-        if turn == 5 and routed:
-            finish = swap_all(place, rows_ref, arrived_ref, swap_send, swap_arrive, swap_own)
-    for n, piece in enumerate(pieces):
-        landed(n, 2 * hops + 3, piece, 1 - pipe, grp)
-        landed(n, 2 * hops + 4, piece, 1 - pipe, far)
-        landed(n, 2 * hops + 5, piece, 1 - pipe, near)
-        landed(n, 2 * hops + 6, piece, 1 - pipe, place.across)
-        for side in both:
-            for hop in range(hops):
-                along(n, side, hop, finish=True)
-    for copy in waits:
-        copy.wait_send()
-    if not hops:
-        for keep in keeps.values():
-            keep.wait()
-    if routed:
+    gather = Gather(place, pieces, shards, fulls, send, arrive, own)
+    greet([ahead for ahead, _ in place.others()] if routed else gather.partners())
+    swaps = []
+
+    def after(turn):
+        if turn == len(pieces) and routed:
+            swaps.append(
+                swap_all(place, rows_ref, arrived_ref, swap_send, swap_arrive, swap_own)
+            )
+
+    run_stages(gather.stages, len(pieces), after)
+    for n in range(len(pieces)):
+        gather.from_core(n)
+    gather.settle()
+    for finish in swaps:
         finish()
 
 
@@ -612,6 +602,7 @@
 
 class Sums:
     block = 16
+    filled = False
 
     def __init__(self, place, sources, chips, others, mine, planes, lines, send, arrive, own, store):
         self.place, self.sources, self.chips, self.others = place, sources, chips, others
@@ -642,8 +633,10 @@
 
     def to_core(self, n):
         place = self.place
-        if self.chips[n] is not None:
-            core = (1 - place.pipe, place.grp, place.dp)
+        core = (1 - place.pipe, place.grp, place.dp)
+        if self.filled:
+            self.launch(n, 0, self.sources[n], self.others[n], core)
+        elif self.chips[n] is not None:
             self.launch(n, 0, self.sources[n].at[1 - place.pipe], self.others[n], core)
             self.keep(n, 0, self.sources[n].at[place.pipe], self.chips[n])
 
@@ -651,7 +644,8 @@
         place, chip, other = self.place, self.chips[n], self.others[n]
         part = self.sources[n]
         if chip is not None:
-            self.kept[n, 0].wait()
+            if not self.filled:
+                self.kept[n, 0].wait()
             self.copies[n, 0].wait_recv()
             for g in range(place.grps):
 
@@ -772,11 +766,7 @@
     greet(line + [near, far, (1 - place.pipe, place.grp, place.dp)])
     stages = [sums.to_core, sums.to_near, sums.to_far, sums.to_lines]
     stages += [sums.to_sum] if place.dps > 1 else []
-    total = len(pieces)
-    for turn in range(total + len(stages) - 1):
-        for at, stage in enumerate(stages):
-            if 0 <= turn - at < total:
-                stage(turn - at)
+    run_stages(stages, len(pieces))
     sums.settle()
 
 
@@ -794,18 +784,17 @@
     )(partial)
 
 
-def finish_kernel(sizes, cut, *refs):
+def finish_kernel(sizes, *refs):
     partials, refs = refs[:3], refs[3:]
     start_ref, chosen_ref, grads, refs = refs[0], refs[1], refs[2:5], refs[5:]
-    logits_ref, normed_ref, rows_ref, blocks_ref, refs = refs[0], refs[1], refs[2], refs[3], refs[4:]
+    rows_ref, blocks_ref, refs = refs[0], refs[1], refs[2:]
     outs, refs = refs[:6], refs[6:]
-    word_ref, arrived_ref, blocks_arrived_ref, refs = refs[0], refs[1], refs[2], refs[3:]
+    arrived_ref, blocks_arrived_ref, refs = refs[0], refs[1], refs[2:]
     cores = (False, False, True, False, False, False)
     scratch, refs = sum_refs(refs, cores)
     start, chosen, held, made, refs = refs[0], refs[1], refs[2:5], refs[5:8], refs[8:]
-    logits, normed, refs = refs[0], refs[1], refs[2:]
     swap_send, swap_arrive, swap_own, plane_send, plane_arrive, plane_own = refs[:6]
-    load, word_load, core_send, core_arrive = refs[6:]
+    load, core_send, core_arrive = refs[6:]
     place = Place(sizes)
     pipe, grp, dp = place.pipe, place.grp, place.dp
     greet([ahead for ahead, _ in place.others()])
@@ -832,36 +821,6 @@
         place, blocks_ref, blocks_arrived_ref, plane_send, plane_arrive, plane_own
     )
     sums.to_near(2)
-
-    steps = logits_ref.shape[0] // cut
-
-    def word_copies(step):
-        slot = step % 2
-        at = pl.ds(pl.multiple_of(step * cut, cut), cut)
-        return (
-            pltpu.make_async_copy(logits_ref.at[at], logits.at[slot], word_load.at[0, slot]),
-            pltpu.make_async_copy(normed_ref.at[at], normed.at[slot], word_load.at[1, slot]),
-        )
-
-    for copy in word_copies(0):
-        copy.start()
-
-    def word_steps(first, last):
-        def one(step, _):
-            @pl.when(step + 1 < steps)
-            def _():
-                for copy in word_copies(step + 1):
-                    copy.start()
-
-            for copy in word_copies(step):
-                copy.wait()
-            slot = step % 2
-            word_ref[...] += left_transposed(logits[slot], normed[slot])
-            return 0
-
-        lax.fori_loop(first, last, one, 0)
-
-    word_ref[...] = jnp.zeros_like(word_ref)
 
     def form(i):
         pltpu.make_async_copy(grads[i], held[i].at[0], load.at[2 + i]).wait()
@@ -892,14 +851,12 @@
     sums.to_far(2)
     sums.to_lines(0)
     sums.to_lines(1)
-    word_steps(0, steps // 2)
     sums.to_far(3)
     sums.to_lines(2)
     sums.to_far(4)
     sums.to_lines(3)
     sums.to_far(5)
     sums.to_lines(4)
-    word_steps(steps // 2, steps)
     sums.to_lines(5)
     for n in range(6):
         sums.to_sum(n)
@@ -910,35 +867,31 @@
     swap()
 
 
-def finish_all(partials, start, chosen, grads, logits, normed, rows, blocks, sizes, collective):
+def finish_all(partials, start, chosen, grads, rows, blocks, sizes, collective):
     low = jnp.bfloat16
     parts = math.prod(sizes)
     _, grps, dps = sizes
     shapes = [(partial.shape[-2], partial.shape[-1]) for partial in partials]
     made = (grps, dps) + shapes[0]
     shapes += [shapes[0]] * 3
-    cut = 512
     anywhere = pl.BlockSpec(memory_space=pl.ANY)
     near = pl.BlockSpec(memory_space=pltpu.VMEM)
     swaps = pltpu.SemaphoreType.DMA((parts - 1,))
     plane_swaps = pltpu.SemaphoreType.DMA((sizes[0] * grps - 1,))
     one = pltpu.SemaphoreType.DMA
-    operands = (*partials, start, chosen, *grads, logits, normed, rows, blocks)
+    operands = (*partials, start, chosen, *grads, rows, blocks)
     out_shape = [jax.ShapeDtypeStruct(shape, jnp.float32) for shape in shapes]
-    out_shape += [jax.ShapeDtypeStruct((logits.shape[1], normed.shape[1]), jnp.float32)]
     out_shape += [jax.ShapeDtypeStruct(extra.shape, extra.dtype) for extra in (rows, blocks)]
     return pl.pallas_call(
-        functools.partial(finish_kernel, sizes, cut),
+        functools.partial(finish_kernel, sizes),
         out_shape=out_shape,
         in_specs=[anywhere] * len(operands),
-        out_specs=[near] * 7 + [anywhere] * 2,
+        out_specs=[near] * 6 + [anywhere] * 2,
         scratch_shapes=sum_scratch(shapes, (False, False, True, False, False, False), sizes)
         + [pltpu.VMEM(start.shape, low), pltpu.VMEM(chosen.shape, low)]
         + [pltpu.VMEM((2,) + grad.shape, low) for grad in grads]
         + [pltpu.VMEM(made, low)] * 3
         + [
-            pltpu.VMEM((2, cut, logits.shape[1]), low),
-            pltpu.VMEM((2, cut, normed.shape[1]), low),
             swaps,
             swaps,
             one,
@@ -946,7 +899,6 @@
             plane_swaps,
             one,
             pltpu.SemaphoreType.DMA((5,)),
-            pltpu.SemaphoreType.DMA((2, 2)),
             pltpu.SemaphoreType.DMA((3,)),
             pltpu.SemaphoreType.DMA((3,)),
         ],
@@ -954,6 +906,196 @@
             collective_id=collective, has_side_effects=True, vmem_limit_bytes=56 << 20
         ),
     )(*operands)
+
+
+def head_kernel(sizes, rows_per, vocab, gather_cuts, sum_cuts, *refs):
+    row_ref, table, bias, info, out, word, bias_out, stats, refs = *refs[:8], refs[8:]
+    full, logits, columns, laid, held, result, slopes, outgoing, refs = *refs[:8], refs[8:]
+    cores = (True,) * sum_cuts
+    scratch, refs = sum_refs(refs, cores)
+    gather_send, gather_arrive, gather_own, swap_send, swap_arrive, swap_own = refs[:6]
+    all_send, all_arrive = refs[6:]
+    place = Place(sizes)
+    pipes, grps, dps = sizes
+    others = place.others()
+    slots, width = row_ref.shape
+    tall = slots // gather_cuts
+    pieces = [(0, i * tall, tall) for i in range(gather_cuts)]
+    gather = Gather(place, pieces, [row_ref], [full], gather_send, gather_arrive, gather_own)
+    greet([ahead for ahead, _ in others])
+    pipe, grp, hops = place.pipe, place.grp, dps - 1
+    me = place.index(pipe, grp, place.dp)
+    cells = table.shape[0]
+    local = lax.broadcasted_iota(jnp.int32, (1, cells), 1)
+    column = me * rows_per + local
+    used = (local < rows_per) & (column < vocab)
+    column = jnp.where(used, column, -1).astype(jnp.float32)
+    groups = pipes * grps
+
+    def parts(body):
+        lax.fori_loop(0, pipes * grps * dps, lambda i, _: (body(i), 0)[1], 0, unroll=8)
+
+    def spot(i):
+        return i // (grps * dps), i // dps % grps, i % dps
+
+    def fill(i):
+        columns[spot(i) + (slice(None), slice(0, 8))] = info[i].T
+
+    def form_logits(n, p, g):
+        _, first, rows = pieces[n]
+        at = pl.ds(first, rows)
+        found = right_transposed(full[p, g, :, at].reshape(dps * rows, width), table[...])
+        found = jnp.where(used, found + bias[...], -1e30)
+        peak = jnp.max(found, -1, keepdims=True)
+        total = jnp.sum(jnp.exp(found - peak), -1, keepdims=True)
+        labels = columns[p, g, :, at, 0:1].reshape(dps * rows, 1)
+        label = jnp.sum(jnp.where(column == labels, found, 0.0), -1, keepdims=True)
+        logits[p, g, :, at] = found.reshape(dps, rows, cells)
+        columns[p, g, :, at, 2:3] = peak.reshape(dps, rows, 1)
+        columns[p, g, :, at, 3:4] = total.reshape(dps, rows, 1)
+        columns[p, g, :, at, 4:5] = label.reshape(dps, rows, 1)
+
+    def after(turn):
+        if turn == 0:
+            parts(fill)
+        arrived = (
+            ((pipe, grp),),
+            ((pipe, gather.near), (pipe, gather.far)),
+            ((pipe, place.across),),
+            (),
+        )
+        for step in range(4):
+            n = turn - hops - step
+            if 0 <= n < gather_cuts:
+                for p, g in arrived[step]:
+                    form_logits(n, p, g)
+                for index, g in gather.core_order()[step]:
+                    gather.landed(n, 2 * hops + index, 1 - pipe, g)
+                    form_logits(n, 1 - pipe, g)
+
+    run_stages(gather.stages, gather_cuts, after)
+    after(gather_cuts + hops + 2)
+
+    def lay(i):
+        laid[i] = columns[spot(i) + (slice(None), slice(0, 8))].T
+
+    parts(lay)
+    swap_all(place, laid, held, swap_send, swap_arrive, swap_own)()
+    peaks = held[:, 2]
+    peak = jnp.max(peaks, 0, keepdims=True)
+    result[...] = jnp.zeros_like(result)
+    result[0:1] = peak
+    result[1:2] = jnp.sum(held[:, 3] * jnp.exp(peaks - peak), 0, keepdims=True)
+    result[2:3] = jnp.sum(held[:, 4], 0, keepdims=True)
+    copies = []
+    for i, (ahead, _) in enumerate(others):
+        copies.append(remote(result, stats.at[me], all_send.at[i], all_arrive.at[i], ahead))
+        copies[-1].start()
+    stats[me] = result[...]
+    for i, (ahead, back) in enumerate(others):
+        copies[i].wait_send()
+        origin = place.index(*back)
+        remote(
+            result, stats.at[origin], all_send.at[i], all_arrive.at[i], ahead
+        ).wait_recv()
+
+    def back(i):
+        columns[spot(i) + (slice(None), slice(8, 16))] = stats[i].T
+
+    parts(back)
+
+    size = slots // sum_cuts
+    half = grps * dps * size
+
+    def store(n, at, total):
+        to = pl.multiple_of(n * size + at.start, Sums.block)
+        out[pl.ds(to, Sums.block)] = total
+
+    sums = Sums(place, [outgoing.at[n] for n in range(sum_cuts)], *scratch, store)
+    sums.filled = True
+    bias_out[...] = jnp.zeros_like(bias_out)
+    word[...] = jnp.zeros_like(word)
+
+    def form_slopes(n):
+        at = pl.ds(n * size, size)
+
+        def one(i, _):
+            p, g = i // grps, i % grps
+            kept = columns[p, g, :, at].reshape(dps * size, columns.shape[-1])
+            found = logits[p, g, :, at].reshape(dps * size, cells)
+            hits = (column == kept[:, 0:1]).astype(jnp.float32)
+            slope = kept[:, 1:2] * (jnp.exp(found - kept[:, 8:9]) / kept[:, 9:10] - hits)
+            bias_out[0:1] += jnp.sum(slope, 0, keepdims=True)
+            slopes[n % 2, i] = slope.astype(jnp.bfloat16)
+            return 0
+
+        lax.fori_loop(0, groups, one, 0)
+        for q, target in ((1 - place.pipe, outgoing.at[n]), (place.pipe, sums.chips[n])):
+            left = slopes[n % 2, pl.ds(q * grps, grps)].reshape(half, cells)
+            target[...] = matmul(left, table[...]).astype(jnp.bfloat16).reshape(target.shape)
+        sums.to_core(n)
+
+    def form_word(n):
+        right = full[:, :, :, pl.ds(n * size, size)].reshape(pipes * half, width)
+        word[...] += left_transposed(slopes[n % 2].reshape(pipes * half, cells), right)
+
+    stages = [form_slopes, sums.to_near, sums.to_far, sums.to_lines, sums.to_sum]
+
+    def then(turn):
+        if turn < sum_cuts:
+            form_word(turn)
+
+    run_stages(stages, sum_cuts, then)
+    sums.settle()
+    gather.settle()
+
+
+def head_all(row, table, bias, info, rows_per, vocab, sizes, collective):
+    low = jnp.bfloat16
+    parts = math.prod(sizes)
+    pipes, grps, dps = sizes
+    slots, width = row.shape
+    cells = table.shape[0]
+    gather_cuts, sum_cuts = 4, 8
+    size = slots // sum_cuts
+    near = pl.BlockSpec(memory_space=pltpu.VMEM)
+    gathers = pltpu.SemaphoreType.DMA((gather_cuts, 2 * (dps - 1) + 7))
+    swaps = pltpu.SemaphoreType.DMA((parts - 1,))
+    return pl.pallas_call(
+        functools.partial(head_kernel, sizes, rows_per, vocab, gather_cuts, sum_cuts),
+        out_shape=(
+            jax.ShapeDtypeStruct(row.shape, jnp.float32),
+            jax.ShapeDtypeStruct(table.shape, jnp.float32),
+            jax.ShapeDtypeStruct((8, cells), jnp.float32),
+            jax.ShapeDtypeStruct(info.shape, jnp.float32),
+        ),
+        in_specs=[near] * 4,
+        out_specs=[near] * 4,
+        scratch_shapes=[
+            pltpu.VMEM(sizes + row.shape, low),
+            pltpu.VMEM(sizes + (slots, cells), jnp.float32),
+            pltpu.VMEM(sizes + (slots, 16), jnp.float32),
+            pltpu.VMEM(info.shape, jnp.float32),
+            pltpu.VMEM(info.shape, jnp.float32),
+            pltpu.VMEM(info.shape[1:], jnp.float32),
+            pltpu.VMEM((2, pipes * grps, dps * size, cells), low),
+            pltpu.VMEM((sum_cuts, grps, dps, size, width), low),
+        ]
+        + sum_scratch([(size, width)] * sum_cuts, (True,) * sum_cuts, sizes)
+        + [
+            gathers,
+            gathers,
+            pltpu.SemaphoreType.DMA((gather_cuts,)),
+            swaps,
+            swaps,
+            pltpu.SemaphoreType.DMA,
+            swaps,
+            swaps,
+        ],
+        compiler_params=pltpu.CompilerParams(
+            collective_id=collective, has_side_effects=True, vmem_limit_bytes=62 << 20
+        ),
+    )(row, table, bias, info)
 
 
 def pair_rows(pair, first):
@@ -1074,17 +1216,17 @@
     return reduce_all(shaped, [(i * size, size) for i in range(cuts)], sizes, collective)
 
 
-def sum_chips(partials, start, chosen, grads, logits, normed, rows, blocks, sizes, collective):
+def sum_chips(partials, start, chosen, grads, rows, blocks, sizes, collective):
     if collective is not None:
         cores = len(partials) - 1
         shaped = [
             p.reshape(sizes[1 if i < cores else 0 :] + (-1, p.shape[1]))
             for i, p in enumerate(partials)
         ]
-        *sums, word, rows, blocks = finish_all(
-            shaped, start, chosen, grads, logits, normed, rows, blocks, sizes, collective
+        *sums, rows, blocks = finish_all(
+            shaped, start, chosen, grads, rows, blocks, sizes, collective
         )
-        return sums, word, rows, blocks
+        return sums, rows, blocks
     made = [
         left_transposed(left, both_cores(right)).astype(jnp.bfloat16)
         for left, right in zip((chosen, start, start), grads)
@@ -1096,7 +1238,7 @@
     ]
     rows = lax.all_to_all(rows, AXES, 0, 0)
     blocks = lax.all_to_all(blocks, PLANE, 0, 0)
-    return sums, left_transposed(logits, normed), rows, blocks
+    return sums, rows, blocks
 
 
 def line_shift(shard, step):
@@ -1137,16 +1279,34 @@
     return spread(row, sizes, collective)
 
 
-def share_stats(peak, total, label, sizes, collective):
-    if collective is None:
-        top = lax.pmax(peak, AXES)
-        total, label = lax.psum((total * jnp.exp(peak - top), label), AXES)
-        return top, total, label
+def output_layer(row, table, bias, labels, weights, rows_per, vocab, sizes, collective):
     parts = math.prod(sizes)
-    stats = jnp.stack([peak, total, label])
-    stats = jnp.pad(stats.reshape(3, parts, -1).swapaxes(0, 1), ((0, 0), (0, 5), (0, 0)))
-    stats = combine_stats(stats, sizes, collective)
-    return [stats[:, i].reshape(-1) for i in range(3)]
+    cells = rows_per + -rows_per % 128
+    if collective is not None:
+        table = jnp.pad(table, ((0, cells - rows_per), (0, 0)))
+        bias = jnp.pad(bias, (0, cells - rows_per))[None]
+        info = jnp.stack([labels.astype(jnp.float32), weights]).reshape(2, parts, -1)
+        info = jnp.pad(info.swapaxes(0, 1), ((0, 0), (0, 6), (0, 0)))
+        grad, word, d_bias, stats = head_all(
+            row, table, bias, info, rows_per, vocab, sizes, collective
+        )
+        stats = [stats[:, i].reshape(-1) for i in range(3)]
+        return grad, word[:rows_per], d_bias[0, :rows_per], stats
+    rows = gather_rows(row, sizes, None, 1)
+    column = lax.axis_index(AXES) * rows_per + jnp.arange(rows_per, dtype=jnp.int32)
+    logits = jnp.where(column < vocab, right_transposed(rows, table) + bias, -1e30)
+    own_peak = jnp.max(logits, -1)
+    own_total = jnp.sum(jnp.exp(logits - own_peak[:, None]), -1)
+    hits = labels[:, None] == column
+    own_label = jnp.sum(jnp.where(hits, logits, 0.0), -1)
+    peak = lax.pmax(own_peak, AXES)
+    total, label = lax.psum((own_total * jnp.exp(own_peak - peak), own_label), AXES)
+    slopes = weights[:, None] * (
+        jnp.exp(logits - peak[:, None]) / total[:, None] - hits.astype(jnp.float32)
+    )
+    low = slopes.astype(jnp.bfloat16)
+    grad = sum_rows(matmul(low, table).astype(jnp.bfloat16), sizes, None, 1)
+    return grad, left_transposed(low, rows), jnp.sum(slopes, 0), (peak, total, label)
 
 
 def adam_step(weight, first, second, grad, factor, rate):
@@ -1291,24 +1451,20 @@
         jax.nn.gelu(turned, approximate=False), vec_rows[13], vec_rows[14]
     )
 
-    all_normed = gather_rows(normed.astype(narrow), sizes, ids[4], 4)
-    column = me * rows_per + jnp.arange(rows_per, dtype=jnp.int32)
     bias_row = jnp.pad(head_bias, (0, parts * rows_per - vocab))
     bias_row = lax.dynamic_slice_in_dim(bias_row, me * rows_per, rows_per, 0)
-    logits = right_transposed(all_normed, word_low) + bias_row
-    logits = jnp.where(column < vocab, logits, -1e30)
-    own_peak = jnp.max(logits, -1)
-    own_total = jnp.sum(jnp.exp(logits - own_peak[:, None]), -1)
-    hits = all_labels[:, None] == column
-    own_label = jnp.sum(jnp.where(hits, logits, 0.0), -1)
-    peak, exp_total, label_logit = share_stats(own_peak, own_total, own_label, sizes, ids[5])
+    d_normed, d_word, d_bias, (peak, exp_total, label_logit) = output_layer(
+        normed.astype(narrow),
+        word_low,
+        bias_row,
+        all_labels,
+        all_valid / total,
+        rows_per,
+        vocab,
+        sizes,
+        ids[4],
+    )
     loss_total = jnp.sum(all_valid * (peak + jnp.log(exp_total) - label_logit))
-    d_logits = (all_valid / total)[:, None] * (
-        jnp.exp(logits - peak[:, None]) / exp_total[:, None] - hits.astype(jnp.float32)
-    )
-    d_bias = jnp.sum(d_logits, 0)
-    d_logits_low = d_logits.astype(narrow)
-    d_normed = sum_rows(matmul(d_logits_low, word_low).astype(narrow), sizes, ids[6], 8)
 
     d_gelu, d_gain_head, d_shift_head = norm_backward(d_normed, norm_head, vec_rows[13])
     d_turned = (d_gelu * gelu_slope(turned)).astype(narrow)
@@ -1324,19 +1480,20 @@
     d_branch = d_pre.astype(narrow)
     d_down_bias = jnp.sum(d_branch.astype(jnp.float32), 0)
     plane_branch = gather_rows(d_branch, plane_sizes, ids[7], 2)
-    own_down = line_sum(
-        left_transposed(activ, plane_branch).reshape(sizes[2], -1, width), ids[7]
-    )
+    d_down = left_transposed(activ, plane_branch).astype(narrow)
     d_inner = (right_transposed(plane_branch, down_low) * gelu_slope(inner)).astype(narrow)
     d_up_bias = jnp.sum(d_inner.astype(jnp.float32), 0)
     d_up_bias = lax.dynamic_update_slice_in_dim(
         jnp.zeros((planes * units,), jnp.float32), d_up_bias, cut * units, 0
     ).reshape(-1, width)
-    d_up = left_transposed(plane_hidden, d_inner).reshape(planes, sizes[2], -1, units)
-    up_blocks = line_sum(d_up.swapaxes(0, 1), ids[7]).astype(narrow)
+    d_up = left_transposed(plane_hidden, d_inner).astype(narrow)
     d_hidden = sum_rows(right_transposed(d_inner, up_low).astype(narrow), plane_sizes, ids[8], 2)
     d_hidden = (d_pre + d_hidden).astype(narrow)
 
+    d_hidden, d_down, d_up = lax.optimization_barrier((d_hidden, d_down, d_up))
+    own_down = line_sum(d_down.reshape(sizes[2], -1, width), ids[7])
+    d_up = d_up.reshape(planes, sizes[2], -1, units).swapaxes(0, 1)
+    up_blocks = line_sum(d_up, ids[7]).astype(narrow)
     d_pre, d_gain_one, d_shift_one = norm_backward(
         d_hidden.astype(jnp.float32), norm_one, vec_rows[7]
     )
@@ -1384,13 +1541,11 @@
         ],
         0,
     )
-    (own_out, own_turn, own_small, own_q, own_k, own_v), d_word, arrived, up_blocks = sum_chips(
+    (own_out, own_turn, own_small, own_q, own_k, own_v), arrived, up_blocks = sum_chips(
         [d_out, d_turn, d_small.T.astype(narrow)],
         start_half,
         chosen_half,
         [d_query, d_key, d_value],
-        d_logits_low,
-        all_normed,
         send,
         up_blocks,
         sizes,

time: 772 us -> 741 us (0.960)
  matrix products: 111 us -> 76.9 us
  Pallas kernels: 450 us -> 483 us
  other arithmetic: 97.7 us -> 73.3 us
  waiting for transfers between devices: 24.8 us -> 14.5 us
    pallas_call x2, Pallas kernels: 124 us -> 245 us  [the longest x1 133 us: head_all(): pl.pallas_call(functools.partial(head_kernel, sizes, rows_per, vocab, gat...]
    pallas_call x4 -> x3, Pallas kernels: 203 us -> 157 us  [gather_all(): pl.pallas_call(functools.partial(gather_kernel, sizes, tuple(pieces), rou...]
    pallas_call x3 -> x2, Pallas kernels: 79.8 us -> 36.4 us  [reduce_all(): pl.pallas_call(functools.partial(reduce_kernel, sizes, tuple(pieces)), ou...]
    reduce_sum x3 -> x0, other arithmetic: 20 us -> none  [the longest x1 10.2 us: per_device(): own_total = jnp.sum(jnp.exp(logits - own_peak[:, None]), -1)]
    dot_general x7 -> x6, matrix products: 34.3 us -> 16.9 us  [right_transposed(): lax.dot_general(left, right, (((1,), (1,)), ((), ())), preferred_element_...]
    dot_general x10 -> x9, matrix products: 47.9 us -> 34.1 us  [matmul(): return jnp.dot(left, right, preferred_element_type=jnp.float32)]
    ppermute x9, waiting for transfers between devices: 24.8 us -> 14.5 us  [line_shift(): lax.ppermute(shard, 'dp', [(i, (i + step) % size) for i in range(size)])]
    unnamed x307 -> x221, local copies, waits for them, and re-layouts: 19.5 us -> 21.8 us
  transfers between devices with their start and end apart: 15 -> 15, of which waited for: 3 -> 2; matrix products, arithmetic and copies ran while one was open for 26% -> 18% of each run, Pallas kernels for 42% -> 47%
where the time goes in v5:
time: 741 us; the launch traced here: 732 us
  Pallas kernels  483 us (65%)
  matrix products  76.9 us (10%)
  other arithmetic  73.3 us (10%)
  local copies, waits for them, and re-layouts  44.7 us (6%)
  starting transfers between devices  27.4 us (4%)
  waiting for transfers between devices  14.5 us (2%)
  between operations  12.4 us (2%)
    pallas_call x3, Pallas kernels, gather_all(): pl.pallas_call(functools.partial(gather_kernel, sizes, tuple(pieces), rou...  157 us
    pallas_call x1, Pallas kernels, head_all(): pl.pallas_call(functools.partial(head_kernel, sizes, rows_per, vocab, gat...  133 us
    pallas_call x1, Pallas kernels, finish_all(): pl.pallas_call(functools.partial(finish_kernel, sizes), out_shape=out_sha...  112 us
    pallas_call x2, Pallas kernels, reduce_all(): pl.pallas_call(functools.partial(reduce_kernel, sizes, tuple(pieces)), ou...  36.4 us
    dot_general x9, matrix products, matmul(): return jnp.dot(left, right, preferred_element_type=jnp.float32)  34.1 us
    ppermute x9, starting transfers between devices, line_shift(): lax.ppermute(shard, 'dp', [(i, (i + step) % size) for i in range(size)])  25.6 us
    unnamed x221, local copies, waits for them, and re-layouts  21.8 us
    dot_general x7, matrix products, left_transposed(): lax.dot_general(left, right, (((0,), (0,)), ((), ())), preferred_element_...  21.7 us
  transfers between devices with their start and end apart: 15, of which 2 were waited for; matrix products, arithmetic and copies ran while one was open for 18% of the time, Pallas kernels for 47%

profile of v5, /device:TPU:0, one launch (start us, length us, event | category | flops | bytes accessed | tf_op | source)
XLA Modules:
  0.0 732.5 jit_solution(8014022560527153345)
XLA Ops:
  3.9 13.9 %shard_map.475 = (s32[32,2,640]{2,1,0:T(2,128)S(1)}, bf16[8,32,512]{2,1,0:T(8,128)(2,1)S(1)}) custom-call(s32[2,640]{1,0:T(2,128)S(1)} %fusion.138.row_ref, bf16[8,32,512]{2,1,0:T(8,128)(2,1)S(1)} %bitcast.226), custom_call_target="tpu_custom_call" | custom-call | tf_op jit(solution)/shard_map/pallas_call | solution.py:344
  31.1 3.9 fusion.23
  35.1 128.3 %shard_map.476 = (bf16[2,4,4,32,640]{4,3,2,1,0:T(8,128)(2,1)S(1)}, bf16[2,4,4,32,3072]{4,3,2,1,0:T(8,128)(2,1)S(1)}, bf16[2,4,4,32,1024]{4,3,2,1,0:T(8,128)(2,1)...) custom-call(bf16[32,640]{1,0:T(8,128)(2,1)S(1)} %maximum_maximum_fusion.refs_0_, ...), custom_call_target="tpu_custom_call" | custom-call | tf_op jit(solution)/shard_map/pallas_call | solution.py:584
  172.1 2.9 slice_convert_fusion
  179.4 5.9 fusion.13
  186.8 3.2 fusion.166
  192.1 3.0 fusion.165
  201.2 8.5 %add_convert_fusion.k_ref.v_ref = bf16[1024,2048]{1,0:T(8,128)(2,1)} fusion(f32[2048]{0:T(1024)S(1)} %concatenate.50, bf16[1024,1024]{1,0:T(8,128)(2,1)S(1)} %get-tuple-element.537, bf16[1024,3072]{1,0:T(8,128)(2,1)} %bitcast.229), kind=kOutput, calls=%fused_computation.25 | convolution fusion | flops 4299161600 | bytes 10493952 | tf_op jit(solution)/shard_map/dot_general | solution.py:32
  209.7 2.8 fusion.61.q_ref
  212.5 8.2 %shard_map.477 = bf16[128,1024]{1,0:T(8,128)(2,1)} custom-call(s32[2]{0:T(128)} %get-tuple-element.542.lengths_ref, bf16[128,1024]{1,0:T(8,128)(2,1)} %fusion.61.q_ref, bf16[1024,2048]{1,0:T(8,128)(2,1)} %add_convert_fusion.k_ref.v_ref, bf16[1024,2048]{1,0:T(8,128)(2,1)} %add_convert_fusion.k_ref.v_ref), custom_call_target="tpu_custom_call" | custom-call | tf_op jit(solution)/shard_map/pallas_call | solution.py:1165
  225.0 3.0 pad.17.refs_1_
  228.3 15.2 %shard_map.478 = bf16[2,4,1,128,1024]{4,3,2,1,0:T(8,128)(2,1)S(1)} custom-call(bf16[128,1024]{1,0:T(8,128)(2,1)S(1)} %add_convert_fusion.4.refs_0_), custom_call_target="tpu_custom_call" | custom-call | tf_op jit(solution)/shard_map/pallas_call | solution.py:584
  256.6 7.9 %fusion.32 = (bf16[1024,512]{1,0:T(8,128)(2,1)S(1)}, f32[1024,512]{1,0:T(8,128)}) fusion(f32[512]{0:T(512)S(1)} %dynamic_slice.81, bf16[1024,1024]{1,0:T(8,128)(2,1)S(1)} %bitcast.221, bf16[1024,512]{1,0:T(8,128)(2,1)} %bitcast.255), kind=kOutput, calls=%fused_computation.73 | convolution fusion | flops 1108344832 | bytes 6293504 | tf_op jit(solution)/shard_map/dot_general | solution.py:32
  265.8 17.3 %shard_map.479 = f32[128,1024]{1,0:T(8,128)S(1)} custom-call(bf16[2,4,1,128,1024]{4,3,2,1,0:T(8,128)(2,1)S(1)} %bitcast.220), custom_call_target="tpu_custom_call" | custom-call | tf_op jit(solution)/shard_map/pallas_call | solution.py:775
  288.4 133.2 %shard_map.480 = (f32[128,1024]{1,0:T(8,128)}, f32[1024,1024]{1,0:T(8,128)}, f32[8,1024]{1,0:T(8,128)}, f32[32,8,128]{2,1,0:T(8,128)}) custom-call(bf16[128,1024]{1,0:T(8,128)(2,1)} %add_convert_fusion.2.refs_0_, bf16[1024,1024]{1,0:T(8,128)(2,1)} %pad.17.refs_1_, f32[1,1024]{1,0:T(1,128)} %bitcast.306, f32[32,8,128]{2,1,0:T(8,128)} %pad.20.refs_3_), custom_call_target="tpu_custom_call" | custom-call | tf_op jit(solution)/shard_map/pallas_call | solution.py:1064
  428.6 13.9 %shard_map.481 = bf16[2,4,1,128,1024]{4,3,2,1,0:T(8,128)(2,1)S(1)} custom-call(bf16[128,1024]{1,0:T(8,128)(2,1)S(1)} %get-tuple-element.529.refs_0_), custom_call_target="tpu_custom_call" | custom-call | tf_op jit(solution)/shard_map/pallas_call | solution.py:584
  451.2 19.0 %shard_map.482 = f32[128,1024]{1,0:T(8,128)S(1)} custom-call(bf16[2,4,1,128,1024]{4,3,2,1,0:T(8,128)(2,1)S(1)} %bitcast.219), custom_call_target="tpu_custom_call" | custom-call | tf_op jit(solution)/shard_map/pallas_call | solution.py:775
  474.3 11.3 %shard_map.483 = (bf16[128,1024]{1,0:T(8,128)(2,1)}, bf16[1024,1024]{1,0:T(8,128)(2,1)}, bf16[1024,1024]{1,0:T(8,128)(2,1)}) custom-call(s32[2]{0:T(128)} %get-tuple-element.542.lengths_ref, bf16[128,1024]{1,0:T(8,128)(2,1)} %fusion.61.q_ref, bf16[1024,2048]{1,0:T(8,128)(2,1)} %add_convert_fusion.k_ref.v_ref, ...), custom_call_target="tpu_custom_call" | custom-call | tf_op jit(solution)/shard_map/pallas_call | solution.py:1172
  490.5 7.6 %multiply_reduce_fusion = (bf16[1024]{0:T(1024)(128)(2,1)S(1)}, f32[1024]{0:T(1024)S(1)}, f32[1024]{0:T(1024)S(1)}, bf16[1024]{0:T(1024)(128)(2,1)S(1)}, f32[1024,1024]{1,0:T(8,128)S(1)}) fusion(f32[1024,1024]{1,0:T(8,128)S(1)} %copy-done.15, f32[1024]{0:T(1024)S(1)} %copy-done.78, f32[1024]{0:T(1024)S(1)} %copy-done.66, f32[1024]{0:T(1024)S(1)} %bitcast.289, ...), kind=kOutput, calls=%fused_computation.42 | convolution fusion | flops 4313837568 | bytes 20996096 | tf_op jit(solution)/shard_map/dot_general | solution.py:42
  499.6 5.2 fusion.22
  507.9 2.7 reduce_sum.471
  521.3 8.5 %collective-permute-done.10 = bf16[8,32,512]{2,1,0:T(8,128)(2,1)S(1)} collective-permute-done((bf16[8,32,512]{2,1,0:T(8,128)(2,1)S(1)}, bf16[8,32,512]{2,1,0:T(8,128)(2,1)S(1)}, u32[]{:S(2)}, u32[]{:S(2)}) %collective-permute-start.10) | collective-permute-done | bytes 262176 | tf_op jit(solution)/shard_map/ppermute | solution.py:1246
  529.8 2.7 collective-permute-start.12
  532.6 12.3 %collective-permute-start.13 = (bf16[128,1024]{1,0:T(8,128)(2,1)S(1)}, bf16[128,1024]{1,0:T(8,128)(2,1)S(1)}, u32[]{:S(2)}, u32[]{:S(2)}) collective-permute-start(bf16[128,1024]{1,0:T(8,128)(2,1)S(1)} %copy-done.55), channel_id=1, source_target_pairs={{0,2},{1,3},{2,0},{3,1},{4,6},{5,7},{6,4},{7,5},{8,10},{9,11},{10,... | collective-permute-start | bytes 786440 | tf_op jit(solution)/shard_map/ppermute | solution.py:1246
  544.8 3.4 collective-permute-start.14
  551.7 6.0 collective-permute-done.13
  559.3 2.7 pad_maximum_fusion.2.refs_3_
  562.0 111.8 %shard_map.484 = (f32[32,1024]{1,0:T(8,128)}, f32[32,1024]{1,0:T(8,128)}, f32[32,640]{1,0:T(8,128)}, f32[32,1024]{1,0:T(8,128)}, f32[32,1024]{1,0:T(8,128)}, /*i...) custom-call(bf16[4,4,32,1024]{3,2,1,0:T(8,128)(2,1)} %bitcast.258, ...), custom_call_target="tpu_custom_call" | custom-call | tf_op jit(solution)/shard_map/pallas_call | solution.py:885
  680.1 7.3 %slice_add_fusion = f32[960,1024]{1,0:T(8,128)} fusion(f32[1024,1024]{1,0:T(8,128)S(1)} %copy-done.97, bf16[1536,1024]{1,0:T(8,128)(2,1)} %bitcast.314, s32[1536]{0:T(1024)S(1)} %copy-done.88), kind=kOutput, calls=%fused_computation.59 | convolution fusion | flops 3022356480 | bytes 11016192 | tf_op jit(solution)/shard_map/dot_general | solution.py:36
  687.7 3.8 multiply_reduce_fusion.3
  698.2 10.4 %shard_map.485 = f32[32,8,128]{2,1,0:T(8,128)S(1)} custom-call(f32[8,128]{1,0:T(8,128)S(1)} %maximum_bitcast_fusion.1.row_ref), custom_call_target="tpu_custom_call" | custom-call | tf_op jit(solution)/shard_map/pallas_call | solution.py:388
  717.6 8.5 %multiply_subtract_fusion = (f32[960,1024]{1,0:T(8,128)}, f32[960,1024]{1,0:T(8,128)}, f32[960,1024]{1,0:T(8,128)}) fusion(f32[960,1024]{1,0:T(8,128)} %param.36, f32[960,1024]{1,0:T(8,128)S(1)} %copy-done.13, f32[]{:T(128)S(6)} %div.260, f32[960,1024]{1,0:T(8,128)} %param.37, f32[960,1024]{1,0:T(8,128)} %param.38), kind=kLoop, calls=%fused_computation.56 | loop fusion | flops 15728640 | bytes 27525124 | tf_op jit(solution)/shard_map/sub | solution.py:1318
  (420 shorter events, 125.8 us)
Async XLA Ops:
  0.7 196.5 %copy-start = (s32[4,64]{1,0:T(4,128)S(1)}, s32[4,64]{1,0:T(4,128)}, u32[]{:S(2)}) copy-start(s32[4,64]{1,0:T(4,128)} %param.34) | copy-start | bytes 3076
  18.8 231.1 %collective-permute-start = (bf16[512,512]{1,0:T(8,128)(2,1)}, bf16[512,512]{1,0:T(8,128)(2,1)}, u32[]{:S(2)}, u32[]{:S(2)}) collective-permute-start(bf16[512,512]{1,0:T(8,128)(2,1)} %get-tuple-element.558), channel_id=1, source_target_pairs={{0,1},{1,2},{2,3},{3,0},{4,5},{5,6},{6,7},{7,4},{8,9},{9,10},{10,1... | collective-permute-start | bytes 1572872 | tf_op jit(solution)/shard_map/ppermute | solution.py:1246
  19.4 230.5 %collective-permute-start.1 = (bf16[512,512]{1,0:T(8,128)(2,1)}, bf16[512,512]{1,0:T(8,128)(2,1)}, u32[]{:S(2)}, u32[]{:S(2)}) collective-permute-start(bf16[512,512]{1,0:T(8,128)(2,1)} %get-tuple-element.558), channel_id=1, source_target_pairs={{0,2},{1,3},{2,0},{3,1},{4,6},{5,7},{6,4},{7,5},{8,10},{9,11},{10,... | collective-permute-start | bytes 1572872 | tf_op jit(solution)/shard_map/ppermute | solution.py:1246
  20.4 229.5 %collective-permute-start.2 = (bf16[512,512]{1,0:T(8,128)(2,1)}, bf16[512,512]{1,0:T(8,128)(2,1)}, u32[]{:S(2)}, u32[]{:S(2)}) collective-permute-start(bf16[512,512]{1,0:T(8,128)(2,1)} %get-tuple-element.558), channel_id=1, source_target_pairs={{0,3},{1,0},{2,1},{3,2},{4,7},{5,4},{6,5},{7,6},{8,11},{9,8},{10,9... | collective-permute-start | bytes 1572872 | tf_op jit(solution)/shard_map/ppermute | solution.py:1246
  196.8 362.6 %collective-permute-start.7 = (bf16[1024,512]{1,0:T(8,128)(2,1)}, bf16[1024,512]{1,0:T(8,128)(2,1)}, u32[]{:S(2)}, u32[]{:S(2)}) collective-permute-start(bf16[1024,512]{1,0:T(8,128)(2,1)} %get-tuple-element.544), channel_id=1, source_target_pairs={{0,16},{16,0},{1,17},{17,1},{2,18},{18,2},{3,19},{19,3},{4,20},{20... | collective-permute-start | bytes 3145736 | tf_op jit(solution)/shard_map/ppermute | solution.py:160
  197.2 27.1 %copy-start.71 = (s32[2,64]{1,0:T(2,128)}, s32[2,64]{1,0:T(2,128)S(1)}, u32[]{:S(2)}) copy-start(s32[2,64]{1,0:T(2,128)S(1)} %constant_dynamic-slice_fusion.13) | copy-start | bytes 1540
  199.8 48.1 %collective-permute-start.8 = (bf16[128,512]{1,0:T(8,128)(2,1)}, bf16[128,512]{1,0:T(8,128)(2,1)}, u32[]{:S(2)}, u32[]{:S(2)}) collective-permute-start(bf16[128,512]{1,0:T(8,128)(2,1)} %get-tuple-element.560), channel_id=1, source_target_pairs={{0,16},{16,0},{1,17},{17,1},{2,18},{18,2},{3,19},{19,3},{4,20},{20... | collective-permute-start | bytes 393224 | tf_op jit(solution)/shard_map/ppermute | solution.py:160
  228.1 15.4 %copy-start.68 = (f32[1,8,4,128]{3,2,1,0:T(4,128)S(1)}, f32[1,8,4,128]{3,2,1,0:T(4,128)}, u32[]{:S(2)}) copy-start(f32[1,8,4,128]{3,2,1,0:T(4,128)} %slice_bitcast_fusion.2) | copy-start | bytes 49156
  228.1 19.1 %copy-start.27 = (bf16[128,1024]{1,0:T(8,128)(2,1)S(1)}, bf16[128,1024]{1,0:T(8,128)(2,1)}, u32[]{:S(2)}) copy-start(bf16[128,1024]{1,0:T(8,128)(2,1)} %shard_map.477) | copy-start | bytes 786436
  247.9 265.7 %collective-permute-start.3 = (bf16[128,512]{1,0:T(8,128)(2,1)}, bf16[128,512]{1,0:T(8,128)(2,1)}, u32[]{:S(2)}, u32[]{:S(2)}) collective-permute-start(bf16[128,512]{1,0:T(8,128)(2,1)} %get-tuple-element.565), channel_id=1, source_target_pairs={{0,16},{16,0},{1,17},{17,1},{2,18},{18,2},{3,19},{19,3},{4,20},{20... | collective-permute-start | bytes 393224 | tf_op jit(solution)/shard_map/ppermute | solution.py:160
  265.8 17.4 %copy-start.83 = (f32[1,1024]{1,0:T(1,128)S(1)}, f32[1,1024]{1,0:T(1,128)}, u32[]{:S(2)}) copy-start(f32[1,1024]{1,0:T(1,128)} %get-tuple-element.577) | copy-start | bytes 12292
  265.8 17.9 %copy-start.64 = (f32[1,1024]{1,0:T(1,128)S(1)}, f32[1,1024]{1,0:T(1,128)}, u32[]{:S(2)}) copy-start(f32[1,1024]{1,0:T(1,128)} %get-tuple-element.576) | copy-start | bytes 12292
  265.8 17.9 %copy-start.82 = (f32[1,1024]{1,0:T(1,128)S(1)}, f32[1,1024]{1,0:T(1,128)}, u32[]{:S(2)}) copy-start(f32[1,1024]{1,0:T(1,128)} %get-tuple-element.575) | copy-start | bytes 12292
  443.9 29.5 %copy-start.26 = (bf16[512,1024]{1,0:T(8,128)(2,1)}, bf16[512,1024]{1,0:T(8,128)(2,1)S(1)}, u32[]{:S(2)}) copy-start(bf16[512,1024]{1,0:T(8,128)(2,1)S(1)} %convolution_convert_fusion.5) | copy-start | bytes 3145732
  450.1 68.6 %collective-permute-start.6 = (bf16[128,1024]{1,0:T(8,128)(2,1)}, bf16[128,1024]{1,0:T(8,128)(2,1)}, u32[]{:S(2)}, u32[]{:S(2)}) collective-permute-start(bf16[128,1024]{1,0:T(8,128)(2,1)} %get-tuple-element.527), channel_id=1, source_target_pairs={{0,16},{16,0},{1,17},{17,1},{2,18},{18,2},{3,19},{19,3},{4,20},{20... | collective-permute-start | bytes 786440 | tf_op jit(solution)/shard_map/ppermute | solution.py:160
  473.4 71.4 %collective-permute-start.4 = (bf16[128,1024]{1,0:T(8,128)(2,1)S(1)}, bf16[128,1024]{1,0:T(8,128)(2,1)}, u32[]{:S(2)}, u32[]{:S(2)}) collective-permute-start(bf16[128,1024]{1,0:T(8,128)(2,1)S(1)} %get-tuple-element.532), channel_id=1, source_target_pairs={{0,16},{16,0},{1,17},{17,1},{2,18},{18,2},{3,19},{19,3},{4,20},{20... | collective-permute-start | bytes 786440 | tf_op jit(solution)/shard_map/ppermute | solution.py:160
  474.3 15.9 %slice-start = ((s8[6291456]{0:T(1024)(128)(4,1)}), s8[2097152]{0:T(1024)(128)(4,1)S(1)}, s32[]{:S(2)}) async-start(s8[6291456]{0:T(1024)(128)(4,1)} %bitcast.232), calls=%async_computation.2 | async-start | bytes 4194304
  505.5 9.5 %collective-permute-start.5 = (bf16[128,512]{1,0:T(8,128)(2,1)}, bf16[128,512]{1,0:T(8,128)(2,1)}, u32[]{:S(2)}, u32[]{:S(2)}) collective-permute-start(bf16[128,512]{1,0:T(8,128)(2,1)} %get-tuple-element.563), channel_id=1, source_target_pairs={{0,16},{16,0},{1,17},{17,1},{2,18},{18,2},{3,19},{19,3},{4,20},{20... | collective-permute-start | bytes 393224 | tf_op jit(solution)/shard_map/ppermute | solution.py:160
  513.5 16.3 %copy-start.56 = (bf16[128,1024]{1,0:T(8,128)(2,1)S(1)}, bf16[128,1024]{1,0:T(8,128)(2,1)}, u32[]{:S(2)}) copy-start(bf16[128,1024]{1,0:T(8,128)(2,1)} %get-tuple-element.551) | copy-start | bytes 786436
  513.5 19.1 %copy-start.55 = (bf16[128,1024]{1,0:T(8,128)(2,1)S(1)}, bf16[128,1024]{1,0:T(8,128)(2,1)}, u32[]{:S(2)}) copy-start(bf16[128,1024]{1,0:T(8,128)(2,1)} %get-tuple-element.553) | copy-start | bytes 786436
  513.5 31.3 %copy-start.54 = (bf16[128,1024]{1,0:T(8,128)(2,1)S(1)}, bf16[128,1024]{1,0:T(8,128)(2,1)}, u32[]{:S(2)}) copy-start(bf16[128,1024]{1,0:T(8,128)(2,1)} %get-tuple-element.552) | copy-start | bytes 786436
  513.5 34.7 %copy-start.60 = (bf16[128,512]{1,0:T(8,128)(2,1)S(1)}, bf16[128,512]{1,0:T(8,128)(2,1)}, u32[]{:S(2)}) copy-start(bf16[128,512]{1,0:T(8,128)(2,1)} %get-tuple-element.564) | copy-start | bytes 393220
  513.6 16.2 %collective-permute-start.10 = (bf16[8,32,512]{2,1,0:T(8,128)(2,1)S(1)}, bf16[8,32,512]{2,1,0:T(8,128)(2,1)S(1)}, u32[]{:S(2)}, u32[]{:S(2)}) collective-permute-start(bf16[8,32,512]{2,1,0:T(8,128)(2,1)S(1)} %get-tuple-element.556), channel_id=1, source_target_pairs={{0,2},{1,3},{2,0},{3,1},{4,6},{5,7},{6,4},{7,5},{8,10},{9,11},{10,... | collective-permute-start | bytes 786440 | tf_op jit(solution)/shard_map/ppermute | solution.py:1246
  515.0 17.6 %collective-permute-start.11 = (bf16[8,32,512]{2,1,0:T(8,128)(2,1)S(1)}, bf16[8,32,512]{2,1,0:T(8,128)(2,1)S(1)}, u32[]{:S(2)}, u32[]{:S(2)}) collective-permute-start(bf16[8,32,512]{2,1,0:T(8,128)(2,1)S(1)} %get-tuple-element.555), channel_id=1, source_target_pairs={{0,3},{1,0},{2,1},{3,2},{4,7},{5,4},{6,5},{7,6},{8,11},{9,8},{10,9... | collective-permute-start | bytes 786440 | tf_op jit(solution)/shard_map/ppermute | solution.py:1246
  518.7 32.1 %collective-permute-start.9 = (bf16[8,32,512]{2,1,0:T(8,128)(2,1)S(1)}, bf16[8,32,512]{2,1,0:T(8,128)(2,1)S(1)}, u32[]{:S(2)}, u32[]{:S(2)}) collective-permute-start(bf16[8,32,512]{2,1,0:T(8,128)(2,1)S(1)} %get-tuple-element.554), channel_id=1, source_target_pairs={{0,1},{1,2},{2,3},{3,0},{4,5},{5,6},{6,7},{7,4},{8,9},{9,10},{10,1... | collective-permute-start | bytes 786440 | tf_op jit(solution)/shard_map/ppermute | solution.py:1246
  529.8 21.8 %collective-permute-start.12 = (bf16[128,1024]{1,0:T(8,128)(2,1)S(1)}, bf16[128,1024]{1,0:T(8,128)(2,1)S(1)}, u32[]{:S(2)}, u32[]{:S(2)}) collective-permute-start(bf16[128,1024]{1,0:T(8,128)(2,1)S(1)} %copy-done.56), channel_id=1, source_target_pairs={{0,1},{1,2},{2,3},{3,0},{4,5},{5,6},{6,7},{7,4},{8,9},{9,10},{10,1... | collective-permute-start | bytes 786440 | tf_op jit(solution)/shard_map/ppermute | solution.py:1246
  532.6 25.1 %collective-permute-start.13 = (bf16[128,1024]{1,0:T(8,128)(2,1)S(1)}, bf16[128,1024]{1,0:T(8,128)(2,1)S(1)}, u32[]{:S(2)}, u32[]{:S(2)}) collective-permute-start(bf16[128,1024]{1,0:T(8,128)(2,1)S(1)} %copy-done.55), channel_id=1, source_target_pairs={{0,2},{1,3},{2,0},{3,1},{4,6},{5,7},{6,4},{7,5},{8,10},{9,11},{10,... | collective-permute-start | bytes 786440 | tf_op jit(solution)/shard_map/ppermute | solution.py:1246
  544.8 12.8 %collective-permute-start.14 = (bf16[128,1024]{1,0:T(8,128)(2,1)S(1)}, bf16[128,1024]{1,0:T(8,128)(2,1)S(1)}, u32[]{:S(2)}, u32[]{:S(2)}) collective-permute-start(bf16[128,1024]{1,0:T(8,128)(2,1)S(1)} %copy-done.54), channel_id=1, source_target_pairs={{0,3},{1,0},{2,1},{3,2},{4,7},{5,4},{6,5},{7,6},{8,11},{9,8},{10,9... | collective-permute-start | bytes 786440 | tf_op jit(solution)/shard_map/ppermute | solution.py:1246
  562.0 118.0 %copy-start.88 = (s32[1536]{0:T(1024)S(1)}, s32[1536]{0:T(1024)}, u32[]{:S(2)}) copy-start(s32[1536]{0:T(1024)} %copy-done.87) | copy-start | bytes 18436
  562.0 118.0 %copy-start.97 = (f32[1024,1024]{1,0:T(8,128)S(1)}, f32[1024,1024]{1,0:T(8,128)}, u32[]{:S(2)}) copy-start(f32[1024,1024]{1,0:T(8,128)} %get-tuple-element.268) | copy-start | bytes 12582916
  687.7 22.5 %copy-start.53 = (f32[32,640]{1,0:T(8,128)S(1)}, f32[32,640]{1,0:T(8,128)}, u32[]{:S(2)}) copy-start(f32[32,640]{1,0:T(8,128)} %get-tuple-element.278) | copy-start | bytes 245764
  691.5 20.8 %copy-start.38 = (f32[2,32,1024]{2,1,0:T(8,128)S(1)}, f32[2,32,1024]{2,1,0:T(8,128)}, u32[]{:S(2)}) copy-start(f32[2,32,1024]{2,1,0:T(8,128)} %param.45) | copy-start | bytes 786436
  (84 other events, 351.2 us)

commit v6 on v5

--- a/solution.py
+++ b/solution.py
@@ -91,7 +91,7 @@
 class Routes:
     def __init__(self, all_ids, all_live, rows_per):
         self.parts, tokens = all_ids.shape
-        self.rows_per = rows_per
+        self.cells = rows_per + -rows_per % 128
         self.me = lax.axis_index(AXES)
         mean = tokens / self.parts
         self.room = max(16, int(math.ceil((mean + 2.8 * math.sqrt(mean)) / 16)) * 16)
@@ -116,7 +116,7 @@
         slots = first + jnp.arange(room, dtype=jnp.int32)
         at = self.out_rank[:, None, :] == slots[None, :, None]
         row = jnp.sum(jnp.where(at, self.out_row[:, None, :] + 1, 0), 2) - 1
-        return one_hot(row.reshape(-1), self.rows_per, jnp.bfloat16)
+        return one_hot(row.reshape(-1), self.cells, jnp.bfloat16)
 
     def token_pick(self, first, room):
         rank = self.in_rank - first
@@ -185,6 +185,12 @@
     keep = lax.dynamic_slice_in_dim(partial, pipe * half, half, 0)
     give = lax.dynamic_slice_in_dim(partial, (1 - pipe) * half, half, 0)
     return (keep.astype(jnp.float32) + swapped(give).astype(jnp.float32)).astype(jnp.bfloat16)
+
+
+def lasting(microseconds):
+    return pl.CostEstimate(
+        flops=int(microseconds * 9e8), bytes_accessed=int(microseconds * 3e6), transcendentals=0
+    )
 
 
 def device(pipe, grp, dp):
@@ -533,6 +539,24 @@
                 keep.wait()
 
 
+class LineGather(Gather):
+    def __init__(self, place, shards, fulls, axes, send, arrive, own):
+        super().__init__(place, [(n, 0, 0) for n in range(len(shards))], shards, fulls, send, arrive, own)
+        self.axes = axes
+        self.stages = [functools.partial(self.over_line, hop=hop) for hop in range(self.hops + 1)]
+
+    def view(self, n, pipe, grp, origin):
+        return self.fulls[n].at[(slice(None),) * self.axes[n] + (origin,)]
+
+    def shard(self, n):
+        return self.shards[n]
+
+    def over_line(self, n, hop):
+        super().over_line(n, hop)
+        if hop == self.hops:
+            self.keeps[n].wait()
+
+
 def run_stages(stages, total, after=None):
     for turn in range(total + len(stages) - 1):
         for at, stage in enumerate(stages):
@@ -542,21 +566,25 @@
             after(turn)
 
 
-def gather_kernel(sizes, pieces, routed, *refs):
-    count = max(piece[0] for piece in pieces) + 1
-    shards, refs = refs[:count], refs[count:]
+def gather_kernel(sizes, pieces, axes, routed, *refs):
+    count, lines = max(piece[0] for piece in pieces) + 1, len(axes)
+    shards, line_shards, refs = refs[:count], refs[count : count + lines], refs[count + lines :]
     if routed:
         rows_ref, refs = refs[0], refs[1:]
-    fulls, refs = refs[:count], refs[count:]
+    fulls, line_fulls, refs = refs[:count], refs[count : count + lines], refs[count + lines :]
     if routed:
         arrived_ref, refs = refs[0], refs[1:]
-    send, arrive, own, swap_send, swap_arrive, swap_own = refs
+    send, arrive, own, line_send, line_arrive, line_own, swap_send, swap_arrive, swap_own = refs
     place = Place(sizes)
     gather = Gather(place, pieces, shards, fulls, send, arrive, own)
+    line = LineGather(place, line_shards, line_fulls, axes, line_send, line_arrive, line_own)
     greet([ahead for ahead, _ in place.others()] if routed else gather.partners())
     swaps = []
 
     def after(turn):
+        for n in range(lines):
+            if 0 <= turn - n <= gather.hops:
+                line.over_line(n, turn - n)
         if turn == len(pieces) and routed:
             swaps.append(
                 swap_all(place, rows_ref, arrived_ref, swap_send, swap_arrive, swap_own)
@@ -566,37 +594,47 @@
     for n in range(len(pieces)):
         gather.from_core(n)
     gather.settle()
+    if lines:
+        line.settle()
     for finish in swaps:
         finish()
 
 
-def gather_all(shards, pieces, sizes, collective, rows=None):
+def gather_all(shards, pieces, sizes, collective, rows=None, lines=(), axes=()):
     parts = math.prod(sizes)
     routed = rows is not None
     kinds = 2 * (sizes[2] - 1) + 7
-    space = pltpu.VMEM if sizes[2] == 1 else pl.ANY
+    near = pl.BlockSpec(memory_space=pltpu.VMEM)
     out_shape = [jax.ShapeDtypeStruct(sizes + shard.shape, shard.dtype) for shard in shards]
+    for line, axis in zip(lines, axes):
+        shape = line.shape[:axis] + sizes[2:] + line.shape[axis:]
+        out_shape.append(jax.ShapeDtypeStruct(shape, line.dtype))
     if routed:
         out_shape.append(jax.ShapeDtypeStruct(rows.shape, rows.dtype))
-    operands = list(shards) + ([rows] if routed else [])
+    operands = list(shards) + list(lines) + ([rows] if routed else [])
     sems = pltpu.SemaphoreType.DMA((len(pieces), kinds))
+    line_sems = pltpu.SemaphoreType.DMA((max(len(lines), 1), kinds))
     swaps = pltpu.SemaphoreType.DMA((parts - 1 if routed else 1,))
     return pl.pallas_call(
-        functools.partial(gather_kernel, sizes, tuple(pieces), routed),
+        functools.partial(gather_kernel, sizes, tuple(pieces), tuple(axes), routed),
         out_shape=out_shape,
-        in_specs=[pl.BlockSpec(memory_space=space)] * len(operands),
-        out_specs=[pl.BlockSpec(memory_space=space)] * len(out_shape),
+        in_specs=[near] * len(operands),
+        out_specs=[near] * len(out_shape),
         scratch_shapes=[
             sems,
             sems,
             pltpu.SemaphoreType.DMA((len(pieces),)),
+            line_sems,
+            line_sems,
+            pltpu.SemaphoreType.DMA((max(len(lines), 1),)),
             swaps,
             swaps,
             pltpu.SemaphoreType.DMA,
         ],
         compiler_params=pltpu.CompilerParams(
-            collective_id=collective, has_side_effects=True, vmem_limit_bytes=16 << 20
+            collective_id=collective, has_side_effects=True, vmem_limit_bytes=40 << 20
         ),
+        cost_estimate=lasting(110 if routed else 15),
     )(*operands)
 
 
@@ -778,6 +816,7 @@
         in_specs=[pl.BlockSpec(memory_space=pl.ANY)],
         out_specs=pl.BlockSpec(memory_space=pltpu.VMEM),
         scratch_shapes=sum_scratch(shapes, (True,) * len(pieces), sizes),
+        cost_estimate=lasting(15),
         compiler_params=pltpu.CompilerParams(
             collective_id=collective, has_side_effects=True, vmem_limit_bytes=48 << 20
         ),
@@ -785,112 +824,124 @@
 
 
 def finish_kernel(sizes, *refs):
-    partials, refs = refs[:3], refs[3:]
-    start_ref, chosen_ref, grads, refs = refs[0], refs[1], refs[2:5], refs[5:]
-    rows_ref, blocks_ref, refs = refs[0], refs[1], refs[2:]
-    outs, refs = refs[:6], refs[6:]
-    arrived_ref, blocks_arrived_ref, refs = refs[0], refs[1], refs[2:]
+    lefts, rights, start, talls, refs = refs[:3], refs[3:6], refs[6], refs[7:9], refs[9:]
+    small, rows_ref, blocks_ref, refs = refs[0], refs[1], refs[2], refs[3:]
+    outs, arrived_ref, blocks_arrived_ref, refs = refs[:4], refs[4], refs[5], refs[6:]
     cores = (False, False, True, False, False, False)
     scratch, refs = sum_refs(refs, cores)
-    start, chosen, held, made, refs = refs[0], refs[1], refs[2:5], refs[5:8], refs[8:]
+    other_lefts, other_rights, other_talls, made, refs = (
+        refs[:3],
+        refs[3:6],
+        refs[6:8],
+        refs[8:13],
+        refs[13:],
+    )
     swap_send, swap_arrive, swap_own, plane_send, plane_arrive, plane_own = refs[:6]
-    load, core_send, core_arrive = refs[6:]
+    core_send, core_arrive = refs[6:]
     place = Place(sizes)
     pipe, grp, dp = place.pipe, place.grp, place.dp
     greet([ahead for ahead, _ in place.others()])
 
-    exchanged = []
-    for i in range(3):
-        pltpu.make_async_copy(grads[i], held[i].at[0], load.at[2 + i]).start()
-        exchanged.append(
-            remote(grads[i], held[i].at[1], core_send.at[i], core_arrive.at[i], (1 - pipe, grp, dp))
+    mine = tuple(lefts) + tuple(rights) + tuple(talls)
+    theirs = tuple(other_lefts) + tuple(other_rights) + tuple(other_talls)
+    exchanged = {}
+    for i in (0, 3, 1, 4, 2, 5, 6, 7):
+        exchanged[i] = remote(
+            mine[i], theirs[i], core_send.at[i], core_arrive.at[i], (1 - pipe, grp, dp)
         )
-        exchanged[-1].start()
-    pltpu.make_async_copy(start_ref, start, load.at[0]).start()
-    pltpu.make_async_copy(chosen_ref, chosen, load.at[1]).start()
+        exchanged[i].start()
 
     def store(n, at, total):
-        outs[n][at] = total
-
-    sums = Sums(place, tuple(partials) + tuple(made), *scratch, store)
+        if n < 3:
+            outs[n][at] = total
+        else:
+            outs[3][at, pl.ds((n - 3) * total.shape[1], total.shape[1])] = total
+
+    sources = (made[0], made[1], small, made[2], made[3], made[4])
+    sums = Sums(place, sources, *scratch, store)
     sums.to_core(2)
-    sums.to_near(0)
-    sums.to_near(1)
     swap = swap_all(place, rows_ref, arrived_ref, swap_send, swap_arrive, swap_own)
     plane_swap = swap_plane(
         place, blocks_ref, blocks_arrived_ref, plane_send, plane_arrive, plane_own
     )
-    sums.to_near(2)
+    wide = made[0].shape[1] * made[0].shape[2]
 
     def form(i):
-        pltpu.make_async_copy(grads[i], held[i].at[0], load.at[2 + i]).wait()
         exchanged[i].wait_recv()
-        if i == 0:
-            pltpu.make_async_copy(chosen_ref, chosen, load.at[1]).wait()
-        if i == 1:
-            pltpu.make_async_copy(start_ref, start, load.at[0]).wait()
-        left = chosen if i == 0 else start
-        right = held[i]
-        wide = left.shape[1] // place.grps
-        tokens = right.shape[1]
-
+        exchanged[3 + i].wait_recv()
+        for g in range(place.grps):
+            first = pl.multiple_of((pipe * place.grps + g) * wide, 128)
+            at = pl.ds(first, wide)
+            total = left_transposed(lefts[i][:, at], rights[i][...])
+            total = total + left_transposed(other_lefts[i][:, at], other_rights[i][...])
+            made[i][g] = total.astype(jnp.bfloat16).reshape(made[i].shape[1:])
+
+    def form_tall(i):
+        exchanged[6 + i].wait_recv()
+        tokens = talls[i].shape[0]
         for g in range(place.grps):
             at = pl.ds(g * wide, wide)
-            total = left_transposed(left[0:tokens, at], right[0])
-            total = total + left_transposed(left[tokens:, at], right[1])
-            made[i][g] = total.astype(jnp.bfloat16).reshape(made[i].shape[1:])
+            total = left_transposed(start[0:tokens, at], talls[i][...])
+            total = total + left_transposed(start[tokens:, at], other_talls[i][...])
+            made[3 + i][g] = total.astype(jnp.bfloat16).reshape(made[3 + i].shape[1:])
 
     form(0)
+    sums.to_near(0)
+    form(1)
+    sums.to_near(1)
+    form(2)
     sums.to_near(3)
+    sums.to_near(2)
     sums.to_far(0)
-    form(1)
+    form_tall(0)
     sums.to_near(4)
     sums.to_far(1)
-    form(2)
+    form_tall(1)
     sums.to_near(5)
+    sums.to_far(3)
     sums.to_far(2)
     sums.to_lines(0)
     sums.to_lines(1)
-    sums.to_far(3)
+    sums.to_lines(3)
+    sums.to_far(4)
     sums.to_lines(2)
-    sums.to_far(4)
-    sums.to_lines(3)
     sums.to_far(5)
     sums.to_lines(4)
     sums.to_lines(5)
-    for n in range(6):
+    for n in (0, 1, 3, 2, 4, 5):
         sums.to_sum(n)
     sums.settle()
-    for copy in exchanged:
+    for copy in exchanged.values():
         copy.wait_send()
     plane_swap()
     swap()
 
 
-def finish_all(partials, start, chosen, grads, rows, blocks, sizes, collective):
+def finish_all(lefts, rights, start, talls, small, rows, blocks, sizes, collective):
     low = jnp.bfloat16
     parts = math.prod(sizes)
     _, grps, dps = sizes
-    shapes = [(partial.shape[-2], partial.shape[-1]) for partial in partials]
-    made = (grps, dps) + shapes[0]
-    shapes += [shapes[0]] * 3
+    width = lefts[0].shape[1]
+    shape = (width // parts, rights[0].shape[1])
+    shapes = [shape, shape, (small.shape[-2], small.shape[-1]), shape, shape, shape]
+    made = pltpu.VMEM((grps, dps) + shape, low)
     anywhere = pl.BlockSpec(memory_space=pl.ANY)
     near = pl.BlockSpec(memory_space=pltpu.VMEM)
     swaps = pltpu.SemaphoreType.DMA((parts - 1,))
     plane_swaps = pltpu.SemaphoreType.DMA((sizes[0] * grps - 1,))
     one = pltpu.SemaphoreType.DMA
-    operands = (*partials, start, chosen, *grads, rows, blocks)
-    out_shape = [jax.ShapeDtypeStruct(shape, jnp.float32) for shape in shapes]
+    operands = (*lefts, *rights, start, *talls, small, rows, blocks)
+    joined = (shape[0], 3 * shape[1])
+    out_shape = [jax.ShapeDtypeStruct(shape, jnp.float32) for shape in shapes[:3] + [joined]]
     out_shape += [jax.ShapeDtypeStruct(extra.shape, extra.dtype) for extra in (rows, blocks)]
     return pl.pallas_call(
         functools.partial(finish_kernel, sizes),
         out_shape=out_shape,
-        in_specs=[anywhere] * len(operands),
-        out_specs=[near] * 6 + [anywhere] * 2,
+        in_specs=[near] * 9 + [anywhere, near, near],
+        out_specs=[near] * 6,
         scratch_shapes=sum_scratch(shapes, (False, False, True, False, False, False), sizes)
-        + [pltpu.VMEM(start.shape, low), pltpu.VMEM(chosen.shape, low)]
-        + [pltpu.VMEM((2,) + grad.shape, low) for grad in grads]
-        + [pltpu.VMEM(made, low)] * 3
+        + [pltpu.VMEM(item.shape, low) for item in (*lefts, *rights, *talls)]
+        + [made] * 5
         + [
             swaps,
             swaps,
@@ -898,9 +949,8 @@
             plane_swaps,
             plane_swaps,
             one,
-            pltpu.SemaphoreType.DMA((5,)),
-            pltpu.SemaphoreType.DMA((3,)),
-            pltpu.SemaphoreType.DMA((3,)),
+            pltpu.SemaphoreType.DMA((8,)),
+            pltpu.SemaphoreType.DMA((8,)),
         ],
         compiler_params=pltpu.CompilerParams(
             collective_id=collective, has_side_effects=True, vmem_limit_bytes=56 << 20
@@ -1168,6 +1218,7 @@
             out_shape=flat,
             in_specs=in_specs,
             out_specs=row,
+            cost_estimate=lasting(8),
         )(lengths, queries, both, both)
     return pl.pallas_call(
         functools.partial(attention_back_kernel, scale, lanes),
@@ -1175,6 +1226,7 @@
         out_shape=(flat, tall, tall),
         in_specs=in_specs + [row],
         out_specs=(row, keys, keys),
+        cost_estimate=lasting(11),
     )(lengths, queries, both, both, grads)
 
 
@@ -1189,13 +1241,17 @@
     return begin(row, blocks, sizes, collective)
 
 
-def gather_weights(shards, pieces, sizes, collective, rows):
+def gather_weights(shards, pieces, lines, axes, sizes, collective, rows):
     if collective is None:
         fulls = [lax.all_gather(shard, AXES, axis=0) for shard in shards]
+        line_fulls = [
+            lax.all_gather(line, "dp", axis=axis) for line, axis in zip(lines, axes)
+        ]
         arrived = lax.all_to_all(rows, AXES, 0, 0)
     else:
-        *fulls, arrived = gather_all(shards, pieces, sizes, collective, rows)
-    return [full.reshape(-1, full.shape[-1]) for full in fulls], arrived
+        *fulls, arrived = gather_all(shards, pieces, sizes, collective, rows, lines, axes)
+        fulls, line_fulls = fulls[: len(shards)], fulls[len(shards) :]
+    return [full.reshape(-1, full.shape[-1]) for full in fulls], line_fulls, arrived
 
 
 def gather_rows(shard, sizes, collective, cuts):
@@ -1216,26 +1272,21 @@
     return reduce_all(shaped, [(i * size, size) for i in range(cuts)], sizes, collective)
 
 
-def sum_chips(partials, start, chosen, grads, rows, blocks, sizes, collective):
+def sum_chips(lefts, rights, start, talls, small, rows, blocks, sizes, collective):
     if collective is not None:
-        cores = len(partials) - 1
-        shaped = [
-            p.reshape(sizes[1 if i < cores else 0 :] + (-1, p.shape[1]))
-            for i, p in enumerate(partials)
-        ]
+        small = small.reshape(sizes + (-1, small.shape[1]))
         *sums, rows, blocks = finish_all(
-            shaped, start, chosen, grads, rows, blocks, sizes, collective
+            lefts, rights, start, talls, small, rows, blocks, sizes, collective
         )
         return sums, rows, blocks
-    made = [
-        left_transposed(left, both_cores(right)).astype(jnp.bfloat16)
-        for left, right in zip((chosen, start, start), grads)
-    ]
-    partials = list(partials[:-1]) + [chip_half(partials[-1])] + made
+    made = [chip_sum(left, right) for left, right in zip(lefts, rights)]
+    made += [left_transposed(start, both_cores(tall)).astype(jnp.bfloat16) for tall in talls]
+    partials = made[:2] + [chip_half(small)] + made[2:]
     sums = [
         lax.psum_scatter(p, CHIPS, scatter_dimension=0, tiled=True).astype(jnp.float32)
         for p in partials
     ]
+    sums = sums[:3] + [jnp.concatenate(sums[3:], 1)]
     rows = lax.all_to_all(rows, AXES, 0, 0)
     blocks = lax.all_to_all(blocks, PLANE, 0, 0)
     return sums, rows, blocks
@@ -1244,16 +1295,6 @@
 def line_shift(shard, step):
     size = lax.axis_size("dp")
     return lax.ppermute(shard, "dp", [(i, (i + step) % size) for i in range(size)])
-
-
-def line_gather(shard, collective):
-    if collective is None:
-        return lax.all_gather(shard, "dp", axis=0)
-    size = lax.axis_size("dp")
-    me = lax.axis_index("dp")
-    kept = jnp.stack([shard] + [line_shift(shard, step) for step in range(1, size)])
-    order = [(me + size - i) % size for i in range(size)]
-    return jnp.concatenate([lax.dynamic_slice_in_dim(kept, at, 1, 0) for at in order], 0)
 
 
 def line_sum(partial, collective):
@@ -1281,20 +1322,21 @@
 
 def output_layer(row, table, bias, labels, weights, rows_per, vocab, sizes, collective):
     parts = math.prod(sizes)
-    cells = rows_per + -rows_per % 128
     if collective is not None:
-        table = jnp.pad(table, ((0, cells - rows_per), (0, 0)))
-        bias = jnp.pad(bias, (0, cells - rows_per))[None]
+        bias = jnp.pad(bias, (0, table.shape[0] - rows_per))[None]
         info = jnp.stack([labels.astype(jnp.float32), weights]).reshape(2, parts, -1)
         info = jnp.pad(info.swapaxes(0, 1), ((0, 0), (0, 6), (0, 0)))
         grad, word, d_bias, stats = head_all(
             row, table, bias, info, rows_per, vocab, sizes, collective
         )
         stats = [stats[:, i].reshape(-1) for i in range(3)]
-        return grad, word[:rows_per], d_bias[0, :rows_per], stats
+        return grad, word, d_bias[0, :rows_per], stats
     rows = gather_rows(row, sizes, None, 1)
-    column = lax.axis_index(AXES) * rows_per + jnp.arange(rows_per, dtype=jnp.int32)
-    logits = jnp.where(column < vocab, right_transposed(rows, table) + bias, -1e30)
+    cells = jnp.arange(table.shape[0], dtype=jnp.int32)
+    column = lax.axis_index(AXES) * rows_per + cells
+    column = jnp.where((cells < rows_per) & (column < vocab), column, -1)
+    bias = jnp.pad(bias, (0, table.shape[0] - rows_per))
+    logits = jnp.where(column >= 0, right_transposed(rows, table) + bias, -1e30)
     own_peak = jnp.max(logits, -1)
     own_total = jnp.sum(jnp.exp(logits - own_peak[:, None]), -1)
     hits = labels[:, None] == column
@@ -1306,7 +1348,7 @@
     )
     low = slopes.astype(jnp.bfloat16)
     grad = sum_rows(matmul(low, table).astype(jnp.bfloat16), sizes, None, 1)
-    return grad, left_transposed(low, rows), jnp.sum(slopes, 0), (peak, total, label)
+    return grad, left_transposed(low, rows), jnp.sum(slopes, 0)[:rows_per], (peak, total, label)
 
 
 def adam_step(weight, first, second, grad, factor, rate):
@@ -1376,12 +1418,6 @@
     cut = me // sizes[2]
     blocks = up_weight.astype(narrow).reshape(up_weight.shape[0], planes, units).swapaxes(0, 1)
     packed, blocks = start_all(packed, blocks, sizes, ids[0])
-    halves_low = down_weight.astype(narrow).reshape(-1, units)
-    both_low = jnp.concatenate([blocks.reshape(-1, units), halves_low], 0)
-    both_low = line_gather(both_low, ids[0])
-    down_low = both_low[:, -halves_low.shape[0] :].reshape(units, width)
-    up_low = both_low[:, : -halves_low.shape[0]].reshape(sizes[2], planes, -1, units)
-    up_low = up_low.swapaxes(0, 1).reshape(width, units)
     all_ids = packed[:, :, :seq_len]
     all_labels = packed[:, :, seq_len : seq_len + slots].reshape(-1)
     all_lengths = packed[:, :, seq_len + slots]
@@ -1394,7 +1430,8 @@
     own_lengths = lax.dynamic_slice_in_dim(lengths, first_own, own, 0)
     masked = lax.dynamic_slice_in_dim(masked_at, first_own, own, 0)
 
-    word_low = word_table.astype(narrow)
+    cells = rows_per + -rows_per % 128
+    word_low = jnp.pad(word_table.astype(narrow), ((0, cells - rows_per), (0, 0)))
     routes = Routes(all_ids.reshape(parts, -1), all_live.reshape(parts, -1), rows_per)
     small = pos_table.shape[0] + vec_table.shape[0]
     spare = -small % 128
@@ -1410,9 +1447,11 @@
     deep = small_low.shape[0]
     pieces = [(0, 0, deep), (1, 0, deep // 2), (1, deep // 2, deep // 2), (2, 0, deep), (3, 0, deep)]
     send = routes.table_rows(word_low, 0, routes.room).reshape(parts, -1, width)
-    (small_full, qkv_low, out_low, turn_low), arrived = gather_weights(
-        low, pieces, sizes, ids[1], send
-    )
+    (small_full, qkv_low, out_low, turn_low), (up_low, down_low), arrived = gather_weights(
+        low, pieces, [blocks, down_weight.astype(narrow)], [1, 0], sizes, ids[1], send
+    )
+    up_low = up_low.reshape(width, units)
+    down_low = down_low.reshape(units, width)
     word_rows = routes.fetch(word_low, arrived.reshape(-1, width))
     small_full = small_full.T
     pos_low = small_full[:seq_len]
@@ -1432,9 +1471,10 @@
     pick = one_hot(masked, seq_len, jnp.float32)
     chosen = rows_by_seq(pick, start.reshape(own, seq_len, width)).reshape(-1, width)
     chosen_low = chosen.astype(narrow)
-    start_half, chosen_half = both_halves(start_low), both_halves(chosen_low)
+    start_half = both_halves(start_low)
     queries = (matmul(chosen_low, query_low) + vec_rows[4]).astype(narrow)
     context = attention(own_lengths, queries, both)
+    context, start_half = lax.optimization_barrier((context, start_half))
     branch = matmul(context, out_low) + vec_rows[6]
     hidden, norm_one = norm_forward(chosen + branch, vec_rows[7], vec_rows[8])
     hidden = hidden.astype(narrow)
@@ -1469,7 +1509,6 @@
     d_gelu, d_gain_head, d_shift_head = norm_backward(d_normed, norm_head, vec_rows[13])
     d_turned = (d_gelu * gelu_slope(turned)).astype(narrow)
     d_turn_bias = jnp.sum(d_turned.astype(jnp.float32), 0)
-    d_turn = chip_sum(picked, d_turned)
     d_picked = right_transposed(d_turned, turn_low)
     same = masked[:, :, None] == masked[:, None, :]
     earlier = slot_index[None, :] < slot_index[:, None]
@@ -1499,7 +1538,7 @@
     )
     d_branch = d_pre.astype(narrow)
     d_out_bias = jnp.sum(d_branch.astype(jnp.float32), 0)
-    d_out = chip_sum(context, d_branch)
+    d_attended = d_branch
     d_context = right_transposed(d_branch, out_low).astype(narrow)
     d_query, d_key, d_value = attention(own_lengths, queries, both, d_context)
     d_query_bias = jnp.sum(d_query.astype(jnp.float32), 0)
@@ -1541,19 +1580,19 @@
         ],
         0,
     )
-    (own_out, own_turn, own_small, own_q, own_k, own_v), arrived, up_blocks = sum_chips(
-        [d_out, d_turn, d_small.T.astype(narrow)],
+    (own_out, own_turn, own_small, own_qkv), arrived, up_blocks = sum_chips(
+        [context, picked, chosen_low],
+        [d_attended, d_turned, d_query],
         start_half,
-        chosen_half,
-        [d_query, d_key, d_value],
+        [d_key, d_value],
+        d_small.T.astype(narrow),
         send,
         up_blocks,
         sizes,
         ids[9],
     )
-    own_qkv = jnp.concatenate([own_q, own_k, own_v], 1)
     own_up = up_blocks.swapaxes(0, 1).reshape(up_weight.shape).astype(jnp.float32)
-    d_word = routes.give(d_embedded_low, arrived.reshape(-1, width), d_word)
+    d_word = routes.give(d_embedded_low, arrived.reshape(-1, width), d_word)[:rows_per]
     owned = (
         d_word,
         own_small[:, :seq_len].T,

time: 741 us -> 695 us (0.938)
  starting transfers between devices: 27.4 us -> 9.59 us
  waiting for transfers between devices: 14.5 us -> 0.02 us
  local copies, waits for them, and re-layouts: 44.7 us -> 35.3 us
    ppermute x9 -> x6, starting transfers between devices: 25.6 us -> 9.16 us  [line_shift(): lax.ppermute(shard, 'dp', [(i, (i + step) % size) for i in range(size)])]
    ppermute x9 -> x6, waiting for transfers between devices: 14.5 us -> 0.02 us  [line_shift(): lax.ppermute(shard, 'dp', [(i, (i + step) % size) for i in range(size)])]
    pallas_call x3, Pallas kernels: 157 us -> 167 us  [gather_all(): pl.pallas_call(functools.partial(gather_kernel, sizes, tuple(pieces), tup...]
    dot_general x7 -> x5, matrix products: 21.7 us -> 15.6 us  [left_transposed(): lax.dot_general(left, right, (((0,), (0,)), ((), ())), preferred_element_...]
    unnamed x221 -> x211, local copies, waits for them, and re-layouts: 21.8 us -> 19.2 us
  transfers between devices with their start and end apart: 15 -> 7, of which waited for: 2 -> 0; matrix products, arithmetic and copies ran while one was open for 18% -> 10% of each run, Pallas kernels for 47% -> 19%
where the time goes in v6:
time: 695 us; the launch traced here: 687 us
  Pallas kernels  489 us (70%)
  matrix products  71 us (10%)
  other arithmetic  69.3 us (10%)
  local copies, waits for them, and re-layouts  35.3 us (5%)
  between operations  12.2 us (2%)
  starting transfers between devices  9.59 us (1%)
    pallas_call x3, Pallas kernels, gather_all(): pl.pallas_call(functools.partial(gather_kernel, sizes, tuple(pieces), tup...  167 us
    pallas_call x1, Pallas kernels, head_all(): pl.pallas_call(functools.partial(head_kernel, sizes, rows_per, vocab, gat...  133 us
    pallas_call x1, Pallas kernels, finish_all(): pl.pallas_call(functools.partial(finish_kernel, sizes), out_shape=out_sha...  111 us
    pallas_call x2, Pallas kernels, reduce_all(): pl.pallas_call(functools.partial(reduce_kernel, sizes, tuple(pieces)), ou...  34 us
    dot_general x9, matrix products, matmul(): return jnp.dot(left, right, preferred_element_type=jnp.float32)  33.1 us
    unnamed x211, local copies, waits for them, and re-layouts  19.2 us
    sub x8, other arithmetic, adam_step(): weight - rate * (first_hat / (jnp.sqrt(second_hat) + epsilon) + weight_de...  17 us
    dot_general x6, matrix products, right_transposed(): lax.dot_general(left, right, (((1,), (1,)), ((), ())), preferred_element_...  15.9 us
  transfers between devices with their start and end apart: 7, of which 0 were waited for; matrix products, arithmetic and copies ran while one was open for 10% of the time, Pallas kernels for 19%

profile of v6, /device:TPU:0, one launch (start us, length us, event | category | flops | bytes accessed | tf_op | source)
XLA Modules:
  0.0 686.6 jit_solution(6651913506628177615)
XLA Ops:
  3.4 13.9 %shard_map.475 = (s32[32,2,640]{2,1,0:T(2,128)S(1)}, bf16[8,32,512]{2,1,0:T(8,128)(2,1)S(1)}) custom-call(s32[2,640]{1,0:T(2,128)S(1)} %fusion.125.row_ref, bf16[8,32,512]{2,1,0:T(8,128)(2,1)S(1)} %bitcast.210), custom_call_target="tpu_custom_call" | custom-call | tf_op jit(solution)/shard_map/pallas_call | solution.py:350
  23.2 2.5 convert_element_type.238
  26.6 5.6 fusion.21
  33.8 137.7 %shard_map.476 = (bf16[2,4,4,32,640]{4,3,2,1,0:T(8,128)(2,1)S(1)}, bf16[2,4,4,32,3072]{4,3,2,1,0:T(8,128)(2,1)}, bf16[2,4,4,32,1024]{4,3,2,1,0:T(8,128)(2,1)S(1)...) custom-call(bf16[32,640]{1,0:T(8,128)(2,1)S(1)} %maximum_maximum_fus, ...), custom_call_target="tpu_custom_call" | custom-call | flops 99000000512 | bytes 330000000 | tf_op jit(solution)/shard_map/pallas_call | solution.py:618
  179.4 2.9 slice_convert_fusion
  186.2 5.3 fusion.11
  193.2 3.2 fusion.151
  198.5 5.0 fusion.150
  209.6 4.0 fusion.103
  216.0 8.8 %add_convert_fusion.k_ref.v_ref = bf16[1024,2048]{1,0:T(8,128)(2,1)} fusion(f32[2048]{0:T(1024)S(1)} %concatenate.26, bf16[1024,1024]{1,0:T(8,128)(2,1)S(1)} %get-tuple-element.514, bf16[1024,3072]{1,0:T(8,128)(2,1)} %bitcast.296), kind=kOutput, calls=%fused_computation.24 | convolution fusion | flops 4299161600 | bytes 10493952 | tf_op jit(solution)/shard_map/dot_general | solution.py:32
  226.5 2.8 fusion.60.q_ref
  229.3 8.2 %shard_map.477.refs_0_ = bf16[128,1024]{1,0:T(8,128)(2,1)} custom-call(s32[2]{0:T(128)} %get-tuple-element.519.lengths_ref, bf16[128,1024]{1,0:T(8,128)(2,1)} %fusion.60.q_ref, bf16[1024,2048]{1,0:T(8,128)(2,1)} %add_convert_fusion.k_ref.v_ref, bf16[1024,2048]{1,0:T(8,128)(2,1)} %add_convert_fusion.k_ref.v_ref), custom_call_target="tpu_custom_call" | custom-call | flops 7200000000 | bytes 24000000 | tf_op jit(solution)/shard_map/pallas_call | solution.py:1215
  237.5 2.8 pad_maximum_fusion.refs_6_
  241.3 14.6 %shard_map.478 = bf16[2,4,1,128,1024]{4,3,2,1,0:T(8,128)(2,1)S(1)} custom-call(bf16[128,1024]{1,0:T(8,128)(2,1)S(1)} %add_convert_fusion.4.refs_0_), custom_call_target="tpu_custom_call" | custom-call | flops 13500000256 | bytes 45000000 | tf_op jit(solution)/shard_map/pallas_call | solution.py:618
  256.0 6.5 fusion.30
  263.7 17.2 %shard_map.479 = f32[128,1024]{1,0:T(8,128)S(1)} custom-call(bf16[2,4,1,128,1024]{4,3,2,1,0:T(8,128)(2,1)S(1)} %bitcast.216), custom_call_target="tpu_custom_call" | custom-call | flops 13500000256 | bytes 45000000 | tf_op jit(solution)/shard_map/pallas_call | solution.py:813
  286.4 132.9 %shard_map.480 = (f32[128,1024]{1,0:T(8,128)}, f32[1024,1024]{1,0:T(8,128)}, f32[8,1024]{1,0:T(8,128)}, f32[32,8,128]{2,1,0:T(8,128)}) custom-call(bf16[128,1024]{1,0:T(8,128)(2,1)} %add_convert_fusion.2.refs_0_, bf16[1024,1024]{1,0:T(8,128)(2,1)} %get-tuple-element.733, f32[1,1024]{1,0:T(1,128)} %bitcast.287, f32[32,8,128]{2,1,0:T(8,128)} %pad.20.refs_3_), custom_call_target="tpu_custom_call" | custom-call | tf_op jit(solution)/shard_map/pallas_call | solution.py:1114
  425.3 14.9 %shard_map.481 = bf16[2,4,1,128,1024]{4,3,2,1,0:T(8,128)(2,1)S(1)} custom-call(bf16[128,1024]{1,0:T(8,128)(2,1)S(1)} %get-tuple-element.506.refs_0_), custom_call_target="tpu_custom_call" | custom-call | flops 13500000256 | bytes 45000000 | tf_op jit(solution)/shard_map/pallas_call | solution.py:618
  446.8 16.8 %shard_map.482 = f32[128,1024]{1,0:T(8,128)S(1)} custom-call(bf16[2,4,1,128,1024]{4,3,2,1,0:T(8,128)(2,1)S(1)} %bitcast.215), custom_call_target="tpu_custom_call" | custom-call | flops 13500000256 | bytes 45000000 | tf_op jit(solution)/shard_map/pallas_call | solution.py:813
  465.4 3.5 collective-permute-start.5
  471.4 2.6 collective-permute-start.3
  476.1 11.1 %shard_map.483 = (bf16[128,1024]{1,0:T(8,128)(2,1)}, bf16[1024,1024]{1,0:T(8,128)(2,1)}, bf16[1024,1024]{1,0:T(8,128)(2,1)}) custom-call(s32[2]{0:T(128)} %get-tuple-element.519.lengths_ref, bf16[128,1024]{1,0:T(8,128)(2,1)} %fusion.60.q_ref, bf16[1024,2048]{1,0:T(8,128)(2,1)} %add_convert_fusion.k_ref.v_ref, ...), custom_call_target="tpu_custom_call" | custom-call | flops 9900000256 | bytes 33000000 | tf_op jit(solution)/shard_map/pallas_call | solution.py:1223
  487.3 2.7 fusion.56
  492.2 7.6 %multiply_reduce_fusion = (bf16[1024]{0:T(1024)(128)(2,1)S(1)}, f32[1024]{0:T(1024)S(1)}, f32[1024]{0:T(1024)S(1)}, bf16[1024]{0:T(1024)(128)(2,1)S(1)}, f32[1024,1024]{1,0:T(8,128)S(1)}) fusion(f32[1024,1024]{1,0:T(8,128)S(1)} %copy-done.20, f32[1024]{0:T(1024)S(1)} %add_rsqrt_fusion, f32[1024]{0:T(1024)S(1)} %broadcast_multiply_fusion.2, ...), kind=kOutput, calls=%fused_computation.41 | convolution fusion | flops 4313837568 | bytes 20996096 | tf_op jit(solution)/shard_map/dot_general | solution.py:42
  501.2 5.0 fusion.20
  507.6 2.7 reduce_sum.471
  519.1 111.5 %shard_map.484 = (f32[32,1024]{1,0:T(8,128)}, f32[32,1024]{1,0:T(8,128)}, f32[32,640]{1,0:T(8,128)}, f32[32,3072]{1,0:T(8,128)}, bf16[32,48,1024]{2,1,0:T(8,128)(2,1)}, /*index=5*/bf16[8,32,512]{2,1,0:T(8,128)(2,1)}) custom-call(bf16[128,1024]{1,0:T(8,128)(2,1)} %shard_map.477.refs_0_, bf16[128,1024]{1,0:T(8,128)(2,1)} %copy-done.49, ...), custom_call_target="tpu_custom_call" | custom-call | tf_op jit(solution)/shard_map/pallas_call | solution.py:937
  630.7 7.7 %fusion.48 = f32[1024,1024]{1,0:T(8,128)} fusion(f32[1024,1024]{1,0:T(8,128)S(1)} %copy-done.95, bf16[1536,1024]{1,0:T(8,128)(2,1)} %bitcast.295, s32[1536]{0:T(1024)S(1)} %copy-done.87), kind=kOutput, calls=%fused_computation.95 | convolution fusion | flops 3223846912 | bytes 11540480 | tf_op jit(solution)/shard_map/dot_general | solution.py:36
  638.7 3.8 multiply_reduce_fusion.3
  653.2 10.0 %shard_map.485 = f32[32,8,128]{2,1,0:T(8,128)S(1)} custom-call(f32[8,128]{1,0:T(8,128)S(1)} %maximum_bitcast_fusion.1.row_ref), custom_call_target="tpu_custom_call" | custom-call | tf_op jit(solution)/shard_map/pallas_call | solution.py:394
  667.8 2.2 multiply_subtract_fusion.4
  672.0 8.5 %multiply_subtract_fusion = (f32[960,1024]{1,0:T(8,128)}, f32[960,1024]{1,0:T(8,128)}, f32[960,1024]{1,0:T(8,128)}) fusion(f32[960,1024]{1,0:T(8,128)} %param.36, f32[]{:T(128)S(6)} %div.260, f32[1024,1024]{1,0:T(8,128)S(1)} %copy-done.18, f32[960,1024]{1,0:T(8,128)} %param.37, f32[960,1024]{1,0:T(8,128)} %param.38), kind=kLoop, calls=%fused_computation.55 | loop fusion | flops 15728640 | bytes 27525124 | tf_op jit(solution)/shard_map/sub | solution.py:1360
  (378 shorter events, 90.0 us)
Async XLA Ops:
  0.7 209.0 %copy-start = (s32[4,64]{1,0:T(4,128)S(1)}, s32[4,64]{1,0:T(4,128)}, u32[]{:S(2)}) copy-start(s32[4,64]{1,0:T(4,128)} %param.34) | copy-start | bytes 3076
  205.1 32.4 %collective-permute-start = (bf16[1024,512]{1,0:T(8,128)(2,1)}, bf16[1024,512]{1,0:T(8,128)(2,1)}, u32[]{:S(2)}, u32[]{:S(2)}) collective-permute-start(bf16[1024,512]{1,0:T(8,128)(2,1)} %get-tuple-element.521), channel_id=1, source_target_pairs={{0,16},{16,0},{1,17},{17,1},{2,18},{18,2},{3,19},{19,3},{4,20},{20... | collective-permute-start | bytes 3145736 | tf_op jit(solution)/shard_map/ppermute | solution.py:160
  213.6 11.2 %copy-start.31 = (f32[2,64,1024]{2,1,0:T(8,128)}, f32[2,64,1024]{2,1,0:T(8,128)S(1)}, u32[]{:S(2)}) copy-start(f32[2,64,1024]{2,1,0:T(8,128)S(1)} %fusion.103) | copy-start | bytes 1572868
  213.7 12.8 %copy-start.46 = (bf16[128,1024]{1,0:T(8,128)(2,1)}, bf16[128,1024]{1,0:T(8,128)(2,1)S(1)}, u32[]{:S(2)}) copy-start(bf16[128,1024]{1,0:T(8,128)(2,1)S(1)} %bitcast_convert_fusion.refs_2_) | copy-start | bytes 786436
  216.0 9.0 %copy-start.83 = (f32[19,32]{1,0:T(8,128)S(1)}, f32[19,32]{1,0:T(8,128)}, u32[]{:S(2)}) copy-start(f32[19,32]{1,0:T(8,128)} %param.55) | copy-start | bytes 7300
  216.0 9.7 %copy-start.84 = (f32[19,32]{1,0:T(8,128)S(1)}, f32[19,32]{1,0:T(8,128)}, u32[]{:S(2)}) copy-start(f32[19,32]{1,0:T(8,128)} %param.56) | copy-start | bytes 7300
  229.3 8.2 %copy-start.33 = (bf16[1024,512]{1,0:T(8,128)(2,1)S(1)}, bf16[1024,512]{1,0:T(8,128)(2,1)}, u32[]{:S(2)}) copy-start(bf16[1024,512]{1,0:T(8,128)(2,1)} %get-tuple-element.520) | copy-start | bytes 3145732
  241.3 14.7 %copy-start.14 = (bf16[8,4,32,512]{3,2,1,0:T(8,128)(2,1)S(1)}, bf16[8,4,32,512]{3,2,1,0:T(8,128)(2,1)}, u32[]{:S(2)}) copy-start(bf16[8,4,32,512]{3,2,1,0:T(8,128)(2,1)} %copy-done.13) | copy-start | bytes 3145732
  425.3 15.0 %copy-start.55 = (bf16[1024,512]{1,0:T(8,128)(2,1)S(1)}, bf16[1024,512]{1,0:T(8,128)(2,1)}, u32[]{:S(2)}) copy-start(bf16[1024,512]{1,0:T(8,128)(2,1)} %copy-done.54) | copy-start | bytes 3145732
  441.6 22.1 %copy-start.34 = (bf16[512,1024]{1,0:T(8,128)(2,1)}, bf16[512,1024]{1,0:T(8,128)(2,1)S(1)}, u32[]{:S(2)}) copy-start(bf16[512,1024]{1,0:T(8,128)(2,1)S(1)} %convolution_convert_fusion.3) | copy-start | bytes 3145732
  445.5 23.3 %copy-start.48 = (bf16[1024,512]{1,0:T(8,128)(2,1)}, bf16[1024,512]{1,0:T(8,128)(2,1)S(1)}, u32[]{:S(2)}) copy-start(bf16[1024,512]{1,0:T(8,128)(2,1)S(1)} %convolution_convert_fusion.2) | copy-start | bytes 3145732
  464.7 9.9 %copy-start.4 = (bf16[2,4,4,32,1024]{4,3,2,1,0:T(8,128)(2,1)S(1)}, bf16[2,4,4,32,1024]{4,3,2,1,0:T(8,128)(2,1)}, u32[]{:S(2)}) copy-start(bf16[2,4,4,32,1024]{4,3,2,1,0:T(8,128)(2,1)} %copy-done.2) | copy-start | bytes 6291460
  464.7 185.1 %collective-permute-start.4 = (bf16[128,1024]{1,0:T(8,128)(2,1)}, bf16[128,1024]{1,0:T(8,128)(2,1)}, u32[]{:S(2)}, u32[]{:S(2)}) collective-permute-start(bf16[128,1024]{1,0:T(8,128)(2,1)} %get-tuple-element.522), channel_id=1, source_target_pairs={{0,1},{1,2},{2,3},{3,0},{4,5},{5,6},{6,7},{7,4},{8,9},{9,10},{10,1... | collective-permute-start | bytes 786440 | tf_op jit(solution)/shard_map/ppermute | solution.py:1297
  465.4 184.4 %collective-permute-start.5 = (bf16[128,1024]{1,0:T(8,128)(2,1)}, bf16[128,1024]{1,0:T(8,128)(2,1)}, u32[]{:S(2)}, u32[]{:S(2)}) collective-permute-start(bf16[128,1024]{1,0:T(8,128)(2,1)} %get-tuple-element.524), channel_id=1, source_target_pairs={{0,2},{1,3},{2,0},{3,1},{4,6},{5,7},{6,4},{7,5},{8,10},{9,11},{10,... | collective-permute-start | bytes 786440 | tf_op jit(solution)/shard_map/ppermute | solution.py:1297
  469.8 46.6 %collective-permute-start.1 = (bf16[8,32,512]{2,1,0:T(8,128)(2,1)}, bf16[8,32,512]{2,1,0:T(8,128)(2,1)}, u32[]{:S(2)}, u32[]{:S(2)}) collective-permute-start(bf16[8,32,512]{2,1,0:T(8,128)(2,1)} %get-tuple-element.525), channel_id=1, source_target_pairs={{0,1},{1,2},{2,3},{3,0},{4,5},{5,6},{6,7},{7,4},{8,9},{9,10},{10,1... | collective-permute-start | bytes 786440 | tf_op jit(solution)/shard_map/ppermute | solution.py:1297
  469.9 47.1 %collective-permute-start.2 = (bf16[8,32,512]{2,1,0:T(8,128)(2,1)}, bf16[8,32,512]{2,1,0:T(8,128)(2,1)}, u32[]{:S(2)}, u32[]{:S(2)}) collective-permute-start(bf16[8,32,512]{2,1,0:T(8,128)(2,1)} %get-tuple-element.527), channel_id=1, source_target_pairs={{0,2},{1,3},{2,0},{3,1},{4,6},{5,7},{6,4},{7,5},{8,10},{9,11},{10,... | collective-permute-start | bytes 786440 | tf_op jit(solution)/shard_map/ppermute | solution.py:1297
  471.4 45.7 %collective-permute-start.3 = (bf16[8,32,512]{2,1,0:T(8,128)(2,1)}, bf16[8,32,512]{2,1,0:T(8,128)(2,1)}, u32[]{:S(2)}, u32[]{:S(2)}) collective-permute-start(bf16[8,32,512]{2,1,0:T(8,128)(2,1)} %get-tuple-element.526), channel_id=1, source_target_pairs={{0,3},{1,0},{2,1},{3,2},{4,7},{5,4},{6,5},{7,6},{8,11},{9,8},{10,9... | collective-permute-start | bytes 786440 | tf_op jit(solution)/shard_map/ppermute | solution.py:1297
  474.6 12.7 %copy-start.35 = (bf16[128,1024]{1,0:T(8,128)(2,1)}, bf16[128,1024]{1,0:T(8,128)(2,1)S(1)}, u32[]{:S(2)}) copy-start(bf16[128,1024]{1,0:T(8,128)(2,1)S(1)} %get-tuple-element.509.refs_3_) | copy-start | bytes 786436
  516.3 133.4 %collective-permute-start.6 = (bf16[128,1024]{1,0:T(8,128)(2,1)}, bf16[128,1024]{1,0:T(8,128)(2,1)}, u32[]{:S(2)}, u32[]{:S(2)}) collective-permute-start(bf16[128,1024]{1,0:T(8,128)(2,1)} %get-tuple-element.523), channel_id=1, source_target_pairs={{0,3},{1,0},{2,1},{3,2},{4,7},{5,4},{6,5},{7,6},{8,11},{9,8},{10,9... | collective-permute-start | bytes 786440 | tf_op jit(solution)/shard_map/ppermute | solution.py:1297
  519.1 111.5 %copy-start.87 = (s32[1536]{0:T(1024)S(1)}, s32[1536]{0:T(1024)}, u32[]{:S(2)}) copy-start(s32[1536]{0:T(1024)} %sub.209) | copy-start | bytes 18436
  519.1 111.5 %copy-start.95 = (f32[1024,1024]{1,0:T(8,128)S(1)}, f32[1024,1024]{1,0:T(8,128)}, u32[]{:S(2)}) copy-start(f32[1024,1024]{1,0:T(8,128)} %get-tuple-element.273) | copy-start | bytes 12582916
  638.7 7.8 %copy-start.62 = (f32[32,1024]{1,0:T(8,128)S(1)}, f32[32,1024]{1,0:T(8,128)}, u32[]{:S(2)}) copy-start(f32[32,1024]{1,0:T(8,128)} %get-tuple-element.286) | copy-start | bytes 393220
  638.7 7.8 %copy-start.63 = (f32[32,1024]{1,0:T(8,128)S(1)}, f32[32,1024]{1,0:T(8,128)}, u32[]{:S(2)}) copy-start(f32[32,1024]{1,0:T(8,128)} %get-tuple-element.287) | copy-start | bytes 393220
  638.7 9.1 %copy-start.53 = (bf16[8,32,512]{2,1,0:T(8,128)(2,1)S(1)}, bf16[8,32,512]{2,1,0:T(8,128)(2,1)}, u32[]{:S(2)}) copy-start(bf16[8,32,512]{2,1,0:T(8,128)(2,1)} %get-tuple-element.288) | copy-start | bytes 786436
  642.5 22.3 %copy-start.77 = (f32[19,32]{0,1:T(8,128)S(1)}, f32[19,32]{0,1:T(8,128)}, u32[]{:S(2)}) copy-start(f32[19,32]{0,1:T(8,128)} %copy.155) | copy-start | bytes 7300
  649.7 18.0 %copy-start.52 = (f32[2,32,1024]{2,1,0:T(8,128)S(1)}, f32[2,32,1024]{2,1,0:T(8,128)}, u32[]{:S(2)}) copy-start(f32[2,32,1024]{2,1,0:T(8,128)} %param.45) | copy-start | bytes 786436
  671.9 8.5 %copy-start.67 = (f32[30522]{0:T(1024)S(1)}, f32[30522]{0:T(1024)}, u32[]{:S(2)}) copy-start(f32[30522]{0:T(1024)} %param.57) | copy-start | bytes 366268
  671.9 8.5 %copy-start.75 = (f32[30522]{0:T(1024)S(1)}, f32[30522]{0:T(1024)}, u32[]{:S(2)}) copy-start(f32[30522]{0:T(1024)} %param.58) | copy-start | bytes 366268
  671.9 8.5 %copy-start.76 = (f32[30522]{0:T(1024)S(1)}, f32[30522]{0:T(1024)}, u32[]{:S(2)}) copy-start(f32[30522]{0:T(1024)} %param.59) | copy-start | bytes 366268
  671.9 9.4 %copy-start.41 = (f32[128,1024]{1,0:T(8,128)S(1)}, f32[128,1024]{1,0:T(8,128)}, u32[]{:S(2)}) copy-start(f32[128,1024]{1,0:T(8,128)} %param.51) | copy-start | bytes 1572868
  671.9 9.4 %copy-start.60 = (f32[128,1024]{1,0:T(8,128)S(1)}, f32[128,1024]{1,0:T(8,128)}, u32[]{:S(2)}) copy-start(f32[128,1024]{1,0:T(8,128)} %param.52) | copy-start | bytes 1572868
  672.0 9.3 %copy-start.61 = (f32[128,1024]{1,0:T(8,128)S(1)}, f32[128,1024]{1,0:T(8,128)}, u32[]{:S(2)}) copy-start(f32[128,1024]{1,0:T(8,128)} %param.53) | copy-start | bytes 1572868
  (72 other events, 263.7 us)

commit v7 on v6

--- a/solution.py
+++ b/solution.py
@@ -171,11 +171,12 @@
 
 def both_halves(rows):
     pipe = lax.axis_index("pipe")
-    return jnp.concatenate([half_columns(rows, pipe), swapped(half_columns(rows, 1 - pipe))], 0)
+    return half_columns(rows, pipe), swapped(half_columns(rows, 1 - pipe))
 
 
 def chip_sum(left, right):
-    return left_transposed(both_halves(left), both_cores(right)).astype(jnp.bfloat16)
+    left = jnp.concatenate(both_halves(left), 0)
+    return left_transposed(left, both_cores(right)).astype(jnp.bfloat16)
 
 
 def chip_half(partial):
@@ -539,6 +540,9 @@
                 keep.wait()
 
 
+LINE_TURN = 3
+
+
 class LineGather(Gather):
     def __init__(self, place, shards, fulls, axes, send, arrive, own):
         super().__init__(place, [(n, 0, 0) for n in range(len(shards))], shards, fulls, send, arrive, own)
@@ -583,8 +587,8 @@
 
     def after(turn):
         for n in range(lines):
-            if 0 <= turn - n <= gather.hops:
-                line.over_line(n, turn - n)
+            if 0 <= turn - n - LINE_TURN <= gather.hops:
+                line.over_line(n, turn - n - LINE_TURN)
         if turn == len(pieces) and routed:
             swaps.append(
                 swap_all(place, rows_ref, arrived_ref, swap_send, swap_arrive, swap_own)
@@ -619,7 +623,7 @@
         functools.partial(gather_kernel, sizes, tuple(pieces), tuple(axes), routed),
         out_shape=out_shape,
         in_specs=[near] * len(operands),
-        out_specs=[near] * len(out_shape),
+        out_specs=[near] + [pl.BlockSpec(memory_space=pltpu.HBM)] * (len(out_shape) - 1),
         scratch_shapes=[
             sems,
             sems,
@@ -824,9 +828,9 @@
 
 
 def finish_kernel(sizes, *refs):
-    lefts, rights, start, talls, refs = refs[:3], refs[3:6], refs[6], refs[7:9], refs[9:]
+    lefts, rights, starts, talls, refs = refs[:3], refs[3:6], refs[6:8], refs[8:10], refs[10:]
     small, rows_ref, blocks_ref, refs = refs[0], refs[1], refs[2], refs[3:]
-    outs, arrived_ref, blocks_arrived_ref, refs = refs[:4], refs[4], refs[5], refs[6:]
+    outs, squares, arrived_ref, blocks_arrived_ref, refs = refs[:4], *refs[4:7], refs[7:]
     cores = (False, False, True, False, False, False)
     scratch, refs = sum_refs(refs, cores)
     other_lefts, other_rights, other_talls, made, refs = (
@@ -851,7 +855,10 @@
         )
         exchanged[i].start()
 
+    squares[...] = jnp.zeros_like(squares)
+
     def store(n, at, total):
+        squares[0:1, 0 : total.shape[1]] += jnp.sum(total * total, 0, keepdims=True)
         if n < 3:
             outs[n][at] = total
         else:
@@ -878,11 +885,10 @@
 
     def form_tall(i):
         exchanged[6 + i].wait_recv()
-        tokens = talls[i].shape[0]
         for g in range(place.grps):
             at = pl.ds(g * wide, wide)
-            total = left_transposed(start[0:tokens, at], talls[i][...])
-            total = total + left_transposed(start[tokens:, at], other_talls[i][...])
+            total = left_transposed(starts[0][:, at], talls[i][...])
+            total = total + left_transposed(starts[1][:, at], other_talls[i][...])
             made[3 + i][g] = total.astype(jnp.bfloat16).reshape(made[3 + i].shape[1:])
 
     form(0)
@@ -917,7 +923,7 @@
     swap()
 
 
-def finish_all(lefts, rights, start, talls, small, rows, blocks, sizes, collective):
+def finish_all(lefts, rights, starts, talls, small, rows, blocks, sizes, collective):
     low = jnp.bfloat16
     parts = math.prod(sizes)
     _, grps, dps = sizes
@@ -930,15 +936,18 @@
     swaps = pltpu.SemaphoreType.DMA((parts - 1,))
     plane_swaps = pltpu.SemaphoreType.DMA((sizes[0] * grps - 1,))
     one = pltpu.SemaphoreType.DMA
-    operands = (*lefts, *rights, start, *talls, small, rows, blocks)
+    operands = (*lefts, *rights, *starts, *talls, small, rows, blocks)
     joined = (shape[0], 3 * shape[1])
-    out_shape = [jax.ShapeDtypeStruct(shape, jnp.float32) for shape in shapes[:3] + [joined]]
+    widest = (8, max(shape[1] for shape in shapes))
+    out_shape = [
+        jax.ShapeDtypeStruct(shape, jnp.float32) for shape in shapes[:3] + [joined, widest]
+    ]
     out_shape += [jax.ShapeDtypeStruct(extra.shape, extra.dtype) for extra in (rows, blocks)]
     return pl.pallas_call(
         functools.partial(finish_kernel, sizes),
         out_shape=out_shape,
-        in_specs=[near] * 9 + [anywhere, near, near],
-        out_specs=[near] * 6,
+        in_specs=[near] * 10 + [anywhere, near, near],
+        out_specs=[near] * 7,
         scratch_shapes=sum_scratch(shapes, (False, False, True, False, False, False), sizes)
         + [pltpu.VMEM(item.shape, low) for item in (*lefts, *rights, *talls)]
         + [made] * 5
@@ -1272,24 +1281,26 @@
     return reduce_all(shaped, [(i * size, size) for i in range(cuts)], sizes, collective)
 
 
-def sum_chips(lefts, rights, start, talls, small, rows, blocks, sizes, collective):
+def sum_chips(lefts, rights, starts, talls, small, rows, blocks, sizes, collective):
     if collective is not None:
         small = small.reshape(sizes + (-1, small.shape[1]))
-        *sums, rows, blocks = finish_all(
-            lefts, rights, start, talls, small, rows, blocks, sizes, collective
+        *sums, squares, rows, blocks = finish_all(
+            lefts, rights, starts, talls, small, rows, blocks, sizes, collective
         )
-        return sums, rows, blocks
+        return sums, jnp.sum(squares), rows, blocks
     made = [chip_sum(left, right) for left, right in zip(lefts, rights)]
+    start = jnp.concatenate(starts, 0)
     made += [left_transposed(start, both_cores(tall)).astype(jnp.bfloat16) for tall in talls]
     partials = made[:2] + [chip_half(small)] + made[2:]
     sums = [
         lax.psum_scatter(p, CHIPS, scatter_dimension=0, tiled=True).astype(jnp.float32)
         for p in partials
     ]
+    squares = sum(jnp.sum(total * total) for total in sums)
     sums = sums[:3] + [jnp.concatenate(sums[3:], 1)]
     rows = lax.all_to_all(rows, AXES, 0, 0)
     blocks = lax.all_to_all(blocks, PLANE, 0, 0)
-    return sums, rows, blocks
+    return sums, squares, rows, blocks
 
 
 def line_shift(shard, step):
@@ -1445,7 +1456,7 @@
         square_weight[1].astype(narrow),
     ]
     deep = small_low.shape[0]
-    pieces = [(0, 0, deep), (1, 0, deep // 2), (1, deep // 2, deep // 2), (2, 0, deep), (3, 0, deep)]
+    pieces = [(i, 0, deep) for i in range(4)]
     send = routes.table_rows(word_low, 0, routes.room).reshape(parts, -1, width)
     (small_full, qkv_low, out_low, turn_low), (up_low, down_low), arrived = gather_weights(
         low, pieces, [blocks, down_weight.astype(narrow)], [1, 0], sizes, ids[1], send
@@ -1471,10 +1482,10 @@
     pick = one_hot(masked, seq_len, jnp.float32)
     chosen = rows_by_seq(pick, start.reshape(own, seq_len, width)).reshape(-1, width)
     chosen_low = chosen.astype(narrow)
-    start_half = both_halves(start_low)
+    start_own, start_other = both_halves(start_low)
     queries = (matmul(chosen_low, query_low) + vec_rows[4]).astype(narrow)
     context = attention(own_lengths, queries, both)
-    context, start_half = lax.optimization_barrier((context, start_half))
+    context, start_other = lax.optimization_barrier((context, start_other))
     branch = matmul(context, out_low) + vec_rows[6]
     hidden, norm_one = norm_forward(chosen + branch, vec_rows[7], vec_rows[8])
     hidden = hidden.astype(narrow)
@@ -1580,10 +1591,10 @@
         ],
         0,
     )
-    (own_out, own_turn, own_small, own_qkv), arrived, up_blocks = sum_chips(
+    (own_out, own_turn, own_small, own_qkv), squares, arrived, up_blocks = sum_chips(
         [context, picked, chosen_low],
         [d_attended, d_turned, d_query],
-        start_half,
+        [start_own, start_other],
         [d_key, d_value],
         d_small.T.astype(narrow),
         send,
@@ -1602,8 +1613,8 @@
         own_down,
         own_small[:, seq_len:small].T,
     )
-    local_squares = jnp.sum(d_bias * d_bias)
-    for grad in owned:
+    local_squares = squares + jnp.sum(d_bias * d_bias)
+    for grad in (d_word, own_up, own_down):
         local_squares = local_squares + jnp.sum(grad * grad)
     spare = -(rows_per + 1) % 128
     last = jnp.concatenate([d_bias, local_squares[None], jnp.zeros((spare,), jnp.float32)])

time: 695 us -> 673 us (0.968)
  Pallas kernels: 489 us -> 472 us
    pallas_call x3, Pallas kernels: 167 us -> 150 us  [gather_all(): pl.pallas_call(functools.partial(gather_kernel, sizes, tuple(pieces), tup...]
  transfers between devices with their start and end apart: 7 -> 7, of which waited for: 0 -> 0; matrix products, arithmetic and copies ran while one was open for 10% -> 10% of each run, Pallas kernels for 19% -> 20%
where the time goes in v7:
time: 673 us; the launch traced here: 664 us
  Pallas kernels  472 us (70%)
  matrix products  72.1 us (11%)
  other arithmetic  64.2 us (10%)
  local copies, waits for them, and re-layouts  35.6 us (5%)
  between operations  10.2 us (2%)
  starting transfers between devices  9.58 us (1%)
    pallas_call x3, Pallas kernels, gather_all(): pl.pallas_call(functools.partial(gather_kernel, sizes, tuple(pieces), tup...  150 us
    pallas_call x1, Pallas kernels, head_all(): pl.pallas_call(functools.partial(head_kernel, sizes, rows_per, vocab, gat...  133 us
    pallas_call x1, Pallas kernels, finish_all(): pl.pallas_call(functools.partial(finish_kernel, sizes), out_shape=out_sha...  111 us
    pallas_call x2, Pallas kernels, reduce_all(): pl.pallas_call(functools.partial(reduce_kernel, sizes, tuple(pieces)), ou...  34.6 us
    dot_general x9, matrix products, matmul(): return jnp.dot(left, right, preferred_element_type=jnp.float32)  34.2 us
    unnamed x211, local copies, waits for them, and re-layouts  19.6 us
    sub x8, other arithmetic, adam_step(): weight - rate * (first_hat / (jnp.sqrt(second_hat) + epsilon) + weight_de...  16.8 us
    dot_general x6, matrix products, right_transposed(): lax.dot_general(left, right, (((1,), (1,)), ((), ())), preferred_element_...  15.9 us
  transfers between devices with their start and end apart: 7, of which 0 were waited for; matrix products, arithmetic and copies ran while one was open for 10% of the time, Pallas kernels for 20%

profile of v7, /device:TPU:0, one launch (start us, length us, event | category | flops | bytes accessed | tf_op | source)
XLA Modules:
  0.0 664.1 jit_solution(2254441196598220897)
XLA Ops:
  3.4 13.9 %shard_map.475 = (s32[32,2,640]{2,1,0:T(2,128)S(1)}, bf16[8,32,512]{2,1,0:T(8,128)(2,1)S(1)}) custom-call(s32[2,640]{1,0:T(2,128)S(1)} %fusion.125.row_ref, bf16[8,32,512]{2,1,0:T(8,128)(2,1)S(1)} %bitcast.210), custom_call_target="tpu_custom_call" | custom-call | tf_op jit(solution)/shard_map/pallas_call | solution.py:351
  23.2 2.5 convert_element_type.238
  26.6 5.6 fusion.21
  33.8 121.6 %shard_map.476 = (bf16[2,4,4,32,640]{4,3,2,1,0:T(8,128)(2,1)S(1)}, bf16[2,4,4,32,3072]{4,3,2,1,0:T(8,128)(2,1)}, bf16[2,4,4,32,1024]{4,3,2,1,0:T(8,128)(2,1)S(1)...) custom-call(bf16[32,640]{1,0:T(8,128)(2,1)S(1)} %maximum_maximum_fus, ...), custom_call_target="tpu_custom_call" | custom-call | flops 99000000512 | bytes 330000000 | tf_op jit(solution)/shard_map/pallas_call | solution.py:622
  163.2 2.9 slice_convert_fusion
  170.0 5.3 fusion.11
  176.9 3.2 fusion.151
  182.2 5.0 fusion.150
  193.4 4.0 fusion.103
  199.8 8.8 %add_convert_fusion.k_ref.v_ref = bf16[1024,2048]{1,0:T(8,128)(2,1)} fusion(f32[2048]{0:T(1024)S(1)} %concatenate.23, bf16[1024,1024]{1,0:T(8,128)(2,1)S(1)} %get-tuple-element.516, bf16[1024,3072]{1,0:T(8,128)(2,1)} %bitcast.294), kind=kOutput, calls=%fused_computation.24 | convolution fusion | flops 4299161600 | bytes 10493952 | tf_op jit(solution)/shard_map/dot_general | solution.py:32
  210.2 2.8 fusion.60.q_ref
  213.0 8.2 %shard_map.477.refs_0_ = bf16[128,1024]{1,0:T(8,128)(2,1)} custom-call(s32[2]{0:T(128)} %get-tuple-element.521.lengths_ref, bf16[128,1024]{1,0:T(8,128)(2,1)} %fusion.60.q_ref, bf16[1024,2048]{1,0:T(8,128)(2,1)} %add_convert_fusion.k_ref.v_ref, bf16[1024,2048]{1,0:T(8,128)(2,1)} %add_convert_fusion.k_ref.v_ref), custom_call_target="tpu_custom_call" | custom-call | flops 7200000000 | bytes 24000000 | tf_op jit(solution)/shard_map/pallas_call | solution.py:1224
  223.3 14.6 %shard_map.478 = bf16[2,4,1,128,1024]{4,3,2,1,0:T(8,128)(2,1)S(1)} custom-call(bf16[128,1024]{1,0:T(8,128)(2,1)S(1)} %add_convert_fusion.4.refs_0_), custom_call_target="tpu_custom_call" | custom-call | flops 13500000256 | bytes 45000000 | tf_op jit(solution)/shard_map/pallas_call | solution.py:622
  237.9 6.5 fusion.30
  245.7 16.5 %shard_map.479 = f32[128,1024]{1,0:T(8,128)S(1)} custom-call(bf16[2,4,1,128,1024]{4,3,2,1,0:T(8,128)(2,1)S(1)} %bitcast.216), custom_call_target="tpu_custom_call" | custom-call | flops 13500000256 | bytes 45000000 | tf_op jit(solution)/shard_map/pallas_call | solution.py:817
  267.7 133.1 %shard_map.480 = (f32[128,1024]{1,0:T(8,128)}, f32[1024,1024]{1,0:T(8,128)}, f32[8,1024]{1,0:T(8,128)}, f32[32,8,128]{2,1,0:T(8,128)}) custom-call(bf16[128,1024]{1,0:T(8,128)(2,1)} %add_convert_fusion.2.refs_0_, bf16[1024,1024]{1,0:T(8,128)(2,1)} %get-tuple-element.735, f32[1,1024]{1,0:T(1,128)} %bitcast.285, f32[32,8,128]{2,1,0:T(8,128)} %pad.20.refs_3_), custom_call_target="tpu_custom_call" | custom-call | tf_op jit(solution)/shard_map/pallas_call | solution.py:1123
  406.8 13.6 %shard_map.481 = bf16[2,4,1,128,1024]{4,3,2,1,0:T(8,128)(2,1)S(1)} custom-call(bf16[128,1024]{1,0:T(8,128)(2,1)S(1)} %get-tuple-element.508.refs_0_), custom_call_target="tpu_custom_call" | custom-call | flops 13500000256 | bytes 45000000 | tf_op jit(solution)/shard_map/pallas_call | solution.py:622
  422.3 2.0 convert_reduce_fusion.1
  426.9 18.1 %shard_map.482 = f32[128,1024]{1,0:T(8,128)S(1)} custom-call(bf16[2,4,1,128,1024]{4,3,2,1,0:T(8,128)(2,1)S(1)} %bitcast.215), custom_call_target="tpu_custom_call" | custom-call | flops 13500000256 | bytes 45000000 | tf_op jit(solution)/shard_map/pallas_call | solution.py:817
  446.8 2.8 collective-permute-start.5
  452.1 2.5 collective-permute-start.3
  456.8 11.1 %shard_map.483 = (bf16[128,1024]{1,0:T(8,128)(2,1)}, bf16[1024,1024]{1,0:T(8,128)(2,1)}, bf16[1024,1024]{1,0:T(8,128)(2,1)}) custom-call(s32[2]{0:T(128)} %get-tuple-element.521.lengths_ref, bf16[128,1024]{1,0:T(8,128)(2,1)} %fusion.60.q_ref, bf16[1024,2048]{1,0:T(8,128)(2,1)} %add_convert_fusion.k_ref.v_ref, ...), custom_call_target="tpu_custom_call" | custom-call | flops 9900000256 | bytes 33000000 | tf_op jit(solution)/shard_map/pallas_call | solution.py:1232
  467.9 2.7 fusion.56
  472.9 7.6 %multiply_reduce_fusion = (bf16[1024]{0:T(1024)(128)(2,1)S(1)}, f32[1024]{0:T(1024)S(1)}, f32[1024]{0:T(1024)S(1)}, bf16[1024]{0:T(1024)(128)(2,1)S(1)}, f32[1024,1024]{1,0:T(8,128)S(1)}) fusion(f32[1024,1024]{1,0:T(8,128)S(1)} %copy-done.19, f32[1024]{0:T(1024)S(1)} %add_rsqrt_fusion, f32[1024]{0:T(1024)S(1)} %broadcast_multiply_fusion.2, ...), kind=kOutput, calls=%fused_computation.41 | convolution fusion | flops 4313837568 | bytes 20996096 | tf_op jit(solution)/shard_map/dot_general | solution.py:42
  481.9 5.0 fusion.20
  488.3 2.7 reduce_sum.444
  498.5 2.0 fusion.91.refs_12_
  500.6 111.5 %shard_map.484 = (f32[32,1024]{1,0:T(8,128)}, f32[32,1024]{1,0:T(8,128)}, f32[32,640]{1,0:T(8,128)}, f32[32,3072]{1,0:T(8,128)}, f32[8,1024]{1,0:T(8,128)}, /*in...) custom-call(bf16[128,1024]{1,0:T(8,128)(2,1)} %shard_map.477.refs_0_, bf16[128,1024]{1,0:T(8,128)(2,1)} %copy-done.44, ...), custom_call_target="tpu_custom_call" | custom-call | tf_op jit(solution)/shard_map/pallas_call | solution.py:946
  612.1 7.7 %fusion.48 = f32[1024,1024]{1,0:T(8,128)} fusion(f32[1024,1024]{1,0:T(8,128)S(1)} %copy-done.95, bf16[1536,1024]{1,0:T(8,128)(2,1)} %bitcast.293, s32[1536]{0:T(1024)S(1)} %copy-done.87), kind=kOutput, calls=%fused_computation.94 | convolution fusion | flops 3223846912 | bytes 11540480 | tf_op jit(solution)/shard_map/dot_general | solution.py:36
  620.1 3.8 multiply_reduce_fusion.3
  630.6 9.8 %shard_map.485 = f32[32,8,128]{2,1,0:T(8,128)S(1)} custom-call(f32[8,128]{1,0:T(8,128)S(1)} %maximum_bitcast_fusion.1.row_ref), custom_call_target="tpu_custom_call" | custom-call | tf_op jit(solution)/shard_map/pallas_call | solution.py:395
  644.9 10.2 %multiply_subtract_fusion = (f32[960,1024]{1,0:T(8,128)}, f32[960,1024]{1,0:T(8,128)}, f32[960,1024]{1,0:T(8,128)}) fusion(f32[960,1024]{1,0:T(8,128)} %param.36, f32[]{:T(128)S(6)} %div.260, f32[1024,1024]{1,0:T(8,128)} %get-tuple-element.283, f32[960,1024]{1,0:T(8,128)} %param.37, f32[960,1024]{1,0:T(8,128)} %param.38), kind=kLoop, calls=%fused_computation.55 | loop fusion | flops 15728640 | bytes 27525124 | tf_op jit(solution)/shard_map/sub | solution.py:1371
  (374 shorter events, 86.4 us)
Async XLA Ops:
  0.7 192.7 %copy-start = (s32[4,64]{1,0:T(4,128)S(1)}, s32[4,64]{1,0:T(4,128)}, u32[]{:S(2)}) copy-start(s32[4,64]{1,0:T(4,128)} %param.34) | copy-start | bytes 3076
  188.8 32.4 %collective-permute-start = (bf16[1024,512]{1,0:T(8,128)(2,1)}, bf16[1024,512]{1,0:T(8,128)(2,1)}, u32[]{:S(2)}, u32[]{:S(2)}) collective-permute-start(bf16[1024,512]{1,0:T(8,128)(2,1)} %get-tuple-element.523), channel_id=1, source_target_pairs={{0,16},{16,0},{1,17},{17,1},{2,18},{18,2},{3,19},{19,3},{4,20},{20... | collective-permute-start | bytes 3145736 | tf_op jit(solution)/shard_map/ppermute | solution.py:160
  197.3 11.2 %copy-start.30 = (f32[2,64,1024]{2,1,0:T(8,128)}, f32[2,64,1024]{2,1,0:T(8,128)S(1)}, u32[]{:S(2)}) copy-start(f32[2,64,1024]{2,1,0:T(8,128)S(1)} %fusion.103) | copy-start | bytes 1572868
  197.4 12.9 %copy-start.42 = (bf16[128,1024]{1,0:T(8,128)(2,1)}, bf16[128,1024]{1,0:T(8,128)(2,1)S(1)}, u32[]{:S(2)}) copy-start(bf16[128,1024]{1,0:T(8,128)(2,1)S(1)} %bitcast_convert_fusion.refs_2_) | copy-start | bytes 786436
  199.8 9.7 %copy-start.84 = (f32[19,32]{1,0:T(8,128)S(1)}, f32[19,32]{1,0:T(8,128)}, u32[]{:S(2)}) copy-start(f32[19,32]{1,0:T(8,128)} %param.56) | copy-start | bytes 7300
  223.3 14.6 %copy-start.14 = (bf16[8,4,32,512]{3,2,1,0:T(8,128)(2,1)S(1)}, bf16[8,4,32,512]{3,2,1,0:T(8,128)(2,1)}, u32[]{:S(2)}) copy-start(bf16[8,4,32,512]{3,2,1,0:T(8,128)(2,1)} %copy-done.13) | copy-start | bytes 3145732
  406.8 13.6 %copy-start.50 = (bf16[1024,512]{1,0:T(8,128)(2,1)S(1)}, bf16[1024,512]{1,0:T(8,128)(2,1)}, u32[]{:S(2)}) copy-start(bf16[1024,512]{1,0:T(8,128)(2,1)} %copy-done.49) | copy-start | bytes 3145732
  421.7 23.5 %copy-start.31 = (bf16[512,1024]{1,0:T(8,128)(2,1)}, bf16[512,1024]{1,0:T(8,128)(2,1)S(1)}, u32[]{:S(2)}) copy-start(bf16[512,1024]{1,0:T(8,128)(2,1)S(1)} %convolution_convert_fusion.3) | copy-start | bytes 3145732
  425.6 23.9 %copy-start.43 = (bf16[1024,512]{1,0:T(8,128)(2,1)}, bf16[1024,512]{1,0:T(8,128)(2,1)S(1)}, u32[]{:S(2)}) copy-start(bf16[1024,512]{1,0:T(8,128)(2,1)S(1)} %convolution_convert_fusion.2) | copy-start | bytes 3145732
  446.1 9.2 %copy-start.4 = (bf16[2,4,4,32,1024]{4,3,2,1,0:T(8,128)(2,1)S(1)}, bf16[2,4,4,32,1024]{4,3,2,1,0:T(8,128)(2,1)}, u32[]{:S(2)}) copy-start(bf16[2,4,4,32,1024]{4,3,2,1,0:T(8,128)(2,1)} %copy-done.2) | copy-start | bytes 6291460
  446.1 181.8 %collective-permute-start.4 = (bf16[128,1024]{1,0:T(8,128)(2,1)}, bf16[128,1024]{1,0:T(8,128)(2,1)}, u32[]{:S(2)}, u32[]{:S(2)}) collective-permute-start(bf16[128,1024]{1,0:T(8,128)(2,1)} %get-tuple-element.524), channel_id=1, source_target_pairs={{0,1},{1,2},{2,3},{3,0},{4,5},{5,6},{6,7},{7,4},{8,9},{9,10},{10,1... | collective-permute-start | bytes 786440 | tf_op jit(solution)/shard_map/ppermute | solution.py:1308
  446.8 181.1 %collective-permute-start.5 = (bf16[128,1024]{1,0:T(8,128)(2,1)}, bf16[128,1024]{1,0:T(8,128)(2,1)}, u32[]{:S(2)}, u32[]{:S(2)}) collective-permute-start(bf16[128,1024]{1,0:T(8,128)(2,1)} %get-tuple-element.526), channel_id=1, source_target_pairs={{0,2},{1,3},{2,0},{3,1},{4,6},{5,7},{6,4},{7,5},{8,10},{9,11},{10,... | collective-permute-start | bytes 786440 | tf_op jit(solution)/shard_map/ppermute | solution.py:1308
  450.4 46.6 %collective-permute-start.1 = (bf16[8,32,512]{2,1,0:T(8,128)(2,1)}, bf16[8,32,512]{2,1,0:T(8,128)(2,1)}, u32[]{:S(2)}, u32[]{:S(2)}) collective-permute-start(bf16[8,32,512]{2,1,0:T(8,128)(2,1)} %get-tuple-element.527), channel_id=1, source_target_pairs={{0,1},{1,2},{2,3},{3,0},{4,5},{5,6},{6,7},{7,4},{8,9},{9,10},{10,1... | collective-permute-start | bytes 786440 | tf_op jit(solution)/shard_map/ppermute | solution.py:1308
  451.4 47.1 %collective-permute-start.2 = (bf16[8,32,512]{2,1,0:T(8,128)(2,1)}, bf16[8,32,512]{2,1,0:T(8,128)(2,1)}, u32[]{:S(2)}, u32[]{:S(2)}) collective-permute-start(bf16[8,32,512]{2,1,0:T(8,128)(2,1)} %get-tuple-element.529), channel_id=1, source_target_pairs={{0,2},{1,3},{2,0},{3,1},{4,6},{5,7},{6,4},{7,5},{8,10},{9,11},{10,... | collective-permute-start | bytes 786440 | tf_op jit(solution)/shard_map/ppermute | solution.py:1308
  452.1 46.4 %collective-permute-start.3 = (bf16[8,32,512]{2,1,0:T(8,128)(2,1)}, bf16[8,32,512]{2,1,0:T(8,128)(2,1)}, u32[]{:S(2)}, u32[]{:S(2)}) collective-permute-start(bf16[8,32,512]{2,1,0:T(8,128)(2,1)} %get-tuple-element.528), channel_id=1, source_target_pairs={{0,3},{1,0},{2,1},{3,2},{4,7},{5,4},{6,5},{7,6},{8,11},{9,8},{10,9... | collective-permute-start | bytes 786440 | tf_op jit(solution)/shard_map/ppermute | solution.py:1308
  455.2 12.7 %copy-start.32 = (bf16[128,1024]{1,0:T(8,128)(2,1)}, bf16[128,1024]{1,0:T(8,128)(2,1)S(1)}, u32[]{:S(2)}) copy-start(bf16[128,1024]{1,0:T(8,128)(2,1)S(1)} %get-tuple-element.511.refs_3_) | copy-start | bytes 786436
  497.0 130.8 %collective-permute-start.6 = (bf16[128,1024]{1,0:T(8,128)(2,1)}, bf16[128,1024]{1,0:T(8,128)(2,1)}, u32[]{:S(2)}, u32[]{:S(2)}) collective-permute-start(bf16[128,1024]{1,0:T(8,128)(2,1)} %get-tuple-element.525), channel_id=1, source_target_pairs={{0,3},{1,0},{2,1},{3,2},{4,7},{5,4},{6,5},{7,6},{8,11},{9,8},{10,9... | collective-permute-start | bytes 786440 | tf_op jit(solution)/shard_map/ppermute | solution.py:1308
  500.5 111.5 %copy-start.87 = (s32[1536]{0:T(1024)S(1)}, s32[1536]{0:T(1024)}, u32[]{:S(2)}) copy-start(s32[1536]{0:T(1024)} %sub.209) | copy-start | bytes 18436
  500.6 111.5 %copy-start.95 = (f32[1024,1024]{1,0:T(8,128)S(1)}, f32[1024,1024]{1,0:T(8,128)}, u32[]{:S(2)}) copy-start(f32[1024,1024]{1,0:T(8,128)} %get-tuple-element.274) | copy-start | bytes 12582916
  623.9 18.2 %copy-start.73 = (f32[32,640]{1,0:T(8,128)S(1)}, f32[32,640]{1,0:T(8,128)}, u32[]{:S(2)}) copy-start(f32[32,640]{1,0:T(8,128)} %get-tuple-element.288) | copy-start | bytes 245764
  623.9 18.2 %copy-start.74 = (f32[19,32]{0,1:T(8,128)S(1)}, f32[19,32]{0,1:T(8,128)}, u32[]{:S(2)}) copy-start(f32[19,32]{0,1:T(8,128)} %copy.155) | copy-start | bytes 7300
  623.9 18.2 %copy-start.75 = (f32[19,32]{0,1:T(8,128)S(1)}, f32[19,32]{0,1:T(8,128)}, u32[]{:S(2)}) copy-start(f32[19,32]{0,1:T(8,128)} %copy.151) | copy-start | bytes 7300
  623.9 18.2 %copy-start.76 = (f32[19,32]{0,1:T(8,128)S(1)}, f32[19,32]{0,1:T(8,128)}, u32[]{:S(2)}) copy-start(f32[19,32]{0,1:T(8,128)} %copy.153) | copy-start | bytes 7300
  627.8 16.3 %copy-start.65 = (f32[512,32]{0,1:T(8,128)S(1)}, f32[512,32]{0,1:T(8,128)}, u32[]{:S(2)}) copy-start(f32[512,32]{0,1:T(8,128)} %param.39) | copy-start | bytes 196612
  627.8 16.3 %copy-start.78 = (f32[512,32]{0,1:T(8,128)S(1)}, f32[512,32]{0,1:T(8,128)}, u32[]{:S(2)}) copy-start(f32[512,32]{0,1:T(8,128)} %param.40) | copy-start | bytes 196612
  627.8 16.3 %copy-start.79 = (f32[512,32]{0,1:T(8,128)S(1)}, f32[512,32]{0,1:T(8,128)}, u32[]{:S(2)}) copy-start(f32[512,32]{0,1:T(8,128)} %param.41) | copy-start | bytes 196612
  644.9 10.2 %copy-start.60 = (f32[30522]{0:T(1024)S(1)}, f32[30522]{0:T(1024)}, u32[]{:S(2)}) copy-start(f32[30522]{0:T(1024)} %param.57) | copy-start | bytes 366268
  644.9 10.2 %copy-start.71 = (f32[30522]{0:T(1024)S(1)}, f32[30522]{0:T(1024)}, u32[]{:S(2)}) copy-start(f32[30522]{0:T(1024)} %param.58) | copy-start | bytes 366268
  644.9 10.2 %copy-start.72 = (f32[30522]{0:T(1024)S(1)}, f32[30522]{0:T(1024)}, u32[]{:S(2)}) copy-start(f32[30522]{0:T(1024)} %param.59) | copy-start | bytes 366268
  644.9 11.1 %copy-start.38 = (f32[128,1024]{1,0:T(8,128)S(1)}, f32[128,1024]{1,0:T(8,128)}, u32[]{:S(2)}) copy-start(f32[128,1024]{1,0:T(8,128)} %param.51) | copy-start | bytes 1572868
  644.9 11.1 %copy-start.55 = (f32[128,1024]{1,0:T(8,128)S(1)}, f32[128,1024]{1,0:T(8,128)}, u32[]{:S(2)}) copy-start(f32[128,1024]{1,0:T(8,128)} %param.52) | copy-start | bytes 1572868
  644.9 11.1 %copy-start.56 = (f32[128,1024]{1,0:T(8,128)S(1)}, f32[128,1024]{1,0:T(8,128)}, u32[]{:S(2)}) copy-start(f32[128,1024]{1,0:T(8,128)} %param.53) | copy-start | bytes 1572868
  (72 other events, 250.3 us)

commit v8 on v7

--- a/solution.py
+++ b/solution.py
@@ -636,7 +636,9 @@
             pltpu.SemaphoreType.DMA,
         ],
         compiler_params=pltpu.CompilerParams(
-            collective_id=collective, has_side_effects=True, vmem_limit_bytes=40 << 20
+            collective_id=collective,
+            has_side_effects=True,
+            vmem_limit_bytes=(60 if routed else 16) << 20,
         ),
         cost_estimate=lasting(110 if routed else 15),
     )(*operands)

time: 673 us -> 674 us (level)
    unnamed x211 -> x207, local copies, waits for them, and re-layouts: 19.6 us -> 9.95 us
  transfers between devices with their start and end apart: 7 -> 7, of which waited for: 0 -> 0; matrix products, arithmetic and copies ran while one was open for 10% -> 11% of each run, Pallas kernels for 20% -> 20%
where the time goes in v8:
time: 674 us; the launch traced here: 666 us
  Pallas kernels  474 us (70%)
  matrix products  73.8 us (11%)
  other arithmetic  68 us (10%)
  local copies, waits for them, and re-layouts  30.2 us (4%)
  between operations  10.3 us (2%)
  starting transfers between devices  9.58 us (1%)
    pallas_call x3, Pallas kernels, gather_all(): pl.pallas_call(functools.partial(gather_kernel, sizes, tuple(pieces), tup...  152 us
    pallas_call x1, Pallas kernels, head_all(): pl.pallas_call(functools.partial(head_kernel, sizes, rows_per, vocab, gat...  133 us
    pallas_call x1, Pallas kernels, finish_all(): pl.pallas_call(functools.partial(finish_kernel, sizes), out_shape=out_sha...  111 us
    dot_general x9, matrix products, matmul(): return jnp.dot(left, right, preferred_element_type=jnp.float32)  36 us
    pallas_call x2, Pallas kernels, reduce_all(): pl.pallas_call(functools.partial(reduce_kernel, sizes, tuple(pieces)), ou...  34.5 us
    sub x8, other arithmetic, adam_step(): weight - rate * (first_hat / (jnp.sqrt(second_hat) + epsilon) + weight_de...  16.8 us
    dot_general x6, matrix products, right_transposed(): lax.dot_general(left, right, (((1,), (1,)), ((), ())), preferred_element_...  15.9 us
    dot_general x5, matrix products, left_transposed(): lax.dot_general(left, right, (((0,), (0,)), ((), ())), preferred_element_...  15.5 us
  transfers between devices with their start and end apart: 7, of which 0 were waited for; matrix products, arithmetic and copies ran while one was open for 11% of the time, Pallas kernels for 20%

profile of v8, /device:TPU:0, one launch (start us, length us, event | category | flops | bytes accessed | tf_op | source)
XLA Modules:
  0.0 665.9 jit_solution(1077927535750871745)
XLA Ops:
  3.4 13.9 %shard_map.475 = (s32[32,2,640]{2,1,0:T(2,128)S(1)}, bf16[8,32,512]{2,1,0:T(8,128)(2,1)S(1)}) custom-call(s32[2,640]{1,0:T(2,128)S(1)} %fusion.125.row_ref, bf16[8,32,512]{2,1,0:T(8,128)(2,1)S(1)} %bitcast.205), custom_call_target="tpu_custom_call" | custom-call | tf_op jit(solution)/shard_map/pallas_call | solution.py:351
  23.0 2.5 convert_element_type.238
  27.9 5.1 fusion.21
  35.4 123.7 %shard_map.476 = (bf16[2,4,4,32,640]{4,3,2,1,0:T(8,128)(2,1)}, bf16[2,4,4,32,3072]{4,3,2,1,0:T(8,128)(2,1)}, bf16[2,4,4,32,1024]{4,3,2,1,0:T(8,128)(2,1)}, bf16[...) custom-call(bf16[32,640]{1,0:T(8,128)(2,1)} %maximum_maximum_fusion., ...), custom_call_target="tpu_custom_call" | custom-call | flops 99000000512 | bytes 330000000 | tf_op jit(solution)/shard_map/pallas_call | solution.py:622
  159.1 2.4 copy.143
  161.5 2.8 slice_convert_fusion
  167.4 7.0 %fusion.11 = f32[1024,1024]{1,0:T(8,128)} fusion(bf16[1536,1024]{1,0:T(8,128)(2,1)} %bitcast.293, s32[1024]{0:T(1024)S(1)} %get-tuple-element.553), kind=kOutput, calls=%fused_computation.32 | convolution fusion | flops 3222798336 | bytes 7344128 | tf_op jit(solution)/shard_map/dot_general | solution.py:32
  174.8 4.5 fusion.151
  181.5 5.0 fusion.150
  191.8 4.0 fusion.103
  198.2 8.8 %add_convert_fusion.k_ref.v_ref = bf16[1024,2048]{1,0:T(8,128)(2,1)} fusion(f32[2048]{0:T(1024)S(1)} %concatenate.23, bf16[1024,1024]{1,0:T(8,128)(2,1)S(1)} %get-tuple-element.516, bf16[1024,3072]{1,0:T(8,128)(2,1)} %bitcast.289), kind=kOutput, calls=%fused_computation.24 | convolution fusion | flops 4299161600 | bytes 10493952 | tf_op jit(solution)/shard_map/dot_general | solution.py:32
  208.7 2.8 fusion.60.q_ref
  211.4 8.1 %shard_map.477.refs_0_ = bf16[128,1024]{1,0:T(8,128)(2,1)} custom-call(s32[2]{0:T(128)} %get-tuple-element.521.lengths_ref, bf16[128,1024]{1,0:T(8,128)(2,1)} %fusion.60.q_ref, bf16[1024,2048]{1,0:T(8,128)(2,1)} %add_convert_fusion.k_ref.v_ref, bf16[1024,2048]{1,0:T(8,128)(2,1)} %add_convert_fusion.k_ref.v_ref), custom_call_target="tpu_custom_call" | custom-call | flops 7200000000 | bytes 24000000 | tf_op jit(solution)/shard_map/pallas_call | solution.py:1226
  222.2 14.4 %shard_map.478 = bf16[2,4,1,128,1024]{4,3,2,1,0:T(8,128)(2,1)S(1)} custom-call(bf16[128,1024]{1,0:T(8,128)(2,1)S(1)} %add_convert_fusion.4.refs_0_), custom_call_target="tpu_custom_call" | custom-call | flops 13500000256 | bytes 45000000 | tf_op jit(solution)/shard_map/pallas_call | solution.py:622
  236.6 6.5 fusion.30
  244.4 16.9 %shard_map.479 = f32[128,1024]{1,0:T(8,128)S(1)} custom-call(bf16[2,4,1,128,1024]{4,3,2,1,0:T(8,128)(2,1)S(1)} %bitcast.210), custom_call_target="tpu_custom_call" | custom-call | flops 13500000256 | bytes 45000000 | tf_op jit(solution)/shard_map/pallas_call | solution.py:819
  266.0 132.7 %shard_map.480 = (f32[128,1024]{1,0:T(8,128)}, f32[1024,1024]{1,0:T(8,128)}, f32[8,1024]{1,0:T(8,128)}, f32[32,8,128]{2,1,0:T(8,128)}) custom-call(bf16[128,1024]{1,0:T(8,128)(2,1)} %add_convert_fusion.2.refs_0_, bf16[1024,1024]{1,0:T(8,128)(2,1)} %copy-done.14, f32[1,1024]{1,0:T(1,128)} %bitcast.280, f32[32,8,128]{2,1,0:T(8,128)} %pad.20.refs_3_), custom_call_target="tpu_custom_call" | custom-call | tf_op jit(solution)/shard_map/pallas_call | solution.py:1125
  403.8 14.0 %shard_map.481 = bf16[2,4,1,128,1024]{4,3,2,1,0:T(8,128)(2,1)S(1)} custom-call(bf16[128,1024]{1,0:T(8,128)(2,1)S(1)} %get-tuple-element.508.refs_0_), custom_call_target="tpu_custom_call" | custom-call | flops 13500000256 | bytes 45000000 | tf_op jit(solution)/shard_map/pallas_call | solution.py:622
  424.4 17.5 %shard_map.482 = f32[128,1024]{1,0:T(8,128)S(1)} custom-call(bf16[2,4,1,128,1024]{4,3,2,1,0:T(8,128)(2,1)S(1)} %bitcast.209), custom_call_target="tpu_custom_call" | custom-call | flops 13500000256 | bytes 45000000 | tf_op jit(solution)/shard_map/pallas_call | solution.py:819
  443.8 2.7 collective-permute-start.5
  449.0 2.5 collective-permute-start.3
  453.7 11.1 %shard_map.483 = (bf16[128,1024]{1,0:T(8,128)(2,1)}, bf16[1024,1024]{1,0:T(8,128)(2,1)}, bf16[1024,1024]{1,0:T(8,128)(2,1)}) custom-call(s32[2]{0:T(128)} %get-tuple-element.521.lengths_ref, bf16[128,1024]{1,0:T(8,128)(2,1)} %fusion.60.q_ref, bf16[1024,2048]{1,0:T(8,128)(2,1)} %add_convert_fusion.k_ref.v_ref, ...), custom_call_target="tpu_custom_call" | custom-call | flops 9900000256 | bytes 33000000 | tf_op jit(solution)/shard_map/pallas_call | solution.py:1234
  464.8 2.7 fusion.56
  469.8 7.5 %multiply_reduce_fusion = (bf16[1024]{0:T(1024)(128)(2,1)S(1)}, f32[1024]{0:T(1024)S(1)}, f32[1024]{0:T(1024)S(1)}, bf16[1024]{0:T(1024)(128)(2,1)S(1)}, f32[1024,1024]{1,0:T(8,128)S(1)}) fusion(f32[1024,1024]{1,0:T(8,128)S(1)} %copy-done.7, f32[1024]{0:T(1024)S(1)} %add_rsqrt_fusion, f32[1024]{0:T(1024)S(1)} %broadcast_multiply_fusion.2, ...), kind=kOutput, calls=%fused_computation.41 | convolution fusion | flops 4313837568 | bytes 20996096 | tf_op jit(solution)/shard_map/dot_general | solution.py:42
  478.8 5.0 fusion.20
  485.9 3.9 reduce_sum.444
  490.3 4.4 concatenate.25
  502.8 111.4 %shard_map.484 = (f32[32,1024]{1,0:T(8,128)}, f32[32,1024]{1,0:T(8,128)}, f32[32,640]{1,0:T(8,128)}, f32[32,3072]{1,0:T(8,128)}, f32[8,1024]{1,0:T(8,128)}, /*in...) custom-call(bf16[128,1024]{1,0:T(8,128)(2,1)} %shard_map.477.refs_0_, bf16[128,1024]{1,0:T(8,128)(2,1)} %copy-done.31, ...), custom_call_target="tpu_custom_call" | custom-call | tf_op jit(solution)/shard_map/pallas_call | solution.py:948
  614.3 7.6 %fusion.48 = f32[1024,1024]{1,0:T(8,128)} fusion(f32[1024,1024]{1,0:T(8,128)S(1)} %copy-done.89, bf16[1536,1024]{1,0:T(8,128)(2,1)} %bitcast.288, s32[1536]{0:T(1024)S(1)} %copy-done.79), kind=kOutput, calls=%fused_computation.94 | convolution fusion | flops 3223846912 | bytes 11540480 | tf_op jit(solution)/shard_map/dot_general | solution.py:36
  622.1 3.8 multiply_reduce_fusion.3
  632.5 9.7 %shard_map.485 = f32[32,8,128]{2,1,0:T(8,128)S(1)} custom-call(f32[8,128]{1,0:T(8,128)S(1)} %maximum_bitcast_fusion.1.row_ref), custom_call_target="tpu_custom_call" | custom-call | tf_op jit(solution)/shard_map/pallas_call | solution.py:395
  646.7 10.2 %multiply_subtract_fusion = (f32[960,1024]{1,0:T(8,128)}, f32[960,1024]{1,0:T(8,128)}, f32[960,1024]{1,0:T(8,128)}) fusion(f32[960,1024]{1,0:T(8,128)} %param.36, f32[]{:T(128)S(6)} %div.260, f32[1024,1024]{1,0:T(8,128)} %get-tuple-element.283, f32[960,1024]{1,0:T(8,128)} %param.37, f32[960,1024]{1,0:T(8,128)} %param.38), kind=kLoop, calls=%fused_computation.55 | loop fusion | flops 15728640 | bytes 27525124 | tf_op jit(solution)/shard_map/sub | solution.py:1373
  (370 shorter events, 80.3 us)
Async XLA Ops:
  0.7 191.1 %copy-start = (s32[4,64]{1,0:T(4,128)S(1)}, s32[4,64]{1,0:T(4,128)}, u32[]{:S(2)}) copy-start(s32[4,64]{1,0:T(4,128)} %param.34) | copy-start | bytes 3076
  188.1 31.5 %collective-permute-start = (bf16[1024,512]{1,0:T(8,128)(2,1)}, bf16[1024,512]{1,0:T(8,128)(2,1)}, u32[]{:S(2)}, u32[]{:S(2)}) collective-permute-start(bf16[1024,512]{1,0:T(8,128)(2,1)} %get-tuple-element.523), channel_id=1, source_target_pairs={{0,16},{16,0},{1,17},{17,1},{2,18},{18,2},{3,19},{19,3},{4,20},{20... | collective-permute-start | bytes 3145736 | tf_op jit(solution)/shard_map/ppermute | solution.py:160
  195.8 12.9 %copy-start.29 = (bf16[128,1024]{1,0:T(8,128)(2,1)}, bf16[128,1024]{1,0:T(8,128)(2,1)S(1)}, u32[]{:S(2)}) copy-start(bf16[128,1024]{1,0:T(8,128)(2,1)S(1)} %bitcast_convert_fusion.refs_2_) | copy-start | bytes 786436
  196.6 10.4 %copy-start.86 = (s32[128]{0:T(128)}, s32[128]{0:T(128)S(1)}, u32[]{:S(2)}) copy-start(s32[128]{0:T(128)S(1)} %lt.211) | copy-start | bytes 1540
  198.2 9.7 %copy-start.76 = (f32[19,32]{1,0:T(8,128)S(1)}, f32[19,32]{1,0:T(8,128)}, u32[]{:S(2)}) copy-start(f32[19,32]{1,0:T(8,128)} %param.56) | copy-start | bytes 7300
  198.2 10.5 %copy-start.81 = (f32[1,1024]{1,0:T(1,128)S(1)}, f32[1,1024]{1,0:T(1,128)}, u32[]{:S(2)}) copy-start(f32[1,1024]{1,0:T(1,128)} %get-tuple-element.547) | copy-start | bytes 12292
  222.2 14.4 %copy-start.90 = (bf16[8,4,32,512]{3,2,1,0:T(8,128)(2,1)S(1)}, bf16[8,4,32,512]{3,2,1,0:T(8,128)(2,1)}, u32[]{:S(2)}) copy-start(bf16[8,4,32,512]{3,2,1,0:T(8,128)(2,1)} %get-tuple-element.271) | copy-start | bytes 3145732
  244.4 17.0 %copy-start.72 = (f32[1,1024]{1,0:T(1,128)S(1)}, f32[1,1024]{1,0:T(1,128)}, u32[]{:S(2)}) copy-start(f32[1,1024]{1,0:T(1,128)} %get-tuple-element.542) | copy-start | bytes 12292
  403.8 14.1 %copy-start.37 = (bf16[1024,512]{1,0:T(8,128)(2,1)S(1)}, bf16[1024,512]{1,0:T(8,128)(2,1)}, u32[]{:S(2)}) copy-start(bf16[1024,512]{1,0:T(8,128)(2,1)} %copy-done.36) | copy-start | bytes 3145732
  423.1 23.3 %copy-start.30 = (bf16[1024,512]{1,0:T(8,128)(2,1)}, bf16[1024,512]{1,0:T(8,128)(2,1)S(1)}, u32[]{:S(2)}) copy-start(bf16[1024,512]{1,0:T(8,128)(2,1)S(1)} %convolution_convert_fusion.2) | copy-start | bytes 3145732
  443.0 187.0 %collective-permute-start.4 = (bf16[128,1024]{1,0:T(8,128)(2,1)}, bf16[128,1024]{1,0:T(8,128)(2,1)}, u32[]{:S(2)}, u32[]{:S(2)}) collective-permute-start(bf16[128,1024]{1,0:T(8,128)(2,1)} %get-tuple-element.524), channel_id=1, source_target_pairs={{0,1},{1,2},{2,3},{3,0},{4,5},{5,6},{6,7},{7,4},{8,9},{9,10},{10,1... | collective-permute-start | bytes 786440 | tf_op jit(solution)/shard_map/ppermute | solution.py:1310
  443.8 186.2 %collective-permute-start.5 = (bf16[128,1024]{1,0:T(8,128)(2,1)}, bf16[128,1024]{1,0:T(8,128)(2,1)}, u32[]{:S(2)}, u32[]{:S(2)}) collective-permute-start(bf16[128,1024]{1,0:T(8,128)(2,1)} %get-tuple-element.526), channel_id=1, source_target_pairs={{0,2},{1,3},{2,0},{3,1},{4,6},{5,7},{6,4},{7,5},{8,10},{9,11},{10,... | collective-permute-start | bytes 786440 | tf_op jit(solution)/shard_map/ppermute | solution.py:1310
  447.3 51.9 %collective-permute-start.1 = (bf16[8,32,512]{2,1,0:T(8,128)(2,1)}, bf16[8,32,512]{2,1,0:T(8,128)(2,1)}, u32[]{:S(2)}, u32[]{:S(2)}) collective-permute-start(bf16[8,32,512]{2,1,0:T(8,128)(2,1)} %get-tuple-element.527), channel_id=1, source_target_pairs={{0,1},{1,2},{2,3},{3,0},{4,5},{5,6},{6,7},{7,4},{8,9},{9,10},{10,1... | collective-permute-start | bytes 786440 | tf_op jit(solution)/shard_map/ppermute | solution.py:1310
  448.2 52.5 %collective-permute-start.2 = (bf16[8,32,512]{2,1,0:T(8,128)(2,1)}, bf16[8,32,512]{2,1,0:T(8,128)(2,1)}, u32[]{:S(2)}, u32[]{:S(2)}) collective-permute-start(bf16[8,32,512]{2,1,0:T(8,128)(2,1)} %get-tuple-element.529), channel_id=1, source_target_pairs={{0,2},{1,3},{2,0},{3,1},{4,6},{5,7},{6,4},{7,5},{8,10},{9,11},{10,... | collective-permute-start | bytes 786440 | tf_op jit(solution)/shard_map/ppermute | solution.py:1310
  449.0 51.7 %collective-permute-start.3 = (bf16[8,32,512]{2,1,0:T(8,128)(2,1)}, bf16[8,32,512]{2,1,0:T(8,128)(2,1)}, u32[]{:S(2)}, u32[]{:S(2)}) collective-permute-start(bf16[8,32,512]{2,1,0:T(8,128)(2,1)} %get-tuple-element.528), channel_id=1, source_target_pairs={{0,3},{1,0},{2,1},{3,2},{4,7},{5,4},{6,5},{7,6},{8,11},{9,8},{10,9... | collective-permute-start | bytes 786440 | tf_op jit(solution)/shard_map/ppermute | solution.py:1310
  452.1 12.7 %copy-start.18 = (bf16[128,1024]{1,0:T(8,128)(2,1)}, bf16[128,1024]{1,0:T(8,128)(2,1)S(1)}, u32[]{:S(2)}) copy-start(bf16[128,1024]{1,0:T(8,128)(2,1)S(1)} %get-tuple-element.511.refs_3_) | copy-start | bytes 786436
  499.3 130.7 %collective-permute-start.6 = (bf16[128,1024]{1,0:T(8,128)(2,1)S(1)}, bf16[128,1024]{1,0:T(8,128)(2,1)S(1)}, u32[]{:S(2)}, u32[]{:S(2)}) collective-permute-start(bf16[128,1024]{1,0:T(8,128)(2,1)S(1)} %copy-done.51), channel_id=1, source_target_pairs={{0,3},{1,0},{2,1},{3,2},{4,7},{5,4},{6,5},{7,6},{8,11},{9,8},{10,9... | collective-permute-start | bytes 786440 | tf_op jit(solution)/shard_map/ppermute | solution.py:1310
  502.8 111.4 %copy-start.79 = (s32[1536]{0:T(1024)S(1)}, s32[1536]{0:T(1024)}, u32[]{:S(2)}) copy-start(s32[1536]{0:T(1024)} %copy-done.78) | copy-start | bytes 18436
  502.8 111.4 %copy-start.89 = (f32[1024,1024]{1,0:T(8,128)S(1)}, f32[1024,1024]{1,0:T(8,128)}, u32[]{:S(2)}) copy-start(f32[1024,1024]{1,0:T(8,128)} %get-tuple-element.274) | copy-start | bytes 12582916
  625.9 17.9 %copy-start.61 = (f32[32,640]{1,0:T(8,128)S(1)}, f32[32,640]{1,0:T(8,128)}, u32[]{:S(2)}) copy-start(f32[32,640]{1,0:T(8,128)} %get-tuple-element.288) | copy-start | bytes 245764
  625.9 17.9 %copy-start.62 = (f32[19,32]{0,1:T(8,128)S(1)}, f32[19,32]{0,1:T(8,128)}, u32[]{:S(2)}) copy-start(f32[19,32]{0,1:T(8,128)} %copy.155) | copy-start | bytes 7300
  625.9 17.9 %copy-start.63 = (f32[19,32]{0,1:T(8,128)S(1)}, f32[19,32]{0,1:T(8,128)}, u32[]{:S(2)}) copy-start(f32[19,32]{0,1:T(8,128)} %copy.151) | copy-start | bytes 7300
  625.9 17.9 %copy-start.64 = (f32[19,32]{0,1:T(8,128)S(1)}, f32[19,32]{0,1:T(8,128)}, u32[]{:S(2)}) copy-start(f32[19,32]{0,1:T(8,128)} %copy.153) | copy-start | bytes 7300
  629.9 16.1 %copy-start.53 = (f32[512,32]{0,1:T(8,128)S(1)}, f32[512,32]{0,1:T(8,128)}, u32[]{:S(2)}) copy-start(f32[512,32]{0,1:T(8,128)} %param.39) | copy-start | bytes 196612
  629.9 16.1 %copy-start.66 = (f32[512,32]{0,1:T(8,128)S(1)}, f32[512,32]{0,1:T(8,128)}, u32[]{:S(2)}) copy-start(f32[512,32]{0,1:T(8,128)} %param.40) | copy-start | bytes 196612
  629.9 16.1 %copy-start.67 = (f32[512,32]{0,1:T(8,128)S(1)}, f32[512,32]{0,1:T(8,128)}, u32[]{:S(2)}) copy-start(f32[512,32]{0,1:T(8,128)} %param.41) | copy-start | bytes 196612
  646.7 10.2 %copy-start.47 = (f32[30522]{0:T(1024)S(1)}, f32[30522]{0:T(1024)}, u32[]{:S(2)}) copy-start(f32[30522]{0:T(1024)} %param.57) | copy-start | bytes 366268
  646.7 10.2 %copy-start.59 = (f32[30522]{0:T(1024)S(1)}, f32[30522]{0:T(1024)}, u32[]{:S(2)}) copy-start(f32[30522]{0:T(1024)} %param.58) | copy-start | bytes 366268
  646.7 10.2 %copy-start.60 = (f32[30522]{0:T(1024)S(1)}, f32[30522]{0:T(1024)}, u32[]{:S(2)}) copy-start(f32[30522]{0:T(1024)} %param.59) | copy-start | bytes 366268
  646.7 11.1 %copy-start.25 = (f32[128,1024]{1,0:T(8,128)S(1)}, f32[128,1024]{1,0:T(8,128)}, u32[]{:S(2)}) copy-start(f32[128,1024]{1,0:T(8,128)} %param.51) | copy-start | bytes 1572868
  646.7 11.1 %copy-start.42 = (f32[128,1024]{1,0:T(8,128)S(1)}, f32[128,1024]{1,0:T(8,128)}, u32[]{:S(2)}) copy-start(f32[128,1024]{1,0:T(8,128)} %param.52) | copy-start | bytes 1572868
  646.7 11.1 %copy-start.43 = (f32[128,1024]{1,0:T(8,128)S(1)}, f32[128,1024]{1,0:T(8,128)}, u32[]{:S(2)}) copy-start(f32[128,1024]{1,0:T(8,128)} %param.53) | copy-start | bytes 1572868
  (70 other events, 271.2 us)
